TPU v7x, 32 devices: a whole 2x2x4 slice. The times are simulated.
32 devices in a mesh: leaf: 8 (over y, x, core), col: 4 (over z).
Axes of the slice: x: 2, y: 2, z: 4, core: 2. Of those that a mesh axis runs over, the one named last changes fastest.
Arguments:
- right_sides: float32 [256, 16384], P('col', 'leaf'), may hold values from -6 to 6
- inverse_first: float32 [32, 128, 128], P('leaf'), may hold values from -0.5 to 0.5
- coupling_first: float32 [32, 3, 128, 128], P('leaf'), may hold values from -0.3125 to 0.3125
- links_first: int32 [32, 3], P('leaf'), may hold values from 0 to 11, as said below
- order_first: int32 [8, 12], P('leaf'), may hold values from 0 to 11, as said below
- inverse_second: float32 [32, 128, 128], P('leaf'), may hold values from -0.5 to 0.5
- coupling_second: float32 [32, 3, 128, 128], P('leaf'), may hold values from -0.3125 to 0.3125
- links_second: int32 [32, 3], P('leaf'), may hold values from 0 to 7, as said below
- order_second: int32 [8, 8], P('leaf'), may hold values from 0 to 7, as said below
- inverse_third: float32 [32, 128, 128], P('leaf'), may hold values from -0.5 to 0.5
- coupling_third: float32 [32, 3, 128, 128], P('leaf'), may hold values from -0.3125 to 0.3125
- links_third: int32 [32, 3], P('leaf'), may hold values from 0 to 3, as said below
- order_third: int32 [8, 4], P('leaf'), may hold values from 0 to 3, as said below
- front_rows: int32 [3, 8], P(None, 'leaf'), may hold values from 128 to 512
- root_inverse: float32 [2, 2048, 2048], P(None, 'leaf', 'col'), may hold values from -0.125 to 0.125
- root_coupling: float32 [2048, 2048], P('leaf', 'col'), may hold values from -0.125 to 0.125
Outputs:
- solved_first: float32 [256, 4096], P('col', 'leaf')
- solved_second: float32 [256, 4096], P('col', 'leaf')
- solved_third: float32 [256, 4096], P('col', 'leaf')
- root_solution: float32 [256, 2, 2048], P('col', None, 'leaf')
Inputs may be any that keep to these rules, and one draw needn't show every extreme that they name: `links_first`: each row names 3 different skeleton blocks of its front. `links_second`: each row names 3 different skeleton blocks of its front. `links_third`: each row names 3 different skeleton blocks of its front. `order_first`: each row is a permutation. `order_second`: each row is a permutation. `order_third`: each row is a permutation.
All inputs are finite; a program needn't handle non-finite values.
Results may differ from a plain program's by a relative error of at most 0.0003.
Values sent between devices are 32-bit elements; how exact they have to be, the bound alone decides.
No kernel may reach another device: no remote copies, remote signals or barrier semaphores. Data moves between devices by JAX's collectives and lax.ppermute only.
A program may use at most 64 MiB of HBM per device.

v0:
```python
import jax
import jax.numpy as jnp
from jax import lax
from jax.sharding import PartitionSpec as P


def partner(block, axis, stride):
    count = lax.axis_size(axis)
    route = []
    for low in range(count):
        high = low | 1 << stride
        if high != low and high < count:
            route += [(low, high), (high, low)]
    return lax.ppermute(block, axis, route)


def eliminate(section, inverse, coupling, link_ids, live_count):
    block_rows = inverse.shape[-1]
    red_blocks = inverse.shape[0]
    link_total = coupling.shape[1]
    rhs_rows = section.shape[0]
    skeleton_count = section.shape[1] // block_rows - red_blocks
    redundant = section[:, : red_blocks * block_rows].reshape(rhs_rows, red_blocks, block_rows)
    positions = lax.broadcasted_iota(
        jnp.int32, (red_blocks, block_rows), 0
    ) * block_rows + lax.broadcasted_iota(jnp.int32, (red_blocks, block_rows), 1)
    live_rows = (positions < live_count).astype(jnp.float32)
    solved = (
        jnp.einsum("rib,iba->ria", redundant * live_rows, inverse, precision=lax.Precision.HIGHEST)
        * live_rows
    )
    pushed = jnp.einsum("ria,ikab->rikb", solved, coupling, precision=lax.Precision.HIGHEST)
    targets = (
        link_ids[:, :, None]
        == lax.broadcasted_iota(jnp.int32, (red_blocks, link_total, skeleton_count), 2)
    ).astype(jnp.float32)
    update = jnp.einsum("rikb,iks->rsb", pushed, targets, precision=lax.Precision.HIGHEST)
    skeleton = (
        section[:, red_blocks * block_rows :].reshape(rhs_rows, skeleton_count, block_rows) - update
    )
    return (solved.reshape(rhs_rows, red_blocks * block_rows), skeleton)


def join_halves(skeleton, level_index):
    half_blocks = skeleton.shape[1] // 2
    upper_half = lax.axis_index("leaf") >> level_index & 1
    kept_half = lax.dynamic_slice_in_dim(skeleton, upper_half * half_blocks, half_blocks, 1)
    sent_half = lax.dynamic_slice_in_dim(skeleton, (1 - upper_half) * half_blocks, half_blocks, 1)
    received = partner(sent_half, "leaf", level_index)
    return jnp.where(
        upper_half == 0,
        jnp.concatenate([kept_half, received], 1),
        jnp.concatenate([received, kept_half], 1),
    )


def spread_columns(values):
    return lax.all_gather(values, "col", axis=0, tiled=True)


def spread_leaf(values):
    return lax.all_gather(values, "leaf", axis=0, tiled=True)


def to_leaf_rows(values):
    full_rows = lax.all_gather(values, "col", axis=1, tiled=True)
    return lax.all_to_all(full_rows, "leaf", split_axis=1, concat_axis=0, tiled=True)


def to_column_rows(values):
    full_rows = lax.all_gather(values, "leaf", axis=1, tiled=True)
    return lax.all_to_all(full_rows, "col", split_axis=1, concat_axis=0, tiled=True)


def forward_product(values, matrix):
    return lax.psum_scatter(
        jnp.dot(
            values, matrix, precision=lax.Precision.HIGHEST, preferred_element_type=jnp.float32
        ),
        "leaf",
        scatter_dimension=0,
        tiled=True,
    )


def backward_product(values, matrix):
    return lax.psum_scatter(
        lax.dot_general(
            values,
            matrix,
            (((1,), (1,)), ((), ())),
            precision=lax.Precision.HIGHEST,
            preferred_element_type=jnp.float32,
        ),
        "col",
        scatter_dimension=0,
        tiled=True,
    )


def local(
    right_sides,
    inverse_first,
    coupling_first,
    links_first,
    order_first,
    inverse_second,
    coupling_second,
    links_second,
    order_second,
    inverse_third,
    coupling_third,
    links_third,
    order_third,
    front_rows,
    root_inverse,
    root_coupling,
):
    level_data = (
        (inverse_first, coupling_first, links_first, order_first),
        (inverse_second, coupling_second, links_second, order_second),
        (inverse_third, coupling_third, links_third, order_third),
    )
    section = right_sides
    outputs = []
    for level_index in range(3):
        inverse, coupling, link_ids, order_map = level_data[level_index]
        solved, skeleton = eliminate(
            section, inverse, coupling, link_ids, front_rows[level_index, 0]
        )
        outputs.append(solved)
        if level_index < 2:
            skeleton = join_halves(skeleton, level_index)
        skeleton = jnp.take(skeleton, order_map[0], axis=1)
        section = skeleton.reshape(skeleton.shape[0], -1)
    rhs_rows = right_sides.shape[0]
    panel_count = root_inverse.shape[0]
    panel_rows = root_inverse.shape[1]
    root_rhs = section.reshape(rhs_rows, panel_count, panel_rows)
    full_rhs = spread_columns(root_rhs)
    first_solve = forward_product(full_rhs[:, 0], root_inverse[0])
    coupled = forward_product(to_leaf_rows(first_solve), root_coupling)
    second_solve = forward_product(full_rhs[:, 1] - to_leaf_rows(coupled), root_inverse[1])
    forward_both = spread_leaf(jnp.stack([first_solve, second_solve], 1))
    last_panel = backward_product(forward_both[:, 1], root_inverse[1])
    back_coupled = backward_product(to_column_rows(last_panel), root_coupling)
    first_panel = backward_product(
        forward_both[:, 0] - to_column_rows(back_coupled), root_inverse[0]
    )
    root_solution = jnp.stack([first_panel, last_panel], 1)
    return (outputs[0], outputs[1], outputs[2], root_solution)


def solution(mesh):
    in_specs = (
        P("col", "leaf"),
        P("leaf", None, None),
        P("leaf", None, None, None),
        P("leaf", None),
        P("leaf", None),
        P("leaf", None, None),
        P("leaf", None, None, None),
        P("leaf", None),
        P("leaf", None),
        P("leaf", None, None),
        P("leaf", None, None, None),
        P("leaf", None),
        P("leaf", None),
        P(None, "leaf"),
        P(None, "leaf", "col"),
        P("leaf", "col"),
    )
    out_specs = (P("col", "leaf"), P("col", "leaf"), P("col", "leaf"), P("col", None, "leaf"))
    return jax.shard_map(local, mesh=mesh, in_specs=in_specs, out_specs=out_specs, check_vma=False)
```

profile of v0, /device:TPU:0, one launch (start us, length us, event | category | flops | bytes accessed | tf_op | source)
XLA Modules:
  0.0 356.1 jit_solution(9245771753027586853)
XLA Ops:
  7.3 0.7 copy-done.12
  8.0 0.6 fusion.51
  8.5 0.1 copy.70
  8.6 1.0 slice-done
  9.7 2.1 fusion.45
  11.8 0.4 convolution_multiply_fusion.2
  12.2 0.6 convolution_bitcast_fusion.3
  12.8 0.8 fusion
  13.7 0.5 collective-permute-start
  14.2 0.7 copy-done.16
  14.9 0.6 copy-done.17
  15.6 0.5 broadcast.169
  16.1 0.1 copy-done.18
  16.2 0.7 reduce.3
  17.2 0.5 copy-done.14
  17.8 0.1 copy.76
  17.9 0.1 maximum_select_fusion
  18.0 0.1 copy.72
  18.2 0.6 gather_fusion
  19.0 0.9 copy-done.8
  19.9 0.4 convolution_multiply_fusion.1
  20.3 0.6 convolution_bitcast_fusion.2
  20.9 0.8 fusion.1
  21.8 2.6 collective-permute-start.1
  24.4 0.7 copy-done.15
  25.1 0.1 copy.82
  25.2 3.4 collective-permute-done.1
  28.5 0.1 maximum_select_fusion.1
  28.7 0.6 gather_fusion.1
  29.5 0.8 copy-done.9
  30.2 0.4 convolution_multiply_fusion
  30.6 0.6 convolution_bitcast_fusion.1
  31.3 0.7 fusion.2
  32.0 0.6 gather_fusion.2
  32.6 0.1 copy.85
  32.7 0.1 gather.23
  32.9 16.3 %all_gather.18 = f32[256,2,256]{2,1,0:T(2,128)S(1)} all-gather(f32[64,2,256]{2,1,0:T(2,128)S(1)} %broadcast_select_fusion), channel_id=1, replica_groups=mesh['leaf'=8,'col'=4] {'col'}, dimensions={0}, use_global_device_ids=true | all-gather | bytes 655360 | tf_op jit(solution)/shard_map/all_gather | solution.py:58
  49.1 0.4 fusion.49
  49.5 1.4 fusion.11
  51.0 36.0 %reduce-scatter.7.cloned.1.call-done = f32[32,512]{1,0:T(8,128)} async-done(((f32[256,512]{1,0:T(8,128)}), f32[32,512]{1,0:T(8,128)}) %reduce-scatter.7.cloned.1.call-update) | async-done | bytes 65552 | tf_op jit(solution)/shard_map/reduce_scatter | solution.py:76
  87.0 14.2 %all_gather.19 = f32[32,2048]{1,0:T(8,128)S(1)} all-gather(f32[32,512]{1,0:T(8,128)} %reduce-scatter.7.cloned.1.call-done), channel_id=1, replica_groups=mesh['leaf'=8,'col'=4] {'col'}, dimensions={1}, use_global_device_ids=true | all-gather | bytes 327680 | tf_op jit(solution)/shard_map/all_gather | solution.py:66
  101.2 9.7 %all_to_all.76 = f32[32,8,256]{2,0,1:T(8,128)S(1)} all-to-all(f32[32,8,256]{2,0,1:T(8,128)S(1)} %bitcast.203), channel_id=1, replica_groups=mesh['leaf'=8,'col'=4] {'leaf'}, dimensions={1} | all-to-all | bytes 524288 | tf_op jit(solution)/shard_map/all_to_all | solution.py:67
  110.9 1.4 fusion.52
  112.4 33.7 %reduce-scatter.9.cloned.1.call-done = f32[32,512]{1,0:T(8,128)} async-done(((f32[256,512]{1,0:T(8,128)}), f32[32,512]{1,0:T(8,128)}) %reduce-scatter.9.cloned.1.call-update) | async-done | bytes 65552 | tf_op jit(solution)/shard_map/reduce_scatter | solution.py:76
  146.1 14.1 %all_gather.20 = f32[32,2048]{1,0:T(8,128)S(1)} all-gather(f32[32,512]{1,0:T(8,128)} %reduce-scatter.9.cloned.1.call-done), channel_id=1, replica_groups=mesh['leaf'=8,'col'=4] {'col'}, dimensions={1}, use_global_device_ids=true | all-gather | bytes 327680 | tf_op jit(solution)/shard_map/all_gather | solution.py:66
  160.3 9.5 %all_to_all.77 = f32[32,8,256]{2,0,1:T(8,128)S(1)} all-to-all(f32[32,8,256]{2,0,1:T(8,128)S(1)} %bitcast.204), channel_id=1, replica_groups=mesh['leaf'=8,'col'=4] {'leaf'}, dimensions={1} | all-to-all | bytes 524288 | tf_op jit(solution)/shard_map/all_to_all | solution.py:67
  169.8 1.5 fusion.8
  171.3 33.7 %reduce-scatter.11.cloned.1.call-done = f32[32,512]{1,0:T(8,128)} async-done(((f32[256,512]{1,0:T(8,128)}), f32[32,512]{1,0:T(8,128)}) %reduce-scatter.11.cloned.1.call-update) | async-done | bytes 65552 | tf_op jit(solution)/shard_map/reduce_scatter | solution.py:76
  205.0 1.5 pad_maximum_fusion
  206.6 24.5 %all-gather.2.cloned.1.call-done = f32[256,2,512]{2,0,1:T(8,128)} async-done(((f32[32,2,512]{2,0,1:T(8,128)}), f32[256,2,512]{2,0,1:T(8,128)}) %all-gather.2.cloned.1.call-update) | async-done | bytes 1048592 | tf_op jit(solution)/shard_map/all_gather | solution.py:62
  231.1 2.4 fusion.3
  233.5 19.7 %reduce-scatter.13.cloned.1.call-done = f32[64,256]{1,0:T(8,128)} async-done(((f32[256,256]{1,0:T(8,128)}), f32[64,256]{1,0:T(8,128)}) %reduce-scatter.13.cloned.1.call-update) | async-done | bytes 65552 | tf_op jit(solution)/shard_map/reduce_scatter | solution.py:87
  253.2 10.2 %all_gather.22 = f32[64,2048]{1,0:T(8,128)S(1)} all-gather(f32[64,256]{1,0:T(8,128)} %reduce-scatter.13.cloned.1.call-done), channel_id=1, replica_groups=mesh['leaf'=8,'col'=4] {'leaf'}, dimensions={1}, use_global_device_ids=true | all-gather | bytes 589824 | tf_op jit(solution)/shard_map/all_gather | solution.py:71
  263.4 17.7 %all_to_all.78 = f32[64,4,512]{2,0,1:T(8,128)S(1)} all-to-all(f32[64,4,512]{2,0,1:T(8,128)S(1)} %bitcast.194), channel_id=1, replica_groups=mesh['leaf'=8,'col'=4] {'col'}, dimensions={1} | all-to-all | bytes 1048576 | tf_op jit(solution)/shard_map/all_to_all | solution.py:72
  281.1 1.3 fusion.53
  282.5 17.9 %reduce-scatter.15.cloned.1.call-done = f32[64,256]{1,0:T(8,128)} async-done(((f32[256,256]{1,0:T(8,128)}), f32[64,256]{1,0:T(8,128)}) %reduce-scatter.15.cloned.1.call-update) | async-done | bytes 65552 | tf_op jit(solution)/shard_map/reduce_scatter | solution.py:87
  300.4 10.1 %all_gather.23 = f32[64,2048]{1,0:T(8,128)S(1)} all-gather(f32[64,256]{1,0:T(8,128)} %reduce-scatter.15.cloned.1.call-done), channel_id=1, replica_groups=mesh['leaf'=8,'col'=4] {'leaf'}, dimensions={1}, use_global_device_ids=true | all-gather | bytes 589824 | tf_op jit(solution)/shard_map/all_gather | solution.py:71
  310.6 17.8 %all_to_all.79 = f32[64,4,512]{2,0,1:T(8,128)S(1)} all-to-all(f32[64,4,512]{2,0,1:T(8,128)S(1)} %bitcast.197), channel_id=1, replica_groups=mesh['leaf'=8,'col'=4] {'col'}, dimensions={1} | all-to-all | bytes 1048576 | tf_op jit(solution)/shard_map/all_to_all | solution.py:72
  328.4 1.3 fusion.5
  329.7 0.7 copy_bitcast_fusion.6
  330.4 0.7 copy_bitcast_fusion.4
  331.1 16.5 %reduce-scatter.17.cloned.1.call-done = f32[64,256]{1,0:T(8,128)} async-done(((f32[256,256]{1,0:T(8,128)}), f32[64,256]{1,0:T(8,128)}) %reduce-scatter.17.cloned.1.call-update) | async-done | bytes 65552 | tf_op jit(solution)/shard_map/reduce_scatter | solution.py:87
  347.7 0.8 pad_maximum_fusion.1
  348.5 0.8 copy.91
  (84 shorter events, 1.6 us)
Async XLA Ops:
  7.2 5.0 %copy-start = (f32[4,3,128,128]{3,2,1,0:T(8,128)S(1)}, f32[4,3,128,128]{3,2,1,0:T(8,128)}, u32[]{:S(2)}) copy-start(f32[4,3,128,128]{3,2,1,0:T(8,128)} %param.18) | copy-start | bytes 2359300
  7.2 79.9 %reduce-scatter.7.cloned.1.call-start = ((), (), s32[]{:S(2)}) async-start(), calls=%async_computation.10 | async-start | bytes 589824 | tf_op jit(solution)/shard_map/reduce_scatter | solution.py:76
  7.2 0.7 copy-start.12
  7.2 1.3 copy-start.13
  8.6 1.0 slice-start
  9.6 2.2 copy-start.3
  9.6 2.2 copy-start.7
  13.7 4.1 %collective-permute-start = (f32[64,6,128]{2,1,0:T(8,128)S(1)}, f32[64,6,128]{2,1,0:T(8,128)S(1)}, u32[]{:S(2)}, u32[]{:S(2)}) collective-permute-start(f32[64,6,128]{2,1,0:T(8,128)S(1)} %get-tuple-element.23), channel_id=1, source_target_pairs={{0,4},{4,0},{8,12},{12,8},{16,20},{20,16},{24,28},{28,24},{1,5},{5... | collective-permute-start | bytes 589832 | tf_op jit(solution)/shard_map/ppermute | solution.py:14
  14.2 0.7 copy-start.16
  14.9 0.7 copy-start.17
  15.6 0.7 copy-start.18
  17.1 0.7 copy-start.14
  18.8 1.4 copy-start.5
  18.9 1.0 copy-start.8
  21.8 6.7 %collective-permute-start.1 = (f32[64,4,128]{2,1,0:T(4,128)S(1)}, f32[64,4,128]{2,1,0:T(4,128)S(1)}, u32[]{:S(2)}, u32[]{:S(2)}) collective-permute-start(f32[64,4,128]{2,1,0:T(4,128)S(1)} %get-tuple-element.27), channel_id=1, source_target_pairs={{0,8},{8,0},{4,12},{12,4},{16,24},{24,16},{20,28},{28,20},{1,9},{9... | collective-permute-start | bytes 393224 | tf_op jit(solution)/shard_map/ppermute | solution.py:14
  24.4 0.7 copy-start.15
  29.3 1.0 copy-start.9
  29.3 1.3 copy-start.6
  32.8 16.7 %copy-start.1 = (f32[2,256,512]{2,1,0:T(8,128)S(1)}, f32[2,256,512]{2,1,0:T(8,128)}, u32[]{:S(2)}) copy-start(f32[2,256,512]{2,1,0:T(8,128)} %param.30) | copy-start | bytes 3145732
  51.0 95.1 %reduce-scatter.9.cloned.1.call-start = ((), (), s32[]{:S(2)}) async-start(), calls=%async_computation.11 | async-start | bytes 589824 | tf_op jit(solution)/shard_map/reduce_scatter | solution.py:76
  101.2 9.7 %copy-start.2 = (f32[256,512]{1,0:T(8,128)S(1)}, f32[256,512]{1,0:T(8,128)}, u32[]{:S(2)}) copy-start(f32[256,512]{1,0:T(8,128)} %param.31) | copy-start | bytes 1572868
  112.4 92.7 %reduce-scatter.11.cloned.1.call-start = ((), (), s32[]{:S(2)}) async-start(), calls=%async_computation.12 | async-start | bytes 589824 | tf_op jit(solution)/shard_map/reduce_scatter | solution.py:76
  171.2 33.8 %copy-start.11 = (f32[32,512]{1,0:T(8,128)S(1)}, f32[32,512]{1,0:T(8,128)}, u32[]{:S(2)}) copy-start(f32[32,512]{1,0:T(8,128)} %reduce-scatter.7.cloned.1.call-done) | copy-start | bytes 196612
  171.2 59.8 %all-gather.2.cloned.1.call-start = ((), (), s32[]{:S(2)}) async-start(), calls=%async_computation.13 | async-start | bytes 1179648 | tf_op jit(solution)/shard_map/all_gather | solution.py:62
  206.6 46.6 %reduce-scatter.13.cloned.1.call-start = ((), (), s32[]{:S(2)}) async-start(), calls=%async_computation.14 | async-start | bytes 327680 | tf_op jit(solution)/shard_map/reduce_scatter | solution.py:87
  233.5 66.9 %reduce-scatter.15.cloned.1.call-start = ((), (), s32[]{:S(2)}) async-start(), calls=%async_computation.15 | async-start | bytes 327680 | tf_op jit(solution)/shard_map/reduce_scatter | solution.py:87
  282.5 65.2 %reduce-scatter.17.cloned.1.call-start = ((), (), s32[]{:S(2)}) async-start(), calls=%async_computation.16 | async-start | bytes 327680 | tf_op jit(solution)/shard_map/reduce_scatter | solution.py:87
  310.5 17.9 %copy-start.4 = (f32[256,2,512]{2,0,1:T(8,128)S(1)}, f32[256,2,512]{2,0,1:T(8,128)}, u32[]{:S(2)}) copy-start(f32[256,2,512]{2,0,1:T(8,128)} %all-gather.2.cloned.1.call-done) | copy-start | bytes 3145732
  330.4 17.3 %copy-start.10 = (f32[64,256]{1,0:T(8,128)S(1)}, f32[64,256]{1,0:T(8,128)}, u32[]{:S(2)}) copy-start(f32[64,256]{1,0:T(8,128)} %reduce-scatter.13.cloned.1.call-done) | copy-start | bytes 196612
Sparse Core Ops, SparseCore 0:
  51.1 35.8 reduce-scatter.6
  112.5 33.5 reduce-scatter.8
  171.4 33.6 reduce-scatter.10
  207.5 23.5 all-gather.1
  233.6 19.5 reduce-scatter.12
  282.6 17.7 reduce-scatter.14
  329.9 17.7 reduce-scatter.16
where the time goes:
time: 357 us; the launch traced here: 356 us
  waiting for transfers between devices  185 us (52%)
  blocking collectives  120 us (34%)
  matrix products  14.7 us (4%)
  between operations  14.6 us (4%)
  local copies, waits for them, and re-layouts  13 us (4%)
  other arithmetic  5.52 us (2%)
    reduce_scatter x3, waiting for transfers between devices, forward_product(): lax.psum_scatter(jnp.dot(values, matrix, precision=lax.Precision.HIGHEST,...  103 us
    reduce_scatter x3, waiting for transfers between devices, backward_product(): lax.psum_scatter(lax.dot_general(values, matrix, (((1,), (1,)), ((), ()))...  54.1 us
    all_to_all x2, blocking collectives, to_column_rows(): lax.all_to_all(full_rows, 'col', split_axis=1, concat_axis=0, tiled=True)  35.5 us
    all_gather x2, blocking collectives, to_leaf_rows(): full_rows = lax.all_gather(values, 'col', axis=1, tiled=True)  28.3 us
    all_gather x1, waiting for transfers between devices, spread_leaf(): return lax.all_gather(values, 'leaf', axis=0, tiled=True)  24.5 us
    all_gather x2, blocking collectives, to_column_rows(): full_rows = lax.all_gather(values, 'leaf', axis=1, tiled=True)  20.3 us
    all_to_all x2, blocking collectives, to_leaf_rows(): lax.all_to_all(full_rows, 'leaf', split_axis=1, concat_axis=0, tiled=True)  19.2 us
    all_gather x1, blocking collectives, spread_columns(): return lax.all_gather(values, 'col', axis=0, tiled=True)  16.3 us
  transfers between devices with their start and end apart: 9, of which 8 were waited for; matrix products, arithmetic and copies ran while one was open for 1% of the time, Pallas kernels for 0%

commit v1 on v0

--- a/solution.py
+++ b/solution.py
@@ -1,6 +1,10 @@
+import functools
+
 import jax
 import jax.numpy as jnp
 from jax import lax
+from jax.experimental import pallas as pl
+from jax.experimental.pallas import tpu as pltpu
 from jax.sharding import PartitionSpec as P
 
 
@@ -95,6 +99,246 @@
         "col",
         scatter_dimension=0,
         tiled=True,
+    )
+
+
+def root_wide(section, root_inverse, root_coupling):
+    rhs_rows = section.shape[0]
+    panel_count = root_inverse.shape[0]
+    panel_rows = root_inverse.shape[1]
+    root_rhs = section.reshape(rhs_rows, panel_count, panel_rows)
+    full_rhs = spread_columns(root_rhs)
+    first_solve = forward_product(full_rhs[:, 0], root_inverse[0])
+    coupled = forward_product(to_leaf_rows(first_solve), root_coupling)
+    second_solve = forward_product(full_rhs[:, 1] - to_leaf_rows(coupled), root_inverse[1])
+    forward_both = spread_leaf(jnp.stack([first_solve, second_solve], 1))
+    last_panel = backward_product(forward_both[:, 1], root_inverse[1])
+    back_coupled = backward_product(to_column_rows(last_panel), root_coupling)
+    first_panel = backward_product(
+        forward_both[:, 0] - to_column_rows(back_coupled), root_inverse[0]
+    )
+    root_solution = jnp.stack([first_panel, last_panel], 1)
+    return root_solution
+
+
+def flip(block, axis, distance):
+    count = lax.axis_size(axis)
+    return lax.ppermute(block, axis, [(i, i ^ distance) for i in range(count)])
+
+
+def swap_columns(parts):
+    return [parts[0]] + [flip(parts[e], "col", e) for e in range(1, len(parts))]
+
+
+def kernel_call(body, out_shapes, *operands):
+    spec = pl.BlockSpec(memory_space=pltpu.VMEM)
+    smem = pl.BlockSpec(memory_space=pltpu.SMEM)
+    return pl.pallas_call(
+        body,
+        out_shape=[jax.ShapeDtypeStruct(s, d) for s, d in out_shapes],
+        in_specs=[smem] + [spec] * (len(operands) - 1),
+        out_specs=[spec] * len(out_shapes),
+        compiler_params=pltpu.CompilerParams(vmem_limit_bytes=40 * 1024 * 1024),
+    )(*operands)
+
+
+def halves(values):
+    high = values.astype(jnp.bfloat16)
+    return high, (values - high.astype(jnp.float32)).astype(jnp.bfloat16)
+
+
+def product(values, high, low, contract):
+    rows = values.shape[0]
+    own_high, own_low = halves(values)
+    dims = (((1,), (contract,)), ((), ()))
+    both = lax.dot_general(
+        jnp.concatenate([own_high, own_low], 0), high, dims, preferred_element_type=jnp.float32
+    )
+    cross = lax.dot_general(own_high, low, dims, preferred_element_type=jnp.float32)
+    return both[:rows] + both[rows:] + cross
+
+
+def regroup(values, distance, parts):
+    if distance == 0:
+        return values
+    size = values.shape[0] // parts
+    return jnp.concatenate(
+        [values[(d ^ distance) * size : (d ^ distance) * size + size] for d in range(parts)], 0
+    )
+
+
+def span(index, size):
+    return pl.ds(pl.multiple_of(index * size, size), size)
+
+
+def assemble_kernel(place, *refs):
+    pieces, (high, low) = refs[:-2], refs[-2:]
+    leaf = place[0]
+    offset = 0
+    for (distance, start), piece in zip(PIECES, pieces, strict=True):
+        rows = piece.shape[0]
+        block_rows = pieces[0].shape[0]
+        first = (leaf ^ distance) * block_rows + start * rows
+        where = pl.ds(pl.multiple_of(first, rows), rows)
+        part_high, part_low = halves(piece[...])
+        high[where, :] = part_high
+        low[where, :] = part_low
+
+
+PIECES = tuple(
+    (plane | core, start) for core in (0, 1) for plane, start in ((0, 0), (2, 0), (4, 0), (6, 0), (6, 1))
+)
+
+
+def spread_matrix(place, block):
+    half = block.shape[0] // 2
+    near = flip(block, "leaf", 2)
+    far = flip(block, "leaf", 4)
+    pieces = [block, near, far, flip(near[:half], "leaf", 4), flip(far[half:], "leaf", 2)]
+    pieces += [flip(piece, "leaf", 1) for piece in pieces]
+    shape = (block.shape[0] * lax.axis_size("leaf"), block.shape[1])
+    return kernel_call(assemble_kernel, [(shape, jnp.bfloat16)] * 2, place, *pieces)
+
+
+def arrange_kernel(place, values, *parts):
+    leaf_count, _, rows, width = values.shape
+    total = leaf_count * width
+    own_width = parts[0].shape[1] - total
+    fronts = own_width // width
+    for e, part in enumerate(parts):
+        for leaf in range(leaf_count):
+            part[:, leaf * width : (leaf + 1) * width] = values[leaf, 0]
+        for j in range(fronts):
+            part[:, total + j * width : total + (j + 1) * width] = values[
+                (place[1] ^ e) * fronts + j, 1
+            ]
+
+
+def first_kernel(place, *refs):
+    parts, (high, low, first, rest) = refs[:-4], refs[-4:]
+    total = high.shape[0]
+    values = jnp.concatenate([part[:, :total] for part in parts], 0)
+    rest[...] = jnp.concatenate([part[:, total:] for part in parts], 0)
+    first[...] = product(values, high[...], low[...], 0)
+
+
+def gathered_product(place, parts, high, low):
+    count = len(parts)
+    width = parts[0].shape[1]
+    total = None
+    for e, part in enumerate(parts):
+        rows = span(place[1] ^ e, width)
+        term = product(regroup(part[...], e, count), high[rows, :], low[rows, :], 0)
+        total = term if total is None else total + term
+    return total
+
+
+def coupled_kernel(place, *refs):
+    parts, (high, low, rest, result) = refs[:-4], refs[-4:]
+    result[...] = rest[...] - gathered_product(place, parts, high, low)
+
+
+def scatter_product(place, values, high, low, sent):
+    count = len(sent)
+    width = sent[0].shape[1]
+    for e, part in enumerate(sent):
+        rows = span(place[1] ^ e, width)
+        part[...] = regroup(product(values, high[rows, :], low[rows, :], 1), e, count)
+
+
+def turn_kernel(place, *refs):
+    count = (len(refs) - 2) // 2
+    parts, (high, low), sent = refs[:count], refs[count : count + 2], refs[count + 2 :]
+    second = gathered_product(place, parts, high, low)
+    scatter_product(place, second, high, low, sent)
+
+
+def back_kernel(place, *refs):
+    count = (len(refs) - 3) // 2
+    parts, (high, low), last, sent = (
+        refs[:count],
+        refs[count : count + 2],
+        refs[count + 2],
+        refs[count + 3 :],
+    )
+    total = sum(part[...] for part in parts[1:]) + parts[0][...]
+    last[...] = total
+    scatter_product(place, total, high, low, sent)
+
+
+def final_kernel(place, *refs):
+    count = (len(refs) - 4) // 2
+    parts = refs[:count]
+    high, low, first, last = refs[count : count + 4]
+    sent = refs[count + 4 :]
+    total = first[...] - (sum(part[...] for part in parts[1:]) + parts[0][...])
+    solved = product(total, high[...], low[...], 1)
+    size = total.shape[0] // count
+    for e, part in enumerate(sent):
+        part[...] = jnp.concatenate(
+            [solved[e * size : (e + 1) * size], last[e * size : (e + 1) * size, :]], 1
+        )
+
+
+def collect_kernel(place, *refs):
+    parts, result = refs[:-1], refs[-1]
+    leaf_count, _, rows, width = result.shape
+    total = leaf_count * width
+    fronts = (parts[0].shape[1] - total) // width
+    for leaf in range(leaf_count):
+        where = slice(leaf * width, (leaf + 1) * width)
+        result[leaf, 0] = sum(part[:, where] for part in parts[1:]) + parts[0][:, where]
+    for e, part in enumerate(parts):
+        for j in range(fronts):
+            start = total + j * width
+            result[(place[1] ^ e) * fronts + j, 1] = part[:, start : start + width]
+
+
+def root_replicated(section, root_inverse, root_coupling):
+    leaf_count, col_count = lax.axis_size("leaf"), lax.axis_size("col")
+    place = jnp.stack([lax.axis_index("leaf"), lax.axis_index("col")]).astype(jnp.int32)
+    first_high, first_low = spread_matrix(place, root_inverse[0])
+    between_high, between_low = spread_matrix(place, root_coupling)
+    second_high, second_low = spread_matrix(place, root_inverse[1])
+    rhs_rows = section.shape[0]
+    panel_count, panel_rows, own_columns = root_inverse.shape
+    rows = rhs_rows // leaf_count
+    group = rows * col_count
+    total = panel_rows * leaf_count
+    split = section.reshape(leaf_count, rows, panel_count, panel_rows).transpose(0, 2, 1, 3)
+    whole = lax.all_to_all(split, "leaf", 0, 0, tiled=True)
+    wide = [((rows, total + own_columns), jnp.float32)] * col_count
+    one = ((group, own_columns), jnp.float32)
+    parts = swap_columns(kernel_call(arrange_kernel, wide, place, whole))
+    first, rest = kernel_call(first_kernel, [one, one], place, *parts, first_high, first_low)
+    parts = swap_columns([first] * col_count)
+    (left,) = kernel_call(coupled_kernel, [one], place, *parts, between_high, between_low, rest)
+    parts = swap_columns([left] * col_count)
+    parts = kernel_call(turn_kernel, [one] * col_count, place, *parts, second_high, second_low)
+    parts = swap_columns(parts)
+    last, *parts = kernel_call(
+        back_kernel, [one] * (col_count + 1), place, *parts, between_high, between_low
+    )
+    parts = swap_columns(parts)
+    parts = kernel_call(
+        final_kernel, wide, place, *parts, first_high, first_low, first, last
+    )
+    parts = swap_columns(parts)
+    (split,) = kernel_call(
+        collect_kernel, [((leaf_count, panel_count, rows, panel_rows), jnp.float32)], place, *parts
+    )
+    whole = lax.all_to_all(split, "leaf", 0, 0, tiled=True)
+    return whole.transpose(0, 2, 1, 3).reshape(rhs_rows, panel_count, panel_rows)
+
+
+def replicates(rhs_rows, root_inverse):
+    leaf_count, col_count = lax.axis_size("leaf"), lax.axis_size("col")
+    panel_rows, own_columns = root_inverse.shape[1:]
+    return (
+        leaf_count == 8
+        and col_count & (col_count - 1) == 0
+        and rhs_rows % (8 * leaf_count) == 0
+        and own_columns % panel_rows == 0
     )
 
 
@@ -133,22 +377,8 @@
             skeleton = join_halves(skeleton, level_index)
         skeleton = jnp.take(skeleton, order_map[0], axis=1)
         section = skeleton.reshape(skeleton.shape[0], -1)
-    rhs_rows = right_sides.shape[0]
-    panel_count = root_inverse.shape[0]
-    panel_rows = root_inverse.shape[1]
-    root_rhs = section.reshape(rhs_rows, panel_count, panel_rows)
-    full_rhs = spread_columns(root_rhs)
-    first_solve = forward_product(full_rhs[:, 0], root_inverse[0])
-    coupled = forward_product(to_leaf_rows(first_solve), root_coupling)
-    second_solve = forward_product(full_rhs[:, 1] - to_leaf_rows(coupled), root_inverse[1])
-    forward_both = spread_leaf(jnp.stack([first_solve, second_solve], 1))
-    last_panel = backward_product(forward_both[:, 1], root_inverse[1])
-    back_coupled = backward_product(to_column_rows(last_panel), root_coupling)
-    first_panel = backward_product(
-        forward_both[:, 0] - to_column_rows(back_coupled), root_inverse[0]
-    )
-    root_solution = jnp.stack([first_panel, last_panel], 1)
-    return (outputs[0], outputs[1], outputs[2], root_solution)
+    solve = root_replicated if replicates(right_sides.shape[0], root_inverse) else root_wide
+    return (*outputs, solve(section, root_inverse, root_coupling))
 
 
 def solution(mesh):

time: 357 us -> 165 us (0.46)
  blocking collectives: 120 us -> 0 us
  waiting for transfers between devices: 185 us -> 76.3 us
  starting transfers between devices: 3.39 us -> 49.1 us
  Pallas kernels: 0 us -> 14.7 us
  between operations: 14.6 us -> 1.23 us
  matrix products: 14.7 us -> 8.47 us
    reduce_scatter x6 -> x0, waiting for transfers between devices: 158 us -> none  [the longest x3 103 us: forward_product(): lax.psum_scatter(jnp.dot(values, matrix, precision=lax.Precision.HIGHEST,...]
    all_gather x5 -> x0, blocking collectives: 64.9 us -> none  [the longest x2 28.3 us: to_leaf_rows(): full_rows = lax.all_gather(values, 'col', axis=1, tiled=True)]
    ppermute x0 -> x45, waiting for transfers between devices: none -> 64.3 us  [flip(): return lax.ppermute(block, axis, [(i, i ^ distance) for i in range(count)])]
    all_to_all x4 -> x0, blocking collectives: 54.7 us -> none  [the longest x2 35.5 us: to_column_rows(): lax.all_to_all(full_rows, 'col', split_axis=1, concat_axis=0, tiled=True)]
    ppermute x0 -> x45, starting transfers between devices: none -> 40.1 us  [flip(): return lax.ppermute(block, axis, [(i, i ^ distance) for i in range(count)])]
    all_gather x1 -> x0, waiting for transfers between devices: 24.5 us -> none  [spread_leaf(): return lax.all_gather(values, 'leaf', axis=0, tiled=True)]
    pallas_call x0 -> x10, Pallas kernels: none -> 14.7 us  [kernel_call(): pl.pallas_call(body, out_shape=[jax.ShapeDtypeStruct(s, d) for s, d in ou...]
    dot_general x6 -> x0, matrix products: 9.39 us -> none  [the longest x3 5.05 us: backward_product(): lax.dot_general(values, matrix, (((1,), (1,)), ((), ())), precision=lax.P...]
  transfers between devices with their start and end apart: 9 -> 49, of which waited for: 8 -> 27; matrix products, arithmetic and copies ran while one was open for 1% -> 9% of each run, Pallas kernels for 0% -> 4%
where the time goes in v1:
time: 165 us; the launch traced here: 164 us
  waiting for transfers between devices  76.3 us (46%)
  starting transfers between devices  49.1 us (30%)
  Pallas kernels  14.7 us (9%)
  local copies, waits for them, and re-layouts  10.8 us (7%)
  matrix products  8.47 us (5%)
  other arithmetic  3.8 us (2%)
    ppermute x45, waiting for transfers between devices, flip(): return lax.ppermute(block, axis, [(i, i ^ distance) for i in range(count)])  64.3 us
    ppermute x45, starting transfers between devices, flip(): return lax.ppermute(block, axis, [(i, i ^ distance) for i in range(count)])  40.1 us
    pallas_call x10, Pallas kernels, kernel_call(): pl.pallas_call(body, out_shape=[jax.ShapeDtypeStruct(s, d) for s, d in ou...  14.7 us
    all_to_all x2, waiting for transfers between devices, root_replicated(): whole = lax.all_to_all(split, 'leaf', 0, 0, tiled=True)  8.66 us
    all_to_all x2, starting transfers between devices, root_replicated(): whole = lax.all_to_all(split, 'leaf', 0, 0, tiled=True)  6.92 us
    ppermute x2, waiting for transfers between devices, partner(): return lax.ppermute(block, axis, route)  3.4 us
  transfers between devices with their start and end apart: 49, of which 27 were waited for; matrix products, arithmetic and copies ran while one was open for 9% of the time, Pallas kernels for 4%

profile of v1, /device:TPU:0, one launch (start us, length us, event | category | flops | bytes accessed | tf_op | source)
XLA Modules:
  0.0 164.4 jit_solution(7791530866287899050)
XLA Ops:
  0.7 1.4 fusion.33
  2.0 0.8 copy.43
  2.8 1.0 slice.53
  3.9 2.0 %fusion.28 = (f32[4,128]{1,0:T(4,128)S(1)}, f32[4,128]{1,0:T(4,128)S(1)}, f32[4,128]{1,0:T(4,128)S(1)}) fusion(s32[]{:T(128)} %bitcast.28, s32[4]{0:T(128)S(1)} %iota_multiply_fusion, s32[]{:T(128)} %bitcast.14, s32[]{:T(128)} %bitcast), kind=kLoop, calls=%fused_computation.68 | loop fusion | flops 3584 | bytes 6172 | tf_op jit(solution)/shard_map/convert_element_type | solution.py:31
  5.9 1.4 convolution_multiply_fusion.2
  8.0 0.8 fusion
  9.5 2.6 %collective-permute-start.18 = (f32[256,512]{1,0:T(8,128)S(1)}, f32[256,512]{1,0:T(8,128)S(1)}, u32[]{:S(2)}, u32[]{:S(2)}) collective-permute-start(f32[256,512]{1,0:T(8,128)S(1)} %copy-done.1), channel_id=1, source_target_pairs={{0,16},{4,20},{8,24},{12,28},{16,0},{20,4},{24,8},{28,12},{1,17},{... | collective-permute-start | bytes 1572872 | tf_op jit(solution)/shard_map/ppermute | solution.py:126
  15.2 1.8 %convolution_bitcast_fusion.2 = f32[64,4,3,128]{3,0,2,1:T(8,128)S(1)} fusion(f32[4,3,128,128]{3,2,1,0:T(8,128)} %param.22, f32[4,64,128]{2,1,0:T(8,128)S(1)} %convolution_multiply_fusion.1), kind=kOutput, calls=%fused_computation.6 | convolution fusion | flops 150994944 | bytes 1310720 | tf_op jit(solution)/shard_map/ria,ikab->rikb/dot_general | solution.py:36
  17.0 0.8 fusion.1
  17.9 1.6 collective-permute-start.1
  20.1 3.4 %collective-permute-done.1 = f32[64,4,128]{2,1,0:T(4,128)S(1)} collective-permute-done((f32[64,4,128]{2,1,0:T(4,128)S(1)}, f32[64,4,128]{2,1,0:T(4,128)S(1)}, u32[]{:S(2)}, u32[]{:S(2)}) %collective-permute-start.1) | collective-permute-done | bytes 131104 | tf_op jit(solution)/shard_map/ppermute | solution.py:18
  24.5 1.3 convolution_multiply_fusion
  28.6 3.6 %all-to-all-start = ((f32[8,2,8,256]{3,2,1,0:T(8,128)}), f32[8,2,8,256]{3,2,1,0:T(8,128)S(1)}, u32[]{:S(2)}, u32[]{:S(2)}) async-start(f32[8,2,8,256]{3,2,1,0:T(8,128)} %fusion.10), calls=%async_computation | async-start | bytes 262144 | tf_op jit(solution)/shard_map/all_to_all | solution.py:309
  32.2 1.7 %collective-permute-start.17 = (f32[256,512]{1,0:T(8,128)S(1)}, f32[256,512]{1,0:T(8,128)S(1)}, u32[]{:S(2)}, u32[]{:S(2)}) collective-permute-start(f32[256,512]{1,0:T(8,128)S(1)} %copy-done.1), channel_id=1, source_target_pairs={{0,8},{4,12},{8,0},{12,4},{16,24},{20,28},{24,16},{28,20},{1,9},{5... | collective-permute-start | bytes 1572872 | tf_op jit(solution)/shard_map/ppermute | solution.py:126
  34.0 3.9 %all-to-all-done.values = f32[8,2,8,256]{3,2,1,0:T(8,128)S(1)} async-done(((f32[8,2,8,256]{3,2,1,0:T(8,128)}), f32[8,2,8,256]{3,2,1,0:T(8,128)S(1)}, u32[]{:S(2)}, u32[]{:S(2)}) %all-to-all-start) | async-done | bytes 131104 | tf_op jit(solution)/shard_map/all_to_all | solution.py:309
  38.5 1.6 collective-permute-start.2
  40.2 2.6 %collective-permute-start.3 = (f32[8,2560]{1,0:T(8,128)S(1)}, f32[8,2560]{1,0:T(8,128)S(1)}, u32[]{:S(2)}, u32[]{:S(2)}) collective-permute-start(f32[8,2560]{1,0:T(8,128)S(1)} %get-tuple-element.31), channel_id=1, source_target_pairs={{0,2},{1,3},{2,0},{3,1},{4,6},{5,7},{6,4},{7,5},{8,10},{9,11},{10,... | collective-permute-start | bytes 245768 | tf_op jit(solution)/shard_map/ppermute | solution.py:126
  42.8 1.3 slice_bitcast_fusion
  44.6 1.7 %collective-permute-done.3.refs_2_ = f32[8,2560]{1,0:T(8,128)S(1)} collective-permute-done((f32[8,2560]{1,0:T(8,128)S(1)}, f32[8,2560]{1,0:T(8,128)S(1)}, u32[]{:S(2)}, u32[]{:S(2)}) %collective-permute-start.3) | collective-permute-done | bytes 81952 | tf_op jit(solution)/shard_map/ppermute | solution.py:126
  46.4 1.8 %collective-permute-start.4 = (f32[8,2560]{1,0:T(8,128)S(1)}, f32[8,2560]{1,0:T(8,128)S(1)}, u32[]{:S(2)}, u32[]{:S(2)}) collective-permute-start(f32[8,2560]{1,0:T(8,128)S(1)} %get-tuple-element.32), channel_id=1, source_target_pairs={{0,3},{1,2},{2,1},{3,0},{4,7},{5,6},{6,5},{7,4},{8,11},{9,10},{10,... | collective-permute-start | bytes 245768 | tf_op jit(solution)/shard_map/ppermute | solution.py:126
  48.2 4.5 %collective-permute-done.4.refs_3_ = f32[8,2560]{1,0:T(8,128)S(1)} collective-permute-done((f32[8,2560]{1,0:T(8,128)S(1)}, f32[8,2560]{1,0:T(8,128)S(1)}, u32[]{:S(2)}, u32[]{:S(2)}) %collective-permute-start.4) | collective-permute-done | bytes 81952 | tf_op jit(solution)/shard_map/ppermute | solution.py:126
  53.8 1.5 collective-permute-start.5
  55.3 1.6 collective-permute-done.30.refs_2_
  57.2 10.2 %collective-permute-done.29.refs_1_ = f32[256,512]{1,0:T(8,128)S(1)} collective-permute-done((f32[256,512]{1,0:T(8,128)S(1)}, f32[256,512]{1,0:T(8,128)S(1)}, u32[]{:S(2)}, u32[]{:S(2)}) %collective-permute-start.29) | collective-permute-done | bytes 524320 | tf_op jit(solution)/shard_map/ppermute | solution.py:126
  68.7 1.4 collective-permute-start.31
  70.1 8.6 %collective-permute-done.5.refs_1_ = f32[256,512]{1,0:T(8,128)S(1)} collective-permute-done((f32[256,512]{1,0:T(8,128)S(1)}, f32[256,512]{1,0:T(8,128)S(1)}, u32[]{:S(2)}, u32[]{:S(2)}) %collective-permute-start.5) | collective-permute-done | bytes 524320 | tf_op jit(solution)/shard_map/ppermute | solution.py:126
  78.7 4.7 %collective-permute-done.20.refs_4_ = f32[128,512]{1,0:T(8,128)S(1)} collective-permute-done((f32[128,512]{1,0:T(8,128)S(1)}, f32[128,512]{1,0:T(8,128)S(1)}, u32[]{:S(2)}, u32[]{:S(2)}) %collective-permute-start.20) | collective-permute-done | bytes 262176 | tf_op jit(solution)/shard_map/ppermute | solution.py:126
  83.8 1.2 collective-permute-start.7
  85.1 3.3 %collective-permute-done.32.refs_4_ = f32[128,512]{1,0:T(8,128)S(1)} collective-permute-done((f32[128,512]{1,0:T(8,128)S(1)}, f32[128,512]{1,0:T(8,128)S(1)}, u32[]{:S(2)}, u32[]{:S(2)}) %collective-permute-start.32) | collective-permute-done | bytes 262176 | tf_op jit(solution)/shard_map/ppermute | solution.py:126
  88.8 2.3 %collective-permute-done.8.refs_4_ = f32[128,512]{1,0:T(8,128)S(1)} collective-permute-done((f32[128,512]{1,0:T(8,128)S(1)}, f32[128,512]{1,0:T(8,128)S(1)}, u32[]{:S(2)}, u32[]{:S(2)}) %collective-permute-start.8) | collective-permute-done | bytes 262176 | tf_op jit(solution)/shard_map/ppermute | solution.py:126
  92.2 1.3 collective-permute-done.13.refs_9_
  95.1 1.3 shard_map.184
  96.3 1.4 shard_map.185
  97.7 1.8 %collective-permute-start.16 = (f32[32,512]{1,0:T(8,128)S(1)}, f32[32,512]{1,0:T(8,128)S(1)}, u32[]{:S(2)}, u32[]{:S(2)}) collective-permute-start(f32[32,512]{1,0:T(8,128)S(1)} %get-tuple-element.35.refs_0_.refs_6_), channel_id=1, source_target_pairs={{0,3},{1,2},{2,1},{3,0},{4,7},{5,6},{6,5},{7,4},{8,11},{9,10},{10,... | collective-permute-start | bytes 196616 | tf_op jit(solution)/shard_map/ppermute | solution.py:126
  99.4 5.0 %collective-permute-done.16.refs_3_ = f32[32,512]{1,0:T(8,128)S(1)} collective-permute-done((f32[32,512]{1,0:T(8,128)S(1)}, f32[32,512]{1,0:T(8,128)S(1)}, u32[]{:S(2)}, u32[]{:S(2)}) %collective-permute-start.16) | collective-permute-done | bytes 65568 | tf_op jit(solution)/shard_map/ppermute | solution.py:126
  104.5 2.1 %collective-permute-done.15.refs_2_ = f32[32,512]{1,0:T(8,128)S(1)} collective-permute-done((f32[32,512]{1,0:T(8,128)S(1)}, f32[32,512]{1,0:T(8,128)S(1)}, u32[]{:S(2)}, u32[]{:S(2)}) %collective-permute-start.15) | collective-permute-done | bytes 65568 | tf_op jit(solution)/shard_map/ppermute | solution.py:126
  106.6 2.2 %collective-permute-done.14.refs_1_ = f32[32,512]{1,0:T(8,128)S(1)} collective-permute-done((f32[32,512]{1,0:T(8,128)S(1)}, f32[32,512]{1,0:T(8,128)S(1)}, u32[]{:S(2)}, u32[]{:S(2)}) %collective-permute-start.14) | collective-permute-done | bytes 65568 | tf_op jit(solution)/shard_map/ppermute | solution.py:126
  108.7 1.3 shard_map.186
  110.0 1.4 shard_map.187.refs_0_
  111.4 1.8 %collective-permute-start.28 = (f32[32,512]{1,0:T(8,128)S(1)}, f32[32,512]{1,0:T(8,128)S(1)}, u32[]{:S(2)}, u32[]{:S(2)}) collective-permute-start(f32[32,512]{1,0:T(8,128)S(1)} %shard_map.187.refs_0_), channel_id=1, source_target_pairs={{0,3},{1,2},{2,1},{3,0},{4,7},{5,6},{6,5},{7,4},{8,11},{9,10},{10,... | collective-permute-start | bytes 196616 | tf_op jit(solution)/shard_map/ppermute | solution.py:126
  113.6 2.2 %collective-permute-start.26 = (f32[32,512]{1,0:T(8,128)S(1)}, f32[32,512]{1,0:T(8,128)S(1)}, u32[]{:S(2)}, u32[]{:S(2)}) collective-permute-start(f32[32,512]{1,0:T(8,128)S(1)} %shard_map.187.refs_0_), channel_id=1, source_target_pairs={{0,1},{1,0},{2,3},{3,2},{4,5},{5,4},{6,7},{7,6},{8,9},{9,8},{10,11... | collective-permute-start | bytes 196616 | tf_op jit(solution)/shard_map/ppermute | solution.py:126
  115.9 1.3 shard_map.188
  117.1 1.1 collective-permute-done.28.refs_3_
  118.2 2.3 %collective-permute-done.27.refs_2_ = f32[32,512]{1,0:T(8,128)S(1)} collective-permute-done((f32[32,512]{1,0:T(8,128)S(1)}, f32[32,512]{1,0:T(8,128)S(1)}, u32[]{:S(2)}, u32[]{:S(2)}) %collective-permute-start.27) | collective-permute-done | bytes 65568 | tf_op jit(solution)/shard_map/ppermute | solution.py:126
  120.6 2.6 %shard_map.189 = (f32[32,512]{1,0:T(8,128)S(1)}, f32[32,512]{1,0:T(8,128)S(1)}, f32[32,512]{1,0:T(8,128)S(1)}, f32[32,512]{1,0:T(8,128)S(1)}) custom-call(s32[2]{0:T(128)S(1)} %pad_add_fusion.place, f32[32,512]{1,0:T(8,128)S(1)} %shard_map.187.refs_0_, f32[32,512]{1,0:T(8,128)S(1)} %collective-permute-done.26.refs_1_, ...), custom_call_target="tpu_custom_call" | custom-call | tf_op jit(solution)/shard_map/pallas_call | solution.py:136
  123.2 3.1 %collective-permute-start.39 = (f32[32,512]{1,0:T(8,128)S(1)}, f32[32,512]{1,0:T(8,128)S(1)}, u32[]{:S(2)}, u32[]{:S(2)}) collective-permute-start(f32[32,512]{1,0:T(8,128)S(1)} %get-tuple-element.43), channel_id=1, source_target_pairs={{0,2},{1,3},{2,0},{3,1},{4,6},{5,7},{6,4},{7,5},{8,10},{9,11},{10,... | collective-permute-start | bytes 196616 | tf_op jit(solution)/shard_map/ppermute | solution.py:126
  126.4 1.2 collective-permute-start.40
  128.3 3.2 %collective-permute-done.39.refs_2_ = f32[32,512]{1,0:T(8,128)S(1)} collective-permute-done((f32[32,512]{1,0:T(8,128)S(1)}, f32[32,512]{1,0:T(8,128)S(1)}, u32[]{:S(2)}, u32[]{:S(2)}) %collective-permute-start.39) | collective-permute-done | bytes 65568 | tf_op jit(solution)/shard_map/ppermute | solution.py:126
  131.4 1.1 collective-permute-done.40.refs_3_
  132.5 1.9 %shard_map.190 = (f32[32,512]{1,0:T(8,128)S(1)}, f32[32,512]{1,0:T(8,128)S(1)}, f32[32,512]{1,0:T(8,128)S(1)}, f32[32,512]{1,0:T(8,128)S(1)}, f32[32,512]{1,0:T(8,128)S(1)}) custom-call(s32[2]{0:T(128)S(1)} %pad_add_fusion.place, f32[32,512]{1,0:T(8,128)S(1)} %get-tuple-element.41.refs_0_, f32[32,512]{1,0:T(8,128)S(1)} %collective-permute-done.38.refs_1_, ...), custom_call_target="tpu_custom_call" | custom-call | tf_op jit(solution)/shard_map/pallas_call | solution.py:136
  134.4 0.9 collective-permute-start.41
  135.3 1.2 collective-permute-start.42
  136.5 2.3 %collective-permute-start.43 = (f32[32,512]{1,0:T(8,128)S(1)}, f32[32,512]{1,0:T(8,128)S(1)}, u32[]{:S(2)}, u32[]{:S(2)}) collective-permute-start(f32[32,512]{1,0:T(8,128)S(1)} %get-tuple-element.48), channel_id=1, source_target_pairs={{0,3},{1,2},{2,1},{3,0},{4,7},{5,6},{6,5},{7,4},{8,11},{9,10},{10,... | collective-permute-start | bytes 196616 | tf_op jit(solution)/shard_map/ppermute | solution.py:126
  139.4 2.0 %collective-permute-done.42.refs_2_ = f32[32,512]{1,0:T(8,128)S(1)} collective-permute-done((f32[32,512]{1,0:T(8,128)S(1)}, f32[32,512]{1,0:T(8,128)S(1)}, u32[]{:S(2)}, u32[]{:S(2)}) %collective-permute-start.42) | collective-permute-done | bytes 65568 | tf_op jit(solution)/shard_map/ppermute | solution.py:126
  141.4 1.2 collective-permute-done.43.refs_3_
  142.6 1.9 %shard_map.191 = (f32[8,2560]{1,0:T(8,128)S(1)}, f32[8,2560]{1,0:T(8,128)S(1)}, f32[8,2560]{1,0:T(8,128)S(1)}, f32[8,2560]{1,0:T(8,128)S(1)}) custom-call(s32[2]{0:T(128)S(1)} %pad_add_fusion.place, f32[32,512]{1,0:T(8,128)S(1)} %get-tuple-element.45.refs_0_, f32[32,512]{1,0:T(8,128)S(1)} %collective-permute-done.41.refs_1_, ...), custom_call_target="tpu_custom_call" | custom-call | tf_op jit(solution)/shard_map/pallas_call | solution.py:136
  145.3 2.1 %collective-permute-start.45 = (f32[8,2560]{1,0:T(8,128)S(1)}, f32[8,2560]{1,0:T(8,128)S(1)}, u32[]{:S(2)}, u32[]{:S(2)}) collective-permute-start(f32[8,2560]{1,0:T(8,128)S(1)} %get-tuple-element.52), channel_id=1, source_target_pairs={{0,2},{1,3},{2,0},{3,1},{4,6},{5,7},{6,4},{7,5},{8,10},{9,11},{10,... | collective-permute-start | bytes 245768 | tf_op jit(solution)/shard_map/ppermute | solution.py:126
  147.3 1.6 collective-permute-start.46
  150.2 1.3 collective-permute-done.45.refs_2_
  151.5 2.1 %collective-permute-done.46.refs_3_ = f32[8,2560]{1,0:T(8,128)S(1)} collective-permute-done((f32[8,2560]{1,0:T(8,128)S(1)}, f32[8,2560]{1,0:T(8,128)S(1)}, u32[]{:S(2)}, u32[]{:S(2)}) %collective-permute-start.46) | collective-permute-done | bytes 81952 | tf_op jit(solution)/shard_map/ppermute | solution.py:126
  153.6 1.2 shard_map.192
  154.8 3.4 %all-to-all-start.1 = ((f32[8,2,8,256]{3,2,1,0:T(8,128)}), f32[8,2,8,256]{3,2,1,0:T(8,128)S(1)}, u32[]{:S(2)}, u32[]{:S(2)}) async-start(f32[8,2,8,256]{3,2,1,0:T(8,128)} %shard_map.192), calls=%async_computation.1 | async-start | bytes 262144 | tf_op jit(solution)/shard_map/all_to_all | solution.py:330
  158.9 4.7 %all-to-all-done.1 = f32[8,2,8,256]{3,2,1,0:T(8,128)S(1)} async-done(((f32[8,2,8,256]{3,2,1,0:T(8,128)}), f32[8,2,8,256]{3,2,1,0:T(8,128)S(1)}, u32[]{:S(2)}, u32[]{:S(2)}) %all-to-all-start.1) | async-done | bytes 131104 | tf_op jit(solution)/shard_map/all_to_all | solution.py:330
  163.6 0.8 copy.61
  (135 shorter events, 20.8 us)
Async XLA Ops:
  0.6 6.7 %copy-start = (f32[4,3,128,128]{3,2,1,0:T(8,128)S(1)}, f32[4,3,128,128]{3,2,1,0:T(8,128)}, u32[]{:S(2)}) copy-start(f32[4,3,128,128]{3,2,1,0:T(8,128)} %param.18) | copy-start | bytes 2359300
  5.9 3.5 %copy-start.1 = (f32[256,512]{1,0:T(8,128)S(1)}, f32[256,512]{1,0:T(8,128)}, u32[]{:S(2)}) copy-start(f32[256,512]{1,0:T(8,128)} %refs_0_.1) | copy-start | bytes 1572868
  5.9 6.1 %copy-start.7 = (s32[1,12]{1,0:T(1,128)S(1)}, s32[1,12]{1,0:T(1,128)}, u32[]{:S(2)}) copy-start(s32[1,12]{1,0:T(1,128)} %param.20) | copy-start | bytes 148
  5.9 6.2 %copy-start.8 = (s32[1,8]{1,0:T(1,128)S(1)}, s32[1,8]{1,0:T(1,128)}, u32[]{:S(2)}) copy-start(s32[1,8]{1,0:T(1,128)} %param.24) | copy-start | bytes 100
  5.9 6.7 %copy-start.9 = (s32[1,4]{1,0:T(1,128)S(1)}, s32[1,4]{1,0:T(1,128)}, u32[]{:S(2)}) copy-start(s32[1,4]{1,0:T(1,128)} %param.28) | copy-start | bytes 52
  5.9 7.7 %copy-start.5 = (s32[4,3]{1,0:T(4,128)S(1)}, s32[4,3]{1,0:T(4,128)}, u32[]{:S(2)}) copy-start(s32[4,3]{1,0:T(4,128)} %param.23) | copy-start | bytes 148
  8.9 4.8 %collective-permute-start = (f32[64,6,128]{2,1,0:T(8,128)S(1)}, f32[64,6,128]{2,1,0:T(8,128)S(1)}, u32[]{:S(2)}, u32[]{:S(2)}) collective-permute-start(f32[64,6,128]{2,1,0:T(8,128)S(1)} %get-tuple-element.65), channel_id=1, source_target_pairs={{0,4},{4,0},{8,12},{12,8},{16,20},{20,16},{24,28},{28,24},{1,5},{5... | collective-permute-start | bytes 589832 | tf_op jit(solution)/shard_map/ppermute | solution.py:18
  9.5 43.6 %collective-permute-start.18 = (f32[256,512]{1,0:T(8,128)S(1)}, f32[256,512]{1,0:T(8,128)S(1)}, u32[]{:S(2)}, u32[]{:S(2)}) collective-permute-start(f32[256,512]{1,0:T(8,128)S(1)} %copy-done.1), channel_id=1, source_target_pairs={{0,16},{4,20},{8,24},{12,28},{16,0},{20,4},{24,8},{28,12},{1,17},{... | collective-permute-start | bytes 1572872 | tf_op jit(solution)/shard_map/ppermute | solution.py:126
  13.9 1.0 copy-start.3
  14.7 5.3 %copy-start.6 = (s32[4,3]{1,0:T(4,128)S(1)}, s32[4,3]{1,0:T(4,128)}, u32[]{:S(2)}) copy-start(s32[4,3]{1,0:T(4,128)} %param.27) | copy-start | bytes 148
  17.9 7.9 %copy-start.2 = (f32[4,3,128,128]{3,2,1,0:T(8,128)S(1)}, f32[4,3,128,128]{3,2,1,0:T(8,128)}, u32[]{:S(2)}) copy-start(f32[4,3,128,128]{3,2,1,0:T(8,128)} %param.26) | copy-start | bytes 2359300
  17.9 5.6 %collective-permute-start.1 = (f32[64,4,128]{2,1,0:T(4,128)S(1)}, f32[64,4,128]{2,1,0:T(4,128)S(1)}, u32[]{:S(2)}, u32[]{:S(2)}) collective-permute-start(f32[64,4,128]{2,1,0:T(4,128)S(1)} %get-tuple-element.69), channel_id=1, source_target_pairs={{0,8},{8,0},{4,12},{12,4},{16,24},{24,16},{20,28},{28,20},{1,9},{9... | collective-permute-start | bytes 393224 | tf_op jit(solution)/shard_map/ppermute | solution.py:18
  24.4 3.6 %copy-start.4 = (pred[1,2,2,128]{3,1,2,0:T(4,128)(4,1)S(1)}, pred[1,2,2,128]{3,1,2,0:T(4,128)(4,1)}, u32[]{:S(2)}) copy-start(pred[1,2,2,128]{3,1,2,0:T(4,128)(4,1)} %copy.100) | copy-start | bytes 1540
  28.6 9.3 %all-to-all-start = ((f32[8,2,8,256]{3,2,1,0:T(8,128)}), f32[8,2,8,256]{3,2,1,0:T(8,128)S(1)}, u32[]{:S(2)}, u32[]{:S(2)}) async-start(f32[8,2,8,256]{3,2,1,0:T(8,128)} %fusion.10), calls=%async_computation | async-start | bytes 262144 | tf_op jit(solution)/shard_map/all_to_all | solution.py:309
  32.2 20.8 %collective-permute-start.17 = (f32[256,512]{1,0:T(8,128)S(1)}, f32[256,512]{1,0:T(8,128)S(1)}, u32[]{:S(2)}, u32[]{:S(2)}) collective-permute-start(f32[256,512]{1,0:T(8,128)S(1)} %copy-done.1), channel_id=1, source_target_pairs={{0,8},{4,12},{8,0},{12,4},{16,24},{20,28},{24,16},{28,20},{1,9},{5... | collective-permute-start | bytes 1572872 | tf_op jit(solution)/shard_map/ppermute | solution.py:126
  33.9 19.8 %collective-permute-start.21 = (f32[256,512]{1,0:T(8,128)S(1)}, f32[256,512]{1,0:T(8,128)S(1)}, u32[]{:S(2)}, u32[]{:S(2)}) collective-permute-start(f32[256,512]{1,0:T(8,128)S(1)} %copy-done.1), channel_id=1, source_target_pairs={{0,4},{4,0},{8,12},{12,8},{16,20},{20,16},{24,28},{28,24},{1,5},{5... | collective-permute-start | bytes 1572872 | tf_op jit(solution)/shard_map/ppermute | solution.py:126
  38.5 5.5 %collective-permute-start.2 = (f32[8,2560]{1,0:T(8,128)S(1)}, f32[8,2560]{1,0:T(8,128)S(1)}, u32[]{:S(2)}, u32[]{:S(2)}) collective-permute-start(f32[8,2560]{1,0:T(8,128)S(1)} %get-tuple-element.30), channel_id=1, source_target_pairs={{0,1},{1,0},{2,3},{3,2},{4,5},{5,4},{6,7},{7,6},{8,9},{9,8},{10,11... | collective-permute-start | bytes 245768 | tf_op jit(solution)/shard_map/ppermute | solution.py:126
  40.2 6.2 %collective-permute-start.3 = (f32[8,2560]{1,0:T(8,128)S(1)}, f32[8,2560]{1,0:T(8,128)S(1)}, u32[]{:S(2)}, u32[]{:S(2)}) collective-permute-start(f32[8,2560]{1,0:T(8,128)S(1)} %get-tuple-element.31), channel_id=1, source_target_pairs={{0,2},{1,3},{2,0},{3,1},{4,6},{5,7},{6,4},{7,5},{8,10},{9,11},{10,... | collective-permute-start | bytes 245768 | tf_op jit(solution)/shard_map/ppermute | solution.py:126
  44.0 12.8 %collective-permute-start.30 = (f32[256,512]{1,0:T(8,128)S(1)}, f32[256,512]{1,0:T(8,128)S(1)}, u32[]{:S(2)}, u32[]{:S(2)}) collective-permute-start(f32[256,512]{1,0:T(8,128)S(1)} %get-tuple-element.62.refs_0_), channel_id=1, source_target_pairs={{0,16},{4,20},{8,24},{12,28},{16,0},{20,4},{24,8},{28,12},{1,17},{... | collective-permute-start | bytes 1572872 | tf_op jit(solution)/shard_map/ppermute | solution.py:126
  46.4 6.2 %collective-permute-start.4 = (f32[8,2560]{1,0:T(8,128)S(1)}, f32[8,2560]{1,0:T(8,128)S(1)}, u32[]{:S(2)}, u32[]{:S(2)}) collective-permute-start(f32[8,2560]{1,0:T(8,128)S(1)} %get-tuple-element.32), channel_id=1, source_target_pairs={{0,3},{1,2},{2,1},{3,0},{4,7},{5,6},{6,5},{7,4},{8,11},{9,10},{10,... | collective-permute-start | bytes 245768 | tf_op jit(solution)/shard_map/ppermute | solution.py:126
  52.6 14.9 %collective-permute-start.29 = (f32[256,512]{1,0:T(8,128)S(1)}, f32[256,512]{1,0:T(8,128)S(1)}, u32[]{:S(2)}, u32[]{:S(2)}) collective-permute-start(f32[256,512]{1,0:T(8,128)S(1)} %get-tuple-element.62.refs_0_), channel_id=1, source_target_pairs={{0,8},{4,12},{8,0},{12,4},{16,24},{20,28},{24,16},{28,20},{1,9},{5... | collective-permute-start | bytes 1572872 | tf_op jit(solution)/shard_map/ppermute | solution.py:126
  53.0 15.0 %collective-permute-start.9 = (f32[256,512]{1,0:T(8,128)S(1)}, f32[256,512]{1,0:T(8,128)S(1)}, u32[]{:S(2)}, u32[]{:S(2)}) collective-permute-start(f32[256,512]{1,0:T(8,128)S(1)} %get-tuple-element.63.refs_0_), channel_id=1, source_target_pairs={{0,4},{4,0},{8,12},{12,8},{16,20},{20,16},{24,28},{28,24},{1,5},{5... | collective-permute-start | bytes 1572872 | tf_op jit(solution)/shard_map/ppermute | solution.py:126
  53.0 15.6 %collective-permute-start.6 = (f32[256,512]{1,0:T(8,128)S(1)}, f32[256,512]{1,0:T(8,128)S(1)}, u32[]{:S(2)}, u32[]{:S(2)}) collective-permute-start(f32[256,512]{1,0:T(8,128)S(1)} %get-tuple-element.63.refs_0_), channel_id=1, source_target_pairs={{0,16},{4,20},{8,24},{12,28},{16,0},{20,4},{24,8},{28,12},{1,17},{... | collective-permute-start | bytes 1572872 | tf_op jit(solution)/shard_map/ppermute | solution.py:126
  53.8 25.0 %collective-permute-start.5 = (f32[256,512]{1,0:T(8,128)S(1)}, f32[256,512]{1,0:T(8,128)S(1)}, u32[]{:S(2)}, u32[]{:S(2)}) collective-permute-start(f32[256,512]{1,0:T(8,128)S(1)} %get-tuple-element.63.refs_0_), channel_id=1, source_target_pairs={{0,8},{4,12},{8,0},{12,4},{16,24},{20,28},{24,16},{28,20},{1,9},{5... | collective-permute-start | bytes 1572872 | tf_op jit(solution)/shard_map/ppermute | solution.py:126
  56.9 26.5 %collective-permute-start.20 = (f32[128,512]{1,0:T(8,128)S(1)}, f32[128,512]{1,0:T(8,128)S(1)}, u32[]{:S(2)}, u32[]{:S(2)}) collective-permute-start(f32[128,512]{1,0:T(8,128)S(1)} %slice.81), channel_id=1, source_target_pairs={{0,8},{4,12},{8,0},{12,4},{16,24},{20,28},{24,16},{28,20},{1,9},{5... | collective-permute-start | bytes 786440 | tf_op jit(solution)/shard_map/ppermute | solution.py:126
  67.5 16.3 %collective-permute-start.19 = (f32[128,512]{1,0:T(8,128)S(1)}, f32[128,512]{1,0:T(8,128)S(1)}, u32[]{:S(2)}, u32[]{:S(2)}) collective-permute-start(f32[128,512]{1,0:T(8,128)S(1)} %slice.80), channel_id=1, source_target_pairs={{0,16},{4,20},{8,24},{12,28},{16,0},{20,4},{24,8},{28,12},{1,17},{... | collective-permute-start | bytes 786440 | tf_op jit(solution)/shard_map/ppermute | solution.py:126
  68.0 20.3 %collective-permute-start.32 = (f32[128,512]{1,0:T(8,128)S(1)}, f32[128,512]{1,0:T(8,128)S(1)}, u32[]{:S(2)}, u32[]{:S(2)}) collective-permute-start(f32[128,512]{1,0:T(8,128)S(1)} %slice.83), channel_id=1, source_target_pairs={{0,8},{4,12},{8,0},{12,4},{16,24},{20,28},{24,16},{28,20},{1,9},{5... | collective-permute-start | bytes 786440 | tf_op jit(solution)/shard_map/ppermute | solution.py:126
  68.7 19.7 %collective-permute-start.31 = (f32[128,512]{1,0:T(8,128)S(1)}, f32[128,512]{1,0:T(8,128)S(1)}, u32[]{:S(2)}, u32[]{:S(2)}) collective-permute-start(f32[128,512]{1,0:T(8,128)S(1)} %slice.82), channel_id=1, source_target_pairs={{0,16},{4,20},{8,24},{12,28},{16,0},{20,4},{24,8},{28,12},{1,17},{... | collective-permute-start | bytes 786440 | tf_op jit(solution)/shard_map/ppermute | solution.py:126
  78.7 13.0 %collective-permute-start.23 = (f32[256,512]{1,0:T(8,128)S(1)}, f32[256,512]{1,0:T(8,128)S(1)}, u32[]{:S(2)}, u32[]{:S(2)}) collective-permute-start(f32[256,512]{1,0:T(8,128)S(1)} %collective-permute-done.18.refs_2_), channel_id=1, source_target_pairs={{0,4},{4,0},{8,12},{12,8},{16,20},{20,16},{24,28},{28,24},{1,5},{5... | collective-permute-start | bytes 1572872 | tf_op jit(solution)/shard_map/ppermute | solution.py:126
  83.4 7.7 %collective-permute-start.8 = (f32[128,512]{1,0:T(8,128)S(1)}, f32[128,512]{1,0:T(8,128)S(1)}, u32[]{:S(2)}, u32[]{:S(2)}) collective-permute-start(f32[128,512]{1,0:T(8,128)S(1)} %slice.79), channel_id=1, source_target_pairs={{0,8},{4,12},{8,0},{12,4},{16,24},{20,28},{24,16},{28,20},{1,9},{5... | collective-permute-start | bytes 786440 | tf_op jit(solution)/shard_map/ppermute | solution.py:126
  83.8 7.3 %collective-permute-start.7 = (f32[128,512]{1,0:T(8,128)S(1)}, f32[128,512]{1,0:T(8,128)S(1)}, u32[]{:S(2)}, u32[]{:S(2)}) collective-permute-start(f32[128,512]{1,0:T(8,128)S(1)} %slice.78), channel_id=1, source_target_pairs={{0,16},{4,20},{8,24},{12,28},{16,0},{20,4},{24,8},{28,12},{1,17},{... | collective-permute-start | bytes 786440 | tf_op jit(solution)/shard_map/ppermute | solution.py:126
  88.3 3.3 %collective-permute-start.25 = (f32[128,512]{1,0:T(8,128)S(1)}, f32[128,512]{1,0:T(8,128)S(1)}, u32[]{:S(2)}, u32[]{:S(2)}) collective-permute-start(f32[128,512]{1,0:T(8,128)S(1)} %collective-permute-done.20.refs_4_), channel_id=1, source_target_pairs={{0,4},{4,0},{8,12},{12,8},{16,20},{20,16},{24,28},{28,24},{1,5},{5... | collective-permute-start | bytes 786440 | tf_op jit(solution)/shard_map/ppermute | solution.py:126
  88.3 5.2 %collective-permute-start.11 = (f32[256,512]{1,0:T(8,128)S(1)}, f32[256,512]{1,0:T(8,128)S(1)}, u32[]{:S(2)}, u32[]{:S(2)}) collective-permute-start(f32[256,512]{1,0:T(8,128)S(1)} %collective-permute-done.6.refs_2_), channel_id=1, source_target_pairs={{0,4},{4,0},{8,12},{12,8},{16,20},{20,16},{24,28},{28,24},{1,5},{5... | collective-permute-start | bytes 1572872 | tf_op jit(solution)/shard_map/ppermute | solution.py:126
  91.1 3.6 %collective-permute-start.10 = (f32[256,512]{1,0:T(8,128)S(1)}, f32[256,512]{1,0:T(8,128)S(1)}, u32[]{:S(2)}, u32[]{:S(2)}) collective-permute-start(f32[256,512]{1,0:T(8,128)S(1)} %collective-permute-done.5.refs_1_), channel_id=1, source_target_pairs={{0,4},{4,0},{8,12},{12,8},{16,20},{20,16},{24,28},{28,24},{1,5},{5... | collective-permute-start | bytes 1572872 | tf_op jit(solution)/shard_map/ppermute | solution.py:126
  91.1 2.3 %collective-permute-start.13 = (f32[128,512]{1,0:T(8,128)S(1)}, f32[128,512]{1,0:T(8,128)S(1)}, u32[]{:S(2)}, u32[]{:S(2)}) collective-permute-start(f32[128,512]{1,0:T(8,128)S(1)} %collective-permute-done.8.refs_4_), channel_id=1, source_target_pairs={{0,4},{4,0},{8,12},{12,8},{16,20},{20,16},{24,28},{28,24},{1,5},{5... | collective-permute-start | bytes 786440 | tf_op jit(solution)/shard_map/ppermute | solution.py:126
  91.6 7.8 %collective-permute-start.22 = (f32[256,512]{1,0:T(8,128)S(1)}, f32[256,512]{1,0:T(8,128)S(1)}, u32[]{:S(2)}, u32[]{:S(2)}) collective-permute-start(f32[256,512]{1,0:T(8,128)S(1)} %collective-permute-done.17.refs_1_), channel_id=1, source_target_pairs={{0,4},{4,0},{8,12},{12,8},{16,20},{20,16},{24,28},{28,24},{1,5},{5... | collective-permute-start | bytes 1572872 | tf_op jit(solution)/shard_map/ppermute | solution.py:126
  91.7 2.8 %collective-permute-start.12 = (f32[128,512]{1,0:T(8,128)S(1)}, f32[128,512]{1,0:T(8,128)S(1)}, u32[]{:S(2)}, u32[]{:S(2)}) collective-permute-start(f32[128,512]{1,0:T(8,128)S(1)} %collective-permute-done.7.refs_3_), channel_id=1, source_target_pairs={{0,4},{4,0},{8,12},{12,8},{16,20},{20,16},{24,28},{28,24},{1,5},{5... | collective-permute-start | bytes 786440 | tf_op jit(solution)/shard_map/ppermute | solution.py:126
  93.4 4.3 %collective-permute-start.24 = (f32[128,512]{1,0:T(8,128)S(1)}, f32[128,512]{1,0:T(8,128)S(1)}, u32[]{:S(2)}, u32[]{:S(2)}) collective-permute-start(f32[128,512]{1,0:T(8,128)S(1)} %collective-permute-done.19.refs_3_), channel_id=1, source_target_pairs={{0,4},{4,0},{8,12},{12,8},{16,20},{20,16},{24,28},{28,24},{1,5},{5... | collective-permute-start | bytes 786440 | tf_op jit(solution)/shard_map/ppermute | solution.py:126
  93.6 17.8 %collective-permute-start.33 = (f32[256,512]{1,0:T(8,128)S(1)}, f32[256,512]{1,0:T(8,128)S(1)}, u32[]{:S(2)}, u32[]{:S(2)}) collective-permute-start(f32[256,512]{1,0:T(8,128)S(1)} %get-tuple-element.62.refs_0_), channel_id=1, source_target_pairs={{0,4},{4,0},{8,12},{12,8},{16,20},{20,16},{24,28},{28,24},{1,5},{5... | collective-permute-start | bytes 1572872 | tf_op jit(solution)/shard_map/ppermute | solution.py:126
  94.5 19.1 %collective-permute-start.35 = (f32[256,512]{1,0:T(8,128)S(1)}, f32[256,512]{1,0:T(8,128)S(1)}, u32[]{:S(2)}, u32[]{:S(2)}) collective-permute-start(f32[256,512]{1,0:T(8,128)S(1)} %collective-permute-done.30.refs_2_), channel_id=1, source_target_pairs={{0,4},{4,0},{8,12},{12,8},{16,20},{20,16},{24,28},{28,24},{1,5},{5... | collective-permute-start | bytes 1572872 | tf_op jit(solution)/shard_map/ppermute | solution.py:126
  94.7 21.2 %collective-permute-start.34 = (f32[256,512]{1,0:T(8,128)S(1)}, f32[256,512]{1,0:T(8,128)S(1)}, u32[]{:S(2)}, u32[]{:S(2)}) collective-permute-start(f32[256,512]{1,0:T(8,128)S(1)} %collective-permute-done.29.refs_1_), channel_id=1, source_target_pairs={{0,4},{4,0},{8,12},{12,8},{16,20},{20,16},{24,28},{28,24},{1,5},{5... | collective-permute-start | bytes 1572872 | tf_op jit(solution)/shard_map/ppermute | solution.py:126
  97.7 6.8 %collective-permute-start.16 = (f32[32,512]{1,0:T(8,128)S(1)}, f32[32,512]{1,0:T(8,128)S(1)}, u32[]{:S(2)}, u32[]{:S(2)}) collective-permute-start(f32[32,512]{1,0:T(8,128)S(1)} %get-tuple-element.35.refs_0_.refs_6_), channel_id=1, source_target_pairs={{0,3},{1,2},{2,1},{3,0},{4,7},{5,6},{6,5},{7,4},{8,11},{9,10},{10,... | collective-permute-start | bytes 196616 | tf_op jit(solution)/shard_map/ppermute | solution.py:126
  99.4 7.1 %collective-permute-start.15 = (f32[32,512]{1,0:T(8,128)S(1)}, f32[32,512]{1,0:T(8,128)S(1)}, u32[]{:S(2)}, u32[]{:S(2)}) collective-permute-start(f32[32,512]{1,0:T(8,128)S(1)} %get-tuple-element.35.refs_0_.refs_6_), channel_id=1, source_target_pairs={{0,2},{1,3},{2,0},{3,1},{4,6},{5,7},{6,4},{7,5},{8,10},{9,11},{10,... | collective-permute-start | bytes 196616 | tf_op jit(solution)/shard_map/ppermute | solution.py:126
  104.5 4.3 %collective-permute-start.14 = (f32[32,512]{1,0:T(8,128)S(1)}, f32[32,512]{1,0:T(8,128)S(1)}, u32[]{:S(2)}, u32[]{:S(2)}) collective-permute-start(f32[32,512]{1,0:T(8,128)S(1)} %get-tuple-element.35.refs_0_.refs_6_), channel_id=1, source_target_pairs={{0,1},{1,0},{2,3},{3,2},{4,5},{5,4},{6,7},{7,6},{8,9},{9,8},{10,11... | collective-permute-start | bytes 196616 | tf_op jit(solution)/shard_map/ppermute | solution.py:126
  106.6 6.6 %collective-permute-start.37 = (f32[128,512]{1,0:T(8,128)S(1)}, f32[128,512]{1,0:T(8,128)S(1)}, u32[]{:S(2)}, u32[]{:S(2)}) collective-permute-start(f32[128,512]{1,0:T(8,128)S(1)} %collective-permute-done.32.refs_4_), channel_id=1, source_target_pairs={{0,4},{4,0},{8,12},{12,8},{16,20},{20,16},{24,28},{28,24},{1,5},{5... | collective-permute-start | bytes 786440 | tf_op jit(solution)/shard_map/ppermute | solution.py:126
  108.7 7.1 %collective-permute-start.36 = (f32[128,512]{1,0:T(8,128)S(1)}, f32[128,512]{1,0:T(8,128)S(1)}, u32[]{:S(2)}, u32[]{:S(2)}) collective-permute-start(f32[128,512]{1,0:T(8,128)S(1)} %collective-permute-done.31.refs_3_), channel_id=1, source_target_pairs={{0,4},{4,0},{8,12},{12,8},{16,20},{20,16},{24,28},{28,24},{1,5},{5... | collective-permute-start | bytes 786440 | tf_op jit(solution)/shard_map/ppermute | solution.py:126
  111.4 6.8 %collective-permute-start.28 = (f32[32,512]{1,0:T(8,128)S(1)}, f32[32,512]{1,0:T(8,128)S(1)}, u32[]{:S(2)}, u32[]{:S(2)}) collective-permute-start(f32[32,512]{1,0:T(8,128)S(1)} %shard_map.187.refs_0_), channel_id=1, source_target_pairs={{0,3},{1,2},{2,1},{3,0},{4,7},{5,6},{6,5},{7,4},{8,11},{9,10},{10,... | collective-permute-start | bytes 196616 | tf_op jit(solution)/shard_map/ppermute | solution.py:126
  113.2 7.4 %collective-permute-start.27 = (f32[32,512]{1,0:T(8,128)S(1)}, f32[32,512]{1,0:T(8,128)S(1)}, u32[]{:S(2)}, u32[]{:S(2)}) collective-permute-start(f32[32,512]{1,0:T(8,128)S(1)} %shard_map.187.refs_0_), channel_id=1, source_target_pairs={{0,2},{1,3},{2,0},{3,1},{4,6},{5,7},{6,4},{7,5},{8,10},{9,11},{10,... | collective-permute-start | bytes 196616 | tf_op jit(solution)/shard_map/ppermute | solution.py:126
  113.6 6.9 %collective-permute-start.26 = (f32[32,512]{1,0:T(8,128)S(1)}, f32[32,512]{1,0:T(8,128)S(1)}, u32[]{:S(2)}, u32[]{:S(2)}) collective-permute-start(f32[32,512]{1,0:T(8,128)S(1)} %shard_map.187.refs_0_), channel_id=1, source_target_pairs={{0,1},{1,0},{2,3},{3,2},{4,5},{5,4},{6,7},{7,6},{8,9},{9,8},{10,11... | collective-permute-start | bytes 196616 | tf_op jit(solution)/shard_map/ppermute | solution.py:126
  123.2 5.1 %collective-permute-start.38 = (f32[32,512]{1,0:T(8,128)S(1)}, f32[32,512]{1,0:T(8,128)S(1)}, u32[]{:S(2)}, u32[]{:S(2)}) collective-permute-start(f32[32,512]{1,0:T(8,128)S(1)} %get-tuple-element.42), channel_id=1, source_target_pairs={{0,1},{1,0},{2,3},{3,2},{4,5},{5,4},{6,7},{7,6},{8,9},{9,8},{10,11... | collective-permute-start | bytes 196616 | tf_op jit(solution)/shard_map/ppermute | solution.py:126
  123.2 8.2 %collective-permute-start.39 = (f32[32,512]{1,0:T(8,128)S(1)}, f32[32,512]{1,0:T(8,128)S(1)}, u32[]{:S(2)}, u32[]{:S(2)}) collective-permute-start(f32[32,512]{1,0:T(8,128)S(1)} %get-tuple-element.43), channel_id=1, source_target_pairs={{0,2},{1,3},{2,0},{3,1},{4,6},{5,7},{6,4},{7,5},{8,10},{9,11},{10,... | collective-permute-start | bytes 196616 | tf_op jit(solution)/shard_map/ppermute | solution.py:126
  126.4 6.2 %collective-permute-start.40 = (f32[32,512]{1,0:T(8,128)S(1)}, f32[32,512]{1,0:T(8,128)S(1)}, u32[]{:S(2)}, u32[]{:S(2)}) collective-permute-start(f32[32,512]{1,0:T(8,128)S(1)} %get-tuple-element.44), channel_id=1, source_target_pairs={{0,3},{1,2},{2,1},{3,0},{4,7},{5,6},{6,5},{7,4},{8,11},{9,10},{10,... | collective-permute-start | bytes 196616 | tf_op jit(solution)/shard_map/ppermute | solution.py:126
  134.4 5.0 %collective-permute-start.41 = (f32[32,512]{1,0:T(8,128)S(1)}, f32[32,512]{1,0:T(8,128)S(1)}, u32[]{:S(2)}, u32[]{:S(2)}) collective-permute-start(f32[32,512]{1,0:T(8,128)S(1)} %get-tuple-element.46), channel_id=1, source_target_pairs={{0,1},{1,0},{2,3},{3,2},{4,5},{5,4},{6,7},{7,6},{8,9},{9,8},{10,11... | collective-permute-start | bytes 196616 | tf_op jit(solution)/shard_map/ppermute | solution.py:126
  135.3 6.1 %collective-permute-start.42 = (f32[32,512]{1,0:T(8,128)S(1)}, f32[32,512]{1,0:T(8,128)S(1)}, u32[]{:S(2)}, u32[]{:S(2)}) collective-permute-start(f32[32,512]{1,0:T(8,128)S(1)} %get-tuple-element.47), channel_id=1, source_target_pairs={{0,2},{1,3},{2,0},{3,1},{4,6},{5,7},{6,4},{7,5},{8,10},{9,11},{10,... | collective-permute-start | bytes 196616 | tf_op jit(solution)/shard_map/ppermute | solution.py:126
  136.5 6.2 %collective-permute-start.43 = (f32[32,512]{1,0:T(8,128)S(1)}, f32[32,512]{1,0:T(8,128)S(1)}, u32[]{:S(2)}, u32[]{:S(2)}) collective-permute-start(f32[32,512]{1,0:T(8,128)S(1)} %get-tuple-element.48), channel_id=1, source_target_pairs={{0,3},{1,2},{2,1},{3,0},{4,7},{5,6},{6,5},{7,4},{8,11},{9,10},{10,... | collective-permute-start | bytes 196616 | tf_op jit(solution)/shard_map/ppermute | solution.py:126
  144.5 5.6 %collective-permute-start.44 = (f32[8,2560]{1,0:T(8,128)S(1)}, f32[8,2560]{1,0:T(8,128)S(1)}, u32[]{:S(2)}, u32[]{:S(2)}) collective-permute-start(f32[8,2560]{1,0:T(8,128)S(1)} %get-tuple-element.51), channel_id=1, source_target_pairs={{0,1},{1,0},{2,3},{3,2},{4,5},{5,4},{6,7},{7,6},{8,9},{9,8},{10,11... | collective-permute-start | bytes 245768 | tf_op jit(solution)/shard_map/ppermute | solution.py:126
  145.3 6.2 %collective-permute-start.45 = (f32[8,2560]{1,0:T(8,128)S(1)}, f32[8,2560]{1,0:T(8,128)S(1)}, u32[]{:S(2)}, u32[]{:S(2)}) collective-permute-start(f32[8,2560]{1,0:T(8,128)S(1)} %get-tuple-element.52), channel_id=1, source_target_pairs={{0,2},{1,3},{2,0},{3,1},{4,6},{5,7},{6,4},{7,5},{8,10},{9,11},{10,... | collective-permute-start | bytes 245768 | tf_op jit(solution)/shard_map/ppermute | solution.py:126
  147.3 6.2 %collective-permute-start.46 = (f32[8,2560]{1,0:T(8,128)S(1)}, f32[8,2560]{1,0:T(8,128)S(1)}, u32[]{:S(2)}, u32[]{:S(2)}) collective-permute-start(f32[8,2560]{1,0:T(8,128)S(1)} %get-tuple-element.53), channel_id=1, source_target_pairs={{0,3},{1,2},{2,1},{3,0},{4,7},{5,6},{6,5},{7,4},{8,11},{9,10},{10,... | collective-permute-start | bytes 245768 | tf_op jit(solution)/shard_map/ppermute | solution.py:126
  154.8 8.8 %all-to-all-start.1 = ((f32[8,2,8,256]{3,2,1,0:T(8,128)}), f32[8,2,8,256]{3,2,1,0:T(8,128)S(1)}, u32[]{:S(2)}, u32[]{:S(2)}) async-start(f32[8,2,8,256]{3,2,1,0:T(8,128)} %shard_map.192), calls=%async_computation.1 | async-start | bytes 262144 | tf_op jit(solution)/shard_map/all_to_all | solution.py:330

commit v2 on v1

--- a/solution.py
+++ b/solution.py
@@ -130,16 +130,24 @@
     return [parts[0]] + [flip(parts[e], "col", e) for e in range(1, len(parts))]
 
 
-def kernel_call(body, out_shapes, *operands):
+def kernel_call(body, out_shapes, scalars, operands, held=(), scratch=()):
     spec = pl.BlockSpec(memory_space=pltpu.VMEM)
     smem = pl.BlockSpec(memory_space=pltpu.SMEM)
+    used = len(scalars) + len(operands)
+
+    def run(*refs):
+        body(*refs[:used], *refs[used + len(held) :])
+
     return pl.pallas_call(
-        body,
-        out_shape=[jax.ShapeDtypeStruct(s, d) for s, d in out_shapes],
-        in_specs=[smem] + [spec] * (len(operands) - 1),
+        run,
+        out_shape=[jax.ShapeDtypeStruct(shape, kind) for shape, kind in out_shapes],
+        in_specs=[smem] * len(scalars)
+        + [spec] * len(operands)
+        + [pl.BlockSpec(memory_space=pl.ANY)] * len(held),
         out_specs=[spec] * len(out_shapes),
+        scratch_shapes=list(scratch),
         compiler_params=pltpu.CompilerParams(vmem_limit_bytes=40 * 1024 * 1024),
-    )(*operands)
+    )(*scalars, *operands, *held)
 
 
 def halves(values):
@@ -197,7 +205,7 @@
     pieces = [block, near, far, flip(near[:half], "leaf", 4), flip(far[half:], "leaf", 2)]
     pieces += [flip(piece, "leaf", 1) for piece in pieces]
     shape = (block.shape[0] * lax.axis_size("leaf"), block.shape[1])
-    return kernel_call(assemble_kernel, [(shape, jnp.bfloat16)] * 2, place, *pieces)
+    return kernel_call(assemble_kernel, [(shape, jnp.bfloat16)] * 2, [place], pieces)
 
 
 def arrange_kernel(place, values, *parts):
@@ -294,38 +302,151 @@
             result[(place[1] ^ e) * fronts + j, 1] = part[:, start : start + width]
 
 
-def root_replicated(section, root_inverse, root_coupling):
+def reduce_blocks(level, live, links, blocks, inverse, coupling, solved):
+    red_blocks, link_total, size = inverse.shape[0], coupling.shape[1], inverse.shape[1]
+    lanes = lax.broadcasted_iota(jnp.int32, (1, size), 1)
+    for i in range(red_blocks):
+        mask = (lanes + i * size < live[level, 0]).astype(jnp.float32)
+        high, low = halves(inverse[i])
+        value = product(blocks[i] * mask, high, low, 0) * mask
+        solved[:, i * size : (i + 1) * size] = value
+        pairs = [halves(coupling[i, k]) for k in range(link_total)]
+        high, low = (jnp.concatenate(part, 1) for part in zip(*pairs, strict=True))
+        pushed = product(value, high, low, 0)
+        for k in range(link_total):
+            target = red_blocks + links[i, k]
+            blocks[target] = blocks[target] - pushed[:, k * size : (k + 1) * size]
+
+
+def send_halves(place, level, blocks, red_blocks, kept, sent):
+    half = kept.shape[0]
+    upper = (place[0] >> level) & 1
+    kept[...] = blocks[pl.ds(red_blocks + upper * half, half)]
+    sent[...] = blocks[pl.ds(red_blocks + (1 - upper) * half, half)]
+
+
+def load_halves(place, level, order, kept, received, joined, blocks):
+    half = kept.shape[0]
+    upper = (place[0] >> level) & 1
+    joined[pl.ds(upper * half, half)] = kept[...]
+    joined[pl.ds((1 - upper) * half, half)] = received[...]
+    for n in range(2 * half):
+        blocks[n] = joined[order[0, n]]
+
+
+def lowest_kernel(place, live, links, section, inverse, coupling, solved, kept, sent, blocks):
+    size = inverse.shape[1]
+    for n in range(blocks.shape[0]):
+        blocks[n] = section[:, n * size : (n + 1) * size]
+    reduce_blocks(0, live, links, blocks, inverse, coupling, solved)
+    send_halves(place, 0, blocks, inverse.shape[0], kept, sent)
+
+
+def middle_kernel(
+    place, live, links, order, old, received, inverse, coupling, solved, kept, sent, joined, blocks
+):
+    load_halves(place, 0, order, old, received, joined, blocks)
+    reduce_blocks(1, live, links, blocks, inverse, coupling, solved)
+    send_halves(place, 1, blocks, inverse.shape[0], kept, sent)
+
+
+def highest_kernel(
+    place, live, links, order, last_order, old, received, inverse, coupling, solved, split, joined, blocks
+):
+    load_halves(place, 1, order, old, received, joined, blocks)
+    reduce_blocks(2, live, links, blocks, inverse, coupling, solved)
+    red_blocks, size = inverse.shape[0], inverse.shape[1]
+    leaf_count, panel_count, rows, width = split.shape
+    per_panel = width // size
+    for panel in range(panel_count):
+        for j in range(per_panel):
+            block = blocks[red_blocks + last_order[0, panel * per_panel + j]]
+            split[:, panel, :, j * size : (j + 1) * size] = block.reshape(leaf_count, rows, size)
+
+
+def eliminate_all(place, right_sides, level_data, front_rows, panel_count, panel_rows):
+    rhs_rows = right_sides.shape[0]
+    red_blocks, size = level_data[0][0].shape[:2]
+    leaf_count = lax.axis_size("leaf")
+    one = ((rhs_rows, red_blocks * size), jnp.float32)
+
+    def many(count):
+        return (count, rhs_rows, size)
+
+    inverse, coupling, links, order = level_data[0]
+    count = right_sides.shape[1] // size
+    half = ((count - red_blocks) // 2, rhs_rows, size)
+    solved_first, kept, sent = kernel_call(
+        lowest_kernel,
+        [one, (half, jnp.float32), (half, jnp.float32)],
+        [place, front_rows, links],
+        [right_sides, inverse, coupling],
+        scratch=[pltpu.VMEM(many(count), jnp.float32)],
+    )
+    received = flip(sent, "leaf", 1)
+    inverse, coupling, links, next_order = level_data[1]
+    count -= red_blocks
+    half = ((count - red_blocks) // 2, rhs_rows, size)
+    solved_second, kept, sent = kernel_call(
+        middle_kernel,
+        [one, (half, jnp.float32), (half, jnp.float32)],
+        [place, front_rows, links, order],
+        [kept, received, inverse, coupling],
+        scratch=[pltpu.VMEM(many(count), jnp.float32)] * 2,
+    )
+    received = flip(sent, "leaf", 2)
+    inverse, coupling, links, last_order = level_data[2]
+    count -= red_blocks
+    rows = rhs_rows // leaf_count
+    solved_third, split = kernel_call(
+        highest_kernel,
+        [one, ((leaf_count, panel_count, rows, panel_rows), jnp.float32)],
+        [place, front_rows, links, next_order, last_order],
+        [kept, received, inverse, coupling],
+        scratch=[pltpu.VMEM(many(count), jnp.float32)] * 2,
+    )
+    return (solved_first, solved_second, solved_third), split
+
+
+def root_replicated(place, split, root_inverse, root_coupling):
     leaf_count, col_count = lax.axis_size("leaf"), lax.axis_size("col")
-    place = jnp.stack([lax.axis_index("leaf"), lax.axis_index("col")]).astype(jnp.int32)
     first_high, first_low = spread_matrix(place, root_inverse[0])
     between_high, between_low = spread_matrix(place, root_coupling)
     second_high, second_low = spread_matrix(place, root_inverse[1])
-    rhs_rows = section.shape[0]
     panel_count, panel_rows, own_columns = root_inverse.shape
-    rows = rhs_rows // leaf_count
+    rows = split.shape[2]
+    rhs_rows = rows * leaf_count
     group = rows * col_count
     total = panel_rows * leaf_count
-    split = section.reshape(leaf_count, rows, panel_count, panel_rows).transpose(0, 2, 1, 3)
     whole = lax.all_to_all(split, "leaf", 0, 0, tiled=True)
     wide = [((rows, total + own_columns), jnp.float32)] * col_count
     one = ((group, own_columns), jnp.float32)
-    parts = swap_columns(kernel_call(arrange_kernel, wide, place, whole))
-    first, rest = kernel_call(first_kernel, [one, one], place, *parts, first_high, first_low)
+    parts = swap_columns(kernel_call(arrange_kernel, wide, [place], [whole]))
+    first, rest = kernel_call(
+        first_kernel, [one, one], [place], [*parts, first_high, first_low]
+    )
     parts = swap_columns([first] * col_count)
-    (left,) = kernel_call(coupled_kernel, [one], place, *parts, between_high, between_low, rest)
+    (left,) = kernel_call(
+        coupled_kernel, [one], [place], [*parts, between_high, between_low, rest]
+    )
     parts = swap_columns([left] * col_count)
-    parts = kernel_call(turn_kernel, [one] * col_count, place, *parts, second_high, second_low)
+    parts = kernel_call(
+        turn_kernel, [one] * col_count, [place], [*parts, second_high, second_low]
+    )
     parts = swap_columns(parts)
     last, *parts = kernel_call(
-        back_kernel, [one] * (col_count + 1), place, *parts, between_high, between_low
+        back_kernel, [one] * (col_count + 1), [place], [*parts, between_high, between_low]
     )
     parts = swap_columns(parts)
     parts = kernel_call(
-        final_kernel, wide, place, *parts, first_high, first_low, first, last
+        final_kernel, wide, [place], [*parts, first_high, first_low, first, last]
     )
     parts = swap_columns(parts)
     (split,) = kernel_call(
-        collect_kernel, [((leaf_count, panel_count, rows, panel_rows), jnp.float32)], place, *parts
+        collect_kernel,
+        [((leaf_count, panel_count, rows, panel_rows), jnp.float32)],
+        [place],
+        parts,
     )
     whole = lax.all_to_all(split, "leaf", 0, 0, tiled=True)
     return whole.transpose(0, 2, 1, 3).reshape(rhs_rows, panel_count, panel_rows)
@@ -365,6 +486,12 @@
         (inverse_second, coupling_second, links_second, order_second),
         (inverse_third, coupling_third, links_third, order_third),
     )
+    if replicates(right_sides.shape[0], root_inverse):
+        place = jnp.stack([lax.axis_index("leaf"), lax.axis_index("col")]).astype(jnp.int32)
+        solved, split = eliminate_all(
+            place, right_sides, level_data, front_rows, *root_inverse.shape[:2]
+        )
+        return (*solved, root_replicated(place, split, root_inverse, root_coupling))
     section = right_sides
     outputs = []
     for level_index in range(3):
@@ -377,8 +504,7 @@
             skeleton = join_halves(skeleton, level_index)
         skeleton = jnp.take(skeleton, order_map[0], axis=1)
         section = skeleton.reshape(skeleton.shape[0], -1)
-    solve = root_replicated if replicates(right_sides.shape[0], root_inverse) else root_wide
-    return (*outputs, solve(section, root_inverse, root_coupling))
+    return (*outputs, root_wide(section, root_inverse, root_coupling))
 
 
 def solution(mesh):

time: 165 us -> 160 us (0.970)
  matrix products: 8.47 us -> 0 us
  blocking collectives: 0 us -> 7.92 us
  Pallas kernels: 14.7 us -> 21.5 us
  other arithmetic: 3.8 us -> 0.07 us
  waiting for transfers between devices: 76.3 us -> 73 us
  starting transfers between devices: 49.1 us -> 47 us
  local copies, waits for them, and re-layouts: 10.8 us -> 8.76 us
    dot_general x9 -> x0, matrix products: 8.47 us -> none  [the longest x3 3.09 us: eliminate(): jnp.einsum('rib,iba->ria', redundant * live_rows, inverse, precision=lax....]
    all_to_all x0 -> x1, blocking collectives: none -> 7.92 us  [root_replicated(): whole = lax.all_to_all(split, 'leaf', 0, 0, tiled=True)]
    pallas_call x10 -> x13, Pallas kernels: 14.7 us -> 21.5 us  [kernel_call(): pl.pallas_call(run, out_shape=[jax.ShapeDtypeStruct(shape, kind) for shap...]
    unnamed x31 -> x32, local copies, waits for them, and re-layouts: 3 us -> 8.57 us
    ppermute x45 -> x47, waiting for transfers between devices: 64.3 us -> 69.1 us  [flip(): return lax.ppermute(block, axis, [(i, i ^ distance) for i in range(count)])]
    all_to_all x2 -> x1, waiting for transfers between devices: 8.66 us -> 3.98 us  [root_replicated(): whole = lax.all_to_all(split, 'leaf', 0, 0, tiled=True)]
    ppermute x2 -> x0, waiting for transfers between devices: 3.4 us -> none  [partner(): return lax.ppermute(block, axis, route)]
    all_to_all x2 -> x1, starting transfers between devices: 6.92 us -> 3.97 us  [root_replicated(): whole = lax.all_to_all(split, 'leaf', 0, 0, tiled=True)]
  transfers between devices with their start and end apart: 49 -> 48, of which waited for: 27 -> 27; matrix products, arithmetic and copies ran while one was open for 9% -> 0% of each run, Pallas kernels for 4% -> 6%
where the time goes in v2:
time: 160 us; the launch traced here: 159 us
  waiting for transfers between devices  73 us (46%)
  starting transfers between devices  47 us (29%)
  Pallas kernels  21.5 us (13%)
  local copies, waits for them, and re-layouts  8.76 us (5%)
  blocking collectives  7.92 us (5%)
    ppermute x47, waiting for transfers between devices, flip(): return lax.ppermute(block, axis, [(i, i ^ distance) for i in range(count)])  69.1 us
    ppermute x47, starting transfers between devices, flip(): return lax.ppermute(block, axis, [(i, i ^ distance) for i in range(count)])  43 us
    pallas_call x13, Pallas kernels, kernel_call(): pl.pallas_call(run, out_shape=[jax.ShapeDtypeStruct(shape, kind) for shap...  21.5 us
    unnamed x32, local copies, waits for them, and re-layouts  8.57 us
    all_to_all x1, blocking collectives, root_replicated(): whole = lax.all_to_all(split, 'leaf', 0, 0, tiled=True)  7.92 us
    all_to_all x1, waiting for transfers between devices, root_replicated(): whole = lax.all_to_all(split, 'leaf', 0, 0, tiled=True)  3.98 us
    all_to_all x1, starting transfers between devices, root_replicated(): whole = lax.all_to_all(split, 'leaf', 0, 0, tiled=True)  3.97 us
  transfers between devices with their start and end apart: 48, of which 27 were waited for; matrix products, arithmetic and copies ran while one was open for 0% of the time, Pallas kernels for 6%

profile of v2, /device:TPU:0, one launch (start us, length us, event | category | flops | bytes accessed | tf_op | source)
XLA Modules:
  0.0 159.1 jit_solution(5728916348117177529)
XLA Ops:
  0.7 0.8 copy.23.refs_1_
  1.5 1.1 copy-done
  2.6 1.0 copy-done.4
  3.7 0.9 copy-done.6
  5.3 2.4 %shard_map.183 = (f32[64,512]{1,0:T(8,128)}, f32[6,64,128]{2,1,0:T(8,128)S(1)}, f32[6,64,128]{2,1,0:T(8,128)S(1)}) custom-call(s32[2]{0:T(128)S(1)} %pad_add_fusion.refs_0_, s32[3,1]{1,0:T(4,128)S(1)} %copy.23.refs_1_, s32[4,3]{1,0:T(4,128)S(1)} %copy-done.8, f32[64,2048]{1,0:T(8,128)S(1)} %copy-done.4, f32[4,128,128]{2,1,0:T(8,128)S(1)} %copy-done.6, ...), custom_call_target="tpu_custom_call" | custom-call | tf_op jit(solution)/shard_map/pallas_call | solution.py:141
  8.2 1.1 collective-permute-done.refs_5_
  9.2 0.9 copy-done.5
  11.5 2.4 %shard_map.184 = (f32[64,512]{1,0:T(8,128)}, f32[4,64,128]{2,1,0:T(8,128)S(1)}, f32[4,64,128]{2,1,0:T(8,128)S(1)}) custom-call(s32[2]{0:T(128)S(1)} %pad_add_fusion.refs_0_, s32[3,1]{1,0:T(4,128)S(1)} %copy.23.refs_1_, s32[4,3]{1,0:T(4,128)S(1)} %copy-done.9, s32[1,12]{1,0:T(1,128)S(1)} %copy-done.11, f32[6,64,128]{2,1,0:T(8,128)S(1)} %get-tuple-element.38.refs_4_, ...), custom_call_target="tpu_custom_call" | custom-call | tf_op jit(solution)/shard_map/pallas_call | solution.py:141
  13.9 2.9 %collective-permute-start.1 = (f32[4,64,128]{2,1,0:T(8,128)S(1)}, f32[4,64,128]{2,1,0:T(8,128)S(1)}, u32[]{:S(2)}, u32[]{:S(2)}) collective-permute-start(f32[4,64,128]{2,1,0:T(8,128)S(1)} %get-tuple-element.42), channel_id=1, source_target_pairs={{0,8},{4,12},{8,0},{12,4},{16,24},{20,28},{24,16},{28,20},{1,9},{5... | collective-permute-start | bytes 393224 | tf_op jit(solution)/shard_map/ppermute | solution.py:126
  16.8 1.5 collective-permute-start.18
  18.3 2.3 %collective-permute-done.1.refs_6_ = f32[4,64,128]{2,1,0:T(8,128)S(1)} collective-permute-done((f32[4,64,128]{2,1,0:T(8,128)S(1)}, f32[4,64,128]{2,1,0:T(8,128)S(1)}, u32[]{:S(2)}, u32[]{:S(2)}) %collective-permute-start.1) | collective-permute-done | bytes 131104 | tf_op jit(solution)/shard_map/ppermute | solution.py:126
  20.6 0.9 copy-done.7
  21.6 2.6 %shard_map.185 = (f32[64,512]{1,0:T(8,128)}, f32[8,2,8,256]{3,2,1,0:T(8,128)}) custom-call(s32[2]{0:T(128)S(1)} %pad_add_fusion.refs_0_, s32[3,1]{1,0:T(4,128)S(1)} %copy.23.refs_1_, s32[4,3]{1,0:T(4,128)S(1)} %copy-done.10, s32[1,8]{1,0:T(1,128)S(1)} %copy-done.12, s32[1,4]{1,0:T(1,128)S(1)} %copy-done.13, f32[4,64,128]{2,1,0:T(8,128)S(1)} %get-tuple-element.41.refs_5_, ...), custom_call_target="tpu_custom_call" | custom-call | tf_op jit(solution)/shard_map/pallas_call | solution.py:141
  24.2 4.0 %all-to-all-start = ((f32[8,2,8,256]{3,2,1,0:T(8,128)}), f32[8,2,8,256]{3,2,1,0:T(8,128)S(1)}, u32[]{:S(2)}, u32[]{:S(2)}) async-start(f32[8,2,8,256]{3,2,1,0:T(8,128)} %get-tuple-element.44), calls=%async_computation | async-start | bytes 262144 | tf_op jit(solution)/shard_map/all_to_all | solution.py:421
  28.1 2.0 %collective-permute-start.17 = (f32[256,512]{1,0:T(8,128)S(1)}, f32[256,512]{1,0:T(8,128)S(1)}, u32[]{:S(2)}, u32[]{:S(2)}) collective-permute-start(f32[256,512]{1,0:T(8,128)S(1)} %copy-done.3), channel_id=1, source_target_pairs={{0,8},{4,12},{8,0},{12,4},{16,24},{20,28},{24,16},{28,20},{1,9},{5... | collective-permute-start | bytes 1572872 | tf_op jit(solution)/shard_map/ppermute | solution.py:126
  30.2 4.0 %all-to-all-done.refs_1_ = f32[8,2,8,256]{3,2,1,0:T(8,128)S(1)} async-done(((f32[8,2,8,256]{3,2,1,0:T(8,128)}), f32[8,2,8,256]{3,2,1,0:T(8,128)S(1)}, u32[]{:S(2)}, u32[]{:S(2)}) %all-to-all-start) | async-done | bytes 131104 | tf_op jit(solution)/shard_map/all_to_all | solution.py:421
  34.7 1.6 %collective-permute-start.2 = (f32[8,2560]{1,0:T(8,128)S(1)}, f32[8,2560]{1,0:T(8,128)S(1)}, u32[]{:S(2)}, u32[]{:S(2)}) collective-permute-start(f32[8,2560]{1,0:T(8,128)S(1)} %get-tuple-element.46), channel_id=1, source_target_pairs={{0,1},{1,0},{2,3},{3,2},{4,5},{5,4},{6,7},{7,6},{8,9},{9,8},{10,11... | collective-permute-start | bytes 245768 | tf_op jit(solution)/shard_map/ppermute | solution.py:126
  36.4 2.6 %collective-permute-start.3 = (f32[8,2560]{1,0:T(8,128)S(1)}, f32[8,2560]{1,0:T(8,128)S(1)}, u32[]{:S(2)}, u32[]{:S(2)}) collective-permute-start(f32[8,2560]{1,0:T(8,128)S(1)} %get-tuple-element.47), channel_id=1, source_target_pairs={{0,2},{1,3},{2,0},{3,1},{4,6},{5,7},{6,4},{7,5},{8,10},{9,11},{10,... | collective-permute-start | bytes 245768 | tf_op jit(solution)/shard_map/ppermute | solution.py:126
  39.0 1.0 collective-permute-done.2.refs_2_
  40.6 2.0 %collective-permute-done.3.refs_3_ = f32[8,2560]{1,0:T(8,128)S(1)} collective-permute-done((f32[8,2560]{1,0:T(8,128)S(1)}, f32[8,2560]{1,0:T(8,128)S(1)}, u32[]{:S(2)}, u32[]{:S(2)}) %collective-permute-start.3) | collective-permute-done | bytes 81952 | tf_op jit(solution)/shard_map/ppermute | solution.py:126
  42.6 1.8 %collective-permute-start.4 = (f32[8,2560]{1,0:T(8,128)S(1)}, f32[8,2560]{1,0:T(8,128)S(1)}, u32[]{:S(2)}, u32[]{:S(2)}) collective-permute-start(f32[8,2560]{1,0:T(8,128)S(1)} %get-tuple-element.48), channel_id=1, source_target_pairs={{0,3},{1,2},{2,1},{3,0},{4,7},{5,6},{6,5},{7,4},{8,11},{9,10},{10,... | collective-permute-start | bytes 245768 | tf_op jit(solution)/shard_map/ppermute | solution.py:126
  44.4 4.5 %collective-permute-done.4.refs_4_ = f32[8,2560]{1,0:T(8,128)S(1)} collective-permute-done((f32[8,2560]{1,0:T(8,128)S(1)}, f32[8,2560]{1,0:T(8,128)S(1)}, u32[]{:S(2)}, u32[]{:S(2)}) %collective-permute-start.4) | collective-permute-done | bytes 81952 | tf_op jit(solution)/shard_map/ppermute | solution.py:126
  50.0 1.5 collective-permute-start.5
  52.3 11.4 %collective-permute-done.29.refs_2_ = f32[256,512]{1,0:T(8,128)S(1)} collective-permute-done((f32[256,512]{1,0:T(8,128)S(1)}, f32[256,512]{1,0:T(8,128)S(1)}, u32[]{:S(2)}, u32[]{:S(2)}) %collective-permute-start.29) | collective-permute-done | bytes 524320 | tf_op jit(solution)/shard_map/ppermute | solution.py:126
  64.9 1.4 collective-permute-start.31
  66.3 8.6 %collective-permute-done.5.refs_2_ = f32[256,512]{1,0:T(8,128)S(1)} collective-permute-done((f32[256,512]{1,0:T(8,128)S(1)}, f32[256,512]{1,0:T(8,128)S(1)}, u32[]{:S(2)}, u32[]{:S(2)}) %collective-permute-start.5) | collective-permute-done | bytes 524320 | tf_op jit(solution)/shard_map/ppermute | solution.py:126
  74.9 4.7 %collective-permute-done.20.refs_5_ = f32[128,512]{1,0:T(8,128)S(1)} collective-permute-done((f32[128,512]{1,0:T(8,128)S(1)}, f32[128,512]{1,0:T(8,128)S(1)}, u32[]{:S(2)}, u32[]{:S(2)}) %collective-permute-start.20) | collective-permute-done | bytes 262176 | tf_op jit(solution)/shard_map/ppermute | solution.py:126
  80.1 1.2 collective-permute-start.7
  81.3 3.2 %collective-permute-done.32.refs_5_ = f32[128,512]{1,0:T(8,128)S(1)} collective-permute-done((f32[128,512]{1,0:T(8,128)S(1)}, f32[128,512]{1,0:T(8,128)S(1)}, u32[]{:S(2)}, u32[]{:S(2)}) %collective-permute-start.32) | collective-permute-done | bytes 262176 | tf_op jit(solution)/shard_map/ppermute | solution.py:126
  85.0 2.3 %collective-permute-done.8.refs_5_ = f32[128,512]{1,0:T(8,128)S(1)} collective-permute-done((f32[128,512]{1,0:T(8,128)S(1)}, f32[128,512]{1,0:T(8,128)S(1)}, u32[]{:S(2)}, u32[]{:S(2)}) %collective-permute-start.8) | collective-permute-done | bytes 262176 | tf_op jit(solution)/shard_map/ppermute | solution.py:126
  88.4 1.3 collective-permute-done.13.refs_10_
  91.3 1.3 shard_map.187
  92.5 1.4 shard_map.188
  93.9 1.8 %collective-permute-start.16 = (f32[32,512]{1,0:T(8,128)S(1)}, f32[32,512]{1,0:T(8,128)S(1)}, u32[]{:S(2)}, u32[]{:S(2)}) collective-permute-start(f32[32,512]{1,0:T(8,128)S(1)} %get-tuple-element.51.refs_1_.refs_7_), channel_id=1, source_target_pairs={{0,3},{1,2},{2,1},{3,0},{4,7},{5,6},{6,5},{7,4},{8,11},{9,10},{10,... | collective-permute-start | bytes 196616 | tf_op jit(solution)/shard_map/ppermute | solution.py:126
  95.7 5.0 %collective-permute-done.16.refs_4_ = f32[32,512]{1,0:T(8,128)S(1)} collective-permute-done((f32[32,512]{1,0:T(8,128)S(1)}, f32[32,512]{1,0:T(8,128)S(1)}, u32[]{:S(2)}, u32[]{:S(2)}) %collective-permute-start.16) | collective-permute-done | bytes 65568 | tf_op jit(solution)/shard_map/ppermute | solution.py:126
  100.7 2.1 %collective-permute-done.15.refs_3_ = f32[32,512]{1,0:T(8,128)S(1)} collective-permute-done((f32[32,512]{1,0:T(8,128)S(1)}, f32[32,512]{1,0:T(8,128)S(1)}, u32[]{:S(2)}, u32[]{:S(2)}) %collective-permute-start.15) | collective-permute-done | bytes 65568 | tf_op jit(solution)/shard_map/ppermute | solution.py:126
  102.8 2.2 %collective-permute-done.14.refs_2_ = f32[32,512]{1,0:T(8,128)S(1)} collective-permute-done((f32[32,512]{1,0:T(8,128)S(1)}, f32[32,512]{1,0:T(8,128)S(1)}, u32[]{:S(2)}, u32[]{:S(2)}) %collective-permute-start.14) | collective-permute-done | bytes 65568 | tf_op jit(solution)/shard_map/ppermute | solution.py:126
  105.0 1.3 shard_map.189
  106.2 1.4 shard_map.190.refs_1_
  107.6 1.8 %collective-permute-start.28 = (f32[32,512]{1,0:T(8,128)S(1)}, f32[32,512]{1,0:T(8,128)S(1)}, u32[]{:S(2)}, u32[]{:S(2)}) collective-permute-start(f32[32,512]{1,0:T(8,128)S(1)} %shard_map.190.refs_1_), channel_id=1, source_target_pairs={{0,3},{1,2},{2,1},{3,0},{4,7},{5,6},{6,5},{7,4},{8,11},{9,10},{10,... | collective-permute-start | bytes 196616 | tf_op jit(solution)/shard_map/ppermute | solution.py:126
  109.9 2.2 %collective-permute-start.26 = (f32[32,512]{1,0:T(8,128)S(1)}, f32[32,512]{1,0:T(8,128)S(1)}, u32[]{:S(2)}, u32[]{:S(2)}) collective-permute-start(f32[32,512]{1,0:T(8,128)S(1)} %shard_map.190.refs_1_), channel_id=1, source_target_pairs={{0,1},{1,0},{2,3},{3,2},{4,5},{5,4},{6,7},{7,6},{8,9},{9,8},{10,11... | collective-permute-start | bytes 196616 | tf_op jit(solution)/shard_map/ppermute | solution.py:126
  112.1 1.3 shard_map.191
  113.4 1.1 collective-permute-done.28.refs_4_
  114.5 2.3 %collective-permute-done.27.refs_3_ = f32[32,512]{1,0:T(8,128)S(1)} collective-permute-done((f32[32,512]{1,0:T(8,128)S(1)}, f32[32,512]{1,0:T(8,128)S(1)}, u32[]{:S(2)}, u32[]{:S(2)}) %collective-permute-start.27) | collective-permute-done | bytes 65568 | tf_op jit(solution)/shard_map/ppermute | solution.py:126
  116.8 2.6 %shard_map.192 = (f32[32,512]{1,0:T(8,128)S(1)}, f32[32,512]{1,0:T(8,128)S(1)}, f32[32,512]{1,0:T(8,128)S(1)}, f32[32,512]{1,0:T(8,128)S(1)}) custom-call(s32[2]{0:T(128)S(1)} %pad_add_fusion.refs_0_, f32[32,512]{1,0:T(8,128)S(1)} %shard_map.190.refs_1_, f32[32,512]{1,0:T(8,128)S(1)} %collective-permute-done.26.refs_2_, ...), custom_call_target="tpu_custom_call" | custom-call | tf_op jit(solution)/shard_map/pallas_call | solution.py:141
  119.5 3.1 %collective-permute-start.39 = (f32[32,512]{1,0:T(8,128)S(1)}, f32[32,512]{1,0:T(8,128)S(1)}, u32[]{:S(2)}, u32[]{:S(2)}) collective-permute-start(f32[32,512]{1,0:T(8,128)S(1)} %get-tuple-element.59), channel_id=1, source_target_pairs={{0,2},{1,3},{2,0},{3,1},{4,6},{5,7},{6,4},{7,5},{8,10},{9,11},{10,... | collective-permute-start | bytes 196616 | tf_op jit(solution)/shard_map/ppermute | solution.py:126
  122.6 1.2 collective-permute-start.40
  124.5 3.1 %collective-permute-done.39.refs_3_ = f32[32,512]{1,0:T(8,128)S(1)} collective-permute-done((f32[32,512]{1,0:T(8,128)S(1)}, f32[32,512]{1,0:T(8,128)S(1)}, u32[]{:S(2)}, u32[]{:S(2)}) %collective-permute-start.39) | collective-permute-done | bytes 65568 | tf_op jit(solution)/shard_map/ppermute | solution.py:126
  127.6 1.1 collective-permute-done.40.refs_4_
  128.8 1.9 %shard_map.193 = (f32[32,512]{1,0:T(8,128)S(1)}, f32[32,512]{1,0:T(8,128)S(1)}, f32[32,512]{1,0:T(8,128)S(1)}, f32[32,512]{1,0:T(8,128)S(1)}, f32[32,512]{1,0:T(8,128)S(1)}) custom-call(s32[2]{0:T(128)S(1)} %pad_add_fusion.refs_0_, f32[32,512]{1,0:T(8,128)S(1)} %get-tuple-element.57.refs_1_, f32[32,512]{1,0:T(8,128)S(1)} %collective-permute-done.38.refs_2_, ...), custom_call_target="tpu_custom_call" | custom-call | tf_op jit(solution)/shard_map/pallas_call | solution.py:141
  130.6 0.9 collective-permute-start.41
  131.5 1.2 collective-permute-start.42
  132.7 2.4 %collective-permute-start.43 = (f32[32,512]{1,0:T(8,128)S(1)}, f32[32,512]{1,0:T(8,128)S(1)}, u32[]{:S(2)}, u32[]{:S(2)}) collective-permute-start(f32[32,512]{1,0:T(8,128)S(1)} %get-tuple-element.64), channel_id=1, source_target_pairs={{0,3},{1,2},{2,1},{3,0},{4,7},{5,6},{6,5},{7,4},{8,11},{9,10},{10,... | collective-permute-start | bytes 196616 | tf_op jit(solution)/shard_map/ppermute | solution.py:126
  135.4 2.3 %collective-permute-done.42.refs_3_ = f32[32,512]{1,0:T(8,128)S(1)} collective-permute-done((f32[32,512]{1,0:T(8,128)S(1)}, f32[32,512]{1,0:T(8,128)S(1)}, u32[]{:S(2)}, u32[]{:S(2)}) %collective-permute-start.42) | collective-permute-done | bytes 65568 | tf_op jit(solution)/shard_map/ppermute | solution.py:126
  137.6 1.2 collective-permute-done.43.refs_4_
  138.9 1.9 %shard_map.194 = (f32[8,2560]{1,0:T(8,128)S(1)}, f32[8,2560]{1,0:T(8,128)S(1)}, f32[8,2560]{1,0:T(8,128)S(1)}, f32[8,2560]{1,0:T(8,128)S(1)}) custom-call(s32[2]{0:T(128)S(1)} %pad_add_fusion.refs_0_, f32[32,512]{1,0:T(8,128)S(1)} %get-tuple-element.61.refs_1_, f32[32,512]{1,0:T(8,128)S(1)} %collective-permute-done.41.refs_2_, ...), custom_call_target="tpu_custom_call" | custom-call | tf_op jit(solution)/shard_map/pallas_call | solution.py:141
  140.7 0.8 collective-permute-start.44
  141.5 2.1 %collective-permute-start.45 = (f32[8,2560]{1,0:T(8,128)S(1)}, f32[8,2560]{1,0:T(8,128)S(1)}, u32[]{:S(2)}, u32[]{:S(2)}) collective-permute-start(f32[8,2560]{1,0:T(8,128)S(1)} %get-tuple-element.68), channel_id=1, source_target_pairs={{0,2},{1,3},{2,0},{3,1},{4,6},{5,7},{6,4},{7,5},{8,10},{9,11},{10,... | collective-permute-start | bytes 245768 | tf_op jit(solution)/shard_map/ppermute | solution.py:126
  143.6 1.6 collective-permute-start.46
  145.1 1.0 collective-permute-done.44.refs_2_
  146.2 1.5 collective-permute-done.45.refs_3_
  147.7 2.1 %collective-permute-done.46.refs_4_ = f32[8,2560]{1,0:T(8,128)S(1)} collective-permute-done((f32[8,2560]{1,0:T(8,128)S(1)}, f32[8,2560]{1,0:T(8,128)S(1)}, u32[]{:S(2)}, u32[]{:S(2)}) %collective-permute-start.46) | collective-permute-done | bytes 81952 | tf_op jit(solution)/shard_map/ppermute | solution.py:126
  150.4 7.9 %all_to_all.10 = f32[8,2,8,256]{3,2,1,0:T(8,128)S(1)} all-to-all(f32[8,2,8,256]{3,2,1,0:T(8,128)S(1)} %shard_map.195), channel_id=1, replica_groups=mesh['leaf'=8,'col'=4] {'leaf'}, dimensions={0} | all-to-all | bytes 262144 | tf_op jit(solution)/shard_map/all_to_all | solution.py:451
  158.3 0.8 copy.27
  (87 shorter events, 12.6 us)
Async XLA Ops:
  0.6 20.0 %copy-start.13 = (s32[1,4]{1,0:T(1,128)S(1)}, s32[1,4]{1,0:T(1,128)}, u32[]{:S(2)}) copy-start(s32[1,4]{1,0:T(1,128)} %refs_4_.3) | copy-start | bytes 52
  0.6 20.0 %copy-start.10 = (s32[4,3]{1,0:T(4,128)S(1)}, s32[4,3]{1,0:T(4,128)}, u32[]{:S(2)}) copy-start(s32[4,3]{1,0:T(4,128)} %refs_2_.5) | copy-start | bytes 148
  0.7 19.9 %copy-start.12 = (s32[1,8]{1,0:T(1,128)S(1)}, s32[1,8]{1,0:T(1,128)}, u32[]{:S(2)}) copy-start(s32[1,8]{1,0:T(1,128)} %refs_3_.5) | copy-start | bytes 100
  1.5 1.1 copy-start
  2.6 1.0 copy-start.4
  3.7 0.9 copy-start.6
  4.6 0.7 copy-start.8
  5.3 3.9 %copy-start.1 = (f32[4,3,128,128]{3,2,1,0:T(8,128)S(1)}, f32[4,3,128,128]{3,2,1,0:T(8,128)}, u32[]{:S(2)}) copy-start(f32[4,3,128,128]{3,2,1,0:T(8,128)} %refs_7_.2) | copy-start | bytes 2359300
  5.3 11.5 %copy-start.3 = (f32[256,512]{1,0:T(8,128)S(1)}, f32[256,512]{1,0:T(8,128)}, u32[]{:S(2)}) copy-start(f32[256,512]{1,0:T(8,128)} %refs_1_.4) | copy-start | bytes 1572868
  5.3 15.3 %copy-start.2 = (f32[4,3,128,128]{3,2,1,0:T(8,128)S(1)}, f32[4,3,128,128]{3,2,1,0:T(8,128)}, u32[]{:S(2)}) copy-start(f32[4,3,128,128]{3,2,1,0:T(8,128)} %refs_8_.1) | copy-start | bytes 2359300
  7.7 1.5 collective-permute-start
  9.2 1.0 copy-start.5
  10.2 0.7 copy-start.9
  10.9 0.7 copy-start.11
  13.9 6.7 %collective-permute-start.1 = (f32[4,64,128]{2,1,0:T(8,128)S(1)}, f32[4,64,128]{2,1,0:T(8,128)S(1)}, u32[]{:S(2)}, u32[]{:S(2)}) collective-permute-start(f32[4,64,128]{2,1,0:T(8,128)S(1)} %get-tuple-element.42), channel_id=1, source_target_pairs={{0,8},{4,12},{8,0},{12,4},{16,24},{20,28},{24,16},{28,20},{1,9},{5... | collective-permute-start | bytes 393224 | tf_op jit(solution)/shard_map/ppermute | solution.py:126
  16.8 32.4 %collective-permute-start.18 = (f32[256,512]{1,0:T(8,128)S(1)}, f32[256,512]{1,0:T(8,128)S(1)}, u32[]{:S(2)}, u32[]{:S(2)}) collective-permute-start(f32[256,512]{1,0:T(8,128)S(1)} %copy-done.3), channel_id=1, source_target_pairs={{0,16},{4,20},{8,24},{12,28},{16,0},{20,4},{24,8},{28,12},{1,17},{... | collective-permute-start | bytes 1572872 | tf_op jit(solution)/shard_map/ppermute | solution.py:126
  20.6 1.0 copy-start.7
  21.6 17.4 %copy-start.14 = (f32[2,256,512]{2,1,0:T(8,128)S(1)}, f32[2,256,512]{2,1,0:T(8,128)}, u32[]{:S(2)}) copy-start(f32[2,256,512]{2,1,0:T(8,128)} %param.30) | copy-start | bytes 3145732
  24.2 10.0 %all-to-all-start = ((f32[8,2,8,256]{3,2,1,0:T(8,128)}), f32[8,2,8,256]{3,2,1,0:T(8,128)S(1)}, u32[]{:S(2)}, u32[]{:S(2)}) async-start(f32[8,2,8,256]{3,2,1,0:T(8,128)} %get-tuple-element.44), calls=%async_computation | async-start | bytes 262144 | tf_op jit(solution)/shard_map/all_to_all | solution.py:421
  28.1 21.1 %collective-permute-start.17 = (f32[256,512]{1,0:T(8,128)S(1)}, f32[256,512]{1,0:T(8,128)S(1)}, u32[]{:S(2)}, u32[]{:S(2)}) collective-permute-start(f32[256,512]{1,0:T(8,128)S(1)} %copy-done.3), channel_id=1, source_target_pairs={{0,8},{4,12},{8,0},{12,4},{16,24},{20,28},{24,16},{28,20},{1,9},{5... | collective-permute-start | bytes 1572872 | tf_op jit(solution)/shard_map/ppermute | solution.py:126
  30.2 19.8 %collective-permute-start.21 = (f32[256,512]{1,0:T(8,128)S(1)}, f32[256,512]{1,0:T(8,128)S(1)}, u32[]{:S(2)}, u32[]{:S(2)}) collective-permute-start(f32[256,512]{1,0:T(8,128)S(1)} %copy-done.3), channel_id=1, source_target_pairs={{0,4},{4,0},{8,12},{12,8},{16,20},{20,16},{24,28},{28,24},{1,5},{5... | collective-permute-start | bytes 1572872 | tf_op jit(solution)/shard_map/ppermute | solution.py:126
  34.7 5.3 %collective-permute-start.2 = (f32[8,2560]{1,0:T(8,128)S(1)}, f32[8,2560]{1,0:T(8,128)S(1)}, u32[]{:S(2)}, u32[]{:S(2)}) collective-permute-start(f32[8,2560]{1,0:T(8,128)S(1)} %get-tuple-element.46), channel_id=1, source_target_pairs={{0,1},{1,0},{2,3},{3,2},{4,5},{5,4},{6,7},{7,6},{8,9},{9,8},{10,11... | collective-permute-start | bytes 245768 | tf_op jit(solution)/shard_map/ppermute | solution.py:126
  36.4 6.2 %collective-permute-start.3 = (f32[8,2560]{1,0:T(8,128)S(1)}, f32[8,2560]{1,0:T(8,128)S(1)}, u32[]{:S(2)}, u32[]{:S(2)}) collective-permute-start(f32[8,2560]{1,0:T(8,128)S(1)} %get-tuple-element.47), channel_id=1, source_target_pairs={{0,2},{1,3},{2,0},{3,1},{4,6},{5,7},{6,4},{7,5},{8,10},{9,11},{10,... | collective-permute-start | bytes 245768 | tf_op jit(solution)/shard_map/ppermute | solution.py:126
  40.0 11.5 %collective-permute-start.30 = (f32[256,512]{1,0:T(8,128)S(1)}, f32[256,512]{1,0:T(8,128)S(1)}, u32[]{:S(2)}, u32[]{:S(2)}) collective-permute-start(f32[256,512]{1,0:T(8,128)S(1)} %get-tuple-element.74.refs_1_), channel_id=1, source_target_pairs={{0,16},{4,20},{8,24},{12,28},{16,0},{20,4},{24,8},{28,12},{1,17},{... | collective-permute-start | bytes 1572872 | tf_op jit(solution)/shard_map/ppermute | solution.py:126
  42.6 6.2 %collective-permute-start.4 = (f32[8,2560]{1,0:T(8,128)S(1)}, f32[8,2560]{1,0:T(8,128)S(1)}, u32[]{:S(2)}, u32[]{:S(2)}) collective-permute-start(f32[8,2560]{1,0:T(8,128)S(1)} %get-tuple-element.48), channel_id=1, source_target_pairs={{0,3},{1,2},{2,1},{3,0},{4,7},{5,6},{6,5},{7,4},{8,11},{9,10},{10,... | collective-permute-start | bytes 245768 | tf_op jit(solution)/shard_map/ppermute | solution.py:126
  48.8 14.9 %collective-permute-start.29 = (f32[256,512]{1,0:T(8,128)S(1)}, f32[256,512]{1,0:T(8,128)S(1)}, u32[]{:S(2)}, u32[]{:S(2)}) collective-permute-start(f32[256,512]{1,0:T(8,128)S(1)} %get-tuple-element.74.refs_1_), channel_id=1, source_target_pairs={{0,8},{4,12},{8,0},{12,4},{16,24},{20,28},{24,16},{28,20},{1,9},{5... | collective-permute-start | bytes 1572872 | tf_op jit(solution)/shard_map/ppermute | solution.py:126
  49.2 15.0 %collective-permute-start.9 = (f32[256,512]{1,0:T(8,128)S(1)}, f32[256,512]{1,0:T(8,128)S(1)}, u32[]{:S(2)}, u32[]{:S(2)}) collective-permute-start(f32[256,512]{1,0:T(8,128)S(1)} %get-tuple-element.75.refs_1_), channel_id=1, source_target_pairs={{0,4},{4,0},{8,12},{12,8},{16,20},{20,16},{24,28},{28,24},{1,5},{5... | collective-permute-start | bytes 1572872 | tf_op jit(solution)/shard_map/ppermute | solution.py:126
  49.2 15.7 %collective-permute-start.6 = (f32[256,512]{1,0:T(8,128)S(1)}, f32[256,512]{1,0:T(8,128)S(1)}, u32[]{:S(2)}, u32[]{:S(2)}) collective-permute-start(f32[256,512]{1,0:T(8,128)S(1)} %get-tuple-element.75.refs_1_), channel_id=1, source_target_pairs={{0,16},{4,20},{8,24},{12,28},{16,0},{20,4},{24,8},{28,12},{1,17},{... | collective-permute-start | bytes 1572872 | tf_op jit(solution)/shard_map/ppermute | solution.py:126
  50.0 24.9 %collective-permute-start.5 = (f32[256,512]{1,0:T(8,128)S(1)}, f32[256,512]{1,0:T(8,128)S(1)}, u32[]{:S(2)}, u32[]{:S(2)}) collective-permute-start(f32[256,512]{1,0:T(8,128)S(1)} %get-tuple-element.75.refs_1_), channel_id=1, source_target_pairs={{0,8},{4,12},{8,0},{12,4},{16,24},{20,28},{24,16},{28,20},{1,9},{5... | collective-permute-start | bytes 1572872 | tf_op jit(solution)/shard_map/ppermute | solution.py:126
  51.5 28.1 %collective-permute-start.20 = (f32[128,512]{1,0:T(8,128)S(1)}, f32[128,512]{1,0:T(8,128)S(1)}, u32[]{:S(2)}, u32[]{:S(2)}) collective-permute-start(f32[128,512]{1,0:T(8,128)S(1)} %slice.35), channel_id=1, source_target_pairs={{0,8},{4,12},{8,0},{12,4},{16,24},{20,28},{24,16},{28,20},{1,9},{5... | collective-permute-start | bytes 786440 | tf_op jit(solution)/shard_map/ppermute | solution.py:126
  63.7 16.4 %collective-permute-start.19 = (f32[128,512]{1,0:T(8,128)S(1)}, f32[128,512]{1,0:T(8,128)S(1)}, u32[]{:S(2)}, u32[]{:S(2)}) collective-permute-start(f32[128,512]{1,0:T(8,128)S(1)} %slice.34), channel_id=1, source_target_pairs={{0,16},{4,20},{8,24},{12,28},{16,0},{20,4},{24,8},{28,12},{1,17},{... | collective-permute-start | bytes 786440 | tf_op jit(solution)/shard_map/ppermute | solution.py:126
  64.3 20.2 %collective-permute-start.32 = (f32[128,512]{1,0:T(8,128)S(1)}, f32[128,512]{1,0:T(8,128)S(1)}, u32[]{:S(2)}, u32[]{:S(2)}) collective-permute-start(f32[128,512]{1,0:T(8,128)S(1)} %slice.37), channel_id=1, source_target_pairs={{0,8},{4,12},{8,0},{12,4},{16,24},{20,28},{24,16},{28,20},{1,9},{5... | collective-permute-start | bytes 786440 | tf_op jit(solution)/shard_map/ppermute | solution.py:126
  64.9 19.6 %collective-permute-start.31 = (f32[128,512]{1,0:T(8,128)S(1)}, f32[128,512]{1,0:T(8,128)S(1)}, u32[]{:S(2)}, u32[]{:S(2)}) collective-permute-start(f32[128,512]{1,0:T(8,128)S(1)} %slice.36), channel_id=1, source_target_pairs={{0,16},{4,20},{8,24},{12,28},{16,0},{20,4},{24,8},{28,12},{1,17},{... | collective-permute-start | bytes 786440 | tf_op jit(solution)/shard_map/ppermute | solution.py:126
  74.9 13.0 %collective-permute-start.23 = (f32[256,512]{1,0:T(8,128)S(1)}, f32[256,512]{1,0:T(8,128)S(1)}, u32[]{:S(2)}, u32[]{:S(2)}) collective-permute-start(f32[256,512]{1,0:T(8,128)S(1)} %collective-permute-done.18.refs_3_), channel_id=1, source_target_pairs={{0,4},{4,0},{8,12},{12,8},{16,20},{20,16},{24,28},{28,24},{1,5},{5... | collective-permute-start | bytes 1572872 | tf_op jit(solution)/shard_map/ppermute | solution.py:126
  79.6 7.7 %collective-permute-start.8 = (f32[128,512]{1,0:T(8,128)S(1)}, f32[128,512]{1,0:T(8,128)S(1)}, u32[]{:S(2)}, u32[]{:S(2)}) collective-permute-start(f32[128,512]{1,0:T(8,128)S(1)} %slice.33), channel_id=1, source_target_pairs={{0,8},{4,12},{8,0},{12,4},{16,24},{20,28},{24,16},{28,20},{1,9},{5... | collective-permute-start | bytes 786440 | tf_op jit(solution)/shard_map/ppermute | solution.py:126
  80.1 7.3 %collective-permute-start.7 = (f32[128,512]{1,0:T(8,128)S(1)}, f32[128,512]{1,0:T(8,128)S(1)}, u32[]{:S(2)}, u32[]{:S(2)}) collective-permute-start(f32[128,512]{1,0:T(8,128)S(1)} %slice.32), channel_id=1, source_target_pairs={{0,16},{4,20},{8,24},{12,28},{16,0},{20,4},{24,8},{28,12},{1,17},{... | collective-permute-start | bytes 786440 | tf_op jit(solution)/shard_map/ppermute | solution.py:126
  84.5 3.3 %collective-permute-start.25 = (f32[128,512]{1,0:T(8,128)S(1)}, f32[128,512]{1,0:T(8,128)S(1)}, u32[]{:S(2)}, u32[]{:S(2)}) collective-permute-start(f32[128,512]{1,0:T(8,128)S(1)} %collective-permute-done.20.refs_5_), channel_id=1, source_target_pairs={{0,4},{4,0},{8,12},{12,8},{16,20},{20,16},{24,28},{28,24},{1,5},{5... | collective-permute-start | bytes 786440 | tf_op jit(solution)/shard_map/ppermute | solution.py:126
  84.5 5.2 %collective-permute-start.11 = (f32[256,512]{1,0:T(8,128)S(1)}, f32[256,512]{1,0:T(8,128)S(1)}, u32[]{:S(2)}, u32[]{:S(2)}) collective-permute-start(f32[256,512]{1,0:T(8,128)S(1)} %collective-permute-done.6.refs_3_), channel_id=1, source_target_pairs={{0,4},{4,0},{8,12},{12,8},{16,20},{20,16},{24,28},{28,24},{1,5},{5... | collective-permute-start | bytes 1572872 | tf_op jit(solution)/shard_map/ppermute | solution.py:126
  87.3 3.6 %collective-permute-start.10 = (f32[256,512]{1,0:T(8,128)S(1)}, f32[256,512]{1,0:T(8,128)S(1)}, u32[]{:S(2)}, u32[]{:S(2)}) collective-permute-start(f32[256,512]{1,0:T(8,128)S(1)} %collective-permute-done.5.refs_2_), channel_id=1, source_target_pairs={{0,4},{4,0},{8,12},{12,8},{16,20},{20,16},{24,28},{28,24},{1,5},{5... | collective-permute-start | bytes 1572872 | tf_op jit(solution)/shard_map/ppermute | solution.py:126
  87.3 2.3 %collective-permute-start.13 = (f32[128,512]{1,0:T(8,128)S(1)}, f32[128,512]{1,0:T(8,128)S(1)}, u32[]{:S(2)}, u32[]{:S(2)}) collective-permute-start(f32[128,512]{1,0:T(8,128)S(1)} %collective-permute-done.8.refs_5_), channel_id=1, source_target_pairs={{0,4},{4,0},{8,12},{12,8},{16,20},{20,16},{24,28},{28,24},{1,5},{5... | collective-permute-start | bytes 786440 | tf_op jit(solution)/shard_map/ppermute | solution.py:126
  87.8 7.8 %collective-permute-start.22 = (f32[256,512]{1,0:T(8,128)S(1)}, f32[256,512]{1,0:T(8,128)S(1)}, u32[]{:S(2)}, u32[]{:S(2)}) collective-permute-start(f32[256,512]{1,0:T(8,128)S(1)} %collective-permute-done.17.refs_2_), channel_id=1, source_target_pairs={{0,4},{4,0},{8,12},{12,8},{16,20},{20,16},{24,28},{28,24},{1,5},{5... | collective-permute-start | bytes 1572872 | tf_op jit(solution)/shard_map/ppermute | solution.py:126
  87.9 2.8 %collective-permute-start.12 = (f32[128,512]{1,0:T(8,128)S(1)}, f32[128,512]{1,0:T(8,128)S(1)}, u32[]{:S(2)}, u32[]{:S(2)}) collective-permute-start(f32[128,512]{1,0:T(8,128)S(1)} %collective-permute-done.7.refs_4_), channel_id=1, source_target_pairs={{0,4},{4,0},{8,12},{12,8},{16,20},{20,16},{24,28},{28,24},{1,5},{5... | collective-permute-start | bytes 786440 | tf_op jit(solution)/shard_map/ppermute | solution.py:126
  89.6 4.3 %collective-permute-start.24 = (f32[128,512]{1,0:T(8,128)S(1)}, f32[128,512]{1,0:T(8,128)S(1)}, u32[]{:S(2)}, u32[]{:S(2)}) collective-permute-start(f32[128,512]{1,0:T(8,128)S(1)} %collective-permute-done.19.refs_4_), channel_id=1, source_target_pairs={{0,4},{4,0},{8,12},{12,8},{16,20},{20,16},{24,28},{28,24},{1,5},{5... | collective-permute-start | bytes 786440 | tf_op jit(solution)/shard_map/ppermute | solution.py:126
  89.8 17.9 %collective-permute-start.33 = (f32[256,512]{1,0:T(8,128)S(1)}, f32[256,512]{1,0:T(8,128)S(1)}, u32[]{:S(2)}, u32[]{:S(2)}) collective-permute-start(f32[256,512]{1,0:T(8,128)S(1)} %get-tuple-element.74.refs_1_), channel_id=1, source_target_pairs={{0,4},{4,0},{8,12},{12,8},{16,20},{20,16},{24,28},{28,24},{1,5},{5... | collective-permute-start | bytes 1572872 | tf_op jit(solution)/shard_map/ppermute | solution.py:126
  90.7 19.1 %collective-permute-start.35 = (f32[256,512]{1,0:T(8,128)S(1)}, f32[256,512]{1,0:T(8,128)S(1)}, u32[]{:S(2)}, u32[]{:S(2)}) collective-permute-start(f32[256,512]{1,0:T(8,128)S(1)} %collective-permute-done.30.refs_3_), channel_id=1, source_target_pairs={{0,4},{4,0},{8,12},{12,8},{16,20},{20,16},{24,28},{28,24},{1,5},{5... | collective-permute-start | bytes 1572872 | tf_op jit(solution)/shard_map/ppermute | solution.py:126
  90.9 21.2 %collective-permute-start.34 = (f32[256,512]{1,0:T(8,128)S(1)}, f32[256,512]{1,0:T(8,128)S(1)}, u32[]{:S(2)}, u32[]{:S(2)}) collective-permute-start(f32[256,512]{1,0:T(8,128)S(1)} %collective-permute-done.29.refs_2_), channel_id=1, source_target_pairs={{0,4},{4,0},{8,12},{12,8},{16,20},{20,16},{24,28},{28,24},{1,5},{5... | collective-permute-start | bytes 1572872 | tf_op jit(solution)/shard_map/ppermute | solution.py:126
  93.9 6.8 %collective-permute-start.16 = (f32[32,512]{1,0:T(8,128)S(1)}, f32[32,512]{1,0:T(8,128)S(1)}, u32[]{:S(2)}, u32[]{:S(2)}) collective-permute-start(f32[32,512]{1,0:T(8,128)S(1)} %get-tuple-element.51.refs_1_.refs_7_), channel_id=1, source_target_pairs={{0,3},{1,2},{2,1},{3,0},{4,7},{5,6},{6,5},{7,4},{8,11},{9,10},{10,... | collective-permute-start | bytes 196616 | tf_op jit(solution)/shard_map/ppermute | solution.py:126
  95.7 7.1 %collective-permute-start.15 = (f32[32,512]{1,0:T(8,128)S(1)}, f32[32,512]{1,0:T(8,128)S(1)}, u32[]{:S(2)}, u32[]{:S(2)}) collective-permute-start(f32[32,512]{1,0:T(8,128)S(1)} %get-tuple-element.51.refs_1_.refs_7_), channel_id=1, source_target_pairs={{0,2},{1,3},{2,0},{3,1},{4,6},{5,7},{6,4},{7,5},{8,10},{9,11},{10,... | collective-permute-start | bytes 196616 | tf_op jit(solution)/shard_map/ppermute | solution.py:126
  100.7 4.3 %collective-permute-start.14 = (f32[32,512]{1,0:T(8,128)S(1)}, f32[32,512]{1,0:T(8,128)S(1)}, u32[]{:S(2)}, u32[]{:S(2)}) collective-permute-start(f32[32,512]{1,0:T(8,128)S(1)} %get-tuple-element.51.refs_1_.refs_7_), channel_id=1, source_target_pairs={{0,1},{1,0},{2,3},{3,2},{4,5},{5,4},{6,7},{7,6},{8,9},{9,8},{10,11... | collective-permute-start | bytes 196616 | tf_op jit(solution)/shard_map/ppermute | solution.py:126
  102.8 6.6 %collective-permute-start.37 = (f32[128,512]{1,0:T(8,128)S(1)}, f32[128,512]{1,0:T(8,128)S(1)}, u32[]{:S(2)}, u32[]{:S(2)}) collective-permute-start(f32[128,512]{1,0:T(8,128)S(1)} %collective-permute-done.32.refs_5_), channel_id=1, source_target_pairs={{0,4},{4,0},{8,12},{12,8},{16,20},{20,16},{24,28},{28,24},{1,5},{5... | collective-permute-start | bytes 786440 | tf_op jit(solution)/shard_map/ppermute | solution.py:126
  105.0 7.1 %collective-permute-start.36 = (f32[128,512]{1,0:T(8,128)S(1)}, f32[128,512]{1,0:T(8,128)S(1)}, u32[]{:S(2)}, u32[]{:S(2)}) collective-permute-start(f32[128,512]{1,0:T(8,128)S(1)} %collective-permute-done.31.refs_4_), channel_id=1, source_target_pairs={{0,4},{4,0},{8,12},{12,8},{16,20},{20,16},{24,28},{28,24},{1,5},{5... | collective-permute-start | bytes 786440 | tf_op jit(solution)/shard_map/ppermute | solution.py:126
  107.6 6.8 %collective-permute-start.28 = (f32[32,512]{1,0:T(8,128)S(1)}, f32[32,512]{1,0:T(8,128)S(1)}, u32[]{:S(2)}, u32[]{:S(2)}) collective-permute-start(f32[32,512]{1,0:T(8,128)S(1)} %shard_map.190.refs_1_), channel_id=1, source_target_pairs={{0,3},{1,2},{2,1},{3,0},{4,7},{5,6},{6,5},{7,4},{8,11},{9,10},{10,... | collective-permute-start | bytes 196616 | tf_op jit(solution)/shard_map/ppermute | solution.py:126
  109.4 7.4 %collective-permute-start.27 = (f32[32,512]{1,0:T(8,128)S(1)}, f32[32,512]{1,0:T(8,128)S(1)}, u32[]{:S(2)}, u32[]{:S(2)}) collective-permute-start(f32[32,512]{1,0:T(8,128)S(1)} %shard_map.190.refs_1_), channel_id=1, source_target_pairs={{0,2},{1,3},{2,0},{3,1},{4,6},{5,7},{6,4},{7,5},{8,10},{9,11},{10,... | collective-permute-start | bytes 196616 | tf_op jit(solution)/shard_map/ppermute | solution.py:126
  109.9 6.9 %collective-permute-start.26 = (f32[32,512]{1,0:T(8,128)S(1)}, f32[32,512]{1,0:T(8,128)S(1)}, u32[]{:S(2)}, u32[]{:S(2)}) collective-permute-start(f32[32,512]{1,0:T(8,128)S(1)} %shard_map.190.refs_1_), channel_id=1, source_target_pairs={{0,1},{1,0},{2,3},{3,2},{4,5},{5,4},{6,7},{7,6},{8,9},{9,8},{10,11... | collective-permute-start | bytes 196616 | tf_op jit(solution)/shard_map/ppermute | solution.py:126
  119.4 5.1 %collective-permute-start.38 = (f32[32,512]{1,0:T(8,128)S(1)}, f32[32,512]{1,0:T(8,128)S(1)}, u32[]{:S(2)}, u32[]{:S(2)}) collective-permute-start(f32[32,512]{1,0:T(8,128)S(1)} %get-tuple-element.58), channel_id=1, source_target_pairs={{0,1},{1,0},{2,3},{3,2},{4,5},{5,4},{6,7},{7,6},{8,9},{9,8},{10,11... | collective-permute-start | bytes 196616 | tf_op jit(solution)/shard_map/ppermute | solution.py:126
  119.5 8.2 %collective-permute-start.39 = (f32[32,512]{1,0:T(8,128)S(1)}, f32[32,512]{1,0:T(8,128)S(1)}, u32[]{:S(2)}, u32[]{:S(2)}) collective-permute-start(f32[32,512]{1,0:T(8,128)S(1)} %get-tuple-element.59), channel_id=1, source_target_pairs={{0,2},{1,3},{2,0},{3,1},{4,6},{5,7},{6,4},{7,5},{8,10},{9,11},{10,... | collective-permute-start | bytes 196616 | tf_op jit(solution)/shard_map/ppermute | solution.py:126
  122.6 6.2 %collective-permute-start.40 = (f32[32,512]{1,0:T(8,128)S(1)}, f32[32,512]{1,0:T(8,128)S(1)}, u32[]{:S(2)}, u32[]{:S(2)}) collective-permute-start(f32[32,512]{1,0:T(8,128)S(1)} %get-tuple-element.60), channel_id=1, source_target_pairs={{0,3},{1,2},{2,1},{3,0},{4,7},{5,6},{6,5},{7,4},{8,11},{9,10},{10,... | collective-permute-start | bytes 196616 | tf_op jit(solution)/shard_map/ppermute | solution.py:126
  130.6 4.7 %collective-permute-start.41 = (f32[32,512]{1,0:T(8,128)S(1)}, f32[32,512]{1,0:T(8,128)S(1)}, u32[]{:S(2)}, u32[]{:S(2)}) collective-permute-start(f32[32,512]{1,0:T(8,128)S(1)} %get-tuple-element.62), channel_id=1, source_target_pairs={{0,1},{1,0},{2,3},{3,2},{4,5},{5,4},{6,7},{7,6},{8,9},{9,8},{10,11... | collective-permute-start | bytes 196616 | tf_op jit(solution)/shard_map/ppermute | solution.py:126
  131.5 6.1 %collective-permute-start.42 = (f32[32,512]{1,0:T(8,128)S(1)}, f32[32,512]{1,0:T(8,128)S(1)}, u32[]{:S(2)}, u32[]{:S(2)}) collective-permute-start(f32[32,512]{1,0:T(8,128)S(1)} %get-tuple-element.63), channel_id=1, source_target_pairs={{0,2},{1,3},{2,0},{3,1},{4,6},{5,7},{6,4},{7,5},{8,10},{9,11},{10,... | collective-permute-start | bytes 196616 | tf_op jit(solution)/shard_map/ppermute | solution.py:126
  132.7 6.2 %collective-permute-start.43 = (f32[32,512]{1,0:T(8,128)S(1)}, f32[32,512]{1,0:T(8,128)S(1)}, u32[]{:S(2)}, u32[]{:S(2)}) collective-permute-start(f32[32,512]{1,0:T(8,128)S(1)} %get-tuple-element.64), channel_id=1, source_target_pairs={{0,3},{1,2},{2,1},{3,0},{4,7},{5,6},{6,5},{7,4},{8,11},{9,10},{10,... | collective-permute-start | bytes 196616 | tf_op jit(solution)/shard_map/ppermute | solution.py:126
  140.7 5.4 %collective-permute-start.44 = (f32[8,2560]{1,0:T(8,128)S(1)}, f32[8,2560]{1,0:T(8,128)S(1)}, u32[]{:S(2)}, u32[]{:S(2)}) collective-permute-start(f32[8,2560]{1,0:T(8,128)S(1)} %get-tuple-element.67), channel_id=1, source_target_pairs={{0,1},{1,0},{2,3},{3,2},{4,5},{5,4},{6,7},{7,6},{8,9},{9,8},{10,11... | collective-permute-start | bytes 245768 | tf_op jit(solution)/shard_map/ppermute | solution.py:126
  141.5 6.2 %collective-permute-start.45 = (f32[8,2560]{1,0:T(8,128)S(1)}, f32[8,2560]{1,0:T(8,128)S(1)}, u32[]{:S(2)}, u32[]{:S(2)}) collective-permute-start(f32[8,2560]{1,0:T(8,128)S(1)} %get-tuple-element.68), channel_id=1, source_target_pairs={{0,2},{1,3},{2,0},{3,1},{4,6},{5,7},{6,4},{7,5},{8,10},{9,11},{10,... | collective-permute-start | bytes 245768 | tf_op jit(solution)/shard_map/ppermute | solution.py:126
  143.6 6.2 %collective-permute-start.46 = (f32[8,2560]{1,0:T(8,128)S(1)}, f32[8,2560]{1,0:T(8,128)S(1)}, u32[]{:S(2)}, u32[]{:S(2)}) collective-permute-start(f32[8,2560]{1,0:T(8,128)S(1)} %get-tuple-element.69), channel_id=1, source_target_pairs={{0,3},{1,2},{2,1},{3,0},{4,7},{5,6},{6,5},{7,4},{8,11},{9,10},{10,... | collective-permute-start | bytes 245768 | tf_op jit(solution)/shard_map/ppermute | solution.py:126

commit v3 on v2

--- a/solution.py
+++ b/solution.py
@@ -121,6 +121,9 @@
     return root_solution
 
 
+GROUP = 8
+
+
 def flip(block, axis, distance):
     count = lax.axis_size(axis)
     return lax.ppermute(block, axis, [(i, i ^ distance) for i in range(count)])
@@ -208,26 +211,45 @@
     return kernel_call(assemble_kernel, [(shape, jnp.bfloat16)] * 2, [place], pieces)
 
 
-def arrange_kernel(place, values, *parts):
-    leaf_count, _, rows, width = values.shape
-    total = leaf_count * width
-    own_width = parts[0].shape[1] - total
-    fronts = own_width // width
-    for e, part in enumerate(parts):
-        for leaf in range(leaf_count):
-            part[:, leaf * width : (leaf + 1) * width] = values[leaf, 0]
-        for j in range(fronts):
-            part[:, total + j * width : total + (j + 1) * width] = values[
-                (place[1] ^ e) * fronts + j, 1
-            ]
+def split_kernel(whole, high, low):
+    high[...], low[...] = halves(whole[...])
+
+
+def pair_kernel(own, other, high, low):
+    rows = own.shape[0]
+    high[:rows, :], low[:rows, :] = halves(own[...])
+    high[rows:, :], low[rows:, :] = halves(other[...])
 
 
 def first_kernel(place, *refs):
-    parts, (high, low, first, rest) = refs[:-4], refs[-4:]
-    total = high.shape[0]
-    values = jnp.concatenate([part[:, :total] for part in parts], 0)
-    rest[...] = jnp.concatenate([part[:, total:] for part in parts], 0)
-    first[...] = product(values, high[...], low[...], 0)
+    count = (len(refs) - 5) // 2
+    parts, (high, low, kept, received) = refs[:count], refs[count : count + 4]
+    sent, pushed = refs[count + 4 : -1], refs[-1]
+    rows, width = parts[0].shape
+    values = product(jnp.concatenate([part[...] for part in parts], 0), high[...], low[...], 0)
+    for e in range(count):
+        pushed[e] = values[e * rows : (e + 1) * rows]
+    chip, lower = place[0] >> 1, (place[0] & 1) == 0
+    half = width // 2
+    for f, part in enumerate(sent):
+        where = span(chip ^ f, GROUP)
+        for e in range(count):
+            part[e * GROUP : (e + 1) * GROUP, :] = pushed[e, where, :]
+        own, other = kept[where, half:], received[where, half:]
+        part[rows:, :half] = jnp.where(lower, own, other)
+        part[rows:, half:] = jnp.where(lower, other, own)
+
+
+def share_kernel(place, *refs):
+    count = (len(refs) - 1) // 2
+    parts, sent, rest = refs[:count], refs[count:-1], refs[-1]
+    rows = parts[0].shape[0] - GROUP
+    total = sum(part[:rows, :] for part in parts[1:]) + parts[0][:rows, :]
+    for f, part in enumerate(parts):
+        rest[f] = part[rows:, :]
+    for e, part in enumerate(sent):
+        part[:rows, :] = total
+        part[rows:, :] = rest[(place[0] >> 1) ^ place[1] ^ e]
 
 
 def gathered_product(place, parts, high, low):
@@ -236,14 +258,16 @@
     total = None
     for e, part in enumerate(parts):
         rows = span(place[1] ^ e, width)
-        term = product(regroup(part[...], e, count), high[rows, :], low[rows, :], 0)
+        values = part[: count * GROUP, :]
+        term = product(regroup(values, e, count), high[rows, :], low[rows, :], 0)
         total = term if total is None else total + term
     return total
 
 
 def coupled_kernel(place, *refs):
-    parts, (high, low, rest, result) = refs[:-4], refs[-4:]
-    result[...] = rest[...] - gathered_product(place, parts, high, low)
+    parts, (high, low, result) = refs[:-3], refs[-3:]
+    rest = jnp.concatenate([part[len(parts) * GROUP :, :] for part in parts], 0)
+    result[...] = rest - gathered_product(place, parts, high, low)
 
 
 def scatter_product(place, values, high, low, sent):
@@ -279,7 +303,7 @@
     parts = refs[:count]
     high, low, first, last = refs[count : count + 4]
     sent = refs[count + 4 :]
-    total = first[...] - (sum(part[...] for part in parts[1:]) + parts[0][...])
+    total = first[: last.shape[0], :] - (sum(part[...] for part in parts[1:]) + parts[0][...])
     solved = product(total, high[...], low[...], 1)
     size = total.shape[0] // count
     for e, part in enumerate(sent):
@@ -351,23 +375,24 @@
 
 
 def highest_kernel(
-    place, live, links, order, last_order, old, received, inverse, coupling, solved, split, joined, blocks
+    place, live, links, order, last_order, old, received, inverse, coupling, solved, kept, sent, joined, blocks
 ):
     load_halves(place, 1, order, old, received, joined, blocks)
     reduce_blocks(2, live, links, blocks, inverse, coupling, solved)
     red_blocks, size = inverse.shape[0], inverse.shape[1]
-    leaf_count, panel_count, rows, width = split.shape
-    per_panel = width // size
-    for panel in range(panel_count):
-        for j in range(per_panel):
-            block = blocks[red_blocks + last_order[0, panel * per_panel + j]]
-            split[:, panel, :, j * size : (j + 1) * size] = block.reshape(leaf_count, rows, size)
-
-
-def eliminate_all(place, right_sides, level_data, front_rows, panel_count, panel_rows):
+    core = place[0] & 1
+    for n in range(blocks.shape[0] - red_blocks):
+        block = red_blocks + last_order[0, n]
+        columns = slice(n * size, (n + 1) * size)
+        for chip in range(kept.shape[0] // GROUP):
+            rows = slice(chip * GROUP, (chip + 1) * GROUP)
+            kept[rows, columns] = blocks[block, span(2 * chip + core, GROUP), :]
+            sent[rows, columns] = blocks[block, span(2 * chip + 1 - core, GROUP), :]
+
+
+def eliminate_all(place, right_sides, level_data, front_rows):
     rhs_rows = right_sides.shape[0]
     red_blocks, size = level_data[0][0].shape[:2]
-    leaf_count = lax.axis_size("leaf")
     one = ((rhs_rows, red_blocks * size), jnp.float32)
 
     def many(count):
@@ -397,38 +422,56 @@
     received = flip(sent, "leaf", 2)
     inverse, coupling, links, last_order = level_data[2]
     count -= red_blocks
-    rows = rhs_rows // leaf_count
-    solved_third, split = kernel_call(
+    half = (rhs_rows // 2, (count - red_blocks) * size)
+    solved_third, kept, sent = kernel_call(
         highest_kernel,
-        [one, ((leaf_count, panel_count, rows, panel_rows), jnp.float32)],
+        [one, (half, jnp.float32), (half, jnp.float32)],
         [place, front_rows, links, next_order, last_order],
         [kept, received, inverse, coupling],
         scratch=[pltpu.VMEM(many(count), jnp.float32)] * 2,
     )
-    return (solved_first, solved_second, solved_third), split
-
-
-def root_replicated(place, split, root_inverse, root_coupling):
+    return (solved_first, solved_second, solved_third), kept, flip(sent, "leaf", 1)
+
+
+def root_replicated(place, kept, received, root_inverse, root_coupling):
     leaf_count, col_count = lax.axis_size("leaf"), lax.axis_size("col")
-    first_high, first_low = spread_matrix(place, root_inverse[0])
-    between_high, between_low = spread_matrix(place, root_coupling)
+    panel_count, panel_rows, own_columns = root_inverse.shape
+    group = GROUP * col_count
+    total = panel_rows * leaf_count
+    rhs_rows = GROUP * leaf_count
+    pair = [((2 * panel_rows, own_columns), jnp.bfloat16)] * 2
+    panel = [((total, own_columns), jnp.bfloat16)] * 2
+    one = ((group, own_columns), jnp.float32)
+    more = ((group + GROUP, own_columns), jnp.float32)
+    wide = [((GROUP, total + own_columns), jnp.float32)] * col_count
+    near_high, near_low = kernel_call(
+        pair_kernel, pair, [], [root_inverse[0], flip(root_inverse[0], "leaf", 1)]
+    )
+    between = lax.all_gather(root_coupling, "leaf", axis=0, tiled=True)
+    between_high, between_low = kernel_call(split_kernel, panel, [], [between])
     second_high, second_low = spread_matrix(place, root_inverse[1])
-    panel_count, panel_rows, own_columns = root_inverse.shape
-    rows = split.shape[2]
-    rhs_rows = rows * leaf_count
-    group = rows * col_count
-    total = panel_rows * leaf_count
-    whole = lax.all_to_all(split, "leaf", 0, 0, tiled=True)
-    wide = [((rows, total + own_columns), jnp.float32)] * col_count
-    one = ((group, own_columns), jnp.float32)
-    parts = swap_columns(kernel_call(arrange_kernel, wide, [place], [whole]))
-    first, rest = kernel_call(
-        first_kernel, [one, one], [place], [*parts, first_high, first_low]
-    )
-    parts = swap_columns([first] * col_count)
-    (left,) = kernel_call(
-        coupled_kernel, [one], [place], [*parts, between_high, between_low, rest]
-    )
+    first = lax.all_gather(root_inverse[0], "leaf", axis=0, tiled=True)
+    first_high, first_low = kernel_call(split_kernel, panel, [], [first])
+    joined = jnp.concatenate([kept[:, :panel_rows], received[:, :panel_rows]], 1)
+    parts = swap_columns([joined] * col_count)
+    parts = kernel_call(
+        first_kernel,
+        [more] * (leaf_count // 2),
+        [place],
+        [*parts, near_high, near_low, kept, received],
+        scratch=[pltpu.VMEM((col_count, group, own_columns), jnp.float32)],
+    )
+    parts = [parts[0]] + [flip(parts[f], "leaf", 2 * f) for f in range(1, leaf_count // 2)]
+    parts = kernel_call(
+        share_kernel,
+        [more] * col_count,
+        [place],
+        parts,
+        scratch=[pltpu.VMEM((leaf_count // 2, GROUP, own_columns), jnp.float32)],
+    )
+    first_sum = parts[0]
+    parts = swap_columns(parts)
+    (left,) = kernel_call(coupled_kernel, [one], [place], [*parts, between_high, between_low])
     parts = swap_columns([left] * col_count)
     parts = kernel_call(
         turn_kernel, [one] * col_count, [place], [*parts, second_high, second_low]
@@ -439,12 +482,12 @@
     )
     parts = swap_columns(parts)
     parts = kernel_call(
-        final_kernel, wide, [place], [*parts, first_high, first_low, first, last]
+        final_kernel, wide, [place], [*parts, first_high, first_low, first_sum, last]
     )
     parts = swap_columns(parts)
     (split,) = kernel_call(
         collect_kernel,
-        [((leaf_count, panel_count, rows, panel_rows), jnp.float32)],
+        [((leaf_count, panel_count, GROUP, panel_rows), jnp.float32)],
         [place],
         parts,
     )
@@ -457,9 +500,9 @@
     panel_rows, own_columns = root_inverse.shape[1:]
     return (
         leaf_count == 8
-        and col_count & (col_count - 1) == 0
-        and rhs_rows % (8 * leaf_count) == 0
-        and own_columns % panel_rows == 0
+        and col_count == 4
+        and rhs_rows == GROUP * leaf_count
+        and own_columns == 2 * panel_rows
     )
 
 
@@ -488,10 +531,8 @@
     )
     if replicates(right_sides.shape[0], root_inverse):
         place = jnp.stack([lax.axis_index("leaf"), lax.axis_index("col")]).astype(jnp.int32)
-        solved, split = eliminate_all(
-            place, right_sides, level_data, front_rows, *root_inverse.shape[:2]
-        )
-        return (*solved, root_replicated(place, split, root_inverse, root_coupling))
+        solved, *sections = eliminate_all(place, right_sides, level_data, front_rows)
+        return (*solved, root_replicated(place, *sections, root_inverse, root_coupling))
     section = right_sides
     outputs = []
     for level_index in range(3):

time: 160 us -> 143 us (0.89)
  waiting for transfers between devices: 73 us -> 45.6 us
  between operations: 0.84 us -> 14.3 us
  starting transfers between devices: 47 us -> 38.6 us
  local copies, waits for them, and re-layouts: 8.76 us -> 12.7 us
  blocking collectives: 7.92 us -> 9.81 us
    ppermute x47 -> x34, waiting for transfers between devices: 69.1 us -> 44.9 us  [flip(): return lax.ppermute(block, axis, [(i, i ^ distance) for i in range(count)])]
    ppermute x47 -> x34, starting transfers between devices: 43 us -> 38.5 us  [flip(): return lax.ppermute(block, axis, [(i, i ^ distance) for i in range(count)])]
    all_to_all x1 -> x0, waiting for transfers between devices: 3.98 us -> none  [root_replicated(): whole = lax.all_to_all(split, 'leaf', 0, 0, tiled=True)]
    all_to_all x1 -> x0, starting transfers between devices: 3.97 us -> none  [root_replicated(): whole = lax.all_to_all(split, 'leaf', 0, 0, tiled=True)]
    slice x0 -> x3, local copies, waits for them, and re-layouts: none -> 2.26 us  [the longest x1 2.26 us: root_replicated(): root_inverse[0]]
    all_to_all x1, blocking collectives: 7.92 us -> 9.81 us  [root_replicated(): whole = lax.all_to_all(split, 'leaf', 0, 0, tiled=True)]
    unnamed x32 -> x46, local copies, waits for them, and re-layouts: 8.57 us -> 10.4 us
    pallas_call x13 -> x14, Pallas kernels: 21.5 us -> 21.5 us  [kernel_call(): pl.pallas_call(run, out_shape=[jax.ShapeDtypeStruct(shape, kind) for shap...]
  transfers between devices with their start and end apart: 48 -> 36, of which waited for: 27 -> 19; matrix products, arithmetic and copies ran while one was open for 0% -> 2% of each run, Pallas kernels for 6% -> 13%
where the time goes in v3:
time: 143 us
  waiting for transfers between devices  45.6 us (32%)
  starting transfers between devices  38.6 us (27%)
  Pallas kernels  21.5 us (15%)
  between operations  14.3 us (10%)
  local copies, waits for them, and re-layouts  12.7 us (9%)
  blocking collectives  9.81 us (7%)
    ppermute x34, waiting for transfers between devices, flip(): return lax.ppermute(block, axis, [(i, i ^ distance) for i in range(count)])  44.9 us
    ppermute x34, starting transfers between devices, flip(): return lax.ppermute(block, axis, [(i, i ^ distance) for i in range(count)])  38.5 us
    pallas_call x14, Pallas kernels, kernel_call(): pl.pallas_call(run, out_shape=[jax.ShapeDtypeStruct(shape, kind) for shap...  21.5 us
    unnamed x46, local copies, waits for them, and re-layouts  10.4 us
    all_to_all x1, blocking collectives, root_replicated(): whole = lax.all_to_all(split, 'leaf', 0, 0, tiled=True)  9.81 us
  transfers between devices with their start and end apart: 36, of which 19 were waited for; matrix products, arithmetic and copies ran while one was open for 2% of the time, Pallas kernels for 13%

profile of v3, /device:TPU:0, one launch (start us, length us, event | category | flops | bytes accessed | tf_op | source)
XLA Modules:
  0.0 142.6 jit_solution(12361627596315569436)
XLA Ops:
  7.2 0.7 all-gather.4.cloned.1.call-update
  8.0 2.3 %fusion = (f32[1,256,512]{2,1,0:T(8,128)}, f32[256,512]{1,0:T(8,128)S(1)}, f32[256,512]{1,0:T(8,128)S(1)}) fusion(f32[2,256,512]{2,1,0:T(8,128)} %param.30), kind=kLoop, calls=%fused_computation.5 | loop fusion | bytes 2621440 | tf_op jit(solution)/shard_map/slice | solution.py:448
  11.0 1.0 copy-done.5
  12.1 0.9 copy-done.7
  13.0 2.4 %shard_map.183 = (f32[64,512]{1,0:T(8,128)}, f32[6,64,128]{2,1,0:T(8,128)S(1)}, f32[6,64,128]{2,1,0:T(8,128)S(1)}) custom-call(s32[2]{0:T(128)S(1)} %pad_add_fusion.refs_0_, s32[3,1]{1,0:T(4,128)S(1)} %copy.23.refs_1_, s32[4,3]{1,0:T(4,128)S(1)} %copy-done.15, f32[64,2048]{1,0:T(8,128)S(1)} %copy-done.5, f32[4,128,128]{2,1,0:T(8,128)S(1)} %copy-done.7, ...), custom_call_target="tpu_custom_call" | custom-call | tf_op jit(solution)/shard_map/pallas_call | solution.py:144
  15.5 1.4 collective-permute-done.refs_5_
  16.9 0.9 copy-done.6
  17.8 2.4 %shard_map.184 = (f32[64,512]{1,0:T(8,128)}, f32[4,64,128]{2,1,0:T(8,128)S(1)}, f32[4,64,128]{2,1,0:T(8,128)S(1)}) custom-call(s32[2]{0:T(128)S(1)} %pad_add_fusion.refs_0_, s32[3,1]{1,0:T(4,128)S(1)} %copy.23.refs_1_, s32[4,3]{1,0:T(4,128)S(1)} %copy-done.16, s32[1,12]{1,0:T(1,128)S(1)} %copy-done.18, f32[6,64,128]{2,1,0:T(8,128)S(1)} %get-tuple-element.43.refs_4_, ...), custom_call_target="tpu_custom_call" | custom-call | tf_op jit(solution)/shard_map/pallas_call | solution.py:144
  20.2 2.7 %collective-permute-start.1 = (f32[4,64,128]{2,1,0:T(8,128)S(1)}, f32[4,64,128]{2,1,0:T(8,128)S(1)}, u32[]{:S(2)}, u32[]{:S(2)}) collective-permute-start(f32[4,64,128]{2,1,0:T(8,128)S(1)} %get-tuple-element.47), channel_id=1, source_target_pairs={{0,8},{4,12},{8,0},{12,4},{16,24},{20,28},{24,16},{28,20},{1,9},{5... | collective-permute-start | bytes 393224 | tf_op jit(solution)/shard_map/ppermute | solution.py:129
  22.9 2.0 %collective-permute-start.17 = (f32[256,512]{1,0:T(8,128)S(1)}, f32[256,512]{1,0:T(8,128)S(1)}, u32[]{:S(2)}, u32[]{:S(2)}) collective-permute-start(f32[256,512]{1,0:T(8,128)S(1)} %get-tuple-element.86.refs_1_), channel_id=1, source_target_pairs={{0,16},{4,20},{8,24},{12,28},{16,0},{20,4},{24,8},{28,12},{1,17},{... | collective-permute-start | bytes 1572872 | tf_op jit(solution)/shard_map/ppermute | solution.py:129
  24.9 4.8 %collective-permute-done.1.refs_6_ = f32[4,64,128]{2,1,0:T(8,128)S(1)} collective-permute-done((f32[4,64,128]{2,1,0:T(8,128)S(1)}, f32[4,64,128]{2,1,0:T(8,128)S(1)}, u32[]{:S(2)}, u32[]{:S(2)}) %collective-permute-start.1) | collective-permute-done | bytes 131104 | tf_op jit(solution)/shard_map/ppermute | solution.py:129
  29.8 2.4 %shard_map.185 = (f32[64,512]{1,0:T(8,128)}, f32[32,512]{1,0:T(8,128)S(1)}, f32[32,512]{1,0:T(8,128)S(1)}) custom-call(s32[2]{0:T(128)S(1)} %pad_add_fusion.refs_0_, s32[3,1]{1,0:T(4,128)S(1)} %copy.23.refs_1_, s32[4,3]{1,0:T(4,128)S(1)} %copy-done.17, s32[1,8]{1,0:T(1,128)S(1)} %copy-done.19, s32[1,4]{1,0:T(1,128)S(1)} %copy-done.20, ...), custom_call_target="tpu_custom_call" | custom-call | tf_op jit(solution)/shard_map/pallas_call | solution.py:144
  32.2 1.2 collective-permute-done.2.refs_8_
  33.5 2.4 %collective-permute-start.3 = (f32[32,512]{1,0:T(8,128)S(1)}, f32[32,512]{1,0:T(8,128)S(1)}, u32[]{:S(2)}, u32[]{:S(2)}) collective-permute-start(f32[32,512]{1,0:T(8,128)S(1)} %pad_maximum_fusion.refs_1_), channel_id=1, source_target_pairs={{0,1},{1,0},{2,3},{3,2},{4,5},{5,4},{6,7},{7,6},{8,9},{9,8},{10,11... | collective-permute-start | bytes 196616 | tf_op jit(solution)/shard_map/ppermute | solution.py:129
  35.9 2.6 %collective-permute-start.4 = (f32[32,512]{1,0:T(8,128)S(1)}, f32[32,512]{1,0:T(8,128)S(1)}, u32[]{:S(2)}, u32[]{:S(2)}) collective-permute-start(f32[32,512]{1,0:T(8,128)S(1)} %pad_maximum_fusion.refs_1_), channel_id=1, source_target_pairs={{0,2},{1,3},{2,0},{3,1},{4,6},{5,7},{6,4},{7,5},{8,10},{9,11},{10,... | collective-permute-start | bytes 196616 | tf_op jit(solution)/shard_map/ppermute | solution.py:129
  38.5 1.2 shard_map.186
  39.7 3.7 %collective-permute-done.4.refs_3_ = f32[32,512]{1,0:T(8,128)S(1)} collective-permute-done((f32[32,512]{1,0:T(8,128)S(1)}, f32[32,512]{1,0:T(8,128)S(1)}, u32[]{:S(2)}, u32[]{:S(2)}) %collective-permute-start.4) | collective-permute-done | bytes 65568 | tf_op jit(solution)/shard_map/ppermute | solution.py:129
  43.4 1.2 collective-permute-done.5.refs_4_
  44.7 0.9 shard_map.187
  45.6 1.3 collective-permute-start.7
  46.9 1.5 %collective-permute-start.8 = (f32[40,512]{1,0:T(8,128)S(1)}, f32[40,512]{1,0:T(8,128)S(1)}, u32[]{:S(2)}, u32[]{:S(2)}) collective-permute-start(f32[40,512]{1,0:T(8,128)S(1)} %get-tuple-element.55), channel_id=1, source_target_pairs={{0,16},{4,20},{8,24},{12,28},{16,0},{20,4},{24,8},{28,12},{1,17},{... | collective-permute-start | bytes 245768 | tf_op jit(solution)/shard_map/ppermute | solution.py:129
  48.4 0.7 collective-permute-start.9
  49.2 3.5 %collective-permute-done.7.refs_2_ = f32[40,512]{1,0:T(8,128)S(1)} collective-permute-done((f32[40,512]{1,0:T(8,128)S(1)}, f32[40,512]{1,0:T(8,128)S(1)}, u32[]{:S(2)}, u32[]{:S(2)}) %collective-permute-start.7) | collective-permute-done | bytes 81952 | tf_op jit(solution)/shard_map/ppermute | solution.py:129
  52.7 1.2 collective-permute-done.8.refs_3_
  53.9 2.4 %collective-permute-done.9.refs_4_ = f32[40,512]{1,0:T(8,128)S(1)} collective-permute-done((f32[40,512]{1,0:T(8,128)S(1)}, f32[40,512]{1,0:T(8,128)S(1)}, u32[]{:S(2)}, u32[]{:S(2)}) %collective-permute-start.9) | collective-permute-done | bytes 81952 | tf_op jit(solution)/shard_map/ppermute | solution.py:129
  56.9 1.1 collective-permute-start.10
  58.0 1.4 collective-permute-start.11
  59.3 2.0 %collective-permute-start.12 = (f32[40,512]{1,0:T(8,128)S(1)}, f32[40,512]{1,0:T(8,128)S(1)}, u32[]{:S(2)}, u32[]{:S(2)}) collective-permute-start(f32[40,512]{1,0:T(8,128)S(1)} %get-tuple-element.60), channel_id=1, source_target_pairs={{0,3},{1,2},{2,1},{3,0},{4,7},{5,6},{6,5},{7,4},{8,11},{9,10},{10,... | collective-permute-start | bytes 245768 | tf_op jit(solution)/shard_map/ppermute | solution.py:129
  61.9 0.6 copy-done.9
  62.6 1.9 %collective-permute-done.11.refs_3_ = f32[40,512]{1,0:T(8,128)S(1)} collective-permute-done((f32[40,512]{1,0:T(8,128)S(1)}, f32[40,512]{1,0:T(8,128)S(1)}, u32[]{:S(2)}, u32[]{:S(2)}) %collective-permute-start.11) | collective-permute-done | bytes 81952 | tf_op jit(solution)/shard_map/ppermute | solution.py:129
  64.6 0.6 copy-done.11
  65.7 0.6 copy-done.13
  66.3 1.5 %collective-permute-start.19 = (f32[128,512]{1,0:T(8,128)S(1)}, f32[128,512]{1,0:T(8,128)}, u32[]{:S(2)}, u32[]{:S(2)}) collective-permute-start(f32[128,512]{1,0:T(8,128)S(1)} %slice.28), channel_id=1, source_target_pairs={{0,8},{4,12},{8,0},{12,4},{16,24},{20,28},{24,16},{28,20},{1,9},{5... | collective-permute-start | bytes 786440 | tf_op jit(solution)/shard_map/ppermute | solution.py:129
  67.8 5.3 %collective-permute-done.18.refs_4_ = f32[128,512]{1,0:T(8,128)S(1)} collective-permute-done((f32[128,512]{1,0:T(8,128)S(1)}, f32[128,512]{1,0:T(8,128)S(1)}, u32[]{:S(2)}, u32[]{:S(2)}) %collective-permute-start.18) | collective-permute-done | bytes 262176 | tf_op jit(solution)/shard_map/ppermute | solution.py:129
  73.0 4.2 %collective-permute-done.19.refs_5_ = f32[128,512]{1,0:T(8,128)} collective-permute-done((f32[128,512]{1,0:T(8,128)S(1)}, f32[128,512]{1,0:T(8,128)}, u32[]{:S(2)}, u32[]{:S(2)}) %collective-permute-start.19) | collective-permute-done | bytes 262176 | tf_op jit(solution)/shard_map/ppermute | solution.py:129
  77.3 2.2 %copy-done.1 = f32[2048,512]{1,0:T(8,128)S(1)} copy-done((f32[2048,512]{1,0:T(8,128)S(1)}, f32[2048,512]{1,0:T(8,128)}, u32[]{:S(2)}) %copy-start.1) | copy-done | bytes 4194328
  79.5 0.7 shard_map.189
  80.4 1.4 shard_map.190.refs_1_
  81.9 3.5 %collective-permute-start.14 = (f32[32,512]{1,0:T(8,128)S(1)}, f32[32,512]{1,0:T(8,128)S(1)}, u32[]{:S(2)}, u32[]{:S(2)}) collective-permute-start(f32[32,512]{1,0:T(8,128)S(1)} %shard_map.190.refs_1_), channel_id=1, source_target_pairs={{0,2},{1,3},{2,0},{3,1},{4,6},{5,7},{6,4},{7,5},{8,10},{9,11},{10,... | collective-permute-start | bytes 196616 | tf_op jit(solution)/shard_map/ppermute | solution.py:129
  85.4 0.8 collective-permute-start.15
  86.3 1.8 %shard_map.191 = (bf16[2048,512]{1,0:T(8,128)(2,1)S(1)}, bf16[2048,512]{1,0:T(8,128)(2,1)S(1)}) custom-call(s32[2]{0:T(128)S(1)} %pad_add_fusion.refs_0_, f32[256,512]{1,0:T(8,128)S(1)} %get-tuple-element.86.refs_1_, f32[256,512]{1,0:T(8,128)S(1)} %collective-permute-done.16.refs_2_, f32[256,512]{1,0:T(8,128)S(1)} %collective-permute-done.17.refs_3_, ...), custom_call_target="tpu_custom_call" | custom-call | tf_op jit(solution)/shard_map/pallas_call | solution.py:144
  88.1 1.5 %collective-permute-done.14.refs_3_ = f32[32,512]{1,0:T(8,128)S(1)} collective-permute-done((f32[32,512]{1,0:T(8,128)S(1)}, f32[32,512]{1,0:T(8,128)S(1)}, u32[]{:S(2)}, u32[]{:S(2)}) %collective-permute-start.14) | collective-permute-done | bytes 65568 | tf_op jit(solution)/shard_map/ppermute | solution.py:129
  89.6 1.9 %collective-permute-done.15.refs_4_ = f32[32,512]{1,0:T(8,128)S(1)} collective-permute-done((f32[32,512]{1,0:T(8,128)S(1)}, f32[32,512]{1,0:T(8,128)S(1)}, u32[]{:S(2)}, u32[]{:S(2)}) %collective-permute-start.15) | collective-permute-done | bytes 65568 | tf_op jit(solution)/shard_map/ppermute | solution.py:129
  91.5 2.6 %shard_map.192 = (f32[32,512]{1,0:T(8,128)S(1)}, f32[32,512]{1,0:T(8,128)S(1)}, f32[32,512]{1,0:T(8,128)S(1)}, f32[32,512]{1,0:T(8,128)S(1)}) custom-call(s32[2]{0:T(128)S(1)} %pad_add_fusion.refs_0_, f32[32,512]{1,0:T(8,128)S(1)} %shard_map.190.refs_1_, f32[32,512]{1,0:T(8,128)S(1)} %collective-permute-done.13.refs_2_, ...), custom_call_target="tpu_custom_call" | custom-call | tf_op jit(solution)/shard_map/pallas_call | solution.py:144
  94.2 1.1 collective-permute-start.25
  95.3 1.5 %collective-permute-start.26 = (f32[32,512]{1,0:T(8,128)S(1)}, f32[32,512]{1,0:T(8,128)S(1)}, u32[]{:S(2)}, u32[]{:S(2)}) collective-permute-start(f32[32,512]{1,0:T(8,128)S(1)} %get-tuple-element.67), channel_id=1, source_target_pairs={{0,2},{1,3},{2,0},{3,1},{4,6},{5,7},{6,4},{7,5},{8,10},{9,11},{10,... | collective-permute-start | bytes 196616 | tf_op jit(solution)/shard_map/ppermute | solution.py:129
  96.8 1.8 %collective-permute-start.27 = (f32[32,512]{1,0:T(8,128)S(1)}, f32[32,512]{1,0:T(8,128)S(1)}, u32[]{:S(2)}, u32[]{:S(2)}) collective-permute-start(f32[32,512]{1,0:T(8,128)S(1)} %get-tuple-element.68), channel_id=1, source_target_pairs={{0,3},{1,2},{2,1},{3,0},{4,7},{5,6},{6,5},{7,4},{8,11},{9,10},{10,... | collective-permute-start | bytes 196616 | tf_op jit(solution)/shard_map/ppermute | solution.py:129
  98.6 4.8 %collective-permute-done.26.refs_3_ = f32[32,512]{1,0:T(8,128)S(1)} collective-permute-done((f32[32,512]{1,0:T(8,128)S(1)}, f32[32,512]{1,0:T(8,128)S(1)}, u32[]{:S(2)}, u32[]{:S(2)}) %collective-permute-start.26) | collective-permute-done | bytes 65568 | tf_op jit(solution)/shard_map/ppermute | solution.py:129
  103.3 1.9 %shard_map.193 = (f32[32,512]{1,0:T(8,128)S(1)}, f32[32,512]{1,0:T(8,128)S(1)}, f32[32,512]{1,0:T(8,128)S(1)}, f32[32,512]{1,0:T(8,128)S(1)}, f32[32,512]{1,0:T(8,128)S(1)}) custom-call(s32[2]{0:T(128)S(1)} %pad_add_fusion.refs_0_, f32[32,512]{1,0:T(8,128)S(1)} %get-tuple-element.65.refs_1_, f32[32,512]{1,0:T(8,128)S(1)} %collective-permute-done.25.refs_2_, ...), custom_call_target="tpu_custom_call" | custom-call | tf_op jit(solution)/shard_map/pallas_call | solution.py:144
  105.2 1.3 collective-permute-start.28
  106.5 1.6 %collective-permute-start.29 = (f32[32,512]{1,0:T(8,128)S(1)}, f32[32,512]{1,0:T(8,128)S(1)}, u32[]{:S(2)}, u32[]{:S(2)}) collective-permute-start(f32[32,512]{1,0:T(8,128)S(1)} %get-tuple-element.71), channel_id=1, source_target_pairs={{0,2},{1,3},{2,0},{3,1},{4,6},{5,7},{6,4},{7,5},{8,10},{9,11},{10,... | collective-permute-start | bytes 196616 | tf_op jit(solution)/shard_map/ppermute | solution.py:129
  108.1 1.5 %collective-permute-start.30 = (f32[32,512]{1,0:T(8,128)S(1)}, f32[32,512]{1,0:T(8,128)S(1)}, u32[]{:S(2)}, u32[]{:S(2)}) collective-permute-start(f32[32,512]{1,0:T(8,128)S(1)} %get-tuple-element.72), channel_id=1, source_target_pairs={{0,3},{1,2},{2,1},{3,0},{4,7},{5,6},{6,5},{7,4},{8,11},{9,10},{10,... | collective-permute-start | bytes 196616 | tf_op jit(solution)/shard_map/ppermute | solution.py:129
  109.6 2.2 %copy-done = f32[1,2048,512]{2,1,0:T(8,128)S(1)} copy-done((f32[1,2048,512]{2,1,0:T(8,128)S(1)}, f32[1,2048,512]{2,1,0:T(8,128)}, u32[]{:S(2)}) %copy-start) | copy-done | bytes 4194328
  111.8 0.7 shard_map.194
  113.0 1.3 collective-permute-done.30.refs_4_
  114.3 1.9 %shard_map.195 = (f32[8,2560]{1,0:T(8,128)S(1)}, f32[8,2560]{1,0:T(8,128)S(1)}, f32[8,2560]{1,0:T(8,128)S(1)}, f32[8,2560]{1,0:T(8,128)S(1)}) custom-call(s32[2]{0:T(128)S(1)} %pad_add_fusion.refs_0_, f32[32,512]{1,0:T(8,128)S(1)} %get-tuple-element.69.refs_1_, f32[32,512]{1,0:T(8,128)S(1)} %collective-permute-done.28.refs_2_, ...), custom_call_target="tpu_custom_call" | custom-call | tf_op jit(solution)/shard_map/pallas_call | solution.py:144
  116.2 0.7 collective-permute-start.31
  116.8 1.4 collective-permute-start.32
  118.2 2.3 %collective-permute-start.33 = (f32[8,2560]{1,0:T(8,128)S(1)}, f32[8,2560]{1,0:T(8,128)S(1)}, u32[]{:S(2)}, u32[]{:S(2)}) collective-permute-start(f32[8,2560]{1,0:T(8,128)S(1)} %get-tuple-element.79), channel_id=1, source_target_pairs={{0,3},{1,2},{2,1},{3,0},{4,7},{5,6},{6,5},{7,4},{8,11},{9,10},{10,... | collective-permute-start | bytes 245768 | tf_op jit(solution)/shard_map/ppermute | solution.py:129
  120.6 0.8 collective-permute-done.31.refs_2_
  121.4 0.9 collective-permute-done.32.refs_3_
  122.3 2.3 %collective-permute-done.33.refs_4_ = f32[8,2560]{1,0:T(8,128)S(1)} collective-permute-done((f32[8,2560]{1,0:T(8,128)S(1)}, f32[8,2560]{1,0:T(8,128)S(1)}, u32[]{:S(2)}, u32[]{:S(2)}) %collective-permute-start.33) | collective-permute-done | bytes 81952 | tf_op jit(solution)/shard_map/ppermute | solution.py:129
  125.2 9.8 %all_to_all.5 = f32[8,2,8,256]{3,2,1,0:T(8,128)S(1)} all-to-all(f32[8,2,8,256]{3,2,1,0:T(8,128)S(1)} %shard_map.196), channel_id=1, replica_groups=mesh['leaf'=8,'col'=4] {'leaf'}, dimensions={0} | all-to-all | bytes 262144 | tf_op jit(solution)/shard_map/all_to_all | solution.py:494
  135.0 0.8 copy.27
  (79 shorter events, 4.0 us)
Async XLA Ops:
  7.2 3.8 %copy-start.21 = (s32[3,1]{0,1:T(1,128)S(1)}, s32[3,1]{0,1:T(1,128)}, u32[]{:S(2)}) copy-start(s32[3,1]{0,1:T(1,128)} %param.29) | copy-start | bytes 40
  7.2 3.8 %copy-start.15 = (s32[4,3]{1,0:T(4,128)S(1)}, s32[4,3]{1,0:T(4,128)}, u32[]{:S(2)}) copy-start(s32[4,3]{1,0:T(4,128)} %refs_2_.3) | copy-start | bytes 148
  7.2 3.8 %copy-start.2 = (f32[4,3,128,128]{3,2,1,0:T(8,128)S(1)}, f32[4,3,128,128]{3,2,1,0:T(8,128)}, u32[]{:S(2)}) copy-start(f32[4,3,128,128]{3,2,1,0:T(8,128)} %refs_5_.1) | copy-start | bytes 2359300
  7.2 70.1 %all-gather.4.cloned.1.call-start = ((), (), s32[]{:S(2)}) async-start(), calls=%async_computation.1 | async-start | bytes 4718592 | tf_op jit(solution)/shard_map/all_gather | solution.py:450
  7.9 8.9 %copy-start.3 = (f32[4,3,128,128]{3,2,1,0:T(8,128)S(1)}, f32[4,3,128,128]{3,2,1,0:T(8,128)}, u32[]{:S(2)}) copy-start(f32[4,3,128,128]{3,2,1,0:T(8,128)} %refs_7_.2) | copy-start | bytes 2359300
  7.9 8.9 %copy-start.16 = (s32[4,3]{1,0:T(4,128)S(1)}, s32[4,3]{1,0:T(4,128)}, u32[]{:S(2)}) copy-start(s32[4,3]{1,0:T(4,128)} %refs_2_.4) | copy-start | bytes 148
  8.0 8.9 %copy-start.18 = (s32[1,12]{1,0:T(1,128)S(1)}, s32[1,12]{1,0:T(1,128)}, u32[]{:S(2)}) copy-start(s32[1,12]{1,0:T(1,128)} %refs_3_.4) | copy-start | bytes 148
  8.0 101.7 %all-gather.6.cloned.1.call-start = ((), (), s32[]{:S(2)}) async-start(), calls=%async_computation.2 | async-start | bytes 4718592 | tf_op jit(solution)/shard_map/all_gather | solution.py:453
  8.0 21.7 %copy-start.17 = (s32[4,3]{1,0:T(4,128)S(1)}, s32[4,3]{1,0:T(4,128)}, u32[]{:S(2)}) copy-start(s32[4,3]{1,0:T(4,128)} %refs_2_.5) | copy-start | bytes 148
  8.0 21.7 %copy-start.19 = (s32[1,8]{1,0:T(1,128)S(1)}, s32[1,8]{1,0:T(1,128)}, u32[]{:S(2)}) copy-start(s32[1,8]{1,0:T(1,128)} %refs_3_.5) | copy-start | bytes 100
  8.0 21.7 %copy-start.20 = (s32[1,4]{1,0:T(1,128)S(1)}, s32[1,4]{1,0:T(1,128)}, u32[]{:S(2)}) copy-start(s32[1,4]{1,0:T(1,128)} %refs_4_.3) | copy-start | bytes 52
  10.3 19.5 %copy-start.4 = (f32[4,3,128,128]{3,2,1,0:T(8,128)S(1)}, f32[4,3,128,128]{3,2,1,0:T(8,128)}, u32[]{:S(2)}) copy-start(f32[4,3,128,128]{3,2,1,0:T(8,128)} %refs_8_.1) | copy-start | bytes 2359300
  10.3 28.2 %collective-permute-start.6 = (f32[256,512]{1,0:T(8,128)S(1)}, f32[256,512]{1,0:T(8,128)}, u32[]{:S(2)}, u32[]{:S(2)}) collective-permute-start(f32[256,512]{1,0:T(8,128)S(1)} %get-tuple-element.85.refs_0_), channel_id=1, source_target_pairs={{0,4},{4,0},{8,12},{12,8},{16,20},{20,16},{24,28},{28,24},{1,5},{5... | collective-permute-start | bytes 1572872 | tf_op jit(solution)/shard_map/ppermute | solution.py:129
  11.0 1.0 copy-start.5
  12.1 0.9 copy-start.7
  13.0 16.7 %copy-start.8 = (f32[4,128,128]{2,1,0:T(8,128)S(1)}, f32[4,128,128]{2,1,0:T(8,128)}, u32[]{:S(2)}) copy-start(f32[4,128,128]{2,1,0:T(8,128)} %refs_7_.3) | copy-start | bytes 786436
  15.4 1.4 %collective-permute-start = (f32[6,64,128]{2,1,0:T(8,128)S(1)}, f32[6,64,128]{2,1,0:T(8,128)S(1)}, u32[]{:S(2)}, u32[]{:S(2)}) collective-permute-start(f32[6,64,128]{2,1,0:T(8,128)S(1)} %get-tuple-element.44), channel_id=1, source_target_pairs={{0,4},{4,0},{8,12},{12,8},{16,20},{20,16},{24,28},{28,24},{1,5},{5... | collective-permute-start | bytes 589832 | tf_op jit(solution)/shard_map/ppermute | solution.py:129
  16.9 1.0 copy-start.6
  20.2 9.5 %collective-permute-start.1 = (f32[4,64,128]{2,1,0:T(8,128)S(1)}, f32[4,64,128]{2,1,0:T(8,128)S(1)}, u32[]{:S(2)}, u32[]{:S(2)}) collective-permute-start(f32[4,64,128]{2,1,0:T(8,128)S(1)} %get-tuple-element.47), channel_id=1, source_target_pairs={{0,8},{4,12},{8,0},{12,4},{16,24},{20,28},{24,16},{28,20},{1,9},{5... | collective-permute-start | bytes 393224 | tf_op jit(solution)/shard_map/ppermute | solution.py:129
  22.9 38.5 %collective-permute-start.16 = (f32[256,512]{1,0:T(8,128)S(1)}, f32[256,512]{1,0:T(8,128)S(1)}, u32[]{:S(2)}, u32[]{:S(2)}) collective-permute-start(f32[256,512]{1,0:T(8,128)S(1)} %get-tuple-element.86.refs_1_), channel_id=1, source_target_pairs={{0,8},{4,12},{8,0},{12,4},{16,24},{20,28},{24,16},{28,20},{1,9},{5... | collective-permute-start | bytes 1572872 | tf_op jit(solution)/shard_map/ppermute | solution.py:129
  22.9 38.4 %collective-permute-start.17 = (f32[256,512]{1,0:T(8,128)S(1)}, f32[256,512]{1,0:T(8,128)S(1)}, u32[]{:S(2)}, u32[]{:S(2)}) collective-permute-start(f32[256,512]{1,0:T(8,128)S(1)} %get-tuple-element.86.refs_1_), channel_id=1, source_target_pairs={{0,16},{4,20},{8,24},{12,28},{16,0},{20,4},{24,8},{28,12},{1,17},{... | collective-permute-start | bytes 1572872 | tf_op jit(solution)/shard_map/ppermute | solution.py:129
  32.2 1.3 collective-permute-start.2
  33.5 6.3 %collective-permute-start.3 = (f32[32,512]{1,0:T(8,128)S(1)}, f32[32,512]{1,0:T(8,128)S(1)}, u32[]{:S(2)}, u32[]{:S(2)}) collective-permute-start(f32[32,512]{1,0:T(8,128)S(1)} %pad_maximum_fusion.refs_1_), channel_id=1, source_target_pairs={{0,1},{1,0},{2,3},{3,2},{4,5},{5,4},{6,7},{7,6},{8,9},{9,8},{10,11... | collective-permute-start | bytes 196616 | tf_op jit(solution)/shard_map/ppermute | solution.py:129
  35.9 7.5 %collective-permute-start.4 = (f32[32,512]{1,0:T(8,128)S(1)}, f32[32,512]{1,0:T(8,128)S(1)}, u32[]{:S(2)}, u32[]{:S(2)}) collective-permute-start(f32[32,512]{1,0:T(8,128)S(1)} %pad_maximum_fusion.refs_1_), channel_id=1, source_target_pairs={{0,2},{1,3},{2,0},{3,1},{4,6},{5,7},{6,4},{7,5},{8,10},{9,11},{10,... | collective-permute-start | bytes 196616 | tf_op jit(solution)/shard_map/ppermute | solution.py:129
  38.5 6.2 %collective-permute-start.5 = (f32[32,512]{1,0:T(8,128)S(1)}, f32[32,512]{1,0:T(8,128)S(1)}, u32[]{:S(2)}, u32[]{:S(2)}) collective-permute-start(f32[32,512]{1,0:T(8,128)S(1)} %pad_maximum_fusion.refs_1_), channel_id=1, source_target_pairs={{0,3},{1,2},{2,1},{3,0},{4,7},{5,6},{6,5},{7,4},{8,11},{9,10},{10,... | collective-permute-start | bytes 196616 | tf_op jit(solution)/shard_map/ppermute | solution.py:129
  45.6 7.1 %collective-permute-start.7 = (f32[40,512]{1,0:T(8,128)S(1)}, f32[40,512]{1,0:T(8,128)S(1)}, u32[]{:S(2)}, u32[]{:S(2)}) collective-permute-start(f32[40,512]{1,0:T(8,128)S(1)} %get-tuple-element.54), channel_id=1, source_target_pairs={{0,8},{4,12},{8,0},{12,4},{16,24},{20,28},{24,16},{28,20},{1,9},{5... | collective-permute-start | bytes 245768 | tf_op jit(solution)/shard_map/ppermute | solution.py:129
  46.9 7.0 %collective-permute-start.8 = (f32[40,512]{1,0:T(8,128)S(1)}, f32[40,512]{1,0:T(8,128)S(1)}, u32[]{:S(2)}, u32[]{:S(2)}) collective-permute-start(f32[40,512]{1,0:T(8,128)S(1)} %get-tuple-element.55), channel_id=1, source_target_pairs={{0,16},{4,20},{8,24},{12,28},{16,0},{20,4},{24,8},{28,12},{1,17},{... | collective-permute-start | bytes 245768 | tf_op jit(solution)/shard_map/ppermute | solution.py:129
  48.4 7.9 %collective-permute-start.9 = (f32[40,512]{1,0:T(8,128)S(1)}, f32[40,512]{1,0:T(8,128)S(1)}, u32[]{:S(2)}, u32[]{:S(2)}) collective-permute-start(f32[40,512]{1,0:T(8,128)S(1)} %get-tuple-element.56), channel_id=1, source_target_pairs={{0,24},{4,28},{8,16},{12,20},{16,8},{20,12},{24,0},{28,4},{1,25},{... | collective-permute-start | bytes 245768 | tf_op jit(solution)/shard_map/ppermute | solution.py:129
  56.9 5.0 %collective-permute-start.10 = (f32[40,512]{1,0:T(8,128)S(1)}, f32[40,512]{1,0:T(8,128)S(1)}, u32[]{:S(2)}, u32[]{:S(2)}) collective-permute-start(f32[40,512]{1,0:T(8,128)S(1)} %get-tuple-element.58), channel_id=1, source_target_pairs={{0,1},{1,0},{2,3},{3,2},{4,5},{5,4},{6,7},{7,6},{8,9},{9,8},{10,11... | collective-permute-start | bytes 245768 | tf_op jit(solution)/shard_map/ppermute | solution.py:129
  58.0 6.6 %collective-permute-start.11 = (f32[40,512]{1,0:T(8,128)S(1)}, f32[40,512]{1,0:T(8,128)S(1)}, u32[]{:S(2)}, u32[]{:S(2)}) collective-permute-start(f32[40,512]{1,0:T(8,128)S(1)} %get-tuple-element.59), channel_id=1, source_target_pairs={{0,2},{1,3},{2,0},{3,1},{4,6},{5,7},{6,4},{7,5},{8,10},{9,11},{10,... | collective-permute-start | bytes 245768 | tf_op jit(solution)/shard_map/ppermute | solution.py:129
  59.3 6.4 %collective-permute-start.12 = (f32[40,512]{1,0:T(8,128)S(1)}, f32[40,512]{1,0:T(8,128)S(1)}, u32[]{:S(2)}, u32[]{:S(2)}) collective-permute-start(f32[40,512]{1,0:T(8,128)S(1)} %get-tuple-element.60), channel_id=1, source_target_pairs={{0,3},{1,2},{2,1},{3,0},{4,7},{5,6},{6,5},{7,4},{8,11},{9,10},{10,... | collective-permute-start | bytes 245768 | tf_op jit(solution)/shard_map/ppermute | solution.py:129
  61.3 20.4 %collective-permute-start.20 = (f32[256,512]{1,0:T(8,128)S(1)}, f32[256,512]{1,0:T(8,128)S(1)}, u32[]{:S(2)}, u32[]{:S(2)}) collective-permute-start(f32[256,512]{1,0:T(8,128)S(1)} %get-tuple-element.86.refs_1_), channel_id=1, source_target_pairs={{0,4},{4,0},{8,12},{12,8},{16,20},{20,16},{24,28},{28,24},{1,5},{5... | collective-permute-start | bytes 1572872 | tf_op jit(solution)/shard_map/ppermute | solution.py:129
  61.4 20.5 %collective-permute-start.21 = (f32[256,512]{1,0:T(8,128)S(1)}, f32[256,512]{1,0:T(8,128)S(1)}, u32[]{:S(2)}, u32[]{:S(2)}) collective-permute-start(f32[256,512]{1,0:T(8,128)S(1)} %collective-permute-done.16.refs_2_), channel_id=1, source_target_pairs={{0,4},{4,0},{8,12},{12,8},{16,20},{20,16},{24,28},{28,24},{1,5},{5... | collective-permute-start | bytes 1572872 | tf_op jit(solution)/shard_map/ppermute | solution.py:129
  61.9 0.6 copy-start.9
  62.5 22.9 %collective-permute-start.22 = (f32[256,512]{1,0:T(8,128)S(1)}, f32[256,512]{1,0:T(8,128)S(1)}, u32[]{:S(2)}, u32[]{:S(2)}) collective-permute-start(f32[256,512]{1,0:T(8,128)S(1)} %collective-permute-done.17.refs_3_), channel_id=1, source_target_pairs={{0,4},{4,0},{8,12},{12,8},{16,20},{20,16},{24,28},{28,24},{1,5},{5... | collective-permute-start | bytes 1572872 | tf_op jit(solution)/shard_map/ppermute | solution.py:129
  64.6 0.6 copy-start.11
  65.2 7.8 %collective-permute-start.18 = (f32[128,512]{1,0:T(8,128)S(1)}, f32[128,512]{1,0:T(8,128)S(1)}, u32[]{:S(2)}, u32[]{:S(2)}) collective-permute-start(f32[128,512]{1,0:T(8,128)S(1)} %slice.27), channel_id=1, source_target_pairs={{0,16},{4,20},{8,24},{12,28},{16,0},{20,4},{24,8},{28,12},{1,17},{... | collective-permute-start | bytes 786440 | tf_op jit(solution)/shard_map/ppermute | solution.py:129
  65.7 0.6 copy-start.13
  66.3 10.9 %collective-permute-start.19 = (f32[128,512]{1,0:T(8,128)S(1)}, f32[128,512]{1,0:T(8,128)}, u32[]{:S(2)}, u32[]{:S(2)}) collective-permute-start(f32[128,512]{1,0:T(8,128)S(1)} %slice.28), channel_id=1, source_target_pairs={{0,8},{4,12},{8,0},{12,4},{16,24},{20,28},{24,16},{28,20},{1,9},{5... | collective-permute-start | bytes 786440 | tf_op jit(solution)/shard_map/ppermute | solution.py:129
  73.0 13.2 %collective-permute-start.23 = (f32[128,512]{1,0:T(8,128)S(1)}, f32[128,512]{1,0:T(8,128)}, u32[]{:S(2)}, u32[]{:S(2)}) collective-permute-start(f32[128,512]{1,0:T(8,128)S(1)} %collective-permute-done.18.refs_4_), channel_id=1, source_target_pairs={{0,4},{4,0},{8,12},{12,8},{16,20},{20,16},{24,28},{28,24},{1,5},{5... | collective-permute-start | bytes 786440 | tf_op jit(solution)/shard_map/ppermute | solution.py:129
  77.3 9.0 %collective-permute-start.24 = (f32[128,512]{1,0:T(8,128)}, f32[128,512]{1,0:T(8,128)}, u32[]{:S(2)}, u32[]{:S(2)}) collective-permute-start(f32[128,512]{1,0:T(8,128)} %collective-permute-done.19.refs_5_), channel_id=1, source_target_pairs={{0,4},{4,0},{8,12},{12,8},{16,20},{20,16},{24,28},{28,24},{1,5},{5... | collective-permute-start | bytes 786440 | tf_op jit(solution)/shard_map/ppermute | solution.py:129
  77.3 2.2 %copy-start.1 = (f32[2048,512]{1,0:T(8,128)S(1)}, f32[2048,512]{1,0:T(8,128)}, u32[]{:S(2)}) copy-start(f32[2048,512]{1,0:T(8,128)} %all-gather.4.cloned.1.call-done.refs_0_) | copy-start | bytes 12582916
  79.4 0.9 copy-start.10
  79.5 0.9 copy-start.12
  79.5 1.0 copy-start.14
  81.8 6.3 %collective-permute-start.13 = (f32[32,512]{1,0:T(8,128)S(1)}, f32[32,512]{1,0:T(8,128)S(1)}, u32[]{:S(2)}, u32[]{:S(2)}) collective-permute-start(f32[32,512]{1,0:T(8,128)S(1)} %shard_map.190.refs_1_), channel_id=1, source_target_pairs={{0,1},{1,0},{2,3},{3,2},{4,5},{5,4},{6,7},{7,6},{8,9},{9,8},{10,11... | collective-permute-start | bytes 196616 | tf_op jit(solution)/shard_map/ppermute | solution.py:129
  81.9 7.7 %collective-permute-start.14 = (f32[32,512]{1,0:T(8,128)S(1)}, f32[32,512]{1,0:T(8,128)S(1)}, u32[]{:S(2)}, u32[]{:S(2)}) collective-permute-start(f32[32,512]{1,0:T(8,128)S(1)} %shard_map.190.refs_1_), channel_id=1, source_target_pairs={{0,2},{1,3},{2,0},{3,1},{4,6},{5,7},{6,4},{7,5},{8,10},{9,11},{10,... | collective-permute-start | bytes 196616 | tf_op jit(solution)/shard_map/ppermute | solution.py:129
  85.4 6.1 %collective-permute-start.15 = (f32[32,512]{1,0:T(8,128)S(1)}, f32[32,512]{1,0:T(8,128)S(1)}, u32[]{:S(2)}, u32[]{:S(2)}) collective-permute-start(f32[32,512]{1,0:T(8,128)S(1)} %shard_map.190.refs_1_), channel_id=1, source_target_pairs={{0,3},{1,2},{2,1},{3,0},{4,7},{5,6},{6,5},{7,4},{8,11},{9,10},{10,... | collective-permute-start | bytes 196616 | tf_op jit(solution)/shard_map/ppermute | solution.py:129
  94.2 4.4 %collective-permute-start.25 = (f32[32,512]{1,0:T(8,128)S(1)}, f32[32,512]{1,0:T(8,128)S(1)}, u32[]{:S(2)}, u32[]{:S(2)}) collective-permute-start(f32[32,512]{1,0:T(8,128)S(1)} %get-tuple-element.66), channel_id=1, source_target_pairs={{0,1},{1,0},{2,3},{3,2},{4,5},{5,4},{6,7},{7,6},{8,9},{9,8},{10,11... | collective-permute-start | bytes 196616 | tf_op jit(solution)/shard_map/ppermute | solution.py:129
  95.3 8.0 %collective-permute-start.26 = (f32[32,512]{1,0:T(8,128)S(1)}, f32[32,512]{1,0:T(8,128)S(1)}, u32[]{:S(2)}, u32[]{:S(2)}) collective-permute-start(f32[32,512]{1,0:T(8,128)S(1)} %get-tuple-element.67), channel_id=1, source_target_pairs={{0,2},{1,3},{2,0},{3,1},{4,6},{5,7},{6,4},{7,5},{8,10},{9,11},{10,... | collective-permute-start | bytes 196616 | tf_op jit(solution)/shard_map/ppermute | solution.py:129
  96.8 6.5 %collective-permute-start.27 = (f32[32,512]{1,0:T(8,128)S(1)}, f32[32,512]{1,0:T(8,128)S(1)}, u32[]{:S(2)}, u32[]{:S(2)}) collective-permute-start(f32[32,512]{1,0:T(8,128)S(1)} %get-tuple-element.68), channel_id=1, source_target_pairs={{0,3},{1,2},{2,1},{3,0},{4,7},{5,6},{6,5},{7,4},{8,11},{9,10},{10,... | collective-permute-start | bytes 196616 | tf_op jit(solution)/shard_map/ppermute | solution.py:129
  105.2 7.3 %collective-permute-start.28 = (f32[32,512]{1,0:T(8,128)S(1)}, f32[32,512]{1,0:T(8,128)S(1)}, u32[]{:S(2)}, u32[]{:S(2)}) collective-permute-start(f32[32,512]{1,0:T(8,128)S(1)} %get-tuple-element.70), channel_id=1, source_target_pairs={{0,1},{1,0},{2,3},{3,2},{4,5},{5,4},{6,7},{7,6},{8,9},{9,8},{10,11... | collective-permute-start | bytes 196616 | tf_op jit(solution)/shard_map/ppermute | solution.py:129
  106.5 6.5 %collective-permute-start.29 = (f32[32,512]{1,0:T(8,128)S(1)}, f32[32,512]{1,0:T(8,128)S(1)}, u32[]{:S(2)}, u32[]{:S(2)}) collective-permute-start(f32[32,512]{1,0:T(8,128)S(1)} %get-tuple-element.71), channel_id=1, source_target_pairs={{0,2},{1,3},{2,0},{3,1},{4,6},{5,7},{6,4},{7,5},{8,10},{9,11},{10,... | collective-permute-start | bytes 196616 | tf_op jit(solution)/shard_map/ppermute | solution.py:129
  108.1 6.2 %collective-permute-start.30 = (f32[32,512]{1,0:T(8,128)S(1)}, f32[32,512]{1,0:T(8,128)S(1)}, u32[]{:S(2)}, u32[]{:S(2)}) collective-permute-start(f32[32,512]{1,0:T(8,128)S(1)} %get-tuple-element.72), channel_id=1, source_target_pairs={{0,3},{1,2},{2,1},{3,0},{4,7},{5,6},{6,5},{7,4},{8,11},{9,10},{10,... | collective-permute-start | bytes 196616 | tf_op jit(solution)/shard_map/ppermute | solution.py:129
  109.6 2.2 %copy-start = (f32[1,2048,512]{2,1,0:T(8,128)S(1)}, f32[1,2048,512]{2,1,0:T(8,128)}, u32[]{:S(2)}) copy-start(f32[1,2048,512]{2,1,0:T(8,128)} %all-gather.6.cloned.1.call-done) | copy-start | bytes 12582916
  116.2 5.2 %collective-permute-start.31 = (f32[8,2560]{1,0:T(8,128)S(1)}, f32[8,2560]{1,0:T(8,128)S(1)}, u32[]{:S(2)}, u32[]{:S(2)}) collective-permute-start(f32[8,2560]{1,0:T(8,128)S(1)} %get-tuple-element.77), channel_id=1, source_target_pairs={{0,1},{1,0},{2,3},{3,2},{4,5},{5,4},{6,7},{7,6},{8,9},{9,8},{10,11... | collective-permute-start | bytes 245768 | tf_op jit(solution)/shard_map/ppermute | solution.py:129
  116.8 5.4 %collective-permute-start.32 = (f32[8,2560]{1,0:T(8,128)S(1)}, f32[8,2560]{1,0:T(8,128)S(1)}, u32[]{:S(2)}, u32[]{:S(2)}) collective-permute-start(f32[8,2560]{1,0:T(8,128)S(1)} %get-tuple-element.78), channel_id=1, source_target_pairs={{0,2},{1,3},{2,0},{3,1},{4,6},{5,7},{6,4},{7,5},{8,10},{9,11},{10,... | collective-permute-start | bytes 245768 | tf_op jit(solution)/shard_map/ppermute | solution.py:129
  118.2 6.3 %collective-permute-start.33 = (f32[8,2560]{1,0:T(8,128)S(1)}, f32[8,2560]{1,0:T(8,128)S(1)}, u32[]{:S(2)}, u32[]{:S(2)}) collective-permute-start(f32[8,2560]{1,0:T(8,128)S(1)} %get-tuple-element.79), channel_id=1, source_target_pairs={{0,3},{1,2},{2,1},{3,0},{4,7},{5,6},{6,5},{7,4},{8,11},{9,10},{10,... | collective-permute-start | bytes 245768 | tf_op jit(solution)/shard_map/ppermute | solution.py:129
Sparse Core Ops, SparseCore 0:
  9.9 48.8 all-gather.3
  60.7 39.0 all-gather.5

commit v4 on v3

--- a/solution.py
+++ b/solution.py
@@ -1,5 +1,3 @@
-import functools
-
 import jax
 import jax.numpy as jnp
 from jax import lax
@@ -133,24 +131,80 @@
     return [parts[0]] + [flip(parts[e], "col", e) for e in range(1, len(parts))]
 
 
-def kernel_call(body, out_shapes, scalars, operands, held=(), scratch=()):
-    spec = pl.BlockSpec(memory_space=pltpu.VMEM)
-    smem = pl.BlockSpec(memory_space=pltpu.SMEM)
-    used = len(scalars) + len(operands)
+def kernel_call(
+    body, out_shapes, scalars, operands, loaded=(), ahead=(), stacks=(), held=(), scratch=(), room=40
+):
+    vmem = pl.BlockSpec(memory_space=pltpu.VMEM)
+    far = pl.BlockSpec(memory_space=pltpu.HBM)
+    out_shapes = [jax.ShapeDtypeStruct(shape, kind) for shape, kind in out_shapes]
+    plain = len(out_shapes)
+    out_shapes += [jax.ShapeDtypeStruct(value.shape, value.dtype) for value in ahead]
+    moves, pieces = [], []
+    for n, stack in enumerate(stacks):
+        first = 0
+        for piece in stack:
+            piece, index = piece if isinstance(piece, tuple) else (piece, None)
+            size = piece.shape[0] if index is None and piece.ndim == 3 else None
+            moves.append((n, first, size, index))
+            pieces.append(piece)
+            first += size or 1
+        out_shapes.append(jax.ShapeDtypeStruct((first, *pieces[-1].shape[-2:]), pieces[-1].dtype))
+    loaded = [value if isinstance(value, tuple) else (value, None) for value in loaded]
+    early = len(scalars) + len(loaded)
+    inputs = (len(scalars), len(loaded), len(ahead), len(pieces), len(held), len(operands))
+    counts = (*inputs, plain, len(ahead), len(stacks), early)
+    waits = early + len(ahead) + 2 * len(pieces)
 
     def run(*refs):
-        body(*refs[:used], *refs[used + len(held) :])
-
+        groups, start = [], 0
+        for count in (*counts, len(refs)):
+            groups.append(refs[start : start + count])
+            start += count
+        ints, loads, nexts, sources, _, ins, outs, next_outs, targets, fetched, rest = groups
+        if waits:
+            *rest, sems = rest
+        loads = [ref if i is None else ref.at[i] for ref, (_, i) in zip(loads, loaded, strict=True)]
+        pairs = list(zip((*ints, *loads, *nexts), (*fetched, *next_outs), strict=True))
+        staged = list(rest[len(rest) - len(moves) :])
+        rest = rest[: len(rest) - len(moves)]
+        for source, stage, (_, _, _, index) in zip(sources, staged, moves, strict=True):
+            pairs.append((source if index is None else source.at[index], stage))
+        ends = [
+            (stage, targets[n].at[first if size is None else pl.ds(first, size)])
+            for stage, (n, first, size, _) in zip(staged, moves, strict=True)
+        ]
+        copies = [
+            pltpu.make_async_copy(*pair, sems.at[n]) for n, pair in enumerate((*pairs, *ends))
+        ]
+        leaving = copies[len(pairs) :]
+        for copy in copies[: len(pairs)]:
+            copy.start()
+        for copy in (*copies[:early], *copies[len(pairs) - len(moves) : len(pairs)]):
+            copy.wait()
+        for copy in leaving:
+            copy.start()
+        place = (lax.axis_index("leaf"), lax.axis_index("col"))
+        body(place, *fetched, *ins, *outs, *rest)
+        for copy in (*copies[early : len(pairs) - len(moves)], *leaving):
+            copy.wait()
+
+    fetched = [pltpu.SMEM(value.shape, value.dtype) for value in scalars]
+    fetched += [pltpu.VMEM(value.shape[i is not None :], value.dtype) for value, i in loaded]
+    stages = [
+        pltpu.VMEM(piece.shape[index is not None :], piece.dtype)
+        for piece, (_, _, _, index) in zip(pieces, moves, strict=True)
+    ]
+    sems = [pltpu.SemaphoreType.DMA((waits,))] if waits else []
     return pl.pallas_call(
         run,
-        out_shape=[jax.ShapeDtypeStruct(shape, kind) for shape, kind in out_shapes],
-        in_specs=[smem] * len(scalars)
-        + [spec] * len(operands)
-        + [pl.BlockSpec(memory_space=pl.ANY)] * len(held),
-        out_specs=[spec] * len(out_shapes),
-        scratch_shapes=list(scratch),
-        compiler_params=pltpu.CompilerParams(vmem_limit_bytes=40 * 1024 * 1024),
-    )(*scalars, *operands, *held)
+        out_shape=out_shapes,
+        in_specs=[far] * sum(inputs[:-2])
+        + [pl.BlockSpec(memory_space=pl.ANY)] * len(held)
+        + [vmem] * len(operands),
+        out_specs=[vmem] * (plain + len(ahead)) + [far] * len(stacks),
+        scratch_shapes=fetched + list(scratch) + stages + sems,
+        compiler_params=pltpu.CompilerParams(vmem_limit_bytes=room * 1024 * 1024),
+    )(*scalars, *[value for value, _ in loaded], *ahead, *pieces, *held, *operands)
 
 
 def halves(values):
@@ -182,40 +236,44 @@
     return pl.ds(pl.multiple_of(index * size, size), size)
 
 
+def gate(values, after):
+    far = pl.BlockSpec(memory_space=pltpu.HBM)
+
+    def run(*refs):
+        pass
+
+    return pl.pallas_call(
+        run,
+        out_shape=[jax.ShapeDtypeStruct(value.shape, value.dtype) for value in values],
+        in_specs=[far] * len(values) + [pl.BlockSpec(memory_space=pltpu.VMEM)] * len(after),
+        out_specs=[far] * len(values),
+        input_output_aliases={n: n for n in range(len(values))},
+        compiler_params=pltpu.CompilerParams(vmem_limit_bytes=1024 * 1024),
+    )(*values, *after)
+
+
+def join_kernel(place, kept, received, joined):
+    half = kept.shape[1] // 2
+    joined[:, :half] = kept[:, :half]
+    joined[:, half:] = received[:, :half]
+
+
 def assemble_kernel(place, *refs):
-    pieces, (high, low) = refs[:-2], refs[-2:]
-    leaf = place[0]
-    offset = 0
-    for (distance, start), piece in zip(PIECES, pieces, strict=True):
-        rows = piece.shape[0]
-        block_rows = pieces[0].shape[0]
-        first = (leaf ^ distance) * block_rows + start * rows
-        where = pl.ds(pl.multiple_of(first, rows), rows)
-        part_high, part_low = halves(piece[...])
-        high[where, :] = part_high
-        low[where, :] = part_low
-
-
-PIECES = tuple(
-    (plane | core, start) for core in (0, 1) for plane, start in ((0, 0), (2, 0), (4, 0), (6, 0), (6, 1))
-)
-
-
-def spread_matrix(place, block):
-    half = block.shape[0] // 2
-    near = flip(block, "leaf", 2)
-    far = flip(block, "leaf", 4)
-    pieces = [block, near, far, flip(near[:half], "leaf", 4), flip(far[half:], "leaf", 2)]
-    pieces += [flip(piece, "leaf", 1) for piece in pieces]
-    shape = (block.shape[0] * lax.axis_size("leaf"), block.shape[1])
-    return kernel_call(assemble_kernel, [(shape, jnp.bfloat16)] * 2, [place], pieces)
-
-
-def split_kernel(whole, high, low):
-    high[...], low[...] = halves(whole[...])
-
-
-def pair_kernel(own, other, high, low):
+    *blocks, high, low = refs
+    rows = blocks[0].shape[0]
+    for n, block in enumerate(blocks):
+        core, chip = divmod(n, len(blocks) // 2)
+        where = span(place[0] ^ core ^ 2 * chip, rows)
+        high[where, :], low[where, :] = halves(block[...])
+
+
+def assemble(parts):
+    rows, width = parts[0][0].shape[-2:]
+    panel = ((rows * lax.axis_size("leaf"), width), jnp.bfloat16)
+    return kernel_call(assemble_kernel, [panel, panel], [], [], loaded=parts)
+
+
+def pair_kernel(place, own, other, high, low):
     rows = own.shape[0]
     high[:rows, :], low[:rows, :] = halves(own[...])
     high[rows:, :], low[rows:, :] = halves(other[...])
@@ -286,60 +344,91 @@
 
 
 def back_kernel(place, *refs):
-    count = (len(refs) - 3) // 2
-    parts, (high, low), last, sent = (
+    count = (len(refs) - 2) // 2
+    parts, (high, low), sent = refs[:count], refs[count : count + 2], refs[count + 2 :]
+    total = sum(part[...] for part in parts[1:]) + parts[0][...]
+    rows, width = total.shape
+    for e, part in enumerate(sent):
+        where = span(place[1] ^ e, width)
+        value = product(total, high[where, :], low[where, :], 1)
+        part[:rows, :] = regroup(value, e, count)
+        part[rows:, :] = total[e * GROUP : (e + 1) * GROUP]
+
+
+def spread_kernel(place, *refs):
+    count = (len(refs) - 2) // 2
+    parts, first, sent, rest = refs[:count], refs[count], refs[count + 1 : -1], refs[-1]
+    rows = parts[0].shape[0] - GROUP
+    total = sum(part[:rows, :] for part in parts[1:]) + parts[0][:rows, :]
+    for e, part in enumerate(parts):
+        rest[e] = part[rows:, :]
+    for f, part in enumerate(sent):
+        part[:rows, :] = first[:rows, :] - total
+        part[rows:, :] = rest[(place[0] >> 1) ^ place[1] ^ f]
+
+
+def last_kernel(place, *refs):
+    count = (len(refs) - 4) // 2
+    parts, (high, low), last, sent, joined = (
         refs[:count],
         refs[count : count + 2],
-        refs[count + 2],
-        refs[count + 3 :],
-    )
+        refs[-2],
+        refs[count + 2 : -2],
+        refs[-1],
+    )
+    rows = parts[0].shape[0] - GROUP
+    chip = place[0] >> 1
+    for f, part in enumerate(parts):
+        for e in range(count):
+            joined[e, span(chip ^ f, GROUP), :] = part[e * GROUP : (e + 1) * GROUP, :]
+        last[span(chip ^ f, GROUP), :] = part[rows:, :]
+    values = jnp.concatenate([joined[e] for e in range(count)], 0)
+    values = product(values, high[...], low[...], 1)
+    for e, part in enumerate(sent):
+        part[...] = values[e * rows : (e + 1) * rows]
+
+
+def part_kernel(place, *refs):
+    parts, (last, kept, sent) = refs[:-3], refs[-3:]
     total = sum(part[...] for part in parts[1:]) + parts[0][...]
-    last[...] = total
-    scatter_product(place, total, high, low, sent)
-
-
-def final_kernel(place, *refs):
-    count = (len(refs) - 4) // 2
-    parts = refs[:count]
-    high, low, first, last = refs[count : count + 4]
-    sent = refs[count + 4 :]
-    total = first[: last.shape[0], :] - (sum(part[...] for part in parts[1:]) + parts[0][...])
-    solved = product(total, high[...], low[...], 1)
-    size = total.shape[0] // count
-    for e, part in enumerate(sent):
-        part[...] = jnp.concatenate(
-            [solved[e * size : (e + 1) * size], last[e * size : (e + 1) * size, :]], 1
-        )
-
-
-def collect_kernel(place, *refs):
-    parts, result = refs[:-1], refs[-1]
-    leaf_count, _, rows, width = result.shape
-    total = leaf_count * width
-    fronts = (parts[0].shape[1] - total) // width
-    for leaf in range(leaf_count):
-        where = slice(leaf * width, (leaf + 1) * width)
-        result[leaf, 0] = sum(part[:, where] for part in parts[1:]) + parts[0][:, where]
-    for e, part in enumerate(parts):
-        for j in range(fronts):
-            start = total + j * width
-            result[(place[1] ^ e) * fronts + j, 1] = part[:, start : start + width]
+    half = total.shape[1] // 2
+    lower = (place[0] & 1) == 0
+    for n, panel in enumerate((total, last[...])):
+        own, other = panel[:, :half], panel[:, half:]
+        if n:
+            own, other = jnp.where(lower, own, other), jnp.where(lower, other, own)
+        kept[:, n * half : (n + 1) * half] = own
+        sent[:, n * half : (n + 1) * half] = other
+
+
+def merge_kernel(place, kept, received, result):
+    panels, half = result.shape[1:]
+    lower = (place[0] & 1) == 0
+    for chip in range(kept.shape[0] // GROUP):
+        rows = slice(chip * GROUP, (chip + 1) * GROUP)
+        for n in range(panels):
+            columns = slice(n * half, (n + 1) * half)
+            own, other = kept[rows, columns], received[rows, columns]
+            start = 2 * chip * GROUP
+            result[start : start + GROUP, n, :] = jnp.where(lower, own, other)
+            result[start + GROUP : start + 2 * GROUP, n, :] = jnp.where(lower, other, own)
 
 
 def reduce_blocks(level, live, links, blocks, inverse, coupling, solved):
     red_blocks, link_total, size = inverse.shape[0], coupling.shape[1], inverse.shape[1]
     lanes = lax.broadcasted_iota(jnp.int32, (1, size), 1)
+    pushed = []
     for i in range(red_blocks):
-        mask = (lanes + i * size < live[level, 0]).astype(jnp.float32)
-        high, low = halves(inverse[i])
-        value = product(blocks[i] * mask, high, low, 0) * mask
+        mask = (lanes + i * size < live[0, level]).astype(jnp.float32)
+        value = product(blocks[i] * mask, *halves(inverse[i]), 0) * mask
         solved[:, i * size : (i + 1) * size] = value
         pairs = [halves(coupling[i, k]) for k in range(link_total)]
         high, low = (jnp.concatenate(part, 1) for part in zip(*pairs, strict=True))
-        pushed = product(value, high, low, 0)
+        pushed.append(product(value, high, low, 0))
+    for i in range(red_blocks):
         for k in range(link_total):
             target = red_blocks + links[i, k]
-            blocks[target] = blocks[target] - pushed[:, k * size : (k + 1) * size]
+            blocks[target] = blocks[target] - pushed[i][:, k * size : (k + 1) * size]
 
 
 def send_halves(place, level, blocks, red_blocks, kept, sent):
@@ -390,109 +479,142 @@
             sent[rows, columns] = blocks[block, span(2 * chip + 1 - core, GROUP), :]
 
 
-def eliminate_all(place, right_sides, level_data, front_rows):
+def swap_chips(parts):
+    return [parts[0]] + [flip(parts[f], "leaf", 2 * f) for f in range(1, len(parts))]
+
+
+def solve_tree(right_sides, level_data, front_rows, root_inverse, root_coupling):
+    leaf_count, col_count = lax.axis_size("leaf"), lax.axis_size("col")
+    chip_count = leaf_count // 2
+    panel_count, panel_rows, own_columns = root_inverse.shape
+    group = GROUP * col_count
     rhs_rows = right_sides.shape[0]
+    front_rows = front_rows.reshape(1, -1)
     red_blocks, size = level_data[0][0].shape[:2]
-    one = ((rhs_rows, red_blocks * size), jnp.float32)
-
-    def many(count):
-        return (count, rhs_rows, size)
+    solved = ((rhs_rows, red_blocks * size), jnp.float32)
+    pair = ((2 * panel_rows, own_columns), jnp.bfloat16)
+    one = ((group, own_columns), jnp.float32)
+    more = ((group + GROUP, own_columns), jnp.float32)
+    both = ((group, panel_count * panel_rows), jnp.float32)
+
+    def halved(count):
+        return (((count - red_blocks) // 2, rhs_rows, size), jnp.float32)
+
+    def scratch(*shape):
+        return pltpu.VMEM(shape, jnp.float32)
 
     inverse, coupling, links, order = level_data[0]
     count = right_sides.shape[1] // size
-    half = ((count - red_blocks) // 2, rhs_rows, size)
-    solved_first, kept, sent = kernel_call(
+    solved_first, kept, sent, second = kernel_call(
         lowest_kernel,
-        [one, (half, jnp.float32), (half, jnp.float32)],
-        [place, front_rows, links],
-        [right_sides, inverse, coupling],
-        scratch=[pltpu.VMEM(many(count), jnp.float32)],
+        [solved, halved(count), halved(count)],
+        [front_rows, links],
+        [],
+        loaded=[right_sides, inverse, coupling],
+        stacks=[[(root_inverse, 1)]],
+        scratch=[scratch(count, rhs_rows, size)],
+        room=64,
     )
     received = flip(sent, "leaf", 1)
+    far = flip(root_coupling, "leaf", 4)
+    second_far = flip(second, "leaf", 4)
+    near = flip(root_coupling, "leaf", 2)
+    partner_inverse = flip(root_inverse, "leaf", 1)
+    partner_coupling = flip(root_coupling, "leaf", 1)
     inverse, coupling, links, next_order = level_data[1]
     count -= red_blocks
-    half = ((count - red_blocks) // 2, rhs_rows, size)
     solved_second, kept, sent = kernel_call(
         middle_kernel,
-        [one, (half, jnp.float32), (half, jnp.float32)],
-        [place, front_rows, links, order],
+        [solved, halved(count), halved(count)],
+        [front_rows, links, order],
         [kept, received, inverse, coupling],
-        scratch=[pltpu.VMEM(many(count), jnp.float32)] * 2,
+        held=[partner_inverse, partner_coupling],
+        scratch=[scratch(count, rhs_rows, size)] * 2,
+        room=64,
     )
     received = flip(sent, "leaf", 2)
     inverse, coupling, links, last_order = level_data[2]
     count -= red_blocks
-    half = (rhs_rows // 2, (count - red_blocks) * size)
-    solved_third, kept, sent = kernel_call(
+    solved_third, kept, sent, near, second = kernel_call(
         highest_kernel,
-        [one, (half, jnp.float32), (half, jnp.float32)],
-        [place, front_rows, links, next_order, last_order],
+        [solved, both, both],
+        [front_rows, links, next_order, last_order],
         [kept, received, inverse, coupling],
-        scratch=[pltpu.VMEM(many(count), jnp.float32)] * 2,
-    )
-    return (solved_first, solved_second, solved_third), kept, flip(sent, "leaf", 1)
-
-
-def root_replicated(place, kept, received, root_inverse, root_coupling):
-    leaf_count, col_count = lax.axis_size("leaf"), lax.axis_size("col")
-    panel_count, panel_rows, own_columns = root_inverse.shape
-    group = GROUP * col_count
-    total = panel_rows * leaf_count
-    rhs_rows = GROUP * leaf_count
-    pair = [((2 * panel_rows, own_columns), jnp.bfloat16)] * 2
-    panel = [((total, own_columns), jnp.bfloat16)] * 2
-    one = ((group, own_columns), jnp.float32)
-    more = ((group + GROUP, own_columns), jnp.float32)
-    wide = [((GROUP, total + own_columns), jnp.float32)] * col_count
-    near_high, near_low = kernel_call(
-        pair_kernel, pair, [], [root_inverse[0], flip(root_inverse[0], "leaf", 1)]
-    )
-    between = lax.all_gather(root_coupling, "leaf", axis=0, tiled=True)
-    between_high, between_low = kernel_call(split_kernel, panel, [], [between])
-    second_high, second_low = spread_matrix(place, root_inverse[1])
-    first = lax.all_gather(root_inverse[0], "leaf", axis=0, tiled=True)
-    first_high, first_low = kernel_call(split_kernel, panel, [], [first])
-    joined = jnp.concatenate([kept[:, :panel_rows], received[:, :panel_rows]], 1)
+        stacks=[[near], [(root_inverse, 1)]],
+        held=[far],
+        scratch=[scratch(count, rhs_rows, size)] * 2,
+        room=64,
+    )
+    received = flip(sent, "leaf", 1)
+    corner = flip(near, "leaf", 4)
+    second_near = flip(second, "leaf", 2)
+    partner_near = flip(near, "leaf", 1)
+    (joined,) = kernel_call(join_kernel, [both], [], [kept, received], held=[partner_near, second_far])
+
+    near_high, near_low = kernel_call(pair_kernel, [pair, pair], [], [], loaded=[(root_inverse, 0), (partner_inverse, 0)])
     parts = swap_columns([joined] * col_count)
     parts = kernel_call(
         first_kernel,
-        [more] * (leaf_count // 2),
-        [place],
+        [more] * chip_count,
+        [],
         [*parts, near_high, near_low, kept, received],
-        scratch=[pltpu.VMEM((col_count, group, own_columns), jnp.float32)],
-    )
-    parts = [parts[0]] + [flip(parts[f], "leaf", 2 * f) for f in range(1, leaf_count // 2)]
+        held=[corner, second_near],
+        scratch=[scratch(col_count, group, own_columns)],
+    )
+    corner, far = gate([corner, far], [parts[-1]])
+    partner_corner = flip(corner, "leaf", 1)
+    partner_far = flip(far, "leaf", 1)
     parts = kernel_call(
         share_kernel,
         [more] * col_count,
-        [place],
-        parts,
-        scratch=[pltpu.VMEM((leaf_count // 2, GROUP, own_columns), jnp.float32)],
+        [],
+        swap_chips(parts),
+        held=[partner_far, partner_corner],
+        scratch=[scratch(chip_count, GROUP, own_columns)],
+    )
+    (second_far,) = gate([second_far], [parts[-1]])
+    second_corner = flip(second_far, "leaf", 2)
+    partner_second = flip(second_far, "leaf", 1)
+    between = assemble(
+        [(root_coupling, None), (near, 0), (far, None), (corner, 0)]
+        + [(partner_coupling, None), (partner_near, 0), (partner_far, None), (partner_corner, 0)]
     )
     first_sum = parts[0]
     parts = swap_columns(parts)
-    (left,) = kernel_call(coupled_kernel, [one], [place], [*parts, between_high, between_low])
+    (left,) = kernel_call(coupled_kernel, [one], [], [*parts, *between])
+    second_near, second_corner = gate([second_near, second_corner], [left])
+    panel = assemble(
+        [(root_inverse, 1), (second_near, 0), (second_far, 0), (second_corner, 0)]
+        + [(partner_inverse, 1), (flip(second_near, "leaf", 1), 0)]
+        + [(partner_second, 0), (flip(second_corner, "leaf", 1), 0)]
+    )
     parts = swap_columns([left] * col_count)
-    parts = kernel_call(
-        turn_kernel, [one] * col_count, [place], [*parts, second_high, second_low]
-    )
+    parts = kernel_call(turn_kernel, [one] * col_count, [], [*parts, *panel])
     parts = swap_columns(parts)
-    last, *parts = kernel_call(
-        back_kernel, [one] * (col_count + 1), [place], [*parts, between_high, between_low]
-    )
+    parts = kernel_call(back_kernel, [more] * col_count, [], [*parts, *between])
     parts = swap_columns(parts)
     parts = kernel_call(
-        final_kernel, wide, [place], [*parts, first_high, first_low, first_sum, last]
-    )
-    parts = swap_columns(parts)
-    (split,) = kernel_call(
-        collect_kernel,
-        [((leaf_count, panel_count, GROUP, panel_rows), jnp.float32)],
-        [place],
-        parts,
-    )
-    whole = lax.all_to_all(split, "leaf", 0, 0, tiled=True)
-    return whole.transpose(0, 2, 1, 3).reshape(rhs_rows, panel_count, panel_rows)
+        spread_kernel,
+        [more] * chip_count,
+        [],
+        [*parts, first_sum],
+        scratch=[scratch(col_count, GROUP, own_columns)],
+    )
+    *parts, last = kernel_call(
+        last_kernel,
+        [one] * (col_count + 1),
+        [],
+        [*swap_chips(parts), near_high, near_low],
+        scratch=[scratch(col_count, group, own_columns)],
+    )
+    kept, sent = kernel_call(part_kernel, [both, both], [], [*swap_columns(parts), last])
+    (result,) = kernel_call(
+        merge_kernel,
+        [((rhs_rows, panel_count, panel_rows), jnp.float32)],
+        [],
+        [kept, flip(sent, "leaf", 1)],
+    )
+    return (solved_first, solved_second, solved_third, result)
 
 
 def replicates(rhs_rows, root_inverse):
@@ -530,9 +652,7 @@
         (inverse_third, coupling_third, links_third, order_third),
     )
     if replicates(right_sides.shape[0], root_inverse):
-        place = jnp.stack([lax.axis_index("leaf"), lax.axis_index("col")]).astype(jnp.int32)
-        solved, *sections = eliminate_all(place, right_sides, level_data, front_rows)
-        return (*solved, root_replicated(place, *sections, root_inverse, root_coupling))
+        return solve_tree(right_sides, level_data, front_rows, root_inverse, root_coupling)
     section = right_sides
     outputs = []
     for level_index in range(3):

time: 143 us -> 112 us (0.78)
  between operations: 14.3 us -> 0.87 us
  local copies, waits for them, and re-layouts: 12.7 us -> 2.08 us
  blocking collectives: 9.81 us -> 0 us
  starting transfers between devices: 38.6 us -> 43.2 us
  waiting for transfers between devices: 45.6 us -> 42.9 us
    all_to_all x1 -> x0, blocking collectives: 9.81 us -> none  [root_replicated(): whole = lax.all_to_all(split, 'leaf', 0, 0, tiled=True)]
    unnamed x46 -> x12, local copies, waits for them, and re-layouts: 10.4 us -> 2.08 us
    ppermute x34 -> x42, starting transfers between devices: 38.5 us -> 43.2 us  [flip(): return lax.ppermute(block, axis, [(i, i ^ distance) for i in range(count)])]
    slice x5 -> x0, local copies, waits for them, and re-layouts: 2.3 us -> none  [the longest x1 2.26 us: root_replicated(): root_inverse[0]]
    ppermute x34 -> x42, waiting for transfers between devices: 44.9 us -> 42.9 us  [flip(): return lax.ppermute(block, axis, [(i, i ^ distance) for i in range(count)])]
    pallas_call x14 -> x19, Pallas kernels: 21.5 us -> 22.9 us  [the longest x16 22.9 us: kernel_call(): pl.pallas_call(run, out_shape=out_shapes, in_specs=[far] * sum(inputs[:-2...]
  transfers between devices with their start and end apart: 36 -> 42, of which waited for: 19 -> 25; matrix products, arithmetic and copies ran while one was open for 2% -> 0% of each run, Pallas kernels for 13% -> 16%
where the time goes in v4:
time: 112 us
  starting transfers between devices  43.2 us (39%)
  waiting for transfers between devices  42.9 us (38%)
  Pallas kernels  22.9 us (20%)
  local copies, waits for them, and re-layouts  2.08 us (2%)
    ppermute x42, starting transfers between devices, flip(): return lax.ppermute(block, axis, [(i, i ^ distance) for i in range(count)])  43.2 us
    ppermute x42, waiting for transfers between devices, flip(): return lax.ppermute(block, axis, [(i, i ^ distance) for i in range(count)])  42.9 us
    pallas_call x16, Pallas kernels, kernel_call(): pl.pallas_call(run, out_shape=out_shapes, in_specs=[far] * sum(inputs[:-2...  22.9 us
  transfers between devices with their start and end apart: 42, of which 25 were waited for; matrix products, arithmetic and copies ran while one was open for 0% of the time, Pallas kernels for 16%

profile of v4, /device:TPU:0, one launch (start us, length us, event | category | flops | bytes accessed | tf_op | source)
XLA Modules:
  0.0 111.8 jit_solution(4095599061551392449)
XLA Ops:
  0.6 0.5 collective-permute-start
  1.2 2.9 %collective-permute-start.4 = (f32[256,512]{1,0:T(8,128)}, f32[256,512]{1,0:T(8,128)}, u32[]{:S(2)}, u32[]{:S(2)}) collective-permute-start(f32[256,512]{1,0:T(8,128)} %refs_0_.4), channel_id=1, source_target_pairs={{0,16},{4,20},{8,24},{12,28},{16,0},{20,4},{24,8},{28,12},{1,17},{... | collective-permute-start | bytes 1572872 | tf_op jit(solution)/shard_map/ppermute | solution.py:127
  4.2 1.5 %collective-permute-start.3 = (f32[256,512]{1,0:T(8,128)}, f32[256,512]{1,0:T(8,128)}, u32[]{:S(2)}, u32[]{:S(2)}) collective-permute-start(f32[256,512]{1,0:T(8,128)} %refs_0_.4), channel_id=1, source_target_pairs={{0,8},{4,12},{8,0},{12,4},{16,24},{20,28},{24,16},{28,20},{1,9},{5... | collective-permute-start | bytes 1572872 | tf_op jit(solution)/shard_map/ppermute | solution.py:127
  5.7 3.3 %shard_map.183 = (f32[64,512]{1,0:T(8,128)}, f32[6,64,128]{2,1,0:T(8,128)}, f32[6,64,128]{2,1,0:T(8,128)}, f32[1,256,512]{2,1,0:T(8,128)}) custom-call(s32[1,3]{1,0:T(1,128)} %bitcast.1, s32[4,3]{1,0:T(4,128)} %refs_1_.3, f32[64,2048]{1,0:T(8,128)} %refs_2_.3, f32[4,128,128]{2,1,0:T(8,128)} %refs_3_.2, f32[4,3,128,128]{3,2,1,0:T(8,128)} %refs_4_.1, ...), custom_call_target="tpu_custom_call" | custom-call | tf_op jit(solution)/shard_map/pallas_call | solution.py:198
  9.1 1.8 %collective-permute-done.2.refs_6_ = f32[6,64,128]{2,1,0:T(8,128)} collective-permute-done((f32[6,64,128]{2,1,0:T(8,128)}, f32[6,64,128]{2,1,0:T(8,128)}, u32[]{:S(2)}, u32[]{:S(2)}) %collective-permute-start.2) | collective-permute-done | bytes 196640 | tf_op jit(solution)/shard_map/ppermute | solution.py:127
  10.9 3.8 %shard_map.184 = (f32[64,512]{1,0:T(8,128)}, f32[4,64,128]{2,1,0:T(8,128)}, f32[4,64,128]{2,1,0:T(8,128)}) custom-call(s32[1,3]{1,0:T(1,128)} %bitcast.2, s32[4,3]{1,0:T(4,128)} %refs_1_.4, s32[1,12]{1,0:T(1,128)} %refs_2_.4, f32[2,256,512]{2,1,0:T(8,128)} %collective-permute-done.refs_3_.refs_1_.refs_4_, f32[256,512]{1,0:T(8,128)} %collective-permute-done.1.refs_4_, ...), custom_call_target="tpu_custom_call" | custom-call | tf_op jit(solution)/shard_map/pallas_call | solution.py:198
  14.7 0.6 collective-permute-start.5
  15.4 1.3 %collective-permute-done.4.refs_6_.refs_1_ = f32[256,512]{1,0:T(8,128)} collective-permute-done((f32[256,512]{1,0:T(8,128)}, f32[256,512]{1,0:T(8,128)}, u32[]{:S(2)}, u32[]{:S(2)}) %collective-permute-start.4) | collective-permute-done | bytes 524320 | tf_op jit(solution)/shard_map/ppermute | solution.py:127
  16.7 1.7 %collective-permute-done.3.refs_4_ = f32[256,512]{1,0:T(8,128)} collective-permute-done((f32[256,512]{1,0:T(8,128)}, f32[256,512]{1,0:T(8,128)}, u32[]{:S(2)}, u32[]{:S(2)}) %collective-permute-start.3) | collective-permute-done | bytes 524320 | tf_op jit(solution)/shard_map/ppermute | solution.py:127
  18.4 2.6 %collective-permute-done.5.refs_8_ = f32[4,64,128]{2,1,0:T(8,128)} collective-permute-done((f32[4,64,128]{2,1,0:T(8,128)}, f32[4,64,128]{2,1,0:T(8,128)}, u32[]{:S(2)}, u32[]{:S(2)}) %collective-permute-start.5) | collective-permute-done | bytes 131104 | tf_op jit(solution)/shard_map/ppermute | solution.py:127
  20.9 4.3 %shard_map.185 = (f32[64,512]{1,0:T(8,128)}, f32[32,512]{1,0:T(8,128)}, f32[32,512]{1,0:T(8,128)}, f32[1,256,512]{2,1,0:T(8,128)}, f32[1,256,512]{2,1,0:T(8,128)}) custom-call(s32[1,3]{1,0:T(1,128)} %bitcast.3, s32[4,3]{1,0:T(4,128)} %refs_1_.5, s32[1,8]{1,0:T(1,128)} %refs_2_.5, s32[1,4]{1,0:T(1,128)} %refs_3_.3, ...), custom_call_target="tpu_custom_call" | custom-call | tf_op jit(solution)/shard_map/pallas_call | solution.py:198
  25.7 1.7 %collective-permute-start.7 = (f32[1,256,512]{2,1,0:T(8,128)}, f32[1,256,512]{2,1,0:T(8,128)S(1)}, u32[]{:S(2)}, u32[]{:S(2)}) collective-permute-start(f32[1,256,512]{2,1,0:T(8,128)} %get-tuple-element.61), channel_id=1, source_target_pairs={{0,8},{4,12},{8,0},{12,4},{16,24},{20,28},{24,16},{28,20},{1,9},{5... | collective-permute-start | bytes 1572872 | tf_op jit(solution)/shard_map/ppermute | solution.py:127
  27.4 2.4 %collective-permute-done.9.refs_1_.refs_0_ = f32[1,256,512]{2,1,0:T(8,128)} collective-permute-done((f32[1,256,512]{2,1,0:T(8,128)}, f32[1,256,512]{2,1,0:T(8,128)}, u32[]{:S(2)}, u32[]{:S(2)}) %collective-permute-start.9) | collective-permute-done | bytes 524320 | tf_op jit(solution)/shard_map/ppermute | solution.py:127
  29.8 0.8 copy-done.4
  30.7 1.6 %collective-permute-start.11 = (f32[32,512]{1,0:T(8,128)S(1)}, f32[32,512]{1,0:T(8,128)S(1)}, u32[]{:S(2)}, u32[]{:S(2)}) collective-permute-start(f32[32,512]{1,0:T(8,128)S(1)} %shard_map.186.refs_2_), channel_id=1, source_target_pairs={{0,1},{1,0},{2,3},{3,2},{4,5},{5,4},{6,7},{7,6},{8,9},{9,8},{10,11... | collective-permute-start | bytes 196616 | tf_op jit(solution)/shard_map/ppermute | solution.py:127
  32.3 2.6 %collective-permute-start.12 = (f32[32,512]{1,0:T(8,128)S(1)}, f32[32,512]{1,0:T(8,128)S(1)}, u32[]{:S(2)}, u32[]{:S(2)}) collective-permute-start(f32[32,512]{1,0:T(8,128)S(1)} %shard_map.186.refs_2_), channel_id=1, source_target_pairs={{0,2},{1,3},{2,0},{3,1},{4,6},{5,7},{6,4},{7,5},{8,10},{9,11},{10,... | collective-permute-start | bytes 196616 | tf_op jit(solution)/shard_map/ppermute | solution.py:127
  35.1 1.2 %copy-done = f32[2,256,512]{2,1,0:T(8,128)S(1)} copy-done((f32[2,256,512]{2,1,0:T(8,128)S(1)}, f32[2,256,512]{2,1,0:T(8,128)}, u32[]{:S(2)}) %copy-start) | copy-done | bytes 1048600
  36.3 1.3 %shard_map.187 = (bf16[512,512]{1,0:T(8,128)(2,1)S(1)}, bf16[512,512]{1,0:T(8,128)(2,1)S(1)}) custom-call(f32[2,256,512]{2,1,0:T(8,128)S(1)} %copy-done, f32[2,256,512]{2,1,0:T(8,128)} %collective-permute-done.refs_3_.refs_1_.refs_4_), custom_call_target="tpu_custom_call" | custom-call | tf_op jit(solution)/shard_map/pallas_call | solution.py:198
  37.6 2.8 %collective-permute-done.6.refs_0_ = f32[1,256,512]{2,1,0:T(8,128)S(1)} collective-permute-done((f32[1,256,512]{2,1,0:T(8,128)}, f32[1,256,512]{2,1,0:T(8,128)S(1)}, u32[]{:S(2)}, u32[]{:S(2)}) %collective-permute-start.6) | collective-permute-done | bytes 524320 | tf_op jit(solution)/shard_map/ppermute | solution.py:127
  40.5 0.5 collective-permute-done.13.refs_5_
  41.5 0.5 collective-permute-start.15
  42.0 1.5 %collective-permute-start.16 = (f32[40,512]{1,0:T(8,128)S(1)}, f32[40,512]{1,0:T(8,128)S(1)}, u32[]{:S(2)}, u32[]{:S(2)}) collective-permute-start(f32[40,512]{1,0:T(8,128)S(1)} %get-tuple-element.71), channel_id=1, source_target_pairs={{0,8},{4,12},{8,0},{12,4},{16,24},{20,28},{24,16},{28,20},{1,9},{5... | collective-permute-start | bytes 245768 | tf_op jit(solution)/shard_map/ppermute | solution.py:127
  43.5 0.7 collective-permute-start.17
  44.2 1.3 %collective-permute-start.18 = (f32[40,512]{1,0:T(8,128)S(1)}, f32[40,512]{1,0:T(8,128)S(1)}, u32[]{:S(2)}, u32[]{:S(2)}) collective-permute-start(f32[40,512]{1,0:T(8,128)S(1)} %get-tuple-element.67.refs_2_), channel_id=1, source_target_pairs={{0,24},{4,28},{8,16},{12,20},{16,8},{20,12},{24,0},{28,4},{1,25},{... | collective-permute-start | bytes 245768 | tf_op jit(solution)/shard_map/ppermute | solution.py:127
  45.5 1.0 collective-permute-done.16.refs_3_
  46.4 3.2 %collective-permute-done.17.refs_4_ = f32[40,512]{1,0:T(8,128)S(1)} collective-permute-done((f32[40,512]{1,0:T(8,128)S(1)}, f32[40,512]{1,0:T(8,128)S(1)}, u32[]{:S(2)}, u32[]{:S(2)}) %collective-permute-start.17) | collective-permute-done | bytes 81952 | tf_op jit(solution)/shard_map/ppermute | solution.py:127
  49.7 0.6 collective-permute-start.25
  50.3 1.4 %collective-permute-start.19 = (f32[40,512]{1,0:T(8,128)S(1)}, f32[40,512]{1,0:T(8,128)S(1)}, u32[]{:S(2)}, u32[]{:S(2)}) collective-permute-start(f32[40,512]{1,0:T(8,128)S(1)} %get-tuple-element.74), channel_id=1, source_target_pairs={{0,1},{1,0},{2,3},{3,2},{4,5},{5,4},{6,7},{7,6},{8,9},{9,8},{10,11... | collective-permute-start | bytes 245768 | tf_op jit(solution)/shard_map/ppermute | solution.py:127
  51.7 2.6 %collective-permute-start.20 = (f32[40,512]{1,0:T(8,128)S(1)}, f32[40,512]{1,0:T(8,128)S(1)}, u32[]{:S(2)}, u32[]{:S(2)}) collective-permute-start(f32[40,512]{1,0:T(8,128)S(1)} %get-tuple-element.75), channel_id=1, source_target_pairs={{0,2},{1,3},{2,0},{3,1},{4,6},{5,7},{6,4},{7,5},{8,10},{9,11},{10,... | collective-permute-start | bytes 245768 | tf_op jit(solution)/shard_map/ppermute | solution.py:127
  54.7 2.1 %shard_map.191 = (bf16[2048,512]{1,0:T(8,128)(2,1)S(1)}, bf16[2048,512]{1,0:T(8,128)(2,1)S(1)}) custom-call(f32[256,512]{1,0:T(8,128)S(1)} %copy-done.2, f32[1,256,512]{2,1,0:T(8,128)S(1)} %copy-done.3, f32[256,512]{1,0:T(8,128)} %get-tuple-element.68.refs_2_, f32[1,256,512]{2,1,0:T(8,128)S(1)} %get-tuple-element.69.refs_3_, ...), custom_call_target="tpu_custom_call" | custom-call | tf_op jit(solution)/shard_map/pallas_call | solution.py:198
  56.9 2.0 %collective-permute-done.20.refs_2_ = f32[40,512]{1,0:T(8,128)S(1)} collective-permute-done((f32[40,512]{1,0:T(8,128)S(1)}, f32[40,512]{1,0:T(8,128)S(1)}, u32[]{:S(2)}, u32[]{:S(2)}) %collective-permute-start.20) | collective-permute-done | bytes 81952 | tf_op jit(solution)/shard_map/ppermute | solution.py:127
  58.8 1.8 %collective-permute-done.21.refs_3_ = f32[40,512]{1,0:T(8,128)S(1)} collective-permute-done((f32[40,512]{1,0:T(8,128)S(1)}, f32[40,512]{1,0:T(8,128)S(1)}, u32[]{:S(2)}, u32[]{:S(2)}) %collective-permute-start.21) | collective-permute-done | bytes 81952 | tf_op jit(solution)/shard_map/ppermute | solution.py:127
  60.6 0.8 shard_map.192.refs_2_.refs_0_
  61.4 0.7 collective-permute-done.25.refs_1_
  62.1 0.5 collective-permute-start.28
  62.7 1.6 %collective-permute-start.22 = (f32[32,512]{1,0:T(8,128)S(1)}, f32[32,512]{1,0:T(8,128)S(1)}, u32[]{:S(2)}, u32[]{:S(2)}) collective-permute-start(f32[32,512]{1,0:T(8,128)S(1)} %shard_map.192.refs_2_.refs_0_), channel_id=1, source_target_pairs={{0,1},{1,0},{2,3},{3,2},{4,5},{5,4},{6,7},{7,6},{8,9},{9,8},{10,11... | collective-permute-start | bytes 196616 | tf_op jit(solution)/shard_map/ppermute | solution.py:127
  64.2 2.6 %collective-permute-start.23 = (f32[32,512]{1,0:T(8,128)S(1)}, f32[32,512]{1,0:T(8,128)S(1)}, u32[]{:S(2)}, u32[]{:S(2)}) collective-permute-start(f32[32,512]{1,0:T(8,128)S(1)} %shard_map.192.refs_2_.refs_0_), channel_id=1, source_target_pairs={{0,2},{1,3},{2,0},{3,1},{4,6},{5,7},{6,4},{7,5},{8,10},{9,11},{10,... | collective-permute-start | bytes 196616 | tf_op jit(solution)/shard_map/ppermute | solution.py:127
  67.1 2.1 %shard_map.195 = (bf16[2048,512]{1,0:T(8,128)(2,1)S(1)}, bf16[2048,512]{1,0:T(8,128)(2,1)S(1)}) custom-call(f32[2,256,512]{2,1,0:T(8,128)S(1)} %copy-done.1, f32[1,256,512]{2,1,0:T(8,128)S(1)} %get-tuple-element.79.refs_1_, f32[1,256,512]{2,1,0:T(8,128)} %shard_map.193.refs_2_, f32[1,256,512]{2,1,0:T(8,128)S(1)} %get-tuple-element.80.refs_3_, ...), custom_call_target="tpu_custom_call" | custom-call | tf_op jit(solution)/shard_map/pallas_call | solution.py:198
  69.2 2.5 %collective-permute-done.23.refs_2_ = f32[32,512]{1,0:T(8,128)S(1)} collective-permute-done((f32[32,512]{1,0:T(8,128)S(1)}, f32[32,512]{1,0:T(8,128)S(1)}, u32[]{:S(2)}, u32[]{:S(2)}) %collective-permute-start.23) | collective-permute-done | bytes 65568 | tf_op jit(solution)/shard_map/ppermute | solution.py:127
  71.7 1.3 %collective-permute-done.24.refs_3_ = f32[32,512]{1,0:T(8,128)S(1)} collective-permute-done((f32[32,512]{1,0:T(8,128)S(1)}, f32[32,512]{1,0:T(8,128)S(1)}, u32[]{:S(2)}, u32[]{:S(2)}) %collective-permute-start.24) | collective-permute-done | bytes 65568 | tf_op jit(solution)/shard_map/ppermute | solution.py:127
  73.0 2.1 %shard_map.196 = (f32[32,512]{1,0:T(8,128)S(1)}, f32[32,512]{1,0:T(8,128)S(1)}, f32[32,512]{1,0:T(8,128)S(1)}, f32[32,512]{1,0:T(8,128)S(1)}) custom-call(f32[32,512]{1,0:T(8,128)S(1)} %shard_map.192.refs_2_.refs_0_, f32[32,512]{1,0:T(8,128)S(1)} %collective-permute-done.22.refs_1_, f32[32,512]{1,0:T(8,128)S(1)} %collective-permute-done.23.refs_2_, ...), custom_call_target="tpu_custom_call" | custom-call | tf_op jit(solution)/shard_map/pallas_call | solution.py:198
  75.1 0.7 collective-permute-start.29
  75.8 1.7 %collective-permute-start.30 = (f32[32,512]{1,0:T(8,128)S(1)}, f32[32,512]{1,0:T(8,128)S(1)}, u32[]{:S(2)}, u32[]{:S(2)}) collective-permute-start(f32[32,512]{1,0:T(8,128)S(1)} %get-tuple-element.85), channel_id=1, source_target_pairs={{0,2},{1,3},{2,0},{3,1},{4,6},{5,7},{6,4},{7,5},{8,10},{9,11},{10,... | collective-permute-start | bytes 196616 | tf_op jit(solution)/shard_map/ppermute | solution.py:127
  77.5 2.0 %collective-permute-start.31 = (f32[32,512]{1,0:T(8,128)S(1)}, f32[32,512]{1,0:T(8,128)S(1)}, u32[]{:S(2)}, u32[]{:S(2)}) collective-permute-start(f32[32,512]{1,0:T(8,128)S(1)} %get-tuple-element.86), channel_id=1, source_target_pairs={{0,3},{1,2},{2,1},{3,0},{4,7},{5,6},{6,5},{7,4},{8,11},{9,10},{10,... | collective-permute-start | bytes 196616 | tf_op jit(solution)/shard_map/ppermute | solution.py:127
  79.6 2.4 %collective-permute-done.30.refs_2_ = f32[32,512]{1,0:T(8,128)S(1)} collective-permute-done((f32[32,512]{1,0:T(8,128)S(1)}, f32[32,512]{1,0:T(8,128)S(1)}, u32[]{:S(2)}, u32[]{:S(2)}) %collective-permute-start.30) | collective-permute-done | bytes 65568 | tf_op jit(solution)/shard_map/ppermute | solution.py:127
  82.0 1.6 %collective-permute-done.31.refs_3_ = f32[32,512]{1,0:T(8,128)S(1)} collective-permute-done((f32[32,512]{1,0:T(8,128)S(1)}, f32[32,512]{1,0:T(8,128)S(1)}, u32[]{:S(2)}, u32[]{:S(2)}) %collective-permute-start.31) | collective-permute-done | bytes 65568 | tf_op jit(solution)/shard_map/ppermute | solution.py:127
  83.6 1.3 %shard_map.197 = (f32[40,512]{1,0:T(8,128)S(1)}, f32[40,512]{1,0:T(8,128)S(1)}, f32[40,512]{1,0:T(8,128)S(1)}, f32[40,512]{1,0:T(8,128)S(1)}) custom-call(f32[32,512]{1,0:T(8,128)S(1)} %get-tuple-element.83.refs_0_, f32[32,512]{1,0:T(8,128)S(1)} %collective-permute-done.29.refs_1_, f32[32,512]{1,0:T(8,128)S(1)} %collective-permute-done.30.refs_2_, ...), custom_call_target="tpu_custom_call" | custom-call | tf_op jit(solution)/shard_map/pallas_call | solution.py:198
  84.9 2.5 %collective-permute-start.33 = (f32[40,512]{1,0:T(8,128)S(1)}, f32[40,512]{1,0:T(8,128)S(1)}, u32[]{:S(2)}, u32[]{:S(2)}) collective-permute-start(f32[40,512]{1,0:T(8,128)S(1)} %get-tuple-element.89), channel_id=1, source_target_pairs={{0,2},{1,3},{2,0},{3,1},{4,6},{5,7},{6,4},{7,5},{8,10},{9,11},{10,... | collective-permute-start | bytes 245768 | tf_op jit(solution)/shard_map/ppermute | solution.py:127
  87.5 1.8 %collective-permute-start.34 = (f32[40,512]{1,0:T(8,128)S(1)}, f32[40,512]{1,0:T(8,128)S(1)}, u32[]{:S(2)}, u32[]{:S(2)}) collective-permute-start(f32[40,512]{1,0:T(8,128)S(1)} %get-tuple-element.90), channel_id=1, source_target_pairs={{0,3},{1,2},{2,1},{3,0},{4,7},{5,6},{6,5},{7,4},{8,11},{9,10},{10,... | collective-permute-start | bytes 245768 | tf_op jit(solution)/shard_map/ppermute | solution.py:127
  89.3 1.6 %collective-permute-done.32.refs_1_ = f32[40,512]{1,0:T(8,128)S(1)} collective-permute-done((f32[40,512]{1,0:T(8,128)S(1)}, f32[40,512]{1,0:T(8,128)S(1)}, u32[]{:S(2)}, u32[]{:S(2)}) %collective-permute-start.32) | collective-permute-done | bytes 81952 | tf_op jit(solution)/shard_map/ppermute | solution.py:127
  90.9 2.8 %collective-permute-done.34.refs_3_ = f32[40,512]{1,0:T(8,128)S(1)} collective-permute-done((f32[40,512]{1,0:T(8,128)S(1)}, f32[40,512]{1,0:T(8,128)S(1)}, u32[]{:S(2)}, u32[]{:S(2)}) %collective-permute-start.34) | collective-permute-done | bytes 81952 | tf_op jit(solution)/shard_map/ppermute | solution.py:127
  93.8 0.8 collective-permute-start.35
  94.6 0.9 collective-permute-start.36
  95.5 1.8 %collective-permute-start.37 = (f32[40,512]{1,0:T(8,128)S(1)}, f32[40,512]{1,0:T(8,128)S(1)}, u32[]{:S(2)}, u32[]{:S(2)}) collective-permute-start(f32[40,512]{1,0:T(8,128)S(1)} %get-tuple-element.94), channel_id=1, source_target_pairs={{0,24},{4,28},{8,16},{12,20},{16,8},{20,12},{24,0},{28,4},{1,25},{... | collective-permute-start | bytes 245768 | tf_op jit(solution)/shard_map/ppermute | solution.py:127
  97.3 1.0 collective-permute-done.35.refs_1_
  98.3 0.8 collective-permute-done.36.refs_2_
  99.0 1.8 %collective-permute-done.37.refs_3_ = f32[40,512]{1,0:T(8,128)S(1)} collective-permute-done((f32[40,512]{1,0:T(8,128)S(1)}, f32[40,512]{1,0:T(8,128)S(1)}, u32[]{:S(2)}, u32[]{:S(2)}) %collective-permute-start.37) | collective-permute-done | bytes 81952 | tf_op jit(solution)/shard_map/ppermute | solution.py:127
  100.8 0.4 shard_map.199
  101.3 2.4 %collective-permute-start.39 = (f32[32,512]{1,0:T(8,128)S(1)}, f32[32,512]{1,0:T(8,128)S(1)}, u32[]{:S(2)}, u32[]{:S(2)}) collective-permute-start(f32[32,512]{1,0:T(8,128)S(1)} %get-tuple-element.97), channel_id=1, source_target_pairs={{0,2},{1,3},{2,0},{3,1},{4,6},{5,7},{6,4},{7,5},{8,10},{9,11},{10,... | collective-permute-start | bytes 196616 | tf_op jit(solution)/shard_map/ppermute | solution.py:127
  103.7 2.0 %collective-permute-start.40 = (f32[32,512]{1,0:T(8,128)S(1)}, f32[32,512]{1,0:T(8,128)S(1)}, u32[]{:S(2)}, u32[]{:S(2)}) collective-permute-start(f32[32,512]{1,0:T(8,128)S(1)} %get-tuple-element.98), channel_id=1, source_target_pairs={{0,3},{1,2},{2,1},{3,0},{4,7},{5,6},{6,5},{7,4},{8,11},{9,10},{10,... | collective-permute-start | bytes 196616 | tf_op jit(solution)/shard_map/ppermute | solution.py:127
  105.7 0.9 collective-permute-done.39.refs_2_
  106.6 3.2 %collective-permute-done.40.refs_3_ = f32[32,512]{1,0:T(8,128)S(1)} collective-permute-done((f32[32,512]{1,0:T(8,128)S(1)}, f32[32,512]{1,0:T(8,128)S(1)}, u32[]{:S(2)}, u32[]{:S(2)}) %collective-permute-start.40) | collective-permute-done | bytes 65568 | tf_op jit(solution)/shard_map/ppermute | solution.py:127
  109.9 1.2 %collective-permute-done.41.refs_1_ = f32[32,512]{1,0:T(8,128)S(1)} collective-permute-done((f32[32,512]{1,0:T(8,128)S(1)}, f32[32,512]{1,0:T(8,128)S(1)}, u32[]{:S(2)}, u32[]{:S(2)}) %collective-permute-start.41) | collective-permute-done | bytes 65568 | tf_op jit(solution)/shard_map/ppermute | solution.py:127
  111.1 0.7 shard_map.201
  (51 shorter events, 2.3 us)
Async XLA Ops:
  0.6 10.2 %collective-permute-start = (f32[2,256,512]{2,1,0:T(8,128)}, f32[2,256,512]{2,1,0:T(8,128)}, u32[]{:S(2)}, u32[]{:S(2)}) collective-permute-start(f32[2,256,512]{2,1,0:T(8,128)} %refs_0_.5), channel_id=1, source_target_pairs={{0,4},{4,0},{8,12},{12,8},{16,20},{20,16},{24,28},{28,24},{1,5},{5... | collective-permute-start | bytes 3145736 | tf_op jit(solution)/shard_map/ppermute | solution.py:127
  1.1 9.7 %collective-permute-start.1 = (f32[256,512]{1,0:T(8,128)}, f32[256,512]{1,0:T(8,128)}, u32[]{:S(2)}, u32[]{:S(2)}) collective-permute-start(f32[256,512]{1,0:T(8,128)} %refs_0_.4), channel_id=1, source_target_pairs={{0,4},{4,0},{8,12},{12,8},{16,20},{20,16},{24,28},{28,24},{1,5},{5... | collective-permute-start | bytes 1572872 | tf_op jit(solution)/shard_map/ppermute | solution.py:127
  1.2 15.4 %collective-permute-start.4 = (f32[256,512]{1,0:T(8,128)}, f32[256,512]{1,0:T(8,128)}, u32[]{:S(2)}, u32[]{:S(2)}) collective-permute-start(f32[256,512]{1,0:T(8,128)} %refs_0_.4), channel_id=1, source_target_pairs={{0,16},{4,20},{8,24},{12,28},{16,0},{20,4},{24,8},{28,12},{1,17},{... | collective-permute-start | bytes 1572872 | tf_op jit(solution)/shard_map/ppermute | solution.py:127
  4.2 14.2 %collective-permute-start.3 = (f32[256,512]{1,0:T(8,128)}, f32[256,512]{1,0:T(8,128)}, u32[]{:S(2)}, u32[]{:S(2)}) collective-permute-start(f32[256,512]{1,0:T(8,128)} %refs_0_.4), channel_id=1, source_target_pairs={{0,8},{4,12},{8,0},{12,4},{16,24},{20,28},{24,16},{28,20},{1,9},{5... | collective-permute-start | bytes 1572872 | tf_op jit(solution)/shard_map/ppermute | solution.py:127
  9.0 1.8 %collective-permute-start.2 = (f32[6,64,128]{2,1,0:T(8,128)}, f32[6,64,128]{2,1,0:T(8,128)}, u32[]{:S(2)}, u32[]{:S(2)}) collective-permute-start(f32[6,64,128]{2,1,0:T(8,128)} %get-tuple-element.55), channel_id=1, source_target_pairs={{0,4},{4,0},{8,12},{12,8},{16,20},{20,16},{24,28},{28,24},{1,5},{5... | collective-permute-start | bytes 589832 | tf_op jit(solution)/shard_map/ppermute | solution.py:127
  14.7 6.2 %collective-permute-start.5 = (f32[4,64,128]{2,1,0:T(8,128)}, f32[4,64,128]{2,1,0:T(8,128)}, u32[]{:S(2)}, u32[]{:S(2)}) collective-permute-start(f32[4,64,128]{2,1,0:T(8,128)} %get-tuple-element.58), channel_id=1, source_target_pairs={{0,8},{4,12},{8,0},{12,4},{16,24},{20,28},{24,16},{28,20},{1,9},{5... | collective-permute-start | bytes 393224 | tf_op jit(solution)/shard_map/ppermute | solution.py:127
  15.3 14.5 %collective-permute-start.9 = (f32[1,256,512]{2,1,0:T(8,128)}, f32[1,256,512]{2,1,0:T(8,128)}, u32[]{:S(2)}, u32[]{:S(2)}) collective-permute-start(f32[1,256,512]{2,1,0:T(8,128)} %get-tuple-element.62), channel_id=1, source_target_pairs={{0,16},{4,20},{8,24},{12,28},{16,0},{20,4},{24,8},{28,12},{1,17},{... | collective-permute-start | bytes 1572872 | tf_op jit(solution)/shard_map/ppermute | solution.py:127
  25.3 4.6 %collective-permute-start.8 = (f32[1,256,512]{2,1,0:T(8,128)}, f32[1,256,512]{2,1,0:T(8,128)S(1)}, u32[]{:S(2)}, u32[]{:S(2)}) collective-permute-start(f32[1,256,512]{2,1,0:T(8,128)} %get-tuple-element.60.refs_1_), channel_id=1, source_target_pairs={{0,4},{4,0},{8,12},{12,8},{16,20},{20,16},{24,28},{28,24},{1,5},{5... | collective-permute-start | bytes 1572872 | tf_op jit(solution)/shard_map/ppermute | solution.py:127
  25.3 15.1 %collective-permute-start.6 = (f32[1,256,512]{2,1,0:T(8,128)}, f32[1,256,512]{2,1,0:T(8,128)S(1)}, u32[]{:S(2)}, u32[]{:S(2)}) collective-permute-start(f32[1,256,512]{2,1,0:T(8,128)} %get-tuple-element.60.refs_1_), channel_id=1, source_target_pairs={{0,16},{4,20},{8,24},{12,28},{16,0},{20,4},{24,8},{28,12},{1,17},{... | collective-permute-start | bytes 1572872 | tf_op jit(solution)/shard_map/ppermute | solution.py:127
  25.7 14.8 %collective-permute-start.7 = (f32[1,256,512]{2,1,0:T(8,128)}, f32[1,256,512]{2,1,0:T(8,128)S(1)}, u32[]{:S(2)}, u32[]{:S(2)}) collective-permute-start(f32[1,256,512]{2,1,0:T(8,128)} %get-tuple-element.61), channel_id=1, source_target_pairs={{0,8},{4,12},{8,0},{12,4},{16,24},{20,28},{24,16},{28,20},{1,9},{5... | collective-permute-start | bytes 1572872 | tf_op jit(solution)/shard_map/ppermute | solution.py:127
  27.4 2.4 %collective-permute-start.10 = (f32[32,512]{1,0:T(8,128)}, f32[32,512]{1,0:T(8,128)S(1)}, u32[]{:S(2)}, u32[]{:S(2)}) collective-permute-start(f32[32,512]{1,0:T(8,128)} %get-tuple-element.64), channel_id=1, source_target_pairs={{0,4},{4,0},{8,12},{12,8},{16,20},{20,16},{24,28},{28,24},{1,5},{5... | collective-permute-start | bytes 196616 | tf_op jit(solution)/shard_map/ppermute | solution.py:127
  29.8 0.8 copy-start.4
  30.7 10.3 %copy-start.5 = (f32[32,512]{1,0:T(8,128)S(1)}, f32[32,512]{1,0:T(8,128)}, u32[]{:S(2)}) copy-start(f32[32,512]{1,0:T(8,128)} %get-tuple-element.63.refs_2_.refs_8_) | copy-start | bytes 196612
  30.7 9.8 %collective-permute-start.11 = (f32[32,512]{1,0:T(8,128)S(1)}, f32[32,512]{1,0:T(8,128)S(1)}, u32[]{:S(2)}, u32[]{:S(2)}) collective-permute-start(f32[32,512]{1,0:T(8,128)S(1)} %shard_map.186.refs_2_), channel_id=1, source_target_pairs={{0,1},{1,0},{2,3},{3,2},{4,5},{5,4},{6,7},{7,6},{8,9},{9,8},{10,11... | collective-permute-start | bytes 196616 | tf_op jit(solution)/shard_map/ppermute | solution.py:127
  32.3 8.2 %collective-permute-start.12 = (f32[32,512]{1,0:T(8,128)S(1)}, f32[32,512]{1,0:T(8,128)S(1)}, u32[]{:S(2)}, u32[]{:S(2)}) collective-permute-start(f32[32,512]{1,0:T(8,128)S(1)} %shard_map.186.refs_2_), channel_id=1, source_target_pairs={{0,2},{1,3},{2,0},{3,1},{4,6},{5,7},{6,4},{7,5},{8,10},{9,11},{10,... | collective-permute-start | bytes 196616 | tf_op jit(solution)/shard_map/ppermute | solution.py:127
  34.9 6.1 %collective-permute-start.13 = (f32[32,512]{1,0:T(8,128)S(1)}, f32[32,512]{1,0:T(8,128)S(1)}, u32[]{:S(2)}, u32[]{:S(2)}) collective-permute-start(f32[32,512]{1,0:T(8,128)S(1)} %shard_map.186.refs_2_), channel_id=1, source_target_pairs={{0,3},{1,2},{2,1},{3,0},{4,7},{5,6},{6,5},{7,4},{8,11},{9,10},{10,... | collective-permute-start | bytes 196616 | tf_op jit(solution)/shard_map/ppermute | solution.py:127
  35.1 1.2 %copy-start = (f32[2,256,512]{2,1,0:T(8,128)S(1)}, f32[2,256,512]{2,1,0:T(8,128)}, u32[]{:S(2)}) copy-start(f32[2,256,512]{2,1,0:T(8,128)} %refs_0_.5) | copy-start | bytes 3145732
  41.4 13.4 %copy-start.2 = (f32[256,512]{1,0:T(8,128)S(1)}, f32[256,512]{1,0:T(8,128)}, u32[]{:S(2)}) copy-start(f32[256,512]{1,0:T(8,128)} %refs_0_.4) | copy-start | bytes 1572868
  41.4 13.4 %copy-start.3 = (f32[1,256,512]{2,1,0:T(8,128)S(1)}, f32[1,256,512]{2,1,0:T(8,128)}, u32[]{:S(2)}) copy-start(f32[1,256,512]{2,1,0:T(8,128)} %get-tuple-element.60.refs_1_) | copy-start | bytes 1572868
  41.4 8.3 %collective-permute-start.14 = (f32[256,512]{1,0:T(8,128)}, f32[256,512]{1,0:T(8,128)S(1)}, u32[]{:S(2)}, u32[]{:S(2)}) collective-permute-start(f32[256,512]{1,0:T(8,128)} %get-tuple-element.68.refs_2_), channel_id=1, source_target_pairs={{0,4},{4,0},{8,12},{12,8},{16,20},{20,16},{24,28},{28,24},{1,5},{5... | collective-permute-start | bytes 1572872 | tf_op jit(solution)/shard_map/ppermute | solution.py:127
  41.5 8.2 %collective-permute-start.15 = (f32[1,256,512]{2,1,0:T(8,128)S(1)}, f32[1,256,512]{2,1,0:T(8,128)S(1)}, u32[]{:S(2)}, u32[]{:S(2)}) collective-permute-start(f32[1,256,512]{2,1,0:T(8,128)S(1)} %get-tuple-element.69.refs_3_), channel_id=1, source_target_pairs={{0,4},{4,0},{8,12},{12,8},{16,20},{20,16},{24,28},{28,24},{1,5},{5... | collective-permute-start | bytes 1572872 | tf_op jit(solution)/shard_map/ppermute | solution.py:127
  42.0 4.4 %collective-permute-start.16 = (f32[40,512]{1,0:T(8,128)S(1)}, f32[40,512]{1,0:T(8,128)S(1)}, u32[]{:S(2)}, u32[]{:S(2)}) collective-permute-start(f32[40,512]{1,0:T(8,128)S(1)} %get-tuple-element.71), channel_id=1, source_target_pairs={{0,8},{4,12},{8,0},{12,4},{16,24},{20,28},{24,16},{28,20},{1,9},{5... | collective-permute-start | bytes 245768 | tf_op jit(solution)/shard_map/ppermute | solution.py:127
  43.5 6.2 %collective-permute-start.17 = (f32[40,512]{1,0:T(8,128)S(1)}, f32[40,512]{1,0:T(8,128)S(1)}, u32[]{:S(2)}, u32[]{:S(2)}) collective-permute-start(f32[40,512]{1,0:T(8,128)S(1)} %get-tuple-element.72), channel_id=1, source_target_pairs={{0,16},{4,20},{8,24},{12,28},{16,0},{20,4},{24,8},{28,12},{1,17},{... | collective-permute-start | bytes 245768 | tf_op jit(solution)/shard_map/ppermute | solution.py:127
  44.2 5.5 %collective-permute-start.18 = (f32[40,512]{1,0:T(8,128)S(1)}, f32[40,512]{1,0:T(8,128)S(1)}, u32[]{:S(2)}, u32[]{:S(2)}) collective-permute-start(f32[40,512]{1,0:T(8,128)S(1)} %get-tuple-element.67.refs_2_), channel_id=1, source_target_pairs={{0,24},{4,28},{8,16},{12,20},{16,8},{20,12},{24,0},{28,4},{1,25},{... | collective-permute-start | bytes 245768 | tf_op jit(solution)/shard_map/ppermute | solution.py:127
  49.7 12.4 %collective-permute-start.25 = (f32[1,256,512]{2,1,0:T(8,128)}, f32[1,256,512]{2,1,0:T(8,128)S(1)}, u32[]{:S(2)}, u32[]{:S(2)}) collective-permute-start(f32[1,256,512]{2,1,0:T(8,128)} %shard_map.193.refs_2_), channel_id=1, source_target_pairs={{0,8},{4,12},{8,0},{12,4},{16,24},{20,28},{24,16},{28,20},{1,9},{5... | collective-permute-start | bytes 1572872 | tf_op jit(solution)/shard_map/ppermute | solution.py:127
  50.3 6.5 %collective-permute-start.19 = (f32[40,512]{1,0:T(8,128)S(1)}, f32[40,512]{1,0:T(8,128)S(1)}, u32[]{:S(2)}, u32[]{:S(2)}) collective-permute-start(f32[40,512]{1,0:T(8,128)S(1)} %get-tuple-element.74), channel_id=1, source_target_pairs={{0,1},{1,0},{2,3},{3,2},{4,5},{5,4},{6,7},{7,6},{8,9},{9,8},{10,11... | collective-permute-start | bytes 245768 | tf_op jit(solution)/shard_map/ppermute | solution.py:127
  51.7 7.1 %collective-permute-start.20 = (f32[40,512]{1,0:T(8,128)S(1)}, f32[40,512]{1,0:T(8,128)S(1)}, u32[]{:S(2)}, u32[]{:S(2)}) collective-permute-start(f32[40,512]{1,0:T(8,128)S(1)} %get-tuple-element.75), channel_id=1, source_target_pairs={{0,2},{1,3},{2,0},{3,1},{4,6},{5,7},{6,4},{7,5},{8,10},{9,11},{10,... | collective-permute-start | bytes 245768 | tf_op jit(solution)/shard_map/ppermute | solution.py:127
  54.3 6.3 %collective-permute-start.21 = (f32[40,512]{1,0:T(8,128)S(1)}, f32[40,512]{1,0:T(8,128)S(1)}, u32[]{:S(2)}, u32[]{:S(2)}) collective-permute-start(f32[40,512]{1,0:T(8,128)S(1)} %get-tuple-element.76.refs_1_), channel_id=1, source_target_pairs={{0,3},{1,2},{2,1},{3,0},{4,7},{5,6},{6,5},{7,4},{8,11},{9,10},{10,... | collective-permute-start | bytes 245768 | tf_op jit(solution)/shard_map/ppermute | solution.py:127
  54.7 12.1 %collective-permute-start.27 = (f32[1,256,512]{2,1,0:T(8,128)}, f32[1,256,512]{2,1,0:T(8,128)S(1)}, u32[]{:S(2)}, u32[]{:S(2)}) collective-permute-start(f32[1,256,512]{2,1,0:T(8,128)} %shard_map.193.refs_2_), channel_id=1, source_target_pairs={{0,4},{4,0},{8,12},{12,8},{16,20},{20,16},{24,28},{28,24},{1,5},{5... | collective-permute-start | bytes 1572872 | tf_op jit(solution)/shard_map/ppermute | solution.py:127
  60.6 6.5 %copy-start.1 = (f32[2,256,512]{2,1,0:T(8,128)S(1)}, f32[2,256,512]{2,1,0:T(8,128)}, u32[]{:S(2)}) copy-start(f32[2,256,512]{2,1,0:T(8,128)} %refs_0_.5) | copy-start | bytes 3145732
  62.1 4.9 %collective-permute-start.26 = (f32[1,256,512]{2,1,0:T(8,128)S(1)}, f32[1,256,512]{2,1,0:T(8,128)S(1)}, u32[]{:S(2)}, u32[]{:S(2)}) collective-permute-start(f32[1,256,512]{2,1,0:T(8,128)S(1)} %get-tuple-element.79.refs_1_), channel_id=1, source_target_pairs={{0,4},{4,0},{8,12},{12,8},{16,20},{20,16},{24,28},{28,24},{1,5},{5... | collective-permute-start | bytes 1572872 | tf_op jit(solution)/shard_map/ppermute | solution.py:127
  62.1 4.9 %collective-permute-start.28 = (f32[1,256,512]{2,1,0:T(8,128)S(1)}, f32[1,256,512]{2,1,0:T(8,128)S(1)}, u32[]{:S(2)}, u32[]{:S(2)}) collective-permute-start(f32[1,256,512]{2,1,0:T(8,128)S(1)} %get-tuple-element.80.refs_3_), channel_id=1, source_target_pairs={{0,4},{4,0},{8,12},{12,8},{16,20},{20,16},{24,28},{28,24},{1,5},{5... | collective-permute-start | bytes 1572872 | tf_op jit(solution)/shard_map/ppermute | solution.py:127
  62.7 6.5 %collective-permute-start.22 = (f32[32,512]{1,0:T(8,128)S(1)}, f32[32,512]{1,0:T(8,128)S(1)}, u32[]{:S(2)}, u32[]{:S(2)}) collective-permute-start(f32[32,512]{1,0:T(8,128)S(1)} %shard_map.192.refs_2_.refs_0_), channel_id=1, source_target_pairs={{0,1},{1,0},{2,3},{3,2},{4,5},{5,4},{6,7},{7,6},{8,9},{9,8},{10,11... | collective-permute-start | bytes 196616 | tf_op jit(solution)/shard_map/ppermute | solution.py:127
  64.2 7.5 %collective-permute-start.23 = (f32[32,512]{1,0:T(8,128)S(1)}, f32[32,512]{1,0:T(8,128)S(1)}, u32[]{:S(2)}, u32[]{:S(2)}) collective-permute-start(f32[32,512]{1,0:T(8,128)S(1)} %shard_map.192.refs_2_.refs_0_), channel_id=1, source_target_pairs={{0,2},{1,3},{2,0},{3,1},{4,6},{5,7},{6,4},{7,5},{8,10},{9,11},{10,... | collective-permute-start | bytes 196616 | tf_op jit(solution)/shard_map/ppermute | solution.py:127
  66.8 6.2 %collective-permute-start.24 = (f32[32,512]{1,0:T(8,128)S(1)}, f32[32,512]{1,0:T(8,128)S(1)}, u32[]{:S(2)}, u32[]{:S(2)}) collective-permute-start(f32[32,512]{1,0:T(8,128)S(1)} %shard_map.192.refs_2_.refs_0_), channel_id=1, source_target_pairs={{0,3},{1,2},{2,1},{3,0},{4,7},{5,6},{6,5},{7,4},{8,11},{9,10},{10,... | collective-permute-start | bytes 196616 | tf_op jit(solution)/shard_map/ppermute | solution.py:127
  75.1 4.5 %collective-permute-start.29 = (f32[32,512]{1,0:T(8,128)S(1)}, f32[32,512]{1,0:T(8,128)S(1)}, u32[]{:S(2)}, u32[]{:S(2)}) collective-permute-start(f32[32,512]{1,0:T(8,128)S(1)} %get-tuple-element.84), channel_id=1, source_target_pairs={{0,1},{1,0},{2,3},{3,2},{4,5},{5,4},{6,7},{7,6},{8,9},{9,8},{10,11... | collective-permute-start | bytes 196616 | tf_op jit(solution)/shard_map/ppermute | solution.py:127
  75.8 6.2 %collective-permute-start.30 = (f32[32,512]{1,0:T(8,128)S(1)}, f32[32,512]{1,0:T(8,128)S(1)}, u32[]{:S(2)}, u32[]{:S(2)}) collective-permute-start(f32[32,512]{1,0:T(8,128)S(1)} %get-tuple-element.85), channel_id=1, source_target_pairs={{0,2},{1,3},{2,0},{3,1},{4,6},{5,7},{6,4},{7,5},{8,10},{9,11},{10,... | collective-permute-start | bytes 196616 | tf_op jit(solution)/shard_map/ppermute | solution.py:127
  77.5 6.1 %collective-permute-start.31 = (f32[32,512]{1,0:T(8,128)S(1)}, f32[32,512]{1,0:T(8,128)S(1)}, u32[]{:S(2)}, u32[]{:S(2)}) collective-permute-start(f32[32,512]{1,0:T(8,128)S(1)} %get-tuple-element.86), channel_id=1, source_target_pairs={{0,3},{1,2},{2,1},{3,0},{4,7},{5,6},{6,5},{7,4},{8,11},{9,10},{10,... | collective-permute-start | bytes 196616 | tf_op jit(solution)/shard_map/ppermute | solution.py:127
  84.9 6.0 %collective-permute-start.32 = (f32[40,512]{1,0:T(8,128)S(1)}, f32[40,512]{1,0:T(8,128)S(1)}, u32[]{:S(2)}, u32[]{:S(2)}) collective-permute-start(f32[40,512]{1,0:T(8,128)S(1)} %get-tuple-element.88), channel_id=1, source_target_pairs={{0,1},{1,0},{2,3},{3,2},{4,5},{5,4},{6,7},{7,6},{8,9},{9,8},{10,11... | collective-permute-start | bytes 245768 | tf_op jit(solution)/shard_map/ppermute | solution.py:127
  84.9 6.0 %collective-permute-start.33 = (f32[40,512]{1,0:T(8,128)S(1)}, f32[40,512]{1,0:T(8,128)S(1)}, u32[]{:S(2)}, u32[]{:S(2)}) collective-permute-start(f32[40,512]{1,0:T(8,128)S(1)} %get-tuple-element.89), channel_id=1, source_target_pairs={{0,2},{1,3},{2,0},{3,1},{4,6},{5,7},{6,4},{7,5},{8,10},{9,11},{10,... | collective-permute-start | bytes 245768 | tf_op jit(solution)/shard_map/ppermute | solution.py:127
  87.5 6.2 %collective-permute-start.34 = (f32[40,512]{1,0:T(8,128)S(1)}, f32[40,512]{1,0:T(8,128)S(1)}, u32[]{:S(2)}, u32[]{:S(2)}) collective-permute-start(f32[40,512]{1,0:T(8,128)S(1)} %get-tuple-element.90), channel_id=1, source_target_pairs={{0,3},{1,2},{2,1},{3,0},{4,7},{5,6},{6,5},{7,4},{8,11},{9,10},{10,... | collective-permute-start | bytes 245768 | tf_op jit(solution)/shard_map/ppermute | solution.py:127
  93.8 4.5 %collective-permute-start.35 = (f32[40,512]{1,0:T(8,128)S(1)}, f32[40,512]{1,0:T(8,128)S(1)}, u32[]{:S(2)}, u32[]{:S(2)}) collective-permute-start(f32[40,512]{1,0:T(8,128)S(1)} %get-tuple-element.92), channel_id=1, source_target_pairs={{0,8},{4,12},{8,0},{12,4},{16,24},{20,28},{24,16},{28,20},{1,9},{5... | collective-permute-start | bytes 245768 | tf_op jit(solution)/shard_map/ppermute | solution.py:127
  94.6 4.4 %collective-permute-start.36 = (f32[40,512]{1,0:T(8,128)S(1)}, f32[40,512]{1,0:T(8,128)S(1)}, u32[]{:S(2)}, u32[]{:S(2)}) collective-permute-start(f32[40,512]{1,0:T(8,128)S(1)} %get-tuple-element.93), channel_id=1, source_target_pairs={{0,16},{4,20},{8,24},{12,28},{16,0},{20,4},{24,8},{28,12},{1,17},{... | collective-permute-start | bytes 245768 | tf_op jit(solution)/shard_map/ppermute | solution.py:127
  95.5 5.3 %collective-permute-start.37 = (f32[40,512]{1,0:T(8,128)S(1)}, f32[40,512]{1,0:T(8,128)S(1)}, u32[]{:S(2)}, u32[]{:S(2)}) collective-permute-start(f32[40,512]{1,0:T(8,128)S(1)} %get-tuple-element.94), channel_id=1, source_target_pairs={{0,24},{4,28},{8,16},{12,20},{16,8},{20,12},{24,0},{28,4},{1,25},{... | collective-permute-start | bytes 245768 | tf_op jit(solution)/shard_map/ppermute | solution.py:127
  101.3 4.5 %collective-permute-start.38 = (f32[32,512]{1,0:T(8,128)S(1)}, f32[32,512]{1,0:T(8,128)S(1)}, u32[]{:S(2)}, u32[]{:S(2)}) collective-permute-start(f32[32,512]{1,0:T(8,128)S(1)} %get-tuple-element.96), channel_id=1, source_target_pairs={{0,1},{1,0},{2,3},{3,2},{4,5},{5,4},{6,7},{7,6},{8,9},{9,8},{10,11... | collective-permute-start | bytes 196616 | tf_op jit(solution)/shard_map/ppermute | solution.py:127
  101.3 5.2 %collective-permute-start.39 = (f32[32,512]{1,0:T(8,128)S(1)}, f32[32,512]{1,0:T(8,128)S(1)}, u32[]{:S(2)}, u32[]{:S(2)}) collective-permute-start(f32[32,512]{1,0:T(8,128)S(1)} %get-tuple-element.97), channel_id=1, source_target_pairs={{0,2},{1,3},{2,0},{3,1},{4,6},{5,7},{6,4},{7,5},{8,10},{9,11},{10,... | collective-permute-start | bytes 196616 | tf_op jit(solution)/shard_map/ppermute | solution.py:127
  103.7 6.1 %collective-permute-start.40 = (f32[32,512]{1,0:T(8,128)S(1)}, f32[32,512]{1,0:T(8,128)S(1)}, u32[]{:S(2)}, u32[]{:S(2)}) collective-permute-start(f32[32,512]{1,0:T(8,128)S(1)} %get-tuple-element.98), channel_id=1, source_target_pairs={{0,3},{1,2},{2,1},{3,0},{4,7},{5,6},{6,5},{7,4},{8,11},{9,10},{10,... | collective-permute-start | bytes 196616 | tf_op jit(solution)/shard_map/ppermute | solution.py:127
  109.8 1.3 %collective-permute-start.41 = (f32[32,512]{1,0:T(8,128)S(1)}, f32[32,512]{1,0:T(8,128)S(1)}, u32[]{:S(2)}, u32[]{:S(2)}) collective-permute-start(f32[32,512]{1,0:T(8,128)S(1)} %get-tuple-element.101), channel_id=1, source_target_pairs={{0,4},{4,0},{8,12},{12,8},{16,20},{20,16},{24,28},{28,24},{1,5},{5... | collective-permute-start | bytes 196616 | tf_op jit(solution)/shard_map/ppermute | solution.py:127

commit v5 on v4

--- a/solution.py
+++ b/solution.py
@@ -132,7 +132,7 @@
 
 
 def kernel_call(
-    body, out_shapes, scalars, operands, loaded=(), ahead=(), stacks=(), held=(), scratch=(), room=40
+    body, out_shapes, scalars, operands, loaded=(), ahead=(), stacks=(), held=(), scratch=(), room=40, late=0
 ):
     vmem = pl.BlockSpec(memory_space=pltpu.VMEM)
     far = pl.BlockSpec(memory_space=pltpu.HBM)
@@ -179,11 +179,18 @@
         leaving = copies[len(pairs) :]
         for copy in copies[: len(pairs)]:
             copy.start()
-        for copy in (*copies[:early], *copies[len(pairs) - len(moves) : len(pairs)]):
+        for copy in copies[: early - late]:
             copy.wait()
-        for copy in leaving:
-            copy.start()
-        place = (lax.axis_index("leaf"), lax.axis_index("col"))
+
+        def ready():
+            for copy in (*copies[early - late : early], *copies[len(pairs) - len(moves) : len(pairs)]):
+                copy.wait()
+            for copy in leaving:
+                copy.start()
+
+        place = (lax.axis_index("leaf"), lax.axis_index("col"), ready)
+        if not late:
+            ready()
         body(place, *fetched, *ins, *outs, *rest)
         for copy in (*copies[early : len(pairs) - len(moves)], *leaving):
             copy.wait()
@@ -414,17 +421,21 @@
             result[start + GROUP : start + 2 * GROUP, n, :] = jnp.where(lower, other, own)
 
 
-def reduce_blocks(level, live, links, blocks, inverse, coupling, solved):
+def reduce_blocks(ready, level, live, links, blocks, inverse, coupling, solved):
     red_blocks, link_total, size = inverse.shape[0], coupling.shape[1], inverse.shape[1]
     lanes = lax.broadcasted_iota(jnp.int32, (1, size), 1)
-    pushed = []
+    values = []
     for i in range(red_blocks):
         mask = (lanes + i * size < live[0, level]).astype(jnp.float32)
         value = product(blocks[i] * mask, *halves(inverse[i]), 0) * mask
         solved[:, i * size : (i + 1) * size] = value
+        values.append(value)
+    ready()
+    pushed = []
+    for i in range(red_blocks):
         pairs = [halves(coupling[i, k]) for k in range(link_total)]
         high, low = (jnp.concatenate(part, 1) for part in zip(*pairs, strict=True))
-        pushed.append(product(value, high, low, 0))
+        pushed.append(product(values[i], high, low, 0))
     for i in range(red_blocks):
         for k in range(link_total):
             target = red_blocks + links[i, k]
@@ -451,7 +462,7 @@
     size = inverse.shape[1]
     for n in range(blocks.shape[0]):
         blocks[n] = section[:, n * size : (n + 1) * size]
-    reduce_blocks(0, live, links, blocks, inverse, coupling, solved)
+    reduce_blocks(place[2], 0, live, links, blocks, inverse, coupling, solved)
     send_halves(place, 0, blocks, inverse.shape[0], kept, sent)
 
 
@@ -459,7 +470,7 @@
     place, live, links, order, old, received, inverse, coupling, solved, kept, sent, joined, blocks
 ):
     load_halves(place, 0, order, old, received, joined, blocks)
-    reduce_blocks(1, live, links, blocks, inverse, coupling, solved)
+    reduce_blocks(place[2], 1, live, links, blocks, inverse, coupling, solved)
     send_halves(place, 1, blocks, inverse.shape[0], kept, sent)
 
 
@@ -467,7 +478,7 @@
     place, live, links, order, last_order, old, received, inverse, coupling, solved, kept, sent, joined, blocks
 ):
     load_halves(place, 1, order, old, received, joined, blocks)
-    reduce_blocks(2, live, links, blocks, inverse, coupling, solved)
+    reduce_blocks(place[2], 2, live, links, blocks, inverse, coupling, solved)
     red_blocks, size = inverse.shape[0], inverse.shape[1]
     core = place[0] & 1
     for n in range(blocks.shape[0] - red_blocks):
@@ -511,6 +522,7 @@
         [front_rows, links],
         [],
         loaded=[right_sides, inverse, coupling],
+        late=1,
         stacks=[[(root_inverse, 1)]],
         scratch=[scratch(count, rhs_rows, size)],
         room=64,
@@ -527,7 +539,9 @@
         middle_kernel,
         [solved, halved(count), halved(count)],
         [front_rows, links, order],
-        [kept, received, inverse, coupling],
+        [],
+        loaded=[kept, received, inverse, coupling],
+        late=1,
         held=[partner_inverse, partner_coupling],
         scratch=[scratch(count, rhs_rows, size)] * 2,
         room=64,
@@ -539,7 +553,9 @@
         highest_kernel,
         [solved, both, both],
         [front_rows, links, next_order, last_order],
-        [kept, received, inverse, coupling],
+        [],
+        loaded=[kept, received, inverse, coupling],
+        late=1,
         stacks=[[near], [(root_inverse, 1)]],
         held=[far],
         scratch=[scratch(count, rhs_rows, size)] * 2,

time: 112 us -> 111 us (level)
  Pallas kernels: 22.9 us -> 20.5 us
    pallas_call x16, Pallas kernels: 22.9 us -> 20.5 us  [kernel_call(): pl.pallas_call(run, out_shape=out_shapes, in_specs=[far] * sum(inputs[:-2...]
  transfers between devices with their start and end apart: 42 -> 42, of which waited for: 25 -> 26; matrix products, arithmetic and copies ran while one was open for 0% -> 0% of each run, Pallas kernels for 16% -> 14%
where the time goes in v5:
time: 111 us
  waiting for transfers between devices  43.8 us (39%)
  starting transfers between devices  43.4 us (39%)
  Pallas kernels  20.5 us (18%)
  local copies, waits for them, and re-layouts  2.08 us (2%)
    ppermute x42, waiting for transfers between devices, flip(): return lax.ppermute(block, axis, [(i, i ^ distance) for i in range(count)])  43.8 us
    ppermute x42, starting transfers between devices, flip(): return lax.ppermute(block, axis, [(i, i ^ distance) for i in range(count)])  43.4 us
    pallas_call x16, Pallas kernels, kernel_call(): pl.pallas_call(run, out_shape=out_shapes, in_specs=[far] * sum(inputs[:-2...  20.5 us
  transfers between devices with their start and end apart: 42, of which 26 were waited for; matrix products, arithmetic and copies ran while one was open for 0% of the time, Pallas kernels for 14%

profile of v5, /device:TPU:0, one launch (start us, length us, event | category | flops | bytes accessed | tf_op | source)
XLA Modules:
  0.0 110.6 jit_solution(10549323364036385547)
XLA Ops:
  0.6 0.5 collective-permute-start.1
  1.2 2.9 %collective-permute-start.5 = (f32[256,512]{1,0:T(8,128)}, f32[256,512]{1,0:T(8,128)}, u32[]{:S(2)}, u32[]{:S(2)}) collective-permute-start(f32[256,512]{1,0:T(8,128)} %refs_0_.4), channel_id=1, source_target_pairs={{0,16},{4,20},{8,24},{12,28},{16,0},{20,4},{24,8},{28,12},{1,17},{... | collective-permute-start | bytes 1572872 | tf_op jit(solution)/shard_map/ppermute | solution.py:127
  4.2 1.5 %collective-permute-start.4 = (f32[256,512]{1,0:T(8,128)}, f32[256,512]{1,0:T(8,128)}, u32[]{:S(2)}, u32[]{:S(2)}) collective-permute-start(f32[256,512]{1,0:T(8,128)} %refs_0_.4), channel_id=1, source_target_pairs={{0,8},{4,12},{8,0},{12,4},{16,24},{20,28},{24,16},{28,20},{1,9},{5... | collective-permute-start | bytes 1572872 | tf_op jit(solution)/shard_map/ppermute | solution.py:127
  5.7 3.2 %shard_map.183 = (f32[64,512]{1,0:T(8,128)}, f32[6,64,128]{2,1,0:T(8,128)}, f32[6,64,128]{2,1,0:T(8,128)}, f32[1,256,512]{2,1,0:T(8,128)}) custom-call(s32[1,3]{1,0:T(1,128)} %bitcast.1, s32[4,3]{1,0:T(4,128)} %refs_1_.3, f32[64,2048]{1,0:T(8,128)} %refs_2_.3, f32[4,128,128]{2,1,0:T(8,128)} %refs_3_.2, f32[4,3,128,128]{3,2,1,0:T(8,128)} %refs_4_.1, ...), custom_call_target="tpu_custom_call" | custom-call | tf_op jit(solution)/shard_map/pallas_call | solution.py:205
  8.9 1.8 %collective-permute-done.refs_4_ = f32[6,64,128]{2,1,0:T(8,128)} collective-permute-done((f32[6,64,128]{2,1,0:T(8,128)}, f32[6,64,128]{2,1,0:T(8,128)}, u32[]{:S(2)}, u32[]{:S(2)}) %collective-permute-start) | collective-permute-done | bytes 196640 | tf_op jit(solution)/shard_map/ppermute | solution.py:127
  10.7 2.5 %shard_map.184 = (f32[64,512]{1,0:T(8,128)}, f32[4,64,128]{2,1,0:T(8,128)}, f32[4,64,128]{2,1,0:T(8,128)}) custom-call(s32[1,3]{1,0:T(1,128)} %bitcast.2, s32[4,3]{1,0:T(4,128)} %refs_1_.4, s32[1,12]{1,0:T(1,128)} %refs_2_.4, f32[6,64,128]{2,1,0:T(8,128)} %get-tuple-element.54.refs_3_, f32[6,64,128]{2,1,0:T(8,128)} %collective-permute-done.refs_4_, ...), custom_call_target="tpu_custom_call" | custom-call | tf_op jit(solution)/shard_map/pallas_call | solution.py:205
  13.2 0.6 collective-permute-start.3
  13.9 2.9 %collective-permute-done.5.refs_10_.refs_1_ = f32[256,512]{1,0:T(8,128)} collective-permute-done((f32[256,512]{1,0:T(8,128)}, f32[256,512]{1,0:T(8,128)}, u32[]{:S(2)}, u32[]{:S(2)}) %collective-permute-start.5) | collective-permute-done | bytes 524320 | tf_op jit(solution)/shard_map/ppermute | solution.py:127
  16.8 2.5 %collective-permute-done.4.refs_8_ = f32[256,512]{1,0:T(8,128)} collective-permute-done((f32[256,512]{1,0:T(8,128)}, f32[256,512]{1,0:T(8,128)}, u32[]{:S(2)}, u32[]{:S(2)}) %collective-permute-start.4) | collective-permute-done | bytes 524320 | tf_op jit(solution)/shard_map/ppermute | solution.py:127
  19.3 1.6 %collective-permute-done.3.refs_5_ = f32[4,64,128]{2,1,0:T(8,128)} collective-permute-done((f32[4,64,128]{2,1,0:T(8,128)}, f32[4,64,128]{2,1,0:T(8,128)}, u32[]{:S(2)}, u32[]{:S(2)}) %collective-permute-start.3) | collective-permute-done | bytes 131104 | tf_op jit(solution)/shard_map/ppermute | solution.py:127
  20.9 3.4 %shard_map.185 = (f32[64,512]{1,0:T(8,128)}, f32[32,512]{1,0:T(8,128)}, f32[32,512]{1,0:T(8,128)}, f32[1,256,512]{2,1,0:T(8,128)}, f32[1,256,512]{2,1,0:T(8,128)}) custom-call(s32[1,3]{1,0:T(1,128)} %bitcast.3, s32[4,3]{1,0:T(4,128)} %refs_1_.5, s32[1,8]{1,0:T(1,128)} %refs_2_.5, s32[1,4]{1,0:T(1,128)} %refs_3_.3, f32[4,64,128]{2,1,0:T(8,128)} %get-tuple-element.57.refs_4_, ...), custom_call_target="tpu_custom_call" | custom-call | tf_op jit(solution)/shard_map/pallas_call | solution.py:205
  24.8 1.7 %collective-permute-start.7 = (f32[1,256,512]{2,1,0:T(8,128)}, f32[1,256,512]{2,1,0:T(8,128)S(1)}, u32[]{:S(2)}, u32[]{:S(2)}) collective-permute-start(f32[1,256,512]{2,1,0:T(8,128)} %get-tuple-element.61), channel_id=1, source_target_pairs={{0,8},{4,12},{8,0},{12,4},{16,24},{20,28},{24,16},{28,20},{1,9},{5... | collective-permute-start | bytes 1572872 | tf_op jit(solution)/shard_map/ppermute | solution.py:127
  26.5 1.5 %collective-permute-done.9.refs_1_.refs_0_ = f32[1,256,512]{2,1,0:T(8,128)} collective-permute-done((f32[1,256,512]{2,1,0:T(8,128)}, f32[1,256,512]{2,1,0:T(8,128)}, u32[]{:S(2)}, u32[]{:S(2)}) %collective-permute-start.9) | collective-permute-done | bytes 524320 | tf_op jit(solution)/shard_map/ppermute | solution.py:127
  28.0 0.8 copy-done.4
  28.9 1.9 %collective-permute-start.11 = (f32[32,512]{1,0:T(8,128)S(1)}, f32[32,512]{1,0:T(8,128)S(1)}, u32[]{:S(2)}, u32[]{:S(2)}) collective-permute-start(f32[32,512]{1,0:T(8,128)S(1)} %shard_map.186.refs_2_), channel_id=1, source_target_pairs={{0,1},{1,0},{2,3},{3,2},{4,5},{5,4},{6,7},{7,6},{8,9},{9,8},{10,11... | collective-permute-start | bytes 196616 | tf_op jit(solution)/shard_map/ppermute | solution.py:127
  30.8 2.6 %collective-permute-start.12 = (f32[32,512]{1,0:T(8,128)S(1)}, f32[32,512]{1,0:T(8,128)S(1)}, u32[]{:S(2)}, u32[]{:S(2)}) collective-permute-start(f32[32,512]{1,0:T(8,128)S(1)} %shard_map.186.refs_2_), channel_id=1, source_target_pairs={{0,2},{1,3},{2,0},{3,1},{4,6},{5,7},{6,4},{7,5},{8,10},{9,11},{10,... | collective-permute-start | bytes 196616 | tf_op jit(solution)/shard_map/ppermute | solution.py:127
  33.4 1.2 %copy-done = f32[2,256,512]{2,1,0:T(8,128)S(1)} copy-done((f32[2,256,512]{2,1,0:T(8,128)S(1)}, f32[2,256,512]{2,1,0:T(8,128)}, u32[]{:S(2)}) %copy-start) | copy-done | bytes 1048600
  34.6 1.3 %shard_map.187 = (bf16[512,512]{1,0:T(8,128)(2,1)S(1)}, bf16[512,512]{1,0:T(8,128)(2,1)S(1)}) custom-call(f32[2,256,512]{2,1,0:T(8,128)S(1)} %copy-done, f32[2,256,512]{2,1,0:T(8,128)} %collective-permute-done.1.refs_7_.refs_1_.refs_4_), custom_call_target="tpu_custom_call" | custom-call | tf_op jit(solution)/shard_map/pallas_call | solution.py:205
  35.9 3.1 %collective-permute-done.6.refs_0_ = f32[1,256,512]{2,1,0:T(8,128)S(1)} collective-permute-done((f32[1,256,512]{2,1,0:T(8,128)}, f32[1,256,512]{2,1,0:T(8,128)S(1)}, u32[]{:S(2)}, u32[]{:S(2)}) %collective-permute-start.6) | collective-permute-done | bytes 524320 | tf_op jit(solution)/shard_map/ppermute | solution.py:127
  40.5 1.4 %collective-permute-start.16 = (f32[40,512]{1,0:T(8,128)S(1)}, f32[40,512]{1,0:T(8,128)S(1)}, u32[]{:S(2)}, u32[]{:S(2)}) collective-permute-start(f32[40,512]{1,0:T(8,128)S(1)} %get-tuple-element.71), channel_id=1, source_target_pairs={{0,8},{4,12},{8,0},{12,4},{16,24},{20,28},{24,16},{28,20},{1,9},{5... | collective-permute-start | bytes 245768 | tf_op jit(solution)/shard_map/ppermute | solution.py:127
  41.9 2.2 %collective-permute-start.17 = (f32[40,512]{1,0:T(8,128)S(1)}, f32[40,512]{1,0:T(8,128)S(1)}, u32[]{:S(2)}, u32[]{:S(2)}) collective-permute-start(f32[40,512]{1,0:T(8,128)S(1)} %get-tuple-element.72), channel_id=1, source_target_pairs={{0,16},{4,20},{8,24},{12,28},{16,0},{20,4},{24,8},{28,12},{1,17},{... | collective-permute-start | bytes 245768 | tf_op jit(solution)/shard_map/ppermute | solution.py:127
  44.2 0.8 collective-permute-done.16.refs_3_
  44.9 2.7 %collective-permute-done.17.refs_4_ = f32[40,512]{1,0:T(8,128)S(1)} collective-permute-done((f32[40,512]{1,0:T(8,128)S(1)}, f32[40,512]{1,0:T(8,128)S(1)}, u32[]{:S(2)}, u32[]{:S(2)}) %collective-permute-start.17) | collective-permute-done | bytes 81952 | tf_op jit(solution)/shard_map/ppermute | solution.py:127
  47.6 1.9 %collective-permute-done.18.refs_5_ = f32[40,512]{1,0:T(8,128)S(1)} collective-permute-done((f32[40,512]{1,0:T(8,128)S(1)}, f32[40,512]{1,0:T(8,128)S(1)}, u32[]{:S(2)}, u32[]{:S(2)}) %collective-permute-start.18) | collective-permute-done | bytes 81952 | tf_op jit(solution)/shard_map/ppermute | solution.py:127
  49.6 0.6 collective-permute-start.25
  50.2 0.7 collective-permute-start.19
  50.9 2.6 %collective-permute-start.20 = (f32[40,512]{1,0:T(8,128)S(1)}, f32[40,512]{1,0:T(8,128)S(1)}, u32[]{:S(2)}, u32[]{:S(2)}) collective-permute-start(f32[40,512]{1,0:T(8,128)S(1)} %get-tuple-element.75), channel_id=1, source_target_pairs={{0,2},{1,3},{2,0},{3,1},{4,6},{5,7},{6,4},{7,5},{8,10},{9,11},{10,... | collective-permute-start | bytes 245768 | tf_op jit(solution)/shard_map/ppermute | solution.py:127
  53.5 1.1 collective-permute-start.21
  54.6 2.1 %shard_map.191 = (bf16[2048,512]{1,0:T(8,128)(2,1)S(1)}, bf16[2048,512]{1,0:T(8,128)(2,1)S(1)}) custom-call(f32[256,512]{1,0:T(8,128)S(1)} %copy-done.2, f32[1,256,512]{2,1,0:T(8,128)S(1)} %copy-done.3, f32[256,512]{1,0:T(8,128)} %get-tuple-element.68.refs_2_, f32[1,256,512]{2,1,0:T(8,128)S(1)} %get-tuple-element.69.refs_3_, ...), custom_call_target="tpu_custom_call" | custom-call | tf_op jit(solution)/shard_map/pallas_call | solution.py:205
  56.7 1.3 %collective-permute-done.20.refs_2_ = f32[40,512]{1,0:T(8,128)S(1)} collective-permute-done((f32[40,512]{1,0:T(8,128)S(1)}, f32[40,512]{1,0:T(8,128)S(1)}, u32[]{:S(2)}, u32[]{:S(2)}) %collective-permute-start.20) | collective-permute-done | bytes 81952 | tf_op jit(solution)/shard_map/ppermute | solution.py:127
  58.0 1.8 %collective-permute-done.21.refs_3_ = f32[40,512]{1,0:T(8,128)S(1)} collective-permute-done((f32[40,512]{1,0:T(8,128)S(1)}, f32[40,512]{1,0:T(8,128)S(1)}, u32[]{:S(2)}, u32[]{:S(2)}) %collective-permute-start.21) | collective-permute-done | bytes 81952 | tf_op jit(solution)/shard_map/ppermute | solution.py:127
  59.7 0.8 shard_map.192.refs_2_.refs_0_
  60.6 1.5 %collective-permute-done.25.refs_1_ = f32[1,256,512]{2,1,0:T(8,128)S(1)} collective-permute-done((f32[1,256,512]{2,1,0:T(8,128)}, f32[1,256,512]{2,1,0:T(8,128)S(1)}, u32[]{:S(2)}, u32[]{:S(2)}) %collective-permute-start.25) | collective-permute-done | bytes 524320 | tf_op jit(solution)/shard_map/ppermute | solution.py:127
  62.0 0.5 collective-permute-start.28
  62.5 0.7 collective-permute-start.22
  63.3 2.6 %collective-permute-start.23 = (f32[32,512]{1,0:T(8,128)S(1)}, f32[32,512]{1,0:T(8,128)S(1)}, u32[]{:S(2)}, u32[]{:S(2)}) collective-permute-start(f32[32,512]{1,0:T(8,128)S(1)} %shard_map.192.refs_2_.refs_0_), channel_id=1, source_target_pairs={{0,2},{1,3},{2,0},{3,1},{4,6},{5,7},{6,4},{7,5},{8,10},{9,11},{10,... | collective-permute-start | bytes 196616 | tf_op jit(solution)/shard_map/ppermute | solution.py:127
  65.9 1.1 collective-permute-start.24
  66.9 2.1 %shard_map.195 = (bf16[2048,512]{1,0:T(8,128)(2,1)S(1)}, bf16[2048,512]{1,0:T(8,128)(2,1)S(1)}) custom-call(f32[2,256,512]{2,1,0:T(8,128)S(1)} %copy-done.1, f32[1,256,512]{2,1,0:T(8,128)S(1)} %get-tuple-element.79.refs_1_, f32[1,256,512]{2,1,0:T(8,128)} %shard_map.193.refs_2_, f32[1,256,512]{2,1,0:T(8,128)S(1)} %get-tuple-element.80.refs_3_, ...), custom_call_target="tpu_custom_call" | custom-call | tf_op jit(solution)/shard_map/pallas_call | solution.py:205
  69.1 1.8 %collective-permute-done.23.refs_2_ = f32[32,512]{1,0:T(8,128)S(1)} collective-permute-done((f32[32,512]{1,0:T(8,128)S(1)}, f32[32,512]{1,0:T(8,128)S(1)}, u32[]{:S(2)}, u32[]{:S(2)}) %collective-permute-start.23) | collective-permute-done | bytes 65568 | tf_op jit(solution)/shard_map/ppermute | solution.py:127
  70.9 1.1 collective-permute-done.24.refs_3_
  72.0 2.1 %shard_map.196 = (f32[32,512]{1,0:T(8,128)S(1)}, f32[32,512]{1,0:T(8,128)S(1)}, f32[32,512]{1,0:T(8,128)S(1)}, f32[32,512]{1,0:T(8,128)S(1)}) custom-call(f32[32,512]{1,0:T(8,128)S(1)} %shard_map.192.refs_2_.refs_0_, f32[32,512]{1,0:T(8,128)S(1)} %collective-permute-done.22.refs_1_, f32[32,512]{1,0:T(8,128)S(1)} %collective-permute-done.23.refs_2_, ...), custom_call_target="tpu_custom_call" | custom-call | tf_op jit(solution)/shard_map/pallas_call | solution.py:205
  74.1 0.9 collective-permute-start.29
  75.0 1.5 %collective-permute-start.30 = (f32[32,512]{1,0:T(8,128)S(1)}, f32[32,512]{1,0:T(8,128)S(1)}, u32[]{:S(2)}, u32[]{:S(2)}) collective-permute-start(f32[32,512]{1,0:T(8,128)S(1)} %get-tuple-element.85), channel_id=1, source_target_pairs={{0,2},{1,3},{2,0},{3,1},{4,6},{5,7},{6,4},{7,5},{8,10},{9,11},{10,... | collective-permute-start | bytes 196616 | tf_op jit(solution)/shard_map/ppermute | solution.py:127
  76.6 2.0 %collective-permute-start.31 = (f32[32,512]{1,0:T(8,128)S(1)}, f32[32,512]{1,0:T(8,128)S(1)}, u32[]{:S(2)}, u32[]{:S(2)}) collective-permute-start(f32[32,512]{1,0:T(8,128)S(1)} %get-tuple-element.86), channel_id=1, source_target_pairs={{0,3},{1,2},{2,1},{3,0},{4,7},{5,6},{6,5},{7,4},{8,11},{9,10},{10,... | collective-permute-start | bytes 196616 | tf_op jit(solution)/shard_map/ppermute | solution.py:127
  78.5 0.6 collective-permute-done.29.refs_1_
  79.1 2.1 %collective-permute-done.30.refs_2_ = f32[32,512]{1,0:T(8,128)S(1)} collective-permute-done((f32[32,512]{1,0:T(8,128)S(1)}, f32[32,512]{1,0:T(8,128)S(1)}, u32[]{:S(2)}, u32[]{:S(2)}) %collective-permute-start.30) | collective-permute-done | bytes 65568 | tf_op jit(solution)/shard_map/ppermute | solution.py:127
  81.2 1.4 %collective-permute-done.31.refs_3_ = f32[32,512]{1,0:T(8,128)S(1)} collective-permute-done((f32[32,512]{1,0:T(8,128)S(1)}, f32[32,512]{1,0:T(8,128)S(1)}, u32[]{:S(2)}, u32[]{:S(2)}) %collective-permute-start.31) | collective-permute-done | bytes 65568 | tf_op jit(solution)/shard_map/ppermute | solution.py:127
  82.6 1.3 %shard_map.197 = (f32[40,512]{1,0:T(8,128)S(1)}, f32[40,512]{1,0:T(8,128)S(1)}, f32[40,512]{1,0:T(8,128)S(1)}, f32[40,512]{1,0:T(8,128)S(1)}) custom-call(f32[32,512]{1,0:T(8,128)S(1)} %get-tuple-element.83.refs_0_, f32[32,512]{1,0:T(8,128)S(1)} %collective-permute-done.29.refs_1_, f32[32,512]{1,0:T(8,128)S(1)} %collective-permute-done.30.refs_2_, ...), custom_call_target="tpu_custom_call" | custom-call | tf_op jit(solution)/shard_map/pallas_call | solution.py:205
  84.0 2.6 %collective-permute-start.33 = (f32[40,512]{1,0:T(8,128)S(1)}, f32[40,512]{1,0:T(8,128)S(1)}, u32[]{:S(2)}, u32[]{:S(2)}) collective-permute-start(f32[40,512]{1,0:T(8,128)S(1)} %get-tuple-element.89), channel_id=1, source_target_pairs={{0,2},{1,3},{2,0},{3,1},{4,6},{5,7},{6,4},{7,5},{8,10},{9,11},{10,... | collective-permute-start | bytes 245768 | tf_op jit(solution)/shard_map/ppermute | solution.py:127
  86.5 1.8 %collective-permute-start.34 = (f32[40,512]{1,0:T(8,128)S(1)}, f32[40,512]{1,0:T(8,128)S(1)}, u32[]{:S(2)}, u32[]{:S(2)}) collective-permute-start(f32[40,512]{1,0:T(8,128)S(1)} %get-tuple-element.90), channel_id=1, source_target_pairs={{0,3},{1,2},{2,1},{3,0},{4,7},{5,6},{6,5},{7,4},{8,11},{9,10},{10,... | collective-permute-start | bytes 245768 | tf_op jit(solution)/shard_map/ppermute | solution.py:127
  88.4 1.7 %collective-permute-done.32.refs_1_ = f32[40,512]{1,0:T(8,128)S(1)} collective-permute-done((f32[40,512]{1,0:T(8,128)S(1)}, f32[40,512]{1,0:T(8,128)S(1)}, u32[]{:S(2)}, u32[]{:S(2)}) %collective-permute-start.32) | collective-permute-done | bytes 81952 | tf_op jit(solution)/shard_map/ppermute | solution.py:127
  90.0 2.7 %collective-permute-done.34.refs_3_ = f32[40,512]{1,0:T(8,128)S(1)} collective-permute-done((f32[40,512]{1,0:T(8,128)S(1)}, f32[40,512]{1,0:T(8,128)S(1)}, u32[]{:S(2)}, u32[]{:S(2)}) %collective-permute-start.34) | collective-permute-done | bytes 81952 | tf_op jit(solution)/shard_map/ppermute | solution.py:127
  92.8 0.9 collective-permute-start.35
  93.7 0.5 collective-permute-start.36
  94.3 2.1 %collective-permute-start.37 = (f32[40,512]{1,0:T(8,128)S(1)}, f32[40,512]{1,0:T(8,128)S(1)}, u32[]{:S(2)}, u32[]{:S(2)}) collective-permute-start(f32[40,512]{1,0:T(8,128)S(1)} %get-tuple-element.94), channel_id=1, source_target_pairs={{0,24},{4,28},{8,16},{12,20},{16,8},{20,12},{24,0},{28,4},{1,25},{... | collective-permute-start | bytes 245768 | tf_op jit(solution)/shard_map/ppermute | solution.py:127
  96.4 1.0 collective-permute-done.35.refs_1_
  97.3 0.9 collective-permute-done.36.refs_2_
  98.2 1.4 %collective-permute-done.37.refs_3_ = f32[40,512]{1,0:T(8,128)S(1)} collective-permute-done((f32[40,512]{1,0:T(8,128)S(1)}, f32[40,512]{1,0:T(8,128)S(1)}, u32[]{:S(2)}, u32[]{:S(2)}) %collective-permute-start.37) | collective-permute-done | bytes 81952 | tf_op jit(solution)/shard_map/ppermute | solution.py:127
  100.1 2.4 %collective-permute-start.39 = (f32[32,512]{1,0:T(8,128)S(1)}, f32[32,512]{1,0:T(8,128)S(1)}, u32[]{:S(2)}, u32[]{:S(2)}) collective-permute-start(f32[32,512]{1,0:T(8,128)S(1)} %get-tuple-element.97), channel_id=1, source_target_pairs={{0,2},{1,3},{2,0},{3,1},{4,6},{5,7},{6,4},{7,5},{8,10},{9,11},{10,... | collective-permute-start | bytes 196616 | tf_op jit(solution)/shard_map/ppermute | solution.py:127
  102.5 2.0 %collective-permute-start.40 = (f32[32,512]{1,0:T(8,128)S(1)}, f32[32,512]{1,0:T(8,128)S(1)}, u32[]{:S(2)}, u32[]{:S(2)}) collective-permute-start(f32[32,512]{1,0:T(8,128)S(1)} %get-tuple-element.98), channel_id=1, source_target_pairs={{0,3},{1,2},{2,1},{3,0},{4,7},{5,6},{6,5},{7,4},{8,11},{9,10},{10,... | collective-permute-start | bytes 196616 | tf_op jit(solution)/shard_map/ppermute | solution.py:127
  104.5 0.9 collective-permute-done.39.refs_2_
  105.4 3.2 %collective-permute-done.40.refs_3_ = f32[32,512]{1,0:T(8,128)S(1)} collective-permute-done((f32[32,512]{1,0:T(8,128)S(1)}, f32[32,512]{1,0:T(8,128)S(1)}, u32[]{:S(2)}, u32[]{:S(2)}) %collective-permute-start.40) | collective-permute-done | bytes 65568 | tf_op jit(solution)/shard_map/ppermute | solution.py:127
  108.7 1.2 %collective-permute-done.41.refs_1_ = f32[32,512]{1,0:T(8,128)S(1)} collective-permute-done((f32[32,512]{1,0:T(8,128)S(1)}, f32[32,512]{1,0:T(8,128)S(1)}, u32[]{:S(2)}, u32[]{:S(2)}) %collective-permute-start.41) | collective-permute-done | bytes 65568 | tf_op jit(solution)/shard_map/ppermute | solution.py:127
  109.9 0.7 shard_map.201
  (51 shorter events, 2.8 us)
Async XLA Ops:
  0.6 10.1 %collective-permute-start.1 = (f32[2,256,512]{2,1,0:T(8,128)}, f32[2,256,512]{2,1,0:T(8,128)}, u32[]{:S(2)}, u32[]{:S(2)}) collective-permute-start(f32[2,256,512]{2,1,0:T(8,128)} %refs_0_.5), channel_id=1, source_target_pairs={{0,4},{4,0},{8,12},{12,8},{16,20},{20,16},{24,28},{28,24},{1,5},{5... | collective-permute-start | bytes 3145736 | tf_op jit(solution)/shard_map/ppermute | solution.py:127
  1.1 9.5 %collective-permute-start.2 = (f32[256,512]{1,0:T(8,128)}, f32[256,512]{1,0:T(8,128)}, u32[]{:S(2)}, u32[]{:S(2)}) collective-permute-start(f32[256,512]{1,0:T(8,128)} %refs_0_.4), channel_id=1, source_target_pairs={{0,4},{4,0},{8,12},{12,8},{16,20},{20,16},{24,28},{28,24},{1,5},{5... | collective-permute-start | bytes 1572872 | tf_op jit(solution)/shard_map/ppermute | solution.py:127
  1.2 15.6 %collective-permute-start.5 = (f32[256,512]{1,0:T(8,128)}, f32[256,512]{1,0:T(8,128)}, u32[]{:S(2)}, u32[]{:S(2)}) collective-permute-start(f32[256,512]{1,0:T(8,128)} %refs_0_.4), channel_id=1, source_target_pairs={{0,16},{4,20},{8,24},{12,28},{16,0},{20,4},{24,8},{28,12},{1,17},{... | collective-permute-start | bytes 1572872 | tf_op jit(solution)/shard_map/ppermute | solution.py:127
  4.2 15.1 %collective-permute-start.4 = (f32[256,512]{1,0:T(8,128)}, f32[256,512]{1,0:T(8,128)}, u32[]{:S(2)}, u32[]{:S(2)}) collective-permute-start(f32[256,512]{1,0:T(8,128)} %refs_0_.4), channel_id=1, source_target_pairs={{0,8},{4,12},{8,0},{12,4},{16,24},{20,28},{24,16},{28,20},{1,9},{5... | collective-permute-start | bytes 1572872 | tf_op jit(solution)/shard_map/ppermute | solution.py:127
  8.8 1.8 %collective-permute-start = (f32[6,64,128]{2,1,0:T(8,128)}, f32[6,64,128]{2,1,0:T(8,128)}, u32[]{:S(2)}, u32[]{:S(2)}) collective-permute-start(f32[6,64,128]{2,1,0:T(8,128)} %get-tuple-element.55), channel_id=1, source_target_pairs={{0,4},{4,0},{8,12},{12,8},{16,20},{20,16},{24,28},{28,24},{1,5},{5... | collective-permute-start | bytes 589832 | tf_op jit(solution)/shard_map/ppermute | solution.py:127
  13.2 7.7 %collective-permute-start.3 = (f32[4,64,128]{2,1,0:T(8,128)}, f32[4,64,128]{2,1,0:T(8,128)}, u32[]{:S(2)}, u32[]{:S(2)}) collective-permute-start(f32[4,64,128]{2,1,0:T(8,128)} %get-tuple-element.58), channel_id=1, source_target_pairs={{0,8},{4,12},{8,0},{12,4},{16,24},{20,28},{24,16},{28,20},{1,9},{5... | collective-permute-start | bytes 393224 | tf_op jit(solution)/shard_map/ppermute | solution.py:127
  13.8 14.2 %collective-permute-start.9 = (f32[1,256,512]{2,1,0:T(8,128)}, f32[1,256,512]{2,1,0:T(8,128)}, u32[]{:S(2)}, u32[]{:S(2)}) collective-permute-start(f32[1,256,512]{2,1,0:T(8,128)} %get-tuple-element.62), channel_id=1, source_target_pairs={{0,16},{4,20},{8,24},{12,28},{16,0},{20,4},{24,8},{28,12},{1,17},{... | collective-permute-start | bytes 1572872 | tf_op jit(solution)/shard_map/ppermute | solution.py:127
  24.4 3.6 %collective-permute-start.8 = (f32[1,256,512]{2,1,0:T(8,128)}, f32[1,256,512]{2,1,0:T(8,128)S(1)}, u32[]{:S(2)}, u32[]{:S(2)}) collective-permute-start(f32[1,256,512]{2,1,0:T(8,128)} %get-tuple-element.60.refs_1_), channel_id=1, source_target_pairs={{0,4},{4,0},{8,12},{12,8},{16,20},{20,16},{24,28},{28,24},{1,5},{5... | collective-permute-start | bytes 1572872 | tf_op jit(solution)/shard_map/ppermute | solution.py:127
  24.5 14.6 %collective-permute-start.6 = (f32[1,256,512]{2,1,0:T(8,128)}, f32[1,256,512]{2,1,0:T(8,128)S(1)}, u32[]{:S(2)}, u32[]{:S(2)}) collective-permute-start(f32[1,256,512]{2,1,0:T(8,128)} %get-tuple-element.60.refs_1_), channel_id=1, source_target_pairs={{0,16},{4,20},{8,24},{12,28},{16,0},{20,4},{24,8},{28,12},{1,17},{... | collective-permute-start | bytes 1572872 | tf_op jit(solution)/shard_map/ppermute | solution.py:127
  24.8 14.2 %collective-permute-start.7 = (f32[1,256,512]{2,1,0:T(8,128)}, f32[1,256,512]{2,1,0:T(8,128)S(1)}, u32[]{:S(2)}, u32[]{:S(2)}) collective-permute-start(f32[1,256,512]{2,1,0:T(8,128)} %get-tuple-element.61), channel_id=1, source_target_pairs={{0,8},{4,12},{8,0},{12,4},{16,24},{20,28},{24,16},{28,20},{1,9},{5... | collective-permute-start | bytes 1572872 | tf_op jit(solution)/shard_map/ppermute | solution.py:127
  26.5 1.5 %collective-permute-start.10 = (f32[32,512]{1,0:T(8,128)}, f32[32,512]{1,0:T(8,128)S(1)}, u32[]{:S(2)}, u32[]{:S(2)}) collective-permute-start(f32[32,512]{1,0:T(8,128)} %get-tuple-element.64), channel_id=1, source_target_pairs={{0,4},{4,0},{8,12},{12,8},{16,20},{20,16},{24,28},{28,24},{1,5},{5... | collective-permute-start | bytes 196616 | tf_op jit(solution)/shard_map/ppermute | solution.py:127
  28.0 0.8 copy-start.4
  28.9 10.6 %copy-start.5 = (f32[32,512]{1,0:T(8,128)S(1)}, f32[32,512]{1,0:T(8,128)}, u32[]{:S(2)}) copy-start(f32[32,512]{1,0:T(8,128)} %get-tuple-element.63.refs_2_.refs_8_) | copy-start | bytes 196612
  28.9 10.2 %collective-permute-start.11 = (f32[32,512]{1,0:T(8,128)S(1)}, f32[32,512]{1,0:T(8,128)S(1)}, u32[]{:S(2)}, u32[]{:S(2)}) collective-permute-start(f32[32,512]{1,0:T(8,128)S(1)} %shard_map.186.refs_2_), channel_id=1, source_target_pairs={{0,1},{1,0},{2,3},{3,2},{4,5},{5,4},{6,7},{7,6},{8,9},{9,8},{10,11... | collective-permute-start | bytes 196616 | tf_op jit(solution)/shard_map/ppermute | solution.py:127
  30.8 8.3 %collective-permute-start.12 = (f32[32,512]{1,0:T(8,128)S(1)}, f32[32,512]{1,0:T(8,128)S(1)}, u32[]{:S(2)}, u32[]{:S(2)}) collective-permute-start(f32[32,512]{1,0:T(8,128)S(1)} %shard_map.186.refs_2_), channel_id=1, source_target_pairs={{0,2},{1,3},{2,0},{3,1},{4,6},{5,7},{6,4},{7,5},{8,10},{9,11},{10,... | collective-permute-start | bytes 196616 | tf_op jit(solution)/shard_map/ppermute | solution.py:127
  33.4 6.1 %collective-permute-start.13 = (f32[32,512]{1,0:T(8,128)S(1)}, f32[32,512]{1,0:T(8,128)S(1)}, u32[]{:S(2)}, u32[]{:S(2)}) collective-permute-start(f32[32,512]{1,0:T(8,128)S(1)} %shard_map.186.refs_2_), channel_id=1, source_target_pairs={{0,3},{1,2},{2,1},{3,0},{4,7},{5,6},{6,5},{7,4},{8,11},{9,10},{10,... | collective-permute-start | bytes 196616 | tf_op jit(solution)/shard_map/ppermute | solution.py:127
  33.4 1.2 %copy-start = (f32[2,256,512]{2,1,0:T(8,128)S(1)}, f32[2,256,512]{2,1,0:T(8,128)}, u32[]{:S(2)}) copy-start(f32[2,256,512]{2,1,0:T(8,128)} %refs_0_.5) | copy-start | bytes 3145732
  39.9 14.7 %copy-start.2 = (f32[256,512]{1,0:T(8,128)S(1)}, f32[256,512]{1,0:T(8,128)}, u32[]{:S(2)}) copy-start(f32[256,512]{1,0:T(8,128)} %refs_0_.4) | copy-start | bytes 1572868
  39.9 14.7 %copy-start.3 = (f32[1,256,512]{2,1,0:T(8,128)S(1)}, f32[1,256,512]{2,1,0:T(8,128)}, u32[]{:S(2)}) copy-start(f32[1,256,512]{2,1,0:T(8,128)} %get-tuple-element.60.refs_1_) | copy-start | bytes 1572868
  39.9 9.6 %collective-permute-start.14 = (f32[256,512]{1,0:T(8,128)}, f32[256,512]{1,0:T(8,128)S(1)}, u32[]{:S(2)}, u32[]{:S(2)}) collective-permute-start(f32[256,512]{1,0:T(8,128)} %get-tuple-element.68.refs_2_), channel_id=1, source_target_pairs={{0,4},{4,0},{8,12},{12,8},{16,20},{20,16},{24,28},{28,24},{1,5},{5... | collective-permute-start | bytes 1572872 | tf_op jit(solution)/shard_map/ppermute | solution.py:127
  40.0 9.5 %collective-permute-start.15 = (f32[1,256,512]{2,1,0:T(8,128)S(1)}, f32[1,256,512]{2,1,0:T(8,128)S(1)}, u32[]{:S(2)}, u32[]{:S(2)}) collective-permute-start(f32[1,256,512]{2,1,0:T(8,128)S(1)} %get-tuple-element.69.refs_3_), channel_id=1, source_target_pairs={{0,4},{4,0},{8,12},{12,8},{16,20},{20,16},{24,28},{28,24},{1,5},{5... | collective-permute-start | bytes 1572872 | tf_op jit(solution)/shard_map/ppermute | solution.py:127
  40.5 4.4 %collective-permute-start.16 = (f32[40,512]{1,0:T(8,128)S(1)}, f32[40,512]{1,0:T(8,128)S(1)}, u32[]{:S(2)}, u32[]{:S(2)}) collective-permute-start(f32[40,512]{1,0:T(8,128)S(1)} %get-tuple-element.71), channel_id=1, source_target_pairs={{0,8},{4,12},{8,0},{12,4},{16,24},{20,28},{24,16},{28,20},{1,9},{5... | collective-permute-start | bytes 245768 | tf_op jit(solution)/shard_map/ppermute | solution.py:127
  41.9 5.7 %collective-permute-start.17 = (f32[40,512]{1,0:T(8,128)S(1)}, f32[40,512]{1,0:T(8,128)S(1)}, u32[]{:S(2)}, u32[]{:S(2)}) collective-permute-start(f32[40,512]{1,0:T(8,128)S(1)} %get-tuple-element.72), channel_id=1, source_target_pairs={{0,16},{4,20},{8,24},{12,28},{16,0},{20,4},{24,8},{28,12},{1,17},{... | collective-permute-start | bytes 245768 | tf_op jit(solution)/shard_map/ppermute | solution.py:127
  44.2 5.3 %collective-permute-start.18 = (f32[40,512]{1,0:T(8,128)S(1)}, f32[40,512]{1,0:T(8,128)S(1)}, u32[]{:S(2)}, u32[]{:S(2)}) collective-permute-start(f32[40,512]{1,0:T(8,128)S(1)} %get-tuple-element.67.refs_2_), channel_id=1, source_target_pairs={{0,24},{4,28},{8,16},{12,20},{16,8},{20,12},{24,0},{28,4},{1,25},{... | collective-permute-start | bytes 245768 | tf_op jit(solution)/shard_map/ppermute | solution.py:127
  49.6 12.5 %collective-permute-start.25 = (f32[1,256,512]{2,1,0:T(8,128)}, f32[1,256,512]{2,1,0:T(8,128)S(1)}, u32[]{:S(2)}, u32[]{:S(2)}) collective-permute-start(f32[1,256,512]{2,1,0:T(8,128)} %shard_map.193.refs_2_), channel_id=1, source_target_pairs={{0,8},{4,12},{8,0},{12,4},{16,24},{20,28},{24,16},{28,20},{1,9},{5... | collective-permute-start | bytes 1572872 | tf_op jit(solution)/shard_map/ppermute | solution.py:127
  50.2 6.5 %collective-permute-start.19 = (f32[40,512]{1,0:T(8,128)S(1)}, f32[40,512]{1,0:T(8,128)S(1)}, u32[]{:S(2)}, u32[]{:S(2)}) collective-permute-start(f32[40,512]{1,0:T(8,128)S(1)} %get-tuple-element.74), channel_id=1, source_target_pairs={{0,1},{1,0},{2,3},{3,2},{4,5},{5,4},{6,7},{7,6},{8,9},{9,8},{10,11... | collective-permute-start | bytes 245768 | tf_op jit(solution)/shard_map/ppermute | solution.py:127
  50.9 7.1 %collective-permute-start.20 = (f32[40,512]{1,0:T(8,128)S(1)}, f32[40,512]{1,0:T(8,128)S(1)}, u32[]{:S(2)}, u32[]{:S(2)}) collective-permute-start(f32[40,512]{1,0:T(8,128)S(1)} %get-tuple-element.75), channel_id=1, source_target_pairs={{0,2},{1,3},{2,0},{3,1},{4,6},{5,7},{6,4},{7,5},{8,10},{9,11},{10,... | collective-permute-start | bytes 245768 | tf_op jit(solution)/shard_map/ppermute | solution.py:127
  53.5 6.3 %collective-permute-start.21 = (f32[40,512]{1,0:T(8,128)S(1)}, f32[40,512]{1,0:T(8,128)S(1)}, u32[]{:S(2)}, u32[]{:S(2)}) collective-permute-start(f32[40,512]{1,0:T(8,128)S(1)} %get-tuple-element.76.refs_1_), channel_id=1, source_target_pairs={{0,3},{1,2},{2,1},{3,0},{4,7},{5,6},{6,5},{7,4},{8,11},{9,10},{10,... | collective-permute-start | bytes 245768 | tf_op jit(solution)/shard_map/ppermute | solution.py:127
  54.5 11.3 %collective-permute-start.27 = (f32[1,256,512]{2,1,0:T(8,128)}, f32[1,256,512]{2,1,0:T(8,128)S(1)}, u32[]{:S(2)}, u32[]{:S(2)}) collective-permute-start(f32[1,256,512]{2,1,0:T(8,128)} %shard_map.193.refs_2_), channel_id=1, source_target_pairs={{0,4},{4,0},{8,12},{12,8},{16,20},{20,16},{24,28},{28,24},{1,5},{5... | collective-permute-start | bytes 1572872 | tf_op jit(solution)/shard_map/ppermute | solution.py:127
  59.7 7.2 %copy-start.1 = (f32[2,256,512]{2,1,0:T(8,128)S(1)}, f32[2,256,512]{2,1,0:T(8,128)}, u32[]{:S(2)}) copy-start(f32[2,256,512]{2,1,0:T(8,128)} %refs_0_.5) | copy-start | bytes 3145732
  62.0 4.9 %collective-permute-start.26 = (f32[1,256,512]{2,1,0:T(8,128)S(1)}, f32[1,256,512]{2,1,0:T(8,128)S(1)}, u32[]{:S(2)}, u32[]{:S(2)}) collective-permute-start(f32[1,256,512]{2,1,0:T(8,128)S(1)} %get-tuple-element.79.refs_1_), channel_id=1, source_target_pairs={{0,4},{4,0},{8,12},{12,8},{16,20},{20,16},{24,28},{28,24},{1,5},{5... | collective-permute-start | bytes 1572872 | tf_op jit(solution)/shard_map/ppermute | solution.py:127
  62.0 4.9 %collective-permute-start.28 = (f32[1,256,512]{2,1,0:T(8,128)S(1)}, f32[1,256,512]{2,1,0:T(8,128)S(1)}, u32[]{:S(2)}, u32[]{:S(2)}) collective-permute-start(f32[1,256,512]{2,1,0:T(8,128)S(1)} %get-tuple-element.80.refs_3_), channel_id=1, source_target_pairs={{0,4},{4,0},{8,12},{12,8},{16,20},{20,16},{24,28},{28,24},{1,5},{5... | collective-permute-start | bytes 1572872 | tf_op jit(solution)/shard_map/ppermute | solution.py:127
  62.5 6.5 %collective-permute-start.22 = (f32[32,512]{1,0:T(8,128)S(1)}, f32[32,512]{1,0:T(8,128)S(1)}, u32[]{:S(2)}, u32[]{:S(2)}) collective-permute-start(f32[32,512]{1,0:T(8,128)S(1)} %shard_map.192.refs_2_.refs_0_), channel_id=1, source_target_pairs={{0,1},{1,0},{2,3},{3,2},{4,5},{5,4},{6,7},{7,6},{8,9},{9,8},{10,11... | collective-permute-start | bytes 196616 | tf_op jit(solution)/shard_map/ppermute | solution.py:127
  63.3 7.7 %collective-permute-start.23 = (f32[32,512]{1,0:T(8,128)S(1)}, f32[32,512]{1,0:T(8,128)S(1)}, u32[]{:S(2)}, u32[]{:S(2)}) collective-permute-start(f32[32,512]{1,0:T(8,128)S(1)} %shard_map.192.refs_2_.refs_0_), channel_id=1, source_target_pairs={{0,2},{1,3},{2,0},{3,1},{4,6},{5,7},{6,4},{7,5},{8,10},{9,11},{10,... | collective-permute-start | bytes 196616 | tf_op jit(solution)/shard_map/ppermute | solution.py:127
  65.9 6.2 %collective-permute-start.24 = (f32[32,512]{1,0:T(8,128)S(1)}, f32[32,512]{1,0:T(8,128)S(1)}, u32[]{:S(2)}, u32[]{:S(2)}) collective-permute-start(f32[32,512]{1,0:T(8,128)S(1)} %shard_map.192.refs_2_.refs_0_), channel_id=1, source_target_pairs={{0,3},{1,2},{2,1},{3,0},{4,7},{5,6},{6,5},{7,4},{8,11},{9,10},{10,... | collective-permute-start | bytes 196616 | tf_op jit(solution)/shard_map/ppermute | solution.py:127
  74.1 5.0 %collective-permute-start.29 = (f32[32,512]{1,0:T(8,128)S(1)}, f32[32,512]{1,0:T(8,128)S(1)}, u32[]{:S(2)}, u32[]{:S(2)}) collective-permute-start(f32[32,512]{1,0:T(8,128)S(1)} %get-tuple-element.84), channel_id=1, source_target_pairs={{0,1},{1,0},{2,3},{3,2},{4,5},{5,4},{6,7},{7,6},{8,9},{9,8},{10,11... | collective-permute-start | bytes 196616 | tf_op jit(solution)/shard_map/ppermute | solution.py:127
  75.0 6.2 %collective-permute-start.30 = (f32[32,512]{1,0:T(8,128)S(1)}, f32[32,512]{1,0:T(8,128)S(1)}, u32[]{:S(2)}, u32[]{:S(2)}) collective-permute-start(f32[32,512]{1,0:T(8,128)S(1)} %get-tuple-element.85), channel_id=1, source_target_pairs={{0,2},{1,3},{2,0},{3,1},{4,6},{5,7},{6,4},{7,5},{8,10},{9,11},{10,... | collective-permute-start | bytes 196616 | tf_op jit(solution)/shard_map/ppermute | solution.py:127
  76.6 6.1 %collective-permute-start.31 = (f32[32,512]{1,0:T(8,128)S(1)}, f32[32,512]{1,0:T(8,128)S(1)}, u32[]{:S(2)}, u32[]{:S(2)}) collective-permute-start(f32[32,512]{1,0:T(8,128)S(1)} %get-tuple-element.86), channel_id=1, source_target_pairs={{0,3},{1,2},{2,1},{3,0},{4,7},{5,6},{6,5},{7,4},{8,11},{9,10},{10,... | collective-permute-start | bytes 196616 | tf_op jit(solution)/shard_map/ppermute | solution.py:127
  83.9 6.1 %collective-permute-start.32 = (f32[40,512]{1,0:T(8,128)S(1)}, f32[40,512]{1,0:T(8,128)S(1)}, u32[]{:S(2)}, u32[]{:S(2)}) collective-permute-start(f32[40,512]{1,0:T(8,128)S(1)} %get-tuple-element.88), channel_id=1, source_target_pairs={{0,1},{1,0},{2,3},{3,2},{4,5},{5,4},{6,7},{7,6},{8,9},{9,8},{10,11... | collective-permute-start | bytes 245768 | tf_op jit(solution)/shard_map/ppermute | solution.py:127
  84.0 6.1 %collective-permute-start.33 = (f32[40,512]{1,0:T(8,128)S(1)}, f32[40,512]{1,0:T(8,128)S(1)}, u32[]{:S(2)}, u32[]{:S(2)}) collective-permute-start(f32[40,512]{1,0:T(8,128)S(1)} %get-tuple-element.89), channel_id=1, source_target_pairs={{0,2},{1,3},{2,0},{3,1},{4,6},{5,7},{6,4},{7,5},{8,10},{9,11},{10,... | collective-permute-start | bytes 245768 | tf_op jit(solution)/shard_map/ppermute | solution.py:127
  86.5 6.2 %collective-permute-start.34 = (f32[40,512]{1,0:T(8,128)S(1)}, f32[40,512]{1,0:T(8,128)S(1)}, u32[]{:S(2)}, u32[]{:S(2)}) collective-permute-start(f32[40,512]{1,0:T(8,128)S(1)} %get-tuple-element.90), channel_id=1, source_target_pairs={{0,3},{1,2},{2,1},{3,0},{4,7},{5,6},{6,5},{7,4},{8,11},{9,10},{10,... | collective-permute-start | bytes 245768 | tf_op jit(solution)/shard_map/ppermute | solution.py:127
  92.8 4.5 %collective-permute-start.35 = (f32[40,512]{1,0:T(8,128)S(1)}, f32[40,512]{1,0:T(8,128)S(1)}, u32[]{:S(2)}, u32[]{:S(2)}) collective-permute-start(f32[40,512]{1,0:T(8,128)S(1)} %get-tuple-element.92), channel_id=1, source_target_pairs={{0,8},{4,12},{8,0},{12,4},{16,24},{20,28},{24,16},{28,20},{1,9},{5... | collective-permute-start | bytes 245768 | tf_op jit(solution)/shard_map/ppermute | solution.py:127
  93.7 4.4 %collective-permute-start.36 = (f32[40,512]{1,0:T(8,128)S(1)}, f32[40,512]{1,0:T(8,128)S(1)}, u32[]{:S(2)}, u32[]{:S(2)}) collective-permute-start(f32[40,512]{1,0:T(8,128)S(1)} %get-tuple-element.93), channel_id=1, source_target_pairs={{0,16},{4,20},{8,24},{12,28},{16,0},{20,4},{24,8},{28,12},{1,17},{... | collective-permute-start | bytes 245768 | tf_op jit(solution)/shard_map/ppermute | solution.py:127
  94.3 5.3 %collective-permute-start.37 = (f32[40,512]{1,0:T(8,128)S(1)}, f32[40,512]{1,0:T(8,128)S(1)}, u32[]{:S(2)}, u32[]{:S(2)}) collective-permute-start(f32[40,512]{1,0:T(8,128)S(1)} %get-tuple-element.94), channel_id=1, source_target_pairs={{0,24},{4,28},{8,16},{12,20},{16,8},{20,12},{24,0},{28,4},{1,25},{... | collective-permute-start | bytes 245768 | tf_op jit(solution)/shard_map/ppermute | solution.py:127
  100.1 4.5 %collective-permute-start.38 = (f32[32,512]{1,0:T(8,128)S(1)}, f32[32,512]{1,0:T(8,128)S(1)}, u32[]{:S(2)}, u32[]{:S(2)}) collective-permute-start(f32[32,512]{1,0:T(8,128)S(1)} %get-tuple-element.96), channel_id=1, source_target_pairs={{0,1},{1,0},{2,3},{3,2},{4,5},{5,4},{6,7},{7,6},{8,9},{9,8},{10,11... | collective-permute-start | bytes 196616 | tf_op jit(solution)/shard_map/ppermute | solution.py:127
  100.1 5.2 %collective-permute-start.39 = (f32[32,512]{1,0:T(8,128)S(1)}, f32[32,512]{1,0:T(8,128)S(1)}, u32[]{:S(2)}, u32[]{:S(2)}) collective-permute-start(f32[32,512]{1,0:T(8,128)S(1)} %get-tuple-element.97), channel_id=1, source_target_pairs={{0,2},{1,3},{2,0},{3,1},{4,6},{5,7},{6,4},{7,5},{8,10},{9,11},{10,... | collective-permute-start | bytes 196616 | tf_op jit(solution)/shard_map/ppermute | solution.py:127
  102.5 6.1 %collective-permute-start.40 = (f32[32,512]{1,0:T(8,128)S(1)}, f32[32,512]{1,0:T(8,128)S(1)}, u32[]{:S(2)}, u32[]{:S(2)}) collective-permute-start(f32[32,512]{1,0:T(8,128)S(1)} %get-tuple-element.98), channel_id=1, source_target_pairs={{0,3},{1,2},{2,1},{3,0},{4,7},{5,6},{6,5},{7,4},{8,11},{9,10},{10,... | collective-permute-start | bytes 196616 | tf_op jit(solution)/shard_map/ppermute | solution.py:127
  108.6 1.3 %collective-permute-start.41 = (f32[32,512]{1,0:T(8,128)S(1)}, f32[32,512]{1,0:T(8,128)S(1)}, u32[]{:S(2)}, u32[]{:S(2)}) collective-permute-start(f32[32,512]{1,0:T(8,128)S(1)} %get-tuple-element.101), channel_id=1, source_target_pairs={{0,4},{4,0},{8,12},{12,8},{16,20},{20,16},{24,28},{28,24},{1,5},{5... | collective-permute-start | bytes 196616 | tf_op jit(solution)/shard_map/ppermute | solution.py:127

commit v6 on v5

--- a/solution.py
+++ b/solution.py
@@ -274,16 +274,18 @@
         high[where, :], low[where, :] = halves(block[...])
 
 
-def assemble(parts):
+def assemble(parts, stacks=()):
     rows, width = parts[0][0].shape[-2:]
     panel = ((rows * lax.axis_size("leaf"), width), jnp.bfloat16)
-    return kernel_call(assemble_kernel, [panel, panel], [], [], loaded=parts)
-
-
-def pair_kernel(place, own, other, high, low):
-    rows = own.shape[0]
-    high[:rows, :], low[:rows, :] = halves(own[...])
-    high[rows:, :], low[rows:, :] = halves(other[...])
+    return kernel_call(assemble_kernel, [panel, panel], [], [], loaded=parts, stacks=stacks)
+
+
+def pair_kernel(place, *refs):
+    *blocks, high, low = refs
+    rows, width = blocks[0].shape
+    for n, block in enumerate(blocks):
+        where = slice(n % 2 * rows, (n % 2 + 1) * rows), slice(n // 2 * width, (n // 2 + 1) * width)
+        high[where], low[where] = halves(block[...])
 
 
 def first_kernel(place, *refs):
@@ -330,9 +332,12 @@
 
 
 def coupled_kernel(place, *refs):
-    parts, (high, low, result) = refs[:-3], refs[-3:]
+    parts, (high, low, result, first) = refs[:-4], refs[-4:]
     rest = jnp.concatenate([part[len(parts) * GROUP :, :] for part in parts], 0)
     result[...] = rest - gathered_product(place, parts, high, low)
+    for n in range(4):
+        start = (n // 2 ^ n % 2 * 2) * GROUP
+        first[n * GROUP : (n + 1) * GROUP, :] = parts[n // 2][start : start + GROUP, :]
 
 
 def scatter_product(place, values, high, low, sent):
@@ -355,10 +360,14 @@
     parts, (high, low), sent = refs[:count], refs[count : count + 2], refs[count + 2 :]
     total = sum(part[...] for part in parts[1:]) + parts[0][...]
     rows, width = total.shape
+    values = []
+    for g in range(count):
+        where = span(place[1] ^ g, width)
+        values.append(product(total, high[where, :], low[where, :], 1))
     for e, part in enumerate(sent):
-        where = span(place[1] ^ e, width)
-        value = product(total, high[where, :], low[where, :], 1)
-        part[:rows, :] = regroup(value, e, count)
+        for n in range(count):
+            start = (e ^ n % 2 * 2) * GROUP
+            part[n * GROUP : (n + 1) * GROUP, :] = values[e ^ n // 2][start : start + GROUP]
         part[rows:, :] = total[e * GROUP : (e + 1) * GROUP]
 
 
@@ -375,29 +384,23 @@
 
 
 def last_kernel(place, *refs):
-    count = (len(refs) - 4) // 2
-    parts, (high, low), last, sent, joined = (
-        refs[:count],
-        refs[count : count + 2],
-        refs[-2],
-        refs[count + 2 : -2],
-        refs[-1],
-    )
-    rows = parts[0].shape[0] - GROUP
+    *parts, high, low, own, other, last, joined = refs
+    rows = own.shape[0]
     chip = place[0] >> 1
     for f, part in enumerate(parts):
-        for e in range(count):
-            joined[e, span(chip ^ f, GROUP), :] = part[e * GROUP : (e + 1) * GROUP, :]
-        last[span(chip ^ f, GROUP), :] = part[rows:, :]
-    values = jnp.concatenate([joined[e] for e in range(count)], 0)
-    values = product(values, high[...], low[...], 1)
-    for e, part in enumerate(sent):
-        part[...] = values[e * rows : (e + 1) * rows]
+        where = span(chip ^ f, GROUP)
+        for n in range(4):
+            joined[n, where, :] = part[n * GROUP : (n + 1) * GROUP, :]
+        last[where, :] = part[rows:, :]
+    columns = [jnp.concatenate([joined[n], joined[n + 1]], 0) for n in (0, 2)]
+    values = product(jnp.concatenate(columns, 1), high[...], low[...], 1)
+    own[...] = values[:rows]
+    other[...] = values[rows:]
 
 
 def part_kernel(place, *refs):
-    parts, (last, kept, sent) = refs[:-3], refs[-3:]
-    total = sum(part[...] for part in parts[1:]) + parts[0][...]
+    own, other, last, kept, sent = refs
+    total = own[...] + other[...]
     half = total.shape[1] // 2
     lower = (place[0] & 1) == 0
     for n, panel in enumerate((total, last[...])):
@@ -504,6 +507,7 @@
     red_blocks, size = level_data[0][0].shape[:2]
     solved = ((rhs_rows, red_blocks * size), jnp.float32)
     pair = ((2 * panel_rows, own_columns), jnp.bfloat16)
+    wide = ((2 * panel_rows, 2 * own_columns), jnp.bfloat16)
     one = ((group, own_columns), jnp.float32)
     more = ((group + GROUP, own_columns), jnp.float32)
     both = ((group, panel_count * panel_rows), jnp.float32)
@@ -516,14 +520,14 @@
 
     inverse, coupling, links, order = level_data[0]
     count = right_sides.shape[1] // size
-    solved_first, kept, sent, second = kernel_call(
+    solved_first, kept, sent, second, first = kernel_call(
         lowest_kernel,
         [solved, halved(count), halved(count)],
         [front_rows, links],
         [],
         loaded=[right_sides, inverse, coupling],
         late=1,
-        stacks=[[(root_inverse, 1)]],
+        stacks=[[(root_inverse, 1)], [(root_inverse, 0)]],
         scratch=[scratch(count, rhs_rows, size)],
         room=64,
     )
@@ -531,6 +535,7 @@
     far = flip(root_coupling, "leaf", 4)
     second_far = flip(second, "leaf", 4)
     near = flip(root_coupling, "leaf", 2)
+    first = flip(first, "col", 1)
     partner_inverse = flip(root_inverse, "leaf", 1)
     partner_coupling = flip(root_coupling, "leaf", 1)
     inverse, coupling, links, next_order = level_data[1]
@@ -564,8 +569,7 @@
     received = flip(sent, "leaf", 1)
     corner = flip(near, "leaf", 4)
     second_near = flip(second, "leaf", 2)
-    partner_near = flip(near, "leaf", 1)
-    (joined,) = kernel_call(join_kernel, [both], [], [kept, received], held=[partner_near, second_far])
+    (joined,) = kernel_call(join_kernel, [both], [], [kept, received], held=[second_far, first])
 
     near_high, near_low = kernel_call(pair_kernel, [pair, pair], [], [], loaded=[(root_inverse, 0), (partner_inverse, 0)])
     parts = swap_columns([joined] * col_count)
@@ -580,29 +584,31 @@
     corner, far = gate([corner, far], [parts[-1]])
     partner_corner = flip(corner, "leaf", 1)
     partner_far = flip(far, "leaf", 1)
+    parts = swap_chips(parts)
     parts = kernel_call(
         share_kernel,
         [more] * col_count,
         [],
-        swap_chips(parts),
-        held=[partner_far, partner_corner],
+        parts,
+        held=[partner_corner],
         scratch=[scratch(chip_count, GROUP, own_columns)],
     )
-    (second_far,) = gate([second_far], [parts[-1]])
-    second_corner = flip(second_far, "leaf", 2)
-    partner_second = flip(second_far, "leaf", 1)
-    between = assemble(
+    second_near, near = gate([second_near, near], [parts[-1]])
+    second_corner = flip(second_near, "leaf", 4)
+    partner_near = flip(near, "leaf", 1)
+    *between, sides = assemble(
         [(root_coupling, None), (near, 0), (far, None), (corner, 0)]
-        + [(partner_coupling, None), (partner_near, 0), (partner_far, None), (partner_corner, 0)]
-    )
-    first_sum = parts[0]
+        + [(partner_coupling, None), (partner_near, 0), (partner_far, None), (partner_corner, 0)],
+        stacks=[[second_near, second_far]],
+    )
     parts = swap_columns(parts)
-    (left,) = kernel_call(coupled_kernel, [one], [], [*parts, *between])
-    second_near, second_corner = gate([second_near, second_corner], [left])
+    left, first_sum = kernel_call(coupled_kernel, [one, one], [], [*parts, *between])
+    sides, second_corner = gate([sides, second_corner], [left])
+    partner_sides = flip(sides, "leaf", 1)
     panel = assemble(
-        [(root_inverse, 1), (second_near, 0), (second_far, 0), (second_corner, 0)]
-        + [(partner_inverse, 1), (flip(second_near, "leaf", 1), 0)]
-        + [(partner_second, 0), (flip(second_corner, "leaf", 1), 0)]
+        [(root_inverse, 1), (sides, 0), (sides, 1), (second_corner, 0)]
+        + [(partner_inverse, 1), (partner_sides, 0), (partner_sides, 1)]
+        + [(flip(second_corner, "leaf", 1), 0)]
     )
     parts = swap_columns([left] * col_count)
     parts = kernel_call(turn_kernel, [one] * col_count, [], [*parts, *panel])
@@ -616,14 +622,22 @@
         [*parts, first_sum],
         scratch=[scratch(col_count, GROUP, own_columns)],
     )
-    *parts, last = kernel_call(
+    (first,) = gate([first], [parts[-1]])
+    first_high, first_low = kernel_call(
+        pair_kernel,
+        [wide, wide],
+        [],
+        [],
+        loaded=[(root_inverse, 0), (partner_inverse, 0), (first, 0), (flip(first, "leaf", 1), 0)],
+    )
+    own, other, last = kernel_call(
         last_kernel,
-        [one] * (col_count + 1),
-        [],
-        [*swap_chips(parts), near_high, near_low],
+        [one, one, one],
+        [],
+        [*swap_chips(parts), first_high, first_low],
         scratch=[scratch(col_count, group, own_columns)],
     )
-    kept, sent = kernel_call(part_kernel, [both, both], [], [*swap_columns(parts), last])
+    kept, sent = kernel_call(part_kernel, [both, both], [], [own, flip(other, "col", 2), last])
     (result,) = kernel_call(
         merge_kernel,
         [((rhs_rows, panel_count, panel_rows), jnp.float32)],

time: 111 us -> 110 us (level)
  Pallas kernels: 20.5 us -> 23.1 us
  starting transfers between devices: 43.4 us -> 40.8 us
  waiting for transfers between devices: 43.8 us -> 42.6 us
    pallas_call x16 -> x17, Pallas kernels: 20.5 us -> 23.1 us  [kernel_call(): pl.pallas_call(run, out_shape=out_shapes, in_specs=[far] * sum(inputs[:-2...]
    ppermute x42 -> x41, starting transfers between devices: 43.4 us -> 40.8 us  [flip(): return lax.ppermute(block, axis, [(i, i ^ distance) for i in range(count)])]
    ppermute x42 -> x41, waiting for transfers between devices: 43.8 us -> 42.6 us  [flip(): return lax.ppermute(block, axis, [(i, i ^ distance) for i in range(count)])]
  transfers between devices with their start and end apart: 42 -> 41, of which waited for: 26 -> 23; matrix products, arithmetic and copies ran while one was open for 0% -> 0% of each run, Pallas kernels for 14% -> 16%
where the time goes in v6:
time: 110 us; the launch traced here: 109 us
  waiting for transfers between devices  42.6 us (39%)
  starting transfers between devices  40.8 us (37%)
  Pallas kernels  23.1 us (21%)
  local copies, waits for them, and re-layouts  2.08 us (2%)
    ppermute x41, waiting for transfers between devices, flip(): return lax.ppermute(block, axis, [(i, i ^ distance) for i in range(count)])  42.6 us
    ppermute x41, starting transfers between devices, flip(): return lax.ppermute(block, axis, [(i, i ^ distance) for i in range(count)])  40.8 us
    pallas_call x17, Pallas kernels, kernel_call(): pl.pallas_call(run, out_shape=out_shapes, in_specs=[far] * sum(inputs[:-2...  23.1 us
  transfers between devices with their start and end apart: 41, of which 23 were waited for; matrix products, arithmetic and copies ran while one was open for 0% of the time, Pallas kernels for 16%

profile of v6, /device:TPU:0, one launch (start us, length us, event | category | flops | bytes accessed | tf_op | source)
XLA Modules:
  0.0 109.5 jit_solution(17276939952590987776)
XLA Ops:
  0.6 0.5 collective-permute-start.1
  1.2 2.9 %collective-permute-start.5 = (f32[256,512]{1,0:T(8,128)}, f32[256,512]{1,0:T(8,128)}, u32[]{:S(2)}, u32[]{:S(2)}) collective-permute-start(f32[256,512]{1,0:T(8,128)} %refs_0_.5), channel_id=1, source_target_pairs={{0,16},{4,20},{8,24},{12,28},{16,0},{20,4},{24,8},{28,12},{1,17},{... | collective-permute-start | bytes 1572872 | tf_op jit(solution)/shard_map/ppermute | solution.py:127
  4.2 1.5 %collective-permute-start.4 = (f32[256,512]{1,0:T(8,128)}, f32[256,512]{1,0:T(8,128)}, u32[]{:S(2)}, u32[]{:S(2)}) collective-permute-start(f32[256,512]{1,0:T(8,128)} %refs_0_.5), channel_id=1, source_target_pairs={{0,8},{4,12},{8,0},{12,4},{16,24},{20,28},{24,16},{28,20},{1,9},{5... | collective-permute-start | bytes 1572872 | tf_op jit(solution)/shard_map/ppermute | solution.py:127
  5.7 3.6 %shard_map.183 = (f32[64,512]{1,0:T(8,128)}, f32[6,64,128]{2,1,0:T(8,128)}, f32[6,64,128]{2,1,0:T(8,128)}, f32[1,256,512]{2,1,0:T(8,128)}, f32[1,256,512]{2,1,0:T(8,128)}) custom-call(s32[1,3]{1,0:T(1,128)} %bitcast.1, s32[4,3]{1,0:T(4,128)} %refs_1_.3, f32[64,2048]{1,0:T(8,128)} %refs_2_.3, f32[4,128,128]{2,1,0:T(8,128)} %refs_3_.2, ...), custom_call_target="tpu_custom_call" | custom-call | tf_op jit(solution)/shard_map/pallas_call | solution.py:205
  9.3 1.8 %collective-permute-done.refs_4_ = f32[6,64,128]{2,1,0:T(8,128)} collective-permute-done((f32[6,64,128]{2,1,0:T(8,128)}, f32[6,64,128]{2,1,0:T(8,128)}, u32[]{:S(2)}, u32[]{:S(2)}) %collective-permute-start) | collective-permute-done | bytes 196640 | tf_op jit(solution)/shard_map/ppermute | solution.py:127
  11.1 2.5 %shard_map.184 = (f32[64,512]{1,0:T(8,128)}, f32[4,64,128]{2,1,0:T(8,128)}, f32[4,64,128]{2,1,0:T(8,128)}) custom-call(s32[1,3]{1,0:T(1,128)} %bitcast.2, s32[4,3]{1,0:T(4,128)} %refs_1_.4, s32[1,12]{1,0:T(1,128)} %refs_2_.4, f32[6,64,128]{2,1,0:T(8,128)} %get-tuple-element.60.refs_3_, f32[6,64,128]{2,1,0:T(8,128)} %collective-permute-done.refs_4_, ...), custom_call_target="tpu_custom_call" | custom-call | tf_op jit(solution)/shard_map/pallas_call | solution.py:205
  13.6 0.6 collective-permute-start.3
  14.3 2.0 %collective-permute-start.9 = (f32[1,256,512]{2,1,0:T(8,128)}, f32[1,256,512]{2,1,0:T(8,128)}, u32[]{:S(2)}, u32[]{:S(2)}) collective-permute-start(f32[1,256,512]{2,1,0:T(8,128)} %get-tuple-element.69), channel_id=1, source_target_pairs={{0,1},{1,0},{2,3},{3,2},{4,5},{5,4},{6,7},{7,6},{8,9},{9,8},{10,11... | collective-permute-start | bytes 1572872 | tf_op jit(solution)/shard_map/ppermute | solution.py:127
  16.3 0.5 collective-permute-done.5.refs_10_.refs_1_
  16.8 2.5 %collective-permute-done.4.refs_8_ = f32[256,512]{1,0:T(8,128)} collective-permute-done((f32[256,512]{1,0:T(8,128)}, f32[256,512]{1,0:T(8,128)}, u32[]{:S(2)}, u32[]{:S(2)}) %collective-permute-start.4) | collective-permute-done | bytes 524320 | tf_op jit(solution)/shard_map/ppermute | solution.py:127
  19.3 1.6 %collective-permute-done.3.refs_5_ = f32[4,64,128]{2,1,0:T(8,128)} collective-permute-done((f32[4,64,128]{2,1,0:T(8,128)}, f32[4,64,128]{2,1,0:T(8,128)}, u32[]{:S(2)}, u32[]{:S(2)}) %collective-permute-start.3) | collective-permute-done | bytes 131104 | tf_op jit(solution)/shard_map/ppermute | solution.py:127
  20.9 3.4 %shard_map.185 = (f32[64,512]{1,0:T(8,128)}, f32[32,512]{1,0:T(8,128)}, f32[32,512]{1,0:T(8,128)}, f32[1,256,512]{2,1,0:T(8,128)}, f32[1,256,512]{2,1,0:T(8,128)}) custom-call(s32[1,3]{1,0:T(1,128)} %bitcast.3, s32[4,3]{1,0:T(4,128)} %refs_1_.5, s32[1,8]{1,0:T(1,128)} %refs_2_.5, s32[1,4]{1,0:T(1,128)} %refs_3_.3, f32[4,64,128]{2,1,0:T(8,128)} %get-tuple-element.63.refs_4_, ...), custom_call_target="tpu_custom_call" | custom-call | tf_op jit(solution)/shard_map/pallas_call | solution.py:205
  24.7 1.7 %collective-permute-start.7 = (f32[1,256,512]{2,1,0:T(8,128)}, f32[1,256,512]{2,1,0:T(8,128)S(1)}, u32[]{:S(2)}, u32[]{:S(2)}) collective-permute-start(f32[1,256,512]{2,1,0:T(8,128)} %get-tuple-element.67), channel_id=1, source_target_pairs={{0,8},{4,12},{8,0},{12,4},{16,24},{20,28},{24,16},{28,20},{1,9},{5... | collective-permute-start | bytes 1572872 | tf_op jit(solution)/shard_map/ppermute | solution.py:127
  26.4 2.9 %collective-permute-done.8.refs_0_.refs_9_ = f32[1,256,512]{2,1,0:T(8,128)} collective-permute-done((f32[1,256,512]{2,1,0:T(8,128)}, f32[1,256,512]{2,1,0:T(8,128)}, u32[]{:S(2)}, u32[]{:S(2)}) %collective-permute-start.8) | collective-permute-done | bytes 524320 | tf_op jit(solution)/shard_map/ppermute | solution.py:127
  29.4 0.8 copy-done.4
  30.2 1.6 %collective-permute-start.11 = (f32[32,512]{1,0:T(8,128)S(1)}, f32[32,512]{1,0:T(8,128)S(1)}, u32[]{:S(2)}, u32[]{:S(2)}) collective-permute-start(f32[32,512]{1,0:T(8,128)S(1)} %shard_map.186.refs_2_), channel_id=1, source_target_pairs={{0,1},{1,0},{2,3},{3,2},{4,5},{5,4},{6,7},{7,6},{8,9},{9,8},{10,11... | collective-permute-start | bytes 196616 | tf_op jit(solution)/shard_map/ppermute | solution.py:127
  31.8 2.6 %collective-permute-start.12 = (f32[32,512]{1,0:T(8,128)S(1)}, f32[32,512]{1,0:T(8,128)S(1)}, u32[]{:S(2)}, u32[]{:S(2)}) collective-permute-start(f32[32,512]{1,0:T(8,128)S(1)} %shard_map.186.refs_2_), channel_id=1, source_target_pairs={{0,2},{1,3},{2,0},{3,1},{4,6},{5,7},{6,4},{7,5},{8,10},{9,11},{10,... | collective-permute-start | bytes 196616 | tf_op jit(solution)/shard_map/ppermute | solution.py:127
  34.6 1.2 %copy-done = f32[2,256,512]{2,1,0:T(8,128)S(1)} copy-done((f32[2,256,512]{2,1,0:T(8,128)S(1)}, f32[2,256,512]{2,1,0:T(8,128)}, u32[]{:S(2)}) %copy-start) | copy-done | bytes 1048600
  35.9 1.3 %shard_map.187 = (bf16[512,512]{1,0:T(8,128)(2,1)S(1)}, bf16[512,512]{1,0:T(8,128)(2,1)S(1)}) custom-call(f32[2,256,512]{2,1,0:T(8,128)S(1)} %copy-done, f32[2,256,512]{2,1,0:T(8,128)} %collective-permute-done.1.refs_7_.refs_1_.refs_4_), custom_call_target="tpu_custom_call" | custom-call | tf_op jit(solution)/shard_map/pallas_call | solution.py:205
  37.2 1.2 %collective-permute-done.12.refs_4_ = f32[32,512]{1,0:T(8,128)S(1)} collective-permute-done((f32[32,512]{1,0:T(8,128)S(1)}, f32[32,512]{1,0:T(8,128)S(1)}, u32[]{:S(2)}, u32[]{:S(2)}) %collective-permute-start.12) | collective-permute-done | bytes 65568 | tf_op jit(solution)/shard_map/ppermute | solution.py:127
  38.4 2.1 %collective-permute-done.13.refs_5_ = f32[32,512]{1,0:T(8,128)S(1)} collective-permute-done((f32[32,512]{1,0:T(8,128)S(1)}, f32[32,512]{1,0:T(8,128)S(1)}, u32[]{:S(2)}, u32[]{:S(2)}) %collective-permute-start.13) | collective-permute-done | bytes 65568 | tf_op jit(solution)/shard_map/ppermute | solution.py:127
  40.5 0.4 shard_map.188
  41.0 1.6 %collective-permute-start.15 = (f32[40,512]{1,0:T(8,128)S(1)}, f32[40,512]{1,0:T(8,128)S(1)}, u32[]{:S(2)}, u32[]{:S(2)}) collective-permute-start(f32[40,512]{1,0:T(8,128)S(1)} %get-tuple-element.77), channel_id=1, source_target_pairs={{0,8},{4,12},{8,0},{12,4},{16,24},{20,28},{24,16},{28,20},{1,9},{5... | collective-permute-start | bytes 245768 | tf_op jit(solution)/shard_map/ppermute | solution.py:127
  42.6 1.2 %collective-permute-start.16 = (f32[40,512]{1,0:T(8,128)S(1)}, f32[40,512]{1,0:T(8,128)S(1)}, u32[]{:S(2)}, u32[]{:S(2)}) collective-permute-start(f32[40,512]{1,0:T(8,128)S(1)} %get-tuple-element.78), channel_id=1, source_target_pairs={{0,16},{4,20},{8,24},{12,28},{16,0},{20,4},{24,8},{28,12},{1,17},{... | collective-permute-start | bytes 245768 | tf_op jit(solution)/shard_map/ppermute | solution.py:127
  43.7 0.8 collective-permute-start.17
  44.6 1.3 %collective-permute-done.15.refs_2_ = f32[40,512]{1,0:T(8,128)S(1)} collective-permute-done((f32[40,512]{1,0:T(8,128)S(1)}, f32[40,512]{1,0:T(8,128)S(1)}, u32[]{:S(2)}, u32[]{:S(2)}) %collective-permute-start.15) | collective-permute-done | bytes 81952 | tf_op jit(solution)/shard_map/ppermute | solution.py:127
  45.9 1.2 %collective-permute-done.16.refs_3_ = f32[40,512]{1,0:T(8,128)S(1)} collective-permute-done((f32[40,512]{1,0:T(8,128)S(1)}, f32[40,512]{1,0:T(8,128)S(1)}, u32[]{:S(2)}, u32[]{:S(2)}) %collective-permute-start.16) | collective-permute-done | bytes 81952 | tf_op jit(solution)/shard_map/ppermute | solution.py:127
  47.1 2.0 %collective-permute-done.17.refs_4_ = f32[40,512]{1,0:T(8,128)S(1)} collective-permute-done((f32[40,512]{1,0:T(8,128)S(1)}, f32[40,512]{1,0:T(8,128)S(1)}, u32[]{:S(2)}, u32[]{:S(2)}) %collective-permute-start.17) | collective-permute-done | bytes 81952 | tf_op jit(solution)/shard_map/ppermute | solution.py:127
  49.2 1.0 collective-permute-start.26
  50.2 0.7 collective-permute-start.18
  50.9 2.6 %collective-permute-start.19 = (f32[40,512]{1,0:T(8,128)S(1)}, f32[40,512]{1,0:T(8,128)S(1)}, u32[]{:S(2)}, u32[]{:S(2)}) collective-permute-start(f32[40,512]{1,0:T(8,128)S(1)} %get-tuple-element.81), channel_id=1, source_target_pairs={{0,2},{1,3},{2,0},{3,1},{4,6},{5,7},{6,4},{7,5},{8,10},{9,11},{10,... | collective-permute-start | bytes 245768 | tf_op jit(solution)/shard_map/ppermute | solution.py:127
  53.5 1.1 %collective-permute-start.20 = (f32[40,512]{1,0:T(8,128)S(1)}, f32[40,512]{1,0:T(8,128)S(1)}, u32[]{:S(2)}, u32[]{:S(2)}) collective-permute-start(f32[40,512]{1,0:T(8,128)S(1)} %get-tuple-element.82.refs_2_), channel_id=1, source_target_pairs={{0,3},{1,2},{2,1},{3,0},{4,7},{5,6},{6,5},{7,4},{8,11},{9,10},{10,... | collective-permute-start | bytes 245768 | tf_op jit(solution)/shard_map/ppermute | solution.py:127
  54.6 2.4 %shard_map.192 = (bf16[2048,512]{1,0:T(8,128)(2,1)S(1)}, bf16[2048,512]{1,0:T(8,128)(2,1)S(1)}, f32[2,256,512]{2,1,0:T(8,128)S(1)}) custom-call(f32[256,512]{1,0:T(8,128)S(1)} %copy-done.3, f32[1,256,512]{2,1,0:T(8,128)S(1)} %get-tuple-element.83.refs_1_, f32[256,512]{1,0:T(8,128)} %get-tuple-element.84.refs_2_, ...), custom_call_target="tpu_custom_call" | custom-call | tf_op jit(solution)/shard_map/pallas_call | solution.py:205
  57.0 3.3 %collective-permute-done.19.refs_2_ = f32[40,512]{1,0:T(8,128)S(1)} collective-permute-done((f32[40,512]{1,0:T(8,128)S(1)}, f32[40,512]{1,0:T(8,128)S(1)}, u32[]{:S(2)}, u32[]{:S(2)}) %collective-permute-start.19) | collective-permute-done | bytes 81952 | tf_op jit(solution)/shard_map/ppermute | solution.py:127
  60.4 0.8 shard_map.193
  61.2 2.4 %collective-permute-done.26.refs_1_ = f32[1,256,512]{2,1,0:T(8,128)S(1)} collective-permute-done((f32[1,256,512]{2,1,0:T(8,128)S(1)}, f32[1,256,512]{2,1,0:T(8,128)S(1)}, u32[]{:S(2)}, u32[]{:S(2)}) %collective-permute-start.26) | collective-permute-done | bytes 524320 | tf_op jit(solution)/shard_map/ppermute | solution.py:127
  63.6 0.5 collective-permute-start.28
  64.1 0.7 collective-permute-start.23
  64.8 2.6 %collective-permute-start.24 = (f32[32,512]{1,0:T(8,128)S(1)}, f32[32,512]{1,0:T(8,128)S(1)}, u32[]{:S(2)}, u32[]{:S(2)}) collective-permute-start(f32[32,512]{1,0:T(8,128)S(1)} %get-tuple-element.88.refs_2_.refs_0_), channel_id=1, source_target_pairs={{0,2},{1,3},{2,0},{3,1},{4,6},{5,7},{6,4},{7,5},{8,10},{9,11},{10,... | collective-permute-start | bytes 196616 | tf_op jit(solution)/shard_map/ppermute | solution.py:127
  67.3 1.1 %collective-permute-start.25 = (f32[32,512]{1,0:T(8,128)S(1)}, f32[32,512]{1,0:T(8,128)S(1)}, u32[]{:S(2)}, u32[]{:S(2)}) collective-permute-start(f32[32,512]{1,0:T(8,128)S(1)} %get-tuple-element.88.refs_2_.refs_0_), channel_id=1, source_target_pairs={{0,3},{1,2},{2,1},{3,0},{4,7},{5,6},{6,5},{7,4},{8,11},{9,10},{10,... | collective-permute-start | bytes 196616 | tf_op jit(solution)/shard_map/ppermute | solution.py:127
  68.5 2.0 %shard_map.195 = (bf16[2048,512]{1,0:T(8,128)(2,1)S(1)}, bf16[2048,512]{1,0:T(8,128)(2,1)S(1)}) custom-call(f32[2,256,512]{2,1,0:T(8,128)S(1)} %copy-done.1, f32[2,256,512]{2,1,0:T(8,128)S(1)} %get-tuple-element.90.refs_1_.refs_2_, f32[2,256,512]{2,1,0:T(8,128)S(1)} %get-tuple-element.90.refs_1_.refs_2_, f32[1,256,512]{2,1,0:T(8,128)S(1)} %get-tuple-element.91.refs_3_, ...), custom_call_target="tpu_custom_call" | custom-call | tf_op jit(solution)/shard_map/pallas_call | solution.py:205
  70.5 1.9 %collective-permute-done.24.refs_2_ = f32[32,512]{1,0:T(8,128)S(1)} collective-permute-done((f32[32,512]{1,0:T(8,128)S(1)}, f32[32,512]{1,0:T(8,128)S(1)}, u32[]{:S(2)}, u32[]{:S(2)}) %collective-permute-start.24) | collective-permute-done | bytes 65568 | tf_op jit(solution)/shard_map/ppermute | solution.py:127
  72.5 1.1 collective-permute-done.25.refs_3_
  73.5 2.1 %shard_map.196 = (f32[32,512]{1,0:T(8,128)S(1)}, f32[32,512]{1,0:T(8,128)S(1)}, f32[32,512]{1,0:T(8,128)S(1)}, f32[32,512]{1,0:T(8,128)S(1)}) custom-call(f32[32,512]{1,0:T(8,128)S(1)} %get-tuple-element.88.refs_2_.refs_0_, f32[32,512]{1,0:T(8,128)S(1)} %collective-permute-done.23.refs_1_, f32[32,512]{1,0:T(8,128)S(1)} %collective-permute-done.24.refs_2_, ...), custom_call_target="tpu_custom_call" | custom-call | tf_op jit(solution)/shard_map/pallas_call | solution.py:205
  75.6 1.0 collective-permute-start.29
  76.6 1.5 %collective-permute-start.30 = (f32[32,512]{1,0:T(8,128)S(1)}, f32[32,512]{1,0:T(8,128)S(1)}, u32[]{:S(2)}, u32[]{:S(2)}) collective-permute-start(f32[32,512]{1,0:T(8,128)S(1)} %get-tuple-element.96), channel_id=1, source_target_pairs={{0,2},{1,3},{2,0},{3,1},{4,6},{5,7},{6,4},{7,5},{8,10},{9,11},{10,... | collective-permute-start | bytes 196616 | tf_op jit(solution)/shard_map/ppermute | solution.py:127
  78.0 2.0 %collective-permute-start.31 = (f32[32,512]{1,0:T(8,128)S(1)}, f32[32,512]{1,0:T(8,128)S(1)}, u32[]{:S(2)}, u32[]{:S(2)}) collective-permute-start(f32[32,512]{1,0:T(8,128)S(1)} %get-tuple-element.97), channel_id=1, source_target_pairs={{0,3},{1,2},{2,1},{3,0},{4,7},{5,6},{6,5},{7,4},{8,11},{9,10},{10,... | collective-permute-start | bytes 196616 | tf_op jit(solution)/shard_map/ppermute | solution.py:127
  80.0 0.6 collective-permute-done.29.refs_1_
  80.7 2.1 %collective-permute-done.30.refs_2_ = f32[32,512]{1,0:T(8,128)S(1)} collective-permute-done((f32[32,512]{1,0:T(8,128)S(1)}, f32[32,512]{1,0:T(8,128)S(1)}, u32[]{:S(2)}, u32[]{:S(2)}) %collective-permute-start.30) | collective-permute-done | bytes 65568 | tf_op jit(solution)/shard_map/ppermute | solution.py:127
  82.7 1.4 %collective-permute-done.31.refs_3_ = f32[32,512]{1,0:T(8,128)S(1)} collective-permute-done((f32[32,512]{1,0:T(8,128)S(1)}, f32[32,512]{1,0:T(8,128)S(1)}, u32[]{:S(2)}, u32[]{:S(2)}) %collective-permute-start.31) | collective-permute-done | bytes 65568 | tf_op jit(solution)/shard_map/ppermute | solution.py:127
  84.1 1.3 %shard_map.197 = (f32[40,512]{1,0:T(8,128)S(1)}, f32[40,512]{1,0:T(8,128)S(1)}, f32[40,512]{1,0:T(8,128)S(1)}, f32[40,512]{1,0:T(8,128)S(1)}) custom-call(f32[32,512]{1,0:T(8,128)S(1)} %get-tuple-element.94.refs_0_, f32[32,512]{1,0:T(8,128)S(1)} %collective-permute-done.29.refs_1_, f32[32,512]{1,0:T(8,128)S(1)} %collective-permute-done.30.refs_2_, ...), custom_call_target="tpu_custom_call" | custom-call | tf_op jit(solution)/shard_map/pallas_call | solution.py:205
  85.5 2.6 %collective-permute-start.33 = (f32[40,512]{1,0:T(8,128)S(1)}, f32[40,512]{1,0:T(8,128)S(1)}, u32[]{:S(2)}, u32[]{:S(2)}) collective-permute-start(f32[40,512]{1,0:T(8,128)S(1)} %get-tuple-element.100), channel_id=1, source_target_pairs={{0,2},{1,3},{2,0},{3,1},{4,6},{5,7},{6,4},{7,5},{8,10},{9,11},{10,... | collective-permute-start | bytes 245768 | tf_op jit(solution)/shard_map/ppermute | solution.py:127
  88.0 1.8 %collective-permute-start.34 = (f32[40,512]{1,0:T(8,128)S(1)}, f32[40,512]{1,0:T(8,128)S(1)}, u32[]{:S(2)}, u32[]{:S(2)}) collective-permute-start(f32[40,512]{1,0:T(8,128)S(1)} %get-tuple-element.101), channel_id=1, source_target_pairs={{0,3},{1,2},{2,1},{3,0},{4,7},{5,6},{6,5},{7,4},{8,11},{9,10},{10,... | collective-permute-start | bytes 245768 | tf_op jit(solution)/shard_map/ppermute | solution.py:127
  89.9 1.8 %collective-permute-done.32.refs_1_ = f32[40,512]{1,0:T(8,128)S(1)} collective-permute-done((f32[40,512]{1,0:T(8,128)S(1)}, f32[40,512]{1,0:T(8,128)S(1)}, u32[]{:S(2)}, u32[]{:S(2)}) %collective-permute-start.32) | collective-permute-done | bytes 81952 | tf_op jit(solution)/shard_map/ppermute | solution.py:127
  91.7 2.6 %collective-permute-done.34.refs_3_ = f32[40,512]{1,0:T(8,128)S(1)} collective-permute-done((f32[40,512]{1,0:T(8,128)S(1)}, f32[40,512]{1,0:T(8,128)S(1)}, u32[]{:S(2)}, u32[]{:S(2)}) %collective-permute-start.34) | collective-permute-done | bytes 81952 | tf_op jit(solution)/shard_map/ppermute | solution.py:127
  94.4 0.7 collective-permute-start.35
  95.1 0.8 collective-permute-start.36
  95.9 2.0 %collective-permute-start.37 = (f32[40,512]{1,0:T(8,128)S(1)}, f32[40,512]{1,0:T(8,128)S(1)}, u32[]{:S(2)}, u32[]{:S(2)}) collective-permute-start(f32[40,512]{1,0:T(8,128)S(1)} %get-tuple-element.106.refs_1_), channel_id=1, source_target_pairs={{0,24},{4,28},{8,16},{12,20},{16,8},{20,12},{24,0},{28,4},{1,25},{... | collective-permute-start | bytes 245768 | tf_op jit(solution)/shard_map/ppermute | solution.py:127
  98.0 1.6 %shard_map.200 = (bf16[512,1024]{1,0:T(8,128)(2,1)S(1)}, bf16[512,1024]{1,0:T(8,128)(2,1)S(1)}) custom-call(f32[2,256,512]{2,1,0:T(8,128)S(1)} %copy-done.1, f32[2,256,512]{2,1,0:T(8,128)} %collective-permute-done.1.refs_7_.refs_1_.refs_4_, f32[1,256,512]{2,1,0:T(8,128)} %shard_map.199.refs_2_, f32[1,256,512]{2,1,0:T(8,128)S(1)} %collective-permute-done.38.refs_3_), custom_call_target="tpu_custom_call" | custom-call | tf_op jit(solution)/shard_map/pallas_call | solution.py:205
  100.0 1.4 %collective-permute-done.37.refs_3_ = f32[40,512]{1,0:T(8,128)S(1)} collective-permute-done((f32[40,512]{1,0:T(8,128)S(1)}, f32[40,512]{1,0:T(8,128)S(1)}, u32[]{:S(2)}, u32[]{:S(2)}) %collective-permute-start.37) | collective-permute-done | bytes 81952 | tf_op jit(solution)/shard_map/ppermute | solution.py:127
  101.4 0.8 shard_map.201
  102.3 5.2 %collective-permute-done.39.refs_1_ = f32[32,512]{1,0:T(8,128)S(1)} collective-permute-done((f32[32,512]{1,0:T(8,128)S(1)}, f32[32,512]{1,0:T(8,128)S(1)}, u32[]{:S(2)}, u32[]{:S(2)}) %collective-permute-start.39) | collective-permute-done | bytes 65568 | tf_op jit(solution)/shard_map/ppermute | solution.py:127
  107.5 1.2 %collective-permute-done.40.refs_1_ = f32[32,512]{1,0:T(8,128)S(1)} collective-permute-done((f32[32,512]{1,0:T(8,128)S(1)}, f32[32,512]{1,0:T(8,128)S(1)}, u32[]{:S(2)}, u32[]{:S(2)}) %collective-permute-start.40) | collective-permute-done | bytes 65568 | tf_op jit(solution)/shard_map/ppermute | solution.py:127
  108.8 0.7 shard_map.203
  (51 shorter events, 1.7 us)
Async XLA Ops:
  0.6 10.5 %collective-permute-start.1 = (f32[2,256,512]{2,1,0:T(8,128)}, f32[2,256,512]{2,1,0:T(8,128)}, u32[]{:S(2)}, u32[]{:S(2)}) collective-permute-start(f32[2,256,512]{2,1,0:T(8,128)} %refs_0_.7), channel_id=1, source_target_pairs={{0,4},{4,0},{8,12},{12,8},{16,20},{20,16},{24,28},{28,24},{1,5},{5... | collective-permute-start | bytes 3145736 | tf_op jit(solution)/shard_map/ppermute | solution.py:127
  1.1 9.9 %collective-permute-start.2 = (f32[256,512]{1,0:T(8,128)}, f32[256,512]{1,0:T(8,128)}, u32[]{:S(2)}, u32[]{:S(2)}) collective-permute-start(f32[256,512]{1,0:T(8,128)} %refs_0_.5), channel_id=1, source_target_pairs={{0,4},{4,0},{8,12},{12,8},{16,20},{20,16},{24,28},{28,24},{1,5},{5... | collective-permute-start | bytes 1572872 | tf_op jit(solution)/shard_map/ppermute | solution.py:127
  1.2 15.6 %collective-permute-start.5 = (f32[256,512]{1,0:T(8,128)}, f32[256,512]{1,0:T(8,128)}, u32[]{:S(2)}, u32[]{:S(2)}) collective-permute-start(f32[256,512]{1,0:T(8,128)} %refs_0_.5), channel_id=1, source_target_pairs={{0,16},{4,20},{8,24},{12,28},{16,0},{20,4},{24,8},{28,12},{1,17},{... | collective-permute-start | bytes 1572872 | tf_op jit(solution)/shard_map/ppermute | solution.py:127
  4.2 15.1 %collective-permute-start.4 = (f32[256,512]{1,0:T(8,128)}, f32[256,512]{1,0:T(8,128)}, u32[]{:S(2)}, u32[]{:S(2)}) collective-permute-start(f32[256,512]{1,0:T(8,128)} %refs_0_.5), channel_id=1, source_target_pairs={{0,8},{4,12},{8,0},{12,4},{16,24},{20,28},{24,16},{28,20},{1,9},{5... | collective-permute-start | bytes 1572872 | tf_op jit(solution)/shard_map/ppermute | solution.py:127
  9.2 1.8 %collective-permute-start = (f32[6,64,128]{2,1,0:T(8,128)}, f32[6,64,128]{2,1,0:T(8,128)}, u32[]{:S(2)}, u32[]{:S(2)}) collective-permute-start(f32[6,64,128]{2,1,0:T(8,128)} %get-tuple-element.61), channel_id=1, source_target_pairs={{0,4},{4,0},{8,12},{12,8},{16,20},{20,16},{24,28},{28,24},{1,5},{5... | collective-permute-start | bytes 589832 | tf_op jit(solution)/shard_map/ppermute | solution.py:127
  13.6 7.3 %collective-permute-start.3 = (f32[4,64,128]{2,1,0:T(8,128)}, f32[4,64,128]{2,1,0:T(8,128)}, u32[]{:S(2)}, u32[]{:S(2)}) collective-permute-start(f32[4,64,128]{2,1,0:T(8,128)} %get-tuple-element.64), channel_id=1, source_target_pairs={{0,8},{4,12},{8,0},{12,4},{16,24},{20,28},{24,16},{28,20},{1,9},{5... | collective-permute-start | bytes 393224 | tf_op jit(solution)/shard_map/ppermute | solution.py:127
  14.2 15.1 %collective-permute-start.8 = (f32[1,256,512]{2,1,0:T(8,128)}, f32[1,256,512]{2,1,0:T(8,128)}, u32[]{:S(2)}, u32[]{:S(2)}) collective-permute-start(f32[1,256,512]{2,1,0:T(8,128)} %get-tuple-element.68), channel_id=1, source_target_pairs={{0,16},{4,20},{8,24},{12,28},{16,0},{20,4},{24,8},{28,12},{1,17},{... | collective-permute-start | bytes 1572872 | tf_op jit(solution)/shard_map/ppermute | solution.py:127
  14.3 15.1 %collective-permute-start.9 = (f32[1,256,512]{2,1,0:T(8,128)}, f32[1,256,512]{2,1,0:T(8,128)}, u32[]{:S(2)}, u32[]{:S(2)}) collective-permute-start(f32[1,256,512]{2,1,0:T(8,128)} %get-tuple-element.69), channel_id=1, source_target_pairs={{0,1},{1,0},{2,3},{3,2},{4,5},{5,4},{6,7},{7,6},{8,9},{9,8},{10,11... | collective-permute-start | bytes 1572872 | tf_op jit(solution)/shard_map/ppermute | solution.py:127
  24.4 16.1 %collective-permute-start.6 = (f32[1,256,512]{2,1,0:T(8,128)}, f32[1,256,512]{2,1,0:T(8,128)S(1)}, u32[]{:S(2)}, u32[]{:S(2)}) collective-permute-start(f32[1,256,512]{2,1,0:T(8,128)} %get-tuple-element.66.refs_1_), channel_id=1, source_target_pairs={{0,16},{4,20},{8,24},{12,28},{16,0},{20,4},{24,8},{28,12},{1,17},{... | collective-permute-start | bytes 1572872 | tf_op jit(solution)/shard_map/ppermute | solution.py:127
  24.7 15.8 %collective-permute-start.7 = (f32[1,256,512]{2,1,0:T(8,128)}, f32[1,256,512]{2,1,0:T(8,128)S(1)}, u32[]{:S(2)}, u32[]{:S(2)}) collective-permute-start(f32[1,256,512]{2,1,0:T(8,128)} %get-tuple-element.67), channel_id=1, source_target_pairs={{0,8},{4,12},{8,0},{12,4},{16,24},{20,28},{24,16},{28,20},{1,9},{5... | collective-permute-start | bytes 1572872 | tf_op jit(solution)/shard_map/ppermute | solution.py:127
  26.4 2.9 %collective-permute-start.10 = (f32[32,512]{1,0:T(8,128)}, f32[32,512]{1,0:T(8,128)S(1)}, u32[]{:S(2)}, u32[]{:S(2)}) collective-permute-start(f32[32,512]{1,0:T(8,128)} %get-tuple-element.71), channel_id=1, source_target_pairs={{0,4},{4,0},{8,12},{12,8},{16,20},{20,16},{24,28},{28,24},{1,5},{5... | collective-permute-start | bytes 196616 | tf_op jit(solution)/shard_map/ppermute | solution.py:127
  29.3 0.8 copy-start.4
  30.2 10.3 %copy-start.5 = (f32[32,512]{1,0:T(8,128)S(1)}, f32[32,512]{1,0:T(8,128)}, u32[]{:S(2)}) copy-start(f32[32,512]{1,0:T(8,128)} %get-tuple-element.70.refs_2_.refs_8_) | copy-start | bytes 196612
  30.2 7.0 %collective-permute-start.11 = (f32[32,512]{1,0:T(8,128)S(1)}, f32[32,512]{1,0:T(8,128)S(1)}, u32[]{:S(2)}, u32[]{:S(2)}) collective-permute-start(f32[32,512]{1,0:T(8,128)S(1)} %shard_map.186.refs_2_), channel_id=1, source_target_pairs={{0,1},{1,0},{2,3},{3,2},{4,5},{5,4},{6,7},{7,6},{8,9},{9,8},{10,11... | collective-permute-start | bytes 196616 | tf_op jit(solution)/shard_map/ppermute | solution.py:127
  31.8 6.6 %collective-permute-start.12 = (f32[32,512]{1,0:T(8,128)S(1)}, f32[32,512]{1,0:T(8,128)S(1)}, u32[]{:S(2)}, u32[]{:S(2)}) collective-permute-start(f32[32,512]{1,0:T(8,128)S(1)} %shard_map.186.refs_2_), channel_id=1, source_target_pairs={{0,2},{1,3},{2,0},{3,1},{4,6},{5,7},{6,4},{7,5},{8,10},{9,11},{10,... | collective-permute-start | bytes 196616 | tf_op jit(solution)/shard_map/ppermute | solution.py:127
  34.4 6.1 %collective-permute-start.13 = (f32[32,512]{1,0:T(8,128)S(1)}, f32[32,512]{1,0:T(8,128)S(1)}, u32[]{:S(2)}, u32[]{:S(2)}) collective-permute-start(f32[32,512]{1,0:T(8,128)S(1)} %shard_map.186.refs_2_), channel_id=1, source_target_pairs={{0,3},{1,2},{2,1},{3,0},{4,7},{5,6},{6,5},{7,4},{8,11},{9,10},{10,... | collective-permute-start | bytes 196616 | tf_op jit(solution)/shard_map/ppermute | solution.py:127
  34.6 1.2 %copy-start = (f32[2,256,512]{2,1,0:T(8,128)S(1)}, f32[2,256,512]{2,1,0:T(8,128)}, u32[]{:S(2)}) copy-start(f32[2,256,512]{2,1,0:T(8,128)} %refs_0_.7) | copy-start | bytes 3145732
  40.5 8.6 %copy-start.2 = (f32[1,256,512]{2,1,0:T(8,128)S(1)}, f32[1,256,512]{2,1,0:T(8,128)}, u32[]{:S(2)}) copy-start(f32[1,256,512]{2,1,0:T(8,128)} %get-tuple-element.66.refs_1_) | copy-start | bytes 1572868
  40.9 13.7 %copy-start.3 = (f32[256,512]{1,0:T(8,128)S(1)}, f32[256,512]{1,0:T(8,128)}, u32[]{:S(2)}) copy-start(f32[256,512]{1,0:T(8,128)} %refs_0_.5) | copy-start | bytes 1572868
  40.9 8.1 %collective-permute-start.14 = (f32[1,256,512]{2,1,0:T(8,128)S(1)}, f32[1,256,512]{2,1,0:T(8,128)S(1)}, u32[]{:S(2)}, u32[]{:S(2)}) collective-permute-start(f32[1,256,512]{2,1,0:T(8,128)S(1)} %get-tuple-element.75.refs_3_), channel_id=1, source_target_pairs={{0,4},{4,0},{8,12},{12,8},{16,20},{20,16},{24,28},{28,24},{1,5},{5... | collective-permute-start | bytes 1572872 | tf_op jit(solution)/shard_map/ppermute | solution.py:127
  41.0 4.9 %collective-permute-start.15 = (f32[40,512]{1,0:T(8,128)S(1)}, f32[40,512]{1,0:T(8,128)S(1)}, u32[]{:S(2)}, u32[]{:S(2)}) collective-permute-start(f32[40,512]{1,0:T(8,128)S(1)} %get-tuple-element.77), channel_id=1, source_target_pairs={{0,8},{4,12},{8,0},{12,4},{16,24},{20,28},{24,16},{28,20},{1,9},{5... | collective-permute-start | bytes 245768 | tf_op jit(solution)/shard_map/ppermute | solution.py:127
  42.6 4.5 %collective-permute-start.16 = (f32[40,512]{1,0:T(8,128)S(1)}, f32[40,512]{1,0:T(8,128)S(1)}, u32[]{:S(2)}, u32[]{:S(2)}) collective-permute-start(f32[40,512]{1,0:T(8,128)S(1)} %get-tuple-element.78), channel_id=1, source_target_pairs={{0,16},{4,20},{8,24},{12,28},{16,0},{20,4},{24,8},{28,12},{1,17},{... | collective-permute-start | bytes 245768 | tf_op jit(solution)/shard_map/ppermute | solution.py:127
  43.7 5.3 %collective-permute-start.17 = (f32[40,512]{1,0:T(8,128)S(1)}, f32[40,512]{1,0:T(8,128)S(1)}, u32[]{:S(2)}, u32[]{:S(2)}) collective-permute-start(f32[40,512]{1,0:T(8,128)S(1)} %get-tuple-element.74.refs_2_), channel_id=1, source_target_pairs={{0,24},{4,28},{8,16},{12,20},{16,8},{20,12},{24,0},{28,4},{1,25},{... | collective-permute-start | bytes 245768 | tf_op jit(solution)/shard_map/ppermute | solution.py:127
  44.6 8.9 %collective-permute-start.22 = (f32[256,512]{1,0:T(8,128)}, f32[256,512]{1,0:T(8,128)S(1)}, u32[]{:S(2)}, u32[]{:S(2)}) collective-permute-start(f32[256,512]{1,0:T(8,128)} %get-tuple-element.84.refs_2_), channel_id=1, source_target_pairs={{0,4},{4,0},{8,12},{12,8},{16,20},{20,16},{24,28},{28,24},{1,5},{5... | collective-permute-start | bytes 1572872 | tf_op jit(solution)/shard_map/ppermute | solution.py:127
  49.1 5.5 %collective-permute-start.21 = (f32[1,256,512]{2,1,0:T(8,128)S(1)}, f32[1,256,512]{2,1,0:T(8,128)S(1)}, u32[]{:S(2)}, u32[]{:S(2)}) collective-permute-start(f32[1,256,512]{2,1,0:T(8,128)S(1)} %get-tuple-element.83.refs_1_), channel_id=1, source_target_pairs={{0,4},{4,0},{8,12},{12,8},{16,20},{20,16},{24,28},{28,24},{1,5},{5... | collective-permute-start | bytes 1572872 | tf_op jit(solution)/shard_map/ppermute | solution.py:127
  49.2 14.3 %collective-permute-start.26 = (f32[1,256,512]{2,1,0:T(8,128)S(1)}, f32[1,256,512]{2,1,0:T(8,128)S(1)}, u32[]{:S(2)}, u32[]{:S(2)}) collective-permute-start(f32[1,256,512]{2,1,0:T(8,128)S(1)} %get-tuple-element.85.refs_8_), channel_id=1, source_target_pairs={{0,16},{4,20},{8,24},{12,28},{16,0},{20,4},{24,8},{28,12},{1,17},{... | collective-permute-start | bytes 1572872 | tf_op jit(solution)/shard_map/ppermute | solution.py:127
  50.2 6.8 %collective-permute-start.18 = (f32[40,512]{1,0:T(8,128)S(1)}, f32[40,512]{1,0:T(8,128)S(1)}, u32[]{:S(2)}, u32[]{:S(2)}) collective-permute-start(f32[40,512]{1,0:T(8,128)S(1)} %get-tuple-element.80), channel_id=1, source_target_pairs={{0,1},{1,0},{2,3},{3,2},{4,5},{5,4},{6,7},{7,6},{8,9},{9,8},{10,11... | collective-permute-start | bytes 245768 | tf_op jit(solution)/shard_map/ppermute | solution.py:127
  50.9 9.5 %collective-permute-start.19 = (f32[40,512]{1,0:T(8,128)S(1)}, f32[40,512]{1,0:T(8,128)S(1)}, u32[]{:S(2)}, u32[]{:S(2)}) collective-permute-start(f32[40,512]{1,0:T(8,128)S(1)} %get-tuple-element.81), channel_id=1, source_target_pairs={{0,2},{1,3},{2,0},{3,1},{4,6},{5,7},{6,4},{7,5},{8,10},{9,11},{10,... | collective-permute-start | bytes 245768 | tf_op jit(solution)/shard_map/ppermute | solution.py:127
  53.5 6.9 %collective-permute-start.20 = (f32[40,512]{1,0:T(8,128)S(1)}, f32[40,512]{1,0:T(8,128)S(1)}, u32[]{:S(2)}, u32[]{:S(2)}) collective-permute-start(f32[40,512]{1,0:T(8,128)S(1)} %get-tuple-element.82.refs_2_), channel_id=1, source_target_pairs={{0,3},{1,2},{2,1},{3,0},{4,7},{5,6},{6,5},{7,4},{8,11},{9,10},{10,... | collective-permute-start | bytes 245768 | tf_op jit(solution)/shard_map/ppermute | solution.py:127
  60.4 8.1 %copy-start.1 = (f32[2,256,512]{2,1,0:T(8,128)S(1)}, f32[2,256,512]{2,1,0:T(8,128)}, u32[]{:S(2)}) copy-start(f32[2,256,512]{2,1,0:T(8,128)} %refs_0_.7) | copy-start | bytes 3145732
  63.6 4.9 %collective-permute-start.27 = (f32[2,256,512]{2,1,0:T(8,128)S(1)}, f32[2,256,512]{2,1,0:T(8,128)S(1)}, u32[]{:S(2)}, u32[]{:S(2)}) collective-permute-start(f32[2,256,512]{2,1,0:T(8,128)S(1)} %get-tuple-element.90.refs_1_.refs_2_), channel_id=1, source_target_pairs={{0,4},{4,0},{8,12},{12,8},{16,20},{20,16},{24,28},{28,24},{1,5},{5... | collective-permute-start | bytes 3145736 | tf_op jit(solution)/shard_map/ppermute | solution.py:127
  63.6 4.9 %collective-permute-start.28 = (f32[1,256,512]{2,1,0:T(8,128)S(1)}, f32[1,256,512]{2,1,0:T(8,128)S(1)}, u32[]{:S(2)}, u32[]{:S(2)}) collective-permute-start(f32[1,256,512]{2,1,0:T(8,128)S(1)} %get-tuple-element.91.refs_3_), channel_id=1, source_target_pairs={{0,4},{4,0},{8,12},{12,8},{16,20},{20,16},{24,28},{28,24},{1,5},{5... | collective-permute-start | bytes 1572872 | tf_op jit(solution)/shard_map/ppermute | solution.py:127
  64.1 6.4 %collective-permute-start.23 = (f32[32,512]{1,0:T(8,128)S(1)}, f32[32,512]{1,0:T(8,128)S(1)}, u32[]{:S(2)}, u32[]{:S(2)}) collective-permute-start(f32[32,512]{1,0:T(8,128)S(1)} %get-tuple-element.88.refs_2_.refs_0_), channel_id=1, source_target_pairs={{0,1},{1,0},{2,3},{3,2},{4,5},{5,4},{6,7},{7,6},{8,9},{9,8},{10,11... | collective-permute-start | bytes 196616 | tf_op jit(solution)/shard_map/ppermute | solution.py:127
  64.8 7.7 %collective-permute-start.24 = (f32[32,512]{1,0:T(8,128)S(1)}, f32[32,512]{1,0:T(8,128)S(1)}, u32[]{:S(2)}, u32[]{:S(2)}) collective-permute-start(f32[32,512]{1,0:T(8,128)S(1)} %get-tuple-element.88.refs_2_.refs_0_), channel_id=1, source_target_pairs={{0,2},{1,3},{2,0},{3,1},{4,6},{5,7},{6,4},{7,5},{8,10},{9,11},{10,... | collective-permute-start | bytes 196616 | tf_op jit(solution)/shard_map/ppermute | solution.py:127
  67.3 6.2 %collective-permute-start.25 = (f32[32,512]{1,0:T(8,128)S(1)}, f32[32,512]{1,0:T(8,128)S(1)}, u32[]{:S(2)}, u32[]{:S(2)}) collective-permute-start(f32[32,512]{1,0:T(8,128)S(1)} %get-tuple-element.88.refs_2_.refs_0_), channel_id=1, source_target_pairs={{0,3},{1,2},{2,1},{3,0},{4,7},{5,6},{6,5},{7,4},{8,11},{9,10},{10,... | collective-permute-start | bytes 196616 | tf_op jit(solution)/shard_map/ppermute | solution.py:127
  75.6 5.0 %collective-permute-start.29 = (f32[32,512]{1,0:T(8,128)S(1)}, f32[32,512]{1,0:T(8,128)S(1)}, u32[]{:S(2)}, u32[]{:S(2)}) collective-permute-start(f32[32,512]{1,0:T(8,128)S(1)} %get-tuple-element.95), channel_id=1, source_target_pairs={{0,1},{1,0},{2,3},{3,2},{4,5},{5,4},{6,7},{7,6},{8,9},{9,8},{10,11... | collective-permute-start | bytes 196616 | tf_op jit(solution)/shard_map/ppermute | solution.py:127
  76.6 6.2 %collective-permute-start.30 = (f32[32,512]{1,0:T(8,128)S(1)}, f32[32,512]{1,0:T(8,128)S(1)}, u32[]{:S(2)}, u32[]{:S(2)}) collective-permute-start(f32[32,512]{1,0:T(8,128)S(1)} %get-tuple-element.96), channel_id=1, source_target_pairs={{0,2},{1,3},{2,0},{3,1},{4,6},{5,7},{6,4},{7,5},{8,10},{9,11},{10,... | collective-permute-start | bytes 196616 | tf_op jit(solution)/shard_map/ppermute | solution.py:127
  78.0 6.1 %collective-permute-start.31 = (f32[32,512]{1,0:T(8,128)S(1)}, f32[32,512]{1,0:T(8,128)S(1)}, u32[]{:S(2)}, u32[]{:S(2)}) collective-permute-start(f32[32,512]{1,0:T(8,128)S(1)} %get-tuple-element.97), channel_id=1, source_target_pairs={{0,3},{1,2},{2,1},{3,0},{4,7},{5,6},{6,5},{7,4},{8,11},{9,10},{10,... | collective-permute-start | bytes 196616 | tf_op jit(solution)/shard_map/ppermute | solution.py:127
  85.5 6.2 %collective-permute-start.32 = (f32[40,512]{1,0:T(8,128)S(1)}, f32[40,512]{1,0:T(8,128)S(1)}, u32[]{:S(2)}, u32[]{:S(2)}) collective-permute-start(f32[40,512]{1,0:T(8,128)S(1)} %get-tuple-element.99), channel_id=1, source_target_pairs={{0,1},{1,0},{2,3},{3,2},{4,5},{5,4},{6,7},{7,6},{8,9},{9,8},{10,11... | collective-permute-start | bytes 245768 | tf_op jit(solution)/shard_map/ppermute | solution.py:127
  85.5 6.2 %collective-permute-start.33 = (f32[40,512]{1,0:T(8,128)S(1)}, f32[40,512]{1,0:T(8,128)S(1)}, u32[]{:S(2)}, u32[]{:S(2)}) collective-permute-start(f32[40,512]{1,0:T(8,128)S(1)} %get-tuple-element.100), channel_id=1, source_target_pairs={{0,2},{1,3},{2,0},{3,1},{4,6},{5,7},{6,4},{7,5},{8,10},{9,11},{10,... | collective-permute-start | bytes 245768 | tf_op jit(solution)/shard_map/ppermute | solution.py:127
  88.0 6.2 %collective-permute-start.34 = (f32[40,512]{1,0:T(8,128)S(1)}, f32[40,512]{1,0:T(8,128)S(1)}, u32[]{:S(2)}, u32[]{:S(2)}) collective-permute-start(f32[40,512]{1,0:T(8,128)S(1)} %get-tuple-element.101), channel_id=1, source_target_pairs={{0,3},{1,2},{2,1},{3,0},{4,7},{5,6},{6,5},{7,4},{8,11},{9,10},{10,... | collective-permute-start | bytes 245768 | tf_op jit(solution)/shard_map/ppermute | solution.py:127
  94.3 3.6 %collective-permute-start.38 = (f32[1,256,512]{2,1,0:T(8,128)}, f32[1,256,512]{2,1,0:T(8,128)S(1)}, u32[]{:S(2)}, u32[]{:S(2)}) collective-permute-start(f32[1,256,512]{2,1,0:T(8,128)} %shard_map.199.refs_2_), channel_id=1, source_target_pairs={{0,4},{4,0},{8,12},{12,8},{16,20},{20,16},{24,28},{28,24},{1,5},{5... | collective-permute-start | bytes 1572872 | tf_op jit(solution)/shard_map/ppermute | solution.py:127
  94.4 5.2 %collective-permute-start.35 = (f32[40,512]{1,0:T(8,128)S(1)}, f32[40,512]{1,0:T(8,128)S(1)}, u32[]{:S(2)}, u32[]{:S(2)}) collective-permute-start(f32[40,512]{1,0:T(8,128)S(1)} %get-tuple-element.104), channel_id=1, source_target_pairs={{0,8},{4,12},{8,0},{12,4},{16,24},{20,28},{24,16},{28,20},{1,9},{5... | collective-permute-start | bytes 245768 | tf_op jit(solution)/shard_map/ppermute | solution.py:127
  95.1 4.8 %collective-permute-start.36 = (f32[40,512]{1,0:T(8,128)S(1)}, f32[40,512]{1,0:T(8,128)S(1)}, u32[]{:S(2)}, u32[]{:S(2)}) collective-permute-start(f32[40,512]{1,0:T(8,128)S(1)} %get-tuple-element.105), channel_id=1, source_target_pairs={{0,16},{4,20},{8,24},{12,28},{16,0},{20,4},{24,8},{28,12},{1,17},{... | collective-permute-start | bytes 245768 | tf_op jit(solution)/shard_map/ppermute | solution.py:127
  95.9 5.5 %collective-permute-start.37 = (f32[40,512]{1,0:T(8,128)S(1)}, f32[40,512]{1,0:T(8,128)S(1)}, u32[]{:S(2)}, u32[]{:S(2)}) collective-permute-start(f32[40,512]{1,0:T(8,128)S(1)} %get-tuple-element.106.refs_1_), channel_id=1, source_target_pairs={{0,24},{4,28},{8,16},{12,20},{16,8},{20,12},{24,0},{28,4},{1,25},{... | collective-permute-start | bytes 245768 | tf_op jit(solution)/shard_map/ppermute | solution.py:127
  102.2 5.2 %collective-permute-start.39 = (f32[32,512]{1,0:T(8,128)S(1)}, f32[32,512]{1,0:T(8,128)S(1)}, u32[]{:S(2)}, u32[]{:S(2)}) collective-permute-start(f32[32,512]{1,0:T(8,128)S(1)} %get-tuple-element.110), channel_id=1, source_target_pairs={{0,2},{1,3},{2,0},{3,1},{4,6},{5,7},{6,4},{7,5},{8,10},{9,11},{10,... | collective-permute-start | bytes 196616 | tf_op jit(solution)/shard_map/ppermute | solution.py:127
  107.4 1.3 %collective-permute-start.40 = (f32[32,512]{1,0:T(8,128)S(1)}, f32[32,512]{1,0:T(8,128)S(1)}, u32[]{:S(2)}, u32[]{:S(2)}) collective-permute-start(f32[32,512]{1,0:T(8,128)S(1)} %get-tuple-element.113), channel_id=1, source_target_pairs={{0,4},{4,0},{8,12},{12,8},{16,20},{20,16},{24,28},{28,24},{1,5},{5... | collective-permute-start | bytes 196616 | tf_op jit(solution)/shard_map/ppermute | solution.py:127

commit v7 on v6

--- a/solution.py
+++ b/solution.py
@@ -540,13 +540,14 @@
     partner_coupling = flip(root_coupling, "leaf", 1)
     inverse, coupling, links, next_order = level_data[1]
     count -= red_blocks
-    solved_second, kept, sent = kernel_call(
+    solved_second, kept, sent, second = kernel_call(
         middle_kernel,
         [solved, halved(count), halved(count)],
         [front_rows, links, order],
         [],
         loaded=[kept, received, inverse, coupling],
         late=1,
+        stacks=[[(root_inverse, 1)]],
         held=[partner_inverse, partner_coupling],
         scratch=[scratch(count, rhs_rows, size)] * 2,
         room=64,
@@ -554,14 +555,14 @@
     received = flip(sent, "leaf", 2)
     inverse, coupling, links, last_order = level_data[2]
     count -= red_blocks
-    solved_third, kept, sent, near, second = kernel_call(
+    solved_third, kept, sent, near = kernel_call(
         highest_kernel,
         [solved, both, both],
         [front_rows, links, next_order, last_order],
         [],
         loaded=[kept, received, inverse, coupling],
         late=1,
-        stacks=[[near], [(root_inverse, 1)]],
+        stacks=[[near]],
         held=[far],
         scratch=[scratch(count, rhs_rows, size)] * 2,
         room=64,

time: 110 us -> 110 us (level)
  transfers between devices with their start and end apart: 41 -> 41, of which waited for: 23 -> 21; matrix products, arithmetic and copies ran while one was open for 0% -> 0% of each run, Pallas kernels for 16% -> 17%
where the time goes in v7:
time: 110 us
  waiting for transfers between devices  42.9 us (39%)
  starting transfers between devices  40.6 us (37%)
  Pallas kernels  23.5 us (21%)
  local copies, waits for them, and re-layouts  2.08 us (2%)
    ppermute x41, waiting for transfers between devices, flip(): return lax.ppermute(block, axis, [(i, i ^ distance) for i in range(count)])  42.9 us
    ppermute x41, starting transfers between devices, flip(): return lax.ppermute(block, axis, [(i, i ^ distance) for i in range(count)])  40.6 us
    pallas_call x17, Pallas kernels, kernel_call(): pl.pallas_call(run, out_shape=out_shapes, in_specs=[far] * sum(inputs[:-2...  23.5 us
  transfers between devices with their start and end apart: 41, of which 21 were waited for; matrix products, arithmetic and copies ran while one was open for 0% of the time, Pallas kernels for 17%

profile of v7, /device:TPU:0, one launch (start us, length us, event | category | flops | bytes accessed | tf_op | source)
XLA Modules:
  0.0 110.0 jit_solution(1517141934699818190)
XLA Ops:
  0.6 0.5 collective-permute-start.1
  1.2 2.9 %collective-permute-start.5 = (f32[256,512]{1,0:T(8,128)}, f32[256,512]{1,0:T(8,128)}, u32[]{:S(2)}, u32[]{:S(2)}) collective-permute-start(f32[256,512]{1,0:T(8,128)} %refs_0_.5), channel_id=1, source_target_pairs={{0,16},{4,20},{8,24},{12,28},{16,0},{20,4},{24,8},{28,12},{1,17},{... | collective-permute-start | bytes 1572872 | tf_op jit(solution)/shard_map/ppermute | solution.py:127
  4.2 1.5 %collective-permute-start.4 = (f32[256,512]{1,0:T(8,128)}, f32[256,512]{1,0:T(8,128)}, u32[]{:S(2)}, u32[]{:S(2)}) collective-permute-start(f32[256,512]{1,0:T(8,128)} %refs_0_.5), channel_id=1, source_target_pairs={{0,8},{4,12},{8,0},{12,4},{16,24},{20,28},{24,16},{28,20},{1,9},{5... | collective-permute-start | bytes 1572872 | tf_op jit(solution)/shard_map/ppermute | solution.py:127
  5.7 3.6 %shard_map.183 = (f32[64,512]{1,0:T(8,128)}, f32[6,64,128]{2,1,0:T(8,128)}, f32[6,64,128]{2,1,0:T(8,128)}, f32[1,256,512]{2,1,0:T(8,128)}, f32[1,256,512]{2,1,0:T(8,128)}) custom-call(s32[1,3]{1,0:T(1,128)} %bitcast.1, s32[4,3]{1,0:T(4,128)} %refs_1_.3, f32[64,2048]{1,0:T(8,128)} %refs_2_.3, f32[4,128,128]{2,1,0:T(8,128)} %refs_3_.2, ...), custom_call_target="tpu_custom_call" | custom-call | tf_op jit(solution)/shard_map/pallas_call | solution.py:205
  9.3 1.8 %collective-permute-done.refs_4_ = f32[6,64,128]{2,1,0:T(8,128)} collective-permute-done((f32[6,64,128]{2,1,0:T(8,128)}, f32[6,64,128]{2,1,0:T(8,128)}, u32[]{:S(2)}, u32[]{:S(2)}) %collective-permute-start) | collective-permute-done | bytes 196640 | tf_op jit(solution)/shard_map/ppermute | solution.py:127
  11.1 3.2 %shard_map.184 = (f32[64,512]{1,0:T(8,128)}, f32[4,64,128]{2,1,0:T(8,128)}, f32[4,64,128]{2,1,0:T(8,128)}, f32[1,256,512]{2,1,0:T(8,128)}) custom-call(s32[1,3]{1,0:T(1,128)} %bitcast.2, s32[4,3]{1,0:T(4,128)} %refs_1_.4, s32[1,12]{1,0:T(1,128)} %refs_2_.4, f32[6,64,128]{2,1,0:T(8,128)} %get-tuple-element.60.refs_3_, ...), custom_call_target="tpu_custom_call" | custom-call | tf_op jit(solution)/shard_map/pallas_call | solution.py:205
  14.3 0.6 collective-permute-start.3
  14.9 2.0 %collective-permute-start.9 = (f32[1,256,512]{2,1,0:T(8,128)}, f32[1,256,512]{2,1,0:T(8,128)}, u32[]{:S(2)}, u32[]{:S(2)}) collective-permute-start(f32[1,256,512]{2,1,0:T(8,128)} %get-tuple-element.69), channel_id=1, source_target_pairs={{0,1},{1,0},{2,3},{3,2},{4,5},{5,4},{6,7},{7,6},{8,9},{9,8},{10,11... | collective-permute-start | bytes 1572872 | tf_op jit(solution)/shard_map/ppermute | solution.py:127
  17.0 1.5 %collective-permute-start.7 = (f32[1,256,512]{2,1,0:T(8,128)}, f32[1,256,512]{2,1,0:T(8,128)}, u32[]{:S(2)}, u32[]{:S(2)}) collective-permute-start(f32[1,256,512]{2,1,0:T(8,128)} %get-tuple-element.67), channel_id=1, source_target_pairs={{0,8},{4,12},{8,0},{12,4},{16,24},{20,28},{24,16},{28,20},{1,9},{5... | collective-permute-start | bytes 1572872 | tf_op jit(solution)/shard_map/ppermute | solution.py:127
  18.5 0.3 collective-permute-done.4.refs_8_
  18.8 2.8 %collective-permute-done.3.refs_5_ = f32[4,64,128]{2,1,0:T(8,128)} collective-permute-done((f32[4,64,128]{2,1,0:T(8,128)}, f32[4,64,128]{2,1,0:T(8,128)}, u32[]{:S(2)}, u32[]{:S(2)}) %collective-permute-start.3) | collective-permute-done | bytes 131104 | tf_op jit(solution)/shard_map/ppermute | solution.py:127
  21.6 3.1 %shard_map.185 = (f32[64,512]{1,0:T(8,128)}, f32[32,512]{1,0:T(8,128)}, f32[32,512]{1,0:T(8,128)}, f32[1,256,512]{2,1,0:T(8,128)}) custom-call(s32[1,3]{1,0:T(1,128)} %bitcast.3, s32[4,3]{1,0:T(4,128)} %refs_1_.5, s32[1,8]{1,0:T(1,128)} %refs_2_.5, s32[1,4]{1,0:T(1,128)} %refs_3_.3, f32[4,64,128]{2,1,0:T(8,128)} %get-tuple-element.63.refs_4_, ...), custom_call_target="tpu_custom_call" | custom-call | tf_op jit(solution)/shard_map/pallas_call | solution.py:205
  24.8 5.2 %collective-permute-done.8.refs_0_.refs_9_ = f32[1,256,512]{2,1,0:T(8,128)} collective-permute-done((f32[1,256,512]{2,1,0:T(8,128)}, f32[1,256,512]{2,1,0:T(8,128)}, u32[]{:S(2)}, u32[]{:S(2)}) %collective-permute-start.8) | collective-permute-done | bytes 524320 | tf_op jit(solution)/shard_map/ppermute | solution.py:127
  30.0 0.8 copy-done.4
  30.9 1.6 %collective-permute-start.11 = (f32[32,512]{1,0:T(8,128)S(1)}, f32[32,512]{1,0:T(8,128)S(1)}, u32[]{:S(2)}, u32[]{:S(2)}) collective-permute-start(f32[32,512]{1,0:T(8,128)S(1)} %shard_map.186.refs_2_), channel_id=1, source_target_pairs={{0,1},{1,0},{2,3},{3,2},{4,5},{5,4},{6,7},{7,6},{8,9},{9,8},{10,11... | collective-permute-start | bytes 196616 | tf_op jit(solution)/shard_map/ppermute | solution.py:127
  32.5 2.6 %collective-permute-start.12 = (f32[32,512]{1,0:T(8,128)S(1)}, f32[32,512]{1,0:T(8,128)S(1)}, u32[]{:S(2)}, u32[]{:S(2)}) collective-permute-start(f32[32,512]{1,0:T(8,128)S(1)} %shard_map.186.refs_2_), channel_id=1, source_target_pairs={{0,2},{1,3},{2,0},{3,1},{4,6},{5,7},{6,4},{7,5},{8,10},{9,11},{10,... | collective-permute-start | bytes 196616 | tf_op jit(solution)/shard_map/ppermute | solution.py:127
  35.3 1.2 %copy-done = f32[2,256,512]{2,1,0:T(8,128)S(1)} copy-done((f32[2,256,512]{2,1,0:T(8,128)S(1)}, f32[2,256,512]{2,1,0:T(8,128)}, u32[]{:S(2)}) %copy-start) | copy-done | bytes 1048600
  36.5 1.3 %shard_map.187 = (bf16[512,512]{1,0:T(8,128)(2,1)S(1)}, bf16[512,512]{1,0:T(8,128)(2,1)S(1)}) custom-call(f32[2,256,512]{2,1,0:T(8,128)S(1)} %copy-done, f32[2,256,512]{2,1,0:T(8,128)} %collective-permute-done.1.refs_8_.refs_1_.refs_4_), custom_call_target="tpu_custom_call" | custom-call | tf_op jit(solution)/shard_map/pallas_call | solution.py:205
  37.8 1.2 %collective-permute-done.12.refs_4_ = f32[32,512]{1,0:T(8,128)S(1)} collective-permute-done((f32[32,512]{1,0:T(8,128)S(1)}, f32[32,512]{1,0:T(8,128)S(1)}, u32[]{:S(2)}, u32[]{:S(2)}) %collective-permute-start.12) | collective-permute-done | bytes 65568 | tf_op jit(solution)/shard_map/ppermute | solution.py:127
  39.0 2.2 %collective-permute-done.13.refs_5_ = f32[32,512]{1,0:T(8,128)S(1)} collective-permute-done((f32[32,512]{1,0:T(8,128)S(1)}, f32[32,512]{1,0:T(8,128)S(1)}, u32[]{:S(2)}, u32[]{:S(2)}) %collective-permute-start.13) | collective-permute-done | bytes 65568 | tf_op jit(solution)/shard_map/ppermute | solution.py:127
  41.2 0.4 shard_map.188
  41.7 1.6 %collective-permute-start.15 = (f32[40,512]{1,0:T(8,128)S(1)}, f32[40,512]{1,0:T(8,128)S(1)}, u32[]{:S(2)}, u32[]{:S(2)}) collective-permute-start(f32[40,512]{1,0:T(8,128)S(1)} %get-tuple-element.77), channel_id=1, source_target_pairs={{0,8},{4,12},{8,0},{12,4},{16,24},{20,28},{24,16},{28,20},{1,9},{5... | collective-permute-start | bytes 245768 | tf_op jit(solution)/shard_map/ppermute | solution.py:127
  43.2 0.6 collective-permute-start.16
  43.9 1.4 %collective-permute-start.17 = (f32[40,512]{1,0:T(8,128)S(1)}, f32[40,512]{1,0:T(8,128)S(1)}, u32[]{:S(2)}, u32[]{:S(2)}) collective-permute-start(f32[40,512]{1,0:T(8,128)S(1)} %get-tuple-element.74.refs_2_), channel_id=1, source_target_pairs={{0,24},{4,28},{8,16},{12,20},{16,8},{20,12},{24,0},{28,4},{1,25},{... | collective-permute-start | bytes 245768 | tf_op jit(solution)/shard_map/ppermute | solution.py:127
  45.2 1.3 %collective-permute-done.15.refs_2_ = f32[40,512]{1,0:T(8,128)S(1)} collective-permute-done((f32[40,512]{1,0:T(8,128)S(1)}, f32[40,512]{1,0:T(8,128)S(1)}, u32[]{:S(2)}, u32[]{:S(2)}) %collective-permute-start.15) | collective-permute-done | bytes 81952 | tf_op jit(solution)/shard_map/ppermute | solution.py:127
  46.5 3.0 %collective-permute-done.16.refs_3_ = f32[40,512]{1,0:T(8,128)S(1)} collective-permute-done((f32[40,512]{1,0:T(8,128)S(1)}, f32[40,512]{1,0:T(8,128)S(1)}, u32[]{:S(2)}, u32[]{:S(2)}) %collective-permute-start.16) | collective-permute-done | bytes 81952 | tf_op jit(solution)/shard_map/ppermute | solution.py:127
  49.7 1.2 %collective-permute-start.26 = (f32[1,256,512]{2,1,0:T(8,128)}, f32[1,256,512]{2,1,0:T(8,128)S(1)}, u32[]{:S(2)}, u32[]{:S(2)}) collective-permute-start(f32[1,256,512]{2,1,0:T(8,128)} %get-tuple-element.85.refs_8_), channel_id=1, source_target_pairs={{0,16},{4,20},{8,24},{12,28},{16,0},{20,4},{24,8},{28,12},{1,17},{... | collective-permute-start | bytes 1572872 | tf_op jit(solution)/shard_map/ppermute | solution.py:127
  50.8 0.4 collective-permute-start.18
  51.2 2.6 %collective-permute-start.19 = (f32[40,512]{1,0:T(8,128)S(1)}, f32[40,512]{1,0:T(8,128)S(1)}, u32[]{:S(2)}, u32[]{:S(2)}) collective-permute-start(f32[40,512]{1,0:T(8,128)S(1)} %get-tuple-element.81), channel_id=1, source_target_pairs={{0,2},{1,3},{2,0},{3,1},{4,6},{5,7},{6,4},{7,5},{8,10},{9,11},{10,... | collective-permute-start | bytes 245768 | tf_op jit(solution)/shard_map/ppermute | solution.py:127
  53.8 1.4 %collective-permute-start.20 = (f32[40,512]{1,0:T(8,128)S(1)}, f32[40,512]{1,0:T(8,128)S(1)}, u32[]{:S(2)}, u32[]{:S(2)}) collective-permute-start(f32[40,512]{1,0:T(8,128)S(1)} %get-tuple-element.82.refs_2_), channel_id=1, source_target_pairs={{0,3},{1,2},{2,1},{3,0},{4,7},{5,6},{6,5},{7,4},{8,11},{9,10},{10,... | collective-permute-start | bytes 245768 | tf_op jit(solution)/shard_map/ppermute | solution.py:127
  55.2 2.6 %shard_map.192 = (bf16[2048,512]{1,0:T(8,128)(2,1)S(1)}, bf16[2048,512]{1,0:T(8,128)(2,1)S(1)}, f32[2,256,512]{2,1,0:T(8,128)S(1)}) custom-call(f32[256,512]{1,0:T(8,128)S(1)} %copy-done.3, f32[1,256,512]{2,1,0:T(8,128)S(1)} %get-tuple-element.83.refs_1_, f32[256,512]{1,0:T(8,128)} %get-tuple-element.84.refs_2_, ...), custom_call_target="tpu_custom_call" | custom-call | tf_op jit(solution)/shard_map/pallas_call | solution.py:205
  57.8 3.0 %collective-permute-done.19.refs_2_ = f32[40,512]{1,0:T(8,128)S(1)} collective-permute-done((f32[40,512]{1,0:T(8,128)S(1)}, f32[40,512]{1,0:T(8,128)S(1)}, u32[]{:S(2)}, u32[]{:S(2)}) %collective-permute-start.19) | collective-permute-done | bytes 81952 | tf_op jit(solution)/shard_map/ppermute | solution.py:127
  60.8 0.8 shard_map.193
  61.7 2.6 %collective-permute-done.26.refs_1_ = f32[1,256,512]{2,1,0:T(8,128)S(1)} collective-permute-done((f32[1,256,512]{2,1,0:T(8,128)}, f32[1,256,512]{2,1,0:T(8,128)S(1)}, u32[]{:S(2)}, u32[]{:S(2)}) %collective-permute-start.26) | collective-permute-done | bytes 524320 | tf_op jit(solution)/shard_map/ppermute | solution.py:127
  64.2 0.5 collective-permute-start.28
  64.7 0.4 collective-permute-start.23
  65.1 2.6 %collective-permute-start.24 = (f32[32,512]{1,0:T(8,128)S(1)}, f32[32,512]{1,0:T(8,128)S(1)}, u32[]{:S(2)}, u32[]{:S(2)}) collective-permute-start(f32[32,512]{1,0:T(8,128)S(1)} %get-tuple-element.88.refs_2_.refs_0_), channel_id=1, source_target_pairs={{0,2},{1,3},{2,0},{3,1},{4,6},{5,7},{6,4},{7,5},{8,10},{9,11},{10,... | collective-permute-start | bytes 196616 | tf_op jit(solution)/shard_map/ppermute | solution.py:127
  67.7 1.4 %collective-permute-start.25 = (f32[32,512]{1,0:T(8,128)S(1)}, f32[32,512]{1,0:T(8,128)S(1)}, u32[]{:S(2)}, u32[]{:S(2)}) collective-permute-start(f32[32,512]{1,0:T(8,128)S(1)} %get-tuple-element.88.refs_2_.refs_0_), channel_id=1, source_target_pairs={{0,3},{1,2},{2,1},{3,0},{4,7},{5,6},{6,5},{7,4},{8,11},{9,10},{10,... | collective-permute-start | bytes 196616 | tf_op jit(solution)/shard_map/ppermute | solution.py:127
  69.1 2.0 %shard_map.195 = (bf16[2048,512]{1,0:T(8,128)(2,1)S(1)}, bf16[2048,512]{1,0:T(8,128)(2,1)S(1)}) custom-call(f32[2,256,512]{2,1,0:T(8,128)S(1)} %copy-done.1, f32[2,256,512]{2,1,0:T(8,128)S(1)} %get-tuple-element.90.refs_1_.refs_2_, f32[2,256,512]{2,1,0:T(8,128)S(1)} %get-tuple-element.90.refs_1_.refs_2_, f32[1,256,512]{2,1,0:T(8,128)S(1)} %get-tuple-element.91.refs_3_, ...), custom_call_target="tpu_custom_call" | custom-call | tf_op jit(solution)/shard_map/pallas_call | solution.py:205
  71.2 1.8 %collective-permute-done.24.refs_2_ = f32[32,512]{1,0:T(8,128)S(1)} collective-permute-done((f32[32,512]{1,0:T(8,128)S(1)}, f32[32,512]{1,0:T(8,128)S(1)}, u32[]{:S(2)}, u32[]{:S(2)}) %collective-permute-start.24) | collective-permute-done | bytes 65568 | tf_op jit(solution)/shard_map/ppermute | solution.py:127
  73.0 0.9 collective-permute-done.25.refs_3_
  73.9 2.1 %shard_map.196 = (f32[32,512]{1,0:T(8,128)S(1)}, f32[32,512]{1,0:T(8,128)S(1)}, f32[32,512]{1,0:T(8,128)S(1)}, f32[32,512]{1,0:T(8,128)S(1)}) custom-call(f32[32,512]{1,0:T(8,128)S(1)} %get-tuple-element.88.refs_2_.refs_0_, f32[32,512]{1,0:T(8,128)S(1)} %collective-permute-done.23.refs_1_, f32[32,512]{1,0:T(8,128)S(1)} %collective-permute-done.24.refs_2_, ...), custom_call_target="tpu_custom_call" | custom-call | tf_op jit(solution)/shard_map/pallas_call | solution.py:205
  76.0 1.1 %collective-permute-start.29 = (f32[32,512]{1,0:T(8,128)S(1)}, f32[32,512]{1,0:T(8,128)S(1)}, u32[]{:S(2)}, u32[]{:S(2)}) collective-permute-start(f32[32,512]{1,0:T(8,128)S(1)} %get-tuple-element.95), channel_id=1, source_target_pairs={{0,1},{1,0},{2,3},{3,2},{4,5},{5,4},{6,7},{7,6},{8,9},{9,8},{10,11... | collective-permute-start | bytes 196616 | tf_op jit(solution)/shard_map/ppermute | solution.py:127
  77.1 1.3 %collective-permute-start.30 = (f32[32,512]{1,0:T(8,128)S(1)}, f32[32,512]{1,0:T(8,128)S(1)}, u32[]{:S(2)}, u32[]{:S(2)}) collective-permute-start(f32[32,512]{1,0:T(8,128)S(1)} %get-tuple-element.96), channel_id=1, source_target_pairs={{0,2},{1,3},{2,0},{3,1},{4,6},{5,7},{6,4},{7,5},{8,10},{9,11},{10,... | collective-permute-start | bytes 196616 | tf_op jit(solution)/shard_map/ppermute | solution.py:127
  78.4 2.0 %collective-permute-start.31 = (f32[32,512]{1,0:T(8,128)S(1)}, f32[32,512]{1,0:T(8,128)S(1)}, u32[]{:S(2)}, u32[]{:S(2)}) collective-permute-start(f32[32,512]{1,0:T(8,128)S(1)} %get-tuple-element.97), channel_id=1, source_target_pairs={{0,3},{1,2},{2,1},{3,0},{4,7},{5,6},{6,5},{7,4},{8,11},{9,10},{10,... | collective-permute-start | bytes 196616 | tf_op jit(solution)/shard_map/ppermute | solution.py:127
  80.4 0.9 collective-permute-done.29.refs_1_
  81.3 2.0 %collective-permute-done.30.refs_2_ = f32[32,512]{1,0:T(8,128)S(1)} collective-permute-done((f32[32,512]{1,0:T(8,128)S(1)}, f32[32,512]{1,0:T(8,128)S(1)}, u32[]{:S(2)}, u32[]{:S(2)}) %collective-permute-start.30) | collective-permute-done | bytes 65568 | tf_op jit(solution)/shard_map/ppermute | solution.py:127
  83.2 1.3 %collective-permute-done.31.refs_3_ = f32[32,512]{1,0:T(8,128)S(1)} collective-permute-done((f32[32,512]{1,0:T(8,128)S(1)}, f32[32,512]{1,0:T(8,128)S(1)}, u32[]{:S(2)}, u32[]{:S(2)}) %collective-permute-start.31) | collective-permute-done | bytes 65568 | tf_op jit(solution)/shard_map/ppermute | solution.py:127
  84.6 1.3 %shard_map.197 = (f32[40,512]{1,0:T(8,128)S(1)}, f32[40,512]{1,0:T(8,128)S(1)}, f32[40,512]{1,0:T(8,128)S(1)}, f32[40,512]{1,0:T(8,128)S(1)}) custom-call(f32[32,512]{1,0:T(8,128)S(1)} %get-tuple-element.94.refs_0_, f32[32,512]{1,0:T(8,128)S(1)} %collective-permute-done.29.refs_1_, f32[32,512]{1,0:T(8,128)S(1)} %collective-permute-done.30.refs_2_, ...), custom_call_target="tpu_custom_call" | custom-call | tf_op jit(solution)/shard_map/pallas_call | solution.py:205
  85.9 0.6 collective-permute-start.32
  86.6 1.9 %collective-permute-start.33 = (f32[40,512]{1,0:T(8,128)S(1)}, f32[40,512]{1,0:T(8,128)S(1)}, u32[]{:S(2)}, u32[]{:S(2)}) collective-permute-start(f32[40,512]{1,0:T(8,128)S(1)} %get-tuple-element.100), channel_id=1, source_target_pairs={{0,2},{1,3},{2,0},{3,1},{4,6},{5,7},{6,4},{7,5},{8,10},{9,11},{10,... | collective-permute-start | bytes 245768 | tf_op jit(solution)/shard_map/ppermute | solution.py:127
  88.4 1.9 %collective-permute-start.34 = (f32[40,512]{1,0:T(8,128)S(1)}, f32[40,512]{1,0:T(8,128)S(1)}, u32[]{:S(2)}, u32[]{:S(2)}) collective-permute-start(f32[40,512]{1,0:T(8,128)S(1)} %get-tuple-element.101), channel_id=1, source_target_pairs={{0,3},{1,2},{2,1},{3,0},{4,7},{5,6},{6,5},{7,4},{8,11},{9,10},{10,... | collective-permute-start | bytes 245768 | tf_op jit(solution)/shard_map/ppermute | solution.py:127
  90.3 1.3 %collective-permute-done.32.refs_1_ = f32[40,512]{1,0:T(8,128)S(1)} collective-permute-done((f32[40,512]{1,0:T(8,128)S(1)}, f32[40,512]{1,0:T(8,128)S(1)}, u32[]{:S(2)}, u32[]{:S(2)}) %collective-permute-start.32) | collective-permute-done | bytes 81952 | tf_op jit(solution)/shard_map/ppermute | solution.py:127
  91.7 1.3 %collective-permute-done.33.refs_2_ = f32[40,512]{1,0:T(8,128)S(1)} collective-permute-done((f32[40,512]{1,0:T(8,128)S(1)}, f32[40,512]{1,0:T(8,128)S(1)}, u32[]{:S(2)}, u32[]{:S(2)}) %collective-permute-start.33) | collective-permute-done | bytes 81952 | tf_op jit(solution)/shard_map/ppermute | solution.py:127
  92.9 1.8 %collective-permute-done.34.refs_3_ = f32[40,512]{1,0:T(8,128)S(1)} collective-permute-done((f32[40,512]{1,0:T(8,128)S(1)}, f32[40,512]{1,0:T(8,128)S(1)}, u32[]{:S(2)}, u32[]{:S(2)}) %collective-permute-start.34) | collective-permute-done | bytes 81952 | tf_op jit(solution)/shard_map/ppermute | solution.py:127
  94.8 0.6 collective-permute-start.35
  95.4 1.2 %collective-permute-start.36 = (f32[40,512]{1,0:T(8,128)S(1)}, f32[40,512]{1,0:T(8,128)S(1)}, u32[]{:S(2)}, u32[]{:S(2)}) collective-permute-start(f32[40,512]{1,0:T(8,128)S(1)} %get-tuple-element.105), channel_id=1, source_target_pairs={{0,16},{4,20},{8,24},{12,28},{16,0},{20,4},{24,8},{28,12},{1,17},{... | collective-permute-start | bytes 245768 | tf_op jit(solution)/shard_map/ppermute | solution.py:127
  96.6 1.7 %collective-permute-start.37 = (f32[40,512]{1,0:T(8,128)S(1)}, f32[40,512]{1,0:T(8,128)S(1)}, u32[]{:S(2)}, u32[]{:S(2)}) collective-permute-start(f32[40,512]{1,0:T(8,128)S(1)} %get-tuple-element.106.refs_1_), channel_id=1, source_target_pairs={{0,24},{4,28},{8,16},{12,20},{16,8},{20,12},{24,0},{28,4},{1,25},{... | collective-permute-start | bytes 245768 | tf_op jit(solution)/shard_map/ppermute | solution.py:127
  98.4 1.6 %shard_map.200 = (bf16[512,1024]{1,0:T(8,128)(2,1)S(1)}, bf16[512,1024]{1,0:T(8,128)(2,1)S(1)}) custom-call(f32[2,256,512]{2,1,0:T(8,128)S(1)} %copy-done.1, f32[2,256,512]{2,1,0:T(8,128)} %collective-permute-done.1.refs_8_.refs_1_.refs_4_, f32[1,256,512]{2,1,0:T(8,128)} %shard_map.199.refs_2_, f32[1,256,512]{2,1,0:T(8,128)S(1)} %collective-permute-done.38.refs_3_), custom_call_target="tpu_custom_call" | custom-call | tf_op jit(solution)/shard_map/pallas_call | solution.py:205
  100.1 1.9 %collective-permute-done.37.refs_3_ = f32[40,512]{1,0:T(8,128)S(1)} collective-permute-done((f32[40,512]{1,0:T(8,128)S(1)}, f32[40,512]{1,0:T(8,128)S(1)}, u32[]{:S(2)}, u32[]{:S(2)}) %collective-permute-start.37) | collective-permute-done | bytes 81952 | tf_op jit(solution)/shard_map/ppermute | solution.py:127
  102.0 0.8 shard_map.201
  102.8 5.2 %collective-permute-done.39.refs_1_ = f32[32,512]{1,0:T(8,128)S(1)} collective-permute-done((f32[32,512]{1,0:T(8,128)S(1)}, f32[32,512]{1,0:T(8,128)S(1)}, u32[]{:S(2)}, u32[]{:S(2)}) %collective-permute-start.39) | collective-permute-done | bytes 65568 | tf_op jit(solution)/shard_map/ppermute | solution.py:127
  108.1 1.2 %collective-permute-done.40.refs_1_ = f32[32,512]{1,0:T(8,128)S(1)} collective-permute-done((f32[32,512]{1,0:T(8,128)S(1)}, f32[32,512]{1,0:T(8,128)S(1)}, u32[]{:S(2)}, u32[]{:S(2)}) %collective-permute-start.40) | collective-permute-done | bytes 65568 | tf_op jit(solution)/shard_map/ppermute | solution.py:127
  109.3 0.7 shard_map.203
  (51 shorter events, 1.1 us)
Async XLA Ops:
  0.6 10.5 %collective-permute-start.1 = (f32[2,256,512]{2,1,0:T(8,128)}, f32[2,256,512]{2,1,0:T(8,128)}, u32[]{:S(2)}, u32[]{:S(2)}) collective-permute-start(f32[2,256,512]{2,1,0:T(8,128)} %refs_0_.7), channel_id=1, source_target_pairs={{0,4},{4,0},{8,12},{12,8},{16,20},{20,16},{24,28},{28,24},{1,5},{5... | collective-permute-start | bytes 3145736 | tf_op jit(solution)/shard_map/ppermute | solution.py:127
  1.1 9.9 %collective-permute-start.2 = (f32[256,512]{1,0:T(8,128)}, f32[256,512]{1,0:T(8,128)}, u32[]{:S(2)}, u32[]{:S(2)}) collective-permute-start(f32[256,512]{1,0:T(8,128)} %refs_0_.5), channel_id=1, source_target_pairs={{0,4},{4,0},{8,12},{12,8},{16,20},{20,16},{24,28},{28,24},{1,5},{5... | collective-permute-start | bytes 1572872 | tf_op jit(solution)/shard_map/ppermute | solution.py:127
  1.2 15.7 %collective-permute-start.5 = (f32[256,512]{1,0:T(8,128)}, f32[256,512]{1,0:T(8,128)}, u32[]{:S(2)}, u32[]{:S(2)}) collective-permute-start(f32[256,512]{1,0:T(8,128)} %refs_0_.5), channel_id=1, source_target_pairs={{0,16},{4,20},{8,24},{12,28},{16,0},{20,4},{24,8},{28,12},{1,17},{... | collective-permute-start | bytes 1572872 | tf_op jit(solution)/shard_map/ppermute | solution.py:127
  4.2 14.6 %collective-permute-start.4 = (f32[256,512]{1,0:T(8,128)}, f32[256,512]{1,0:T(8,128)}, u32[]{:S(2)}, u32[]{:S(2)}) collective-permute-start(f32[256,512]{1,0:T(8,128)} %refs_0_.5), channel_id=1, source_target_pairs={{0,8},{4,12},{8,0},{12,4},{16,24},{20,28},{24,16},{28,20},{1,9},{5... | collective-permute-start | bytes 1572872 | tf_op jit(solution)/shard_map/ppermute | solution.py:127
  9.2 1.8 %collective-permute-start = (f32[6,64,128]{2,1,0:T(8,128)}, f32[6,64,128]{2,1,0:T(8,128)}, u32[]{:S(2)}, u32[]{:S(2)}) collective-permute-start(f32[6,64,128]{2,1,0:T(8,128)} %get-tuple-element.61), channel_id=1, source_target_pairs={{0,4},{4,0},{8,12},{12,8},{16,20},{20,16},{24,28},{28,24},{1,5},{5... | collective-permute-start | bytes 589832 | tf_op jit(solution)/shard_map/ppermute | solution.py:127
  14.3 7.3 %collective-permute-start.3 = (f32[4,64,128]{2,1,0:T(8,128)}, f32[4,64,128]{2,1,0:T(8,128)}, u32[]{:S(2)}, u32[]{:S(2)}) collective-permute-start(f32[4,64,128]{2,1,0:T(8,128)} %get-tuple-element.64), channel_id=1, source_target_pairs={{0,8},{4,12},{8,0},{12,4},{16,24},{20,28},{24,16},{28,20},{1,9},{5... | collective-permute-start | bytes 393224 | tf_op jit(solution)/shard_map/ppermute | solution.py:127
  14.9 15.1 %collective-permute-start.8 = (f32[1,256,512]{2,1,0:T(8,128)}, f32[1,256,512]{2,1,0:T(8,128)}, u32[]{:S(2)}, u32[]{:S(2)}) collective-permute-start(f32[1,256,512]{2,1,0:T(8,128)} %get-tuple-element.68), channel_id=1, source_target_pairs={{0,16},{4,20},{8,24},{12,28},{16,0},{20,4},{24,8},{28,12},{1,17},{... | collective-permute-start | bytes 1572872 | tf_op jit(solution)/shard_map/ppermute | solution.py:127
  14.9 15.1 %collective-permute-start.9 = (f32[1,256,512]{2,1,0:T(8,128)}, f32[1,256,512]{2,1,0:T(8,128)}, u32[]{:S(2)}, u32[]{:S(2)}) collective-permute-start(f32[1,256,512]{2,1,0:T(8,128)} %get-tuple-element.69), channel_id=1, source_target_pairs={{0,1},{1,0},{2,3},{3,2},{4,5},{5,4},{6,7},{7,6},{8,9},{9,8},{10,11... | collective-permute-start | bytes 1572872 | tf_op jit(solution)/shard_map/ppermute | solution.py:127
  17.0 24.2 %collective-permute-start.7 = (f32[1,256,512]{2,1,0:T(8,128)}, f32[1,256,512]{2,1,0:T(8,128)}, u32[]{:S(2)}, u32[]{:S(2)}) collective-permute-start(f32[1,256,512]{2,1,0:T(8,128)} %get-tuple-element.67), channel_id=1, source_target_pairs={{0,8},{4,12},{8,0},{12,4},{16,24},{20,28},{24,16},{28,20},{1,9},{5... | collective-permute-start | bytes 1572872 | tf_op jit(solution)/shard_map/ppermute | solution.py:127
  24.7 16.5 %collective-permute-start.6 = (f32[1,256,512]{2,1,0:T(8,128)}, f32[1,256,512]{2,1,0:T(8,128)S(1)}, u32[]{:S(2)}, u32[]{:S(2)}) collective-permute-start(f32[1,256,512]{2,1,0:T(8,128)} %get-tuple-element.66.refs_1_), channel_id=1, source_target_pairs={{0,16},{4,20},{8,24},{12,28},{16,0},{20,4},{24,8},{28,12},{1,17},{... | collective-permute-start | bytes 1572872 | tf_op jit(solution)/shard_map/ppermute | solution.py:127
  24.8 5.2 %collective-permute-start.10 = (f32[32,512]{1,0:T(8,128)}, f32[32,512]{1,0:T(8,128)S(1)}, u32[]{:S(2)}, u32[]{:S(2)}) collective-permute-start(f32[32,512]{1,0:T(8,128)} %get-tuple-element.71), channel_id=1, source_target_pairs={{0,4},{4,0},{8,12},{12,8},{16,20},{20,16},{24,28},{28,24},{1,5},{5... | collective-permute-start | bytes 196616 | tf_op jit(solution)/shard_map/ppermute | solution.py:127
  30.0 0.8 copy-start.4
  30.9 10.3 %copy-start.5 = (f32[32,512]{1,0:T(8,128)S(1)}, f32[32,512]{1,0:T(8,128)}, u32[]{:S(2)}) copy-start(f32[32,512]{1,0:T(8,128)} %get-tuple-element.70.refs_2_.refs_8_) | copy-start | bytes 196612
  30.9 7.0 %collective-permute-start.11 = (f32[32,512]{1,0:T(8,128)S(1)}, f32[32,512]{1,0:T(8,128)S(1)}, u32[]{:S(2)}, u32[]{:S(2)}) collective-permute-start(f32[32,512]{1,0:T(8,128)S(1)} %shard_map.186.refs_2_), channel_id=1, source_target_pairs={{0,1},{1,0},{2,3},{3,2},{4,5},{5,4},{6,7},{7,6},{8,9},{9,8},{10,11... | collective-permute-start | bytes 196616 | tf_op jit(solution)/shard_map/ppermute | solution.py:127
  32.5 6.5 %collective-permute-start.12 = (f32[32,512]{1,0:T(8,128)S(1)}, f32[32,512]{1,0:T(8,128)S(1)}, u32[]{:S(2)}, u32[]{:S(2)}) collective-permute-start(f32[32,512]{1,0:T(8,128)S(1)} %shard_map.186.refs_2_), channel_id=1, source_target_pairs={{0,2},{1,3},{2,0},{3,1},{4,6},{5,7},{6,4},{7,5},{8,10},{9,11},{10,... | collective-permute-start | bytes 196616 | tf_op jit(solution)/shard_map/ppermute | solution.py:127
  35.1 6.1 %collective-permute-start.13 = (f32[32,512]{1,0:T(8,128)S(1)}, f32[32,512]{1,0:T(8,128)S(1)}, u32[]{:S(2)}, u32[]{:S(2)}) collective-permute-start(f32[32,512]{1,0:T(8,128)S(1)} %shard_map.186.refs_2_), channel_id=1, source_target_pairs={{0,3},{1,2},{2,1},{3,0},{4,7},{5,6},{6,5},{7,4},{8,11},{9,10},{10,... | collective-permute-start | bytes 196616 | tf_op jit(solution)/shard_map/ppermute | solution.py:127
  35.3 1.2 %copy-start = (f32[2,256,512]{2,1,0:T(8,128)S(1)}, f32[2,256,512]{2,1,0:T(8,128)}, u32[]{:S(2)}) copy-start(f32[2,256,512]{2,1,0:T(8,128)} %refs_0_.7) | copy-start | bytes 3145732
  41.2 8.4 %copy-start.2 = (f32[1,256,512]{2,1,0:T(8,128)S(1)}, f32[1,256,512]{2,1,0:T(8,128)}, u32[]{:S(2)}) copy-start(f32[1,256,512]{2,1,0:T(8,128)} %get-tuple-element.66.refs_1_) | copy-start | bytes 1572868
  41.6 13.6 %copy-start.3 = (f32[256,512]{1,0:T(8,128)S(1)}, f32[256,512]{1,0:T(8,128)}, u32[]{:S(2)}) copy-start(f32[256,512]{1,0:T(8,128)} %refs_0_.5) | copy-start | bytes 1572868
  41.6 7.9 %collective-permute-start.14 = (f32[1,256,512]{2,1,0:T(8,128)S(1)}, f32[1,256,512]{2,1,0:T(8,128)S(1)}, u32[]{:S(2)}, u32[]{:S(2)}) collective-permute-start(f32[1,256,512]{2,1,0:T(8,128)S(1)} %get-tuple-element.75.refs_3_), channel_id=1, source_target_pairs={{0,4},{4,0},{8,12},{12,8},{16,20},{20,16},{24,28},{28,24},{1,5},{5... | collective-permute-start | bytes 1572872 | tf_op jit(solution)/shard_map/ppermute | solution.py:127
  41.7 4.9 %collective-permute-start.15 = (f32[40,512]{1,0:T(8,128)S(1)}, f32[40,512]{1,0:T(8,128)S(1)}, u32[]{:S(2)}, u32[]{:S(2)}) collective-permute-start(f32[40,512]{1,0:T(8,128)S(1)} %get-tuple-element.77), channel_id=1, source_target_pairs={{0,8},{4,12},{8,0},{12,4},{16,24},{20,28},{24,16},{28,20},{1,9},{5... | collective-permute-start | bytes 245768 | tf_op jit(solution)/shard_map/ppermute | solution.py:127
  43.2 6.3 %collective-permute-start.16 = (f32[40,512]{1,0:T(8,128)S(1)}, f32[40,512]{1,0:T(8,128)S(1)}, u32[]{:S(2)}, u32[]{:S(2)}) collective-permute-start(f32[40,512]{1,0:T(8,128)S(1)} %get-tuple-element.78), channel_id=1, source_target_pairs={{0,16},{4,20},{8,24},{12,28},{16,0},{20,4},{24,8},{28,12},{1,17},{... | collective-permute-start | bytes 245768 | tf_op jit(solution)/shard_map/ppermute | solution.py:127
  43.9 5.6 %collective-permute-start.17 = (f32[40,512]{1,0:T(8,128)S(1)}, f32[40,512]{1,0:T(8,128)S(1)}, u32[]{:S(2)}, u32[]{:S(2)}) collective-permute-start(f32[40,512]{1,0:T(8,128)S(1)} %get-tuple-element.74.refs_2_), channel_id=1, source_target_pairs={{0,24},{4,28},{8,16},{12,20},{16,8},{20,12},{24,0},{28,4},{1,25},{... | collective-permute-start | bytes 245768 | tf_op jit(solution)/shard_map/ppermute | solution.py:127
  45.2 8.6 %collective-permute-start.22 = (f32[256,512]{1,0:T(8,128)}, f32[256,512]{1,0:T(8,128)S(1)}, u32[]{:S(2)}, u32[]{:S(2)}) collective-permute-start(f32[256,512]{1,0:T(8,128)} %get-tuple-element.84.refs_2_), channel_id=1, source_target_pairs={{0,4},{4,0},{8,12},{12,8},{16,20},{20,16},{24,28},{28,24},{1,5},{5... | collective-permute-start | bytes 1572872 | tf_op jit(solution)/shard_map/ppermute | solution.py:127
  49.6 5.6 %collective-permute-start.21 = (f32[1,256,512]{2,1,0:T(8,128)S(1)}, f32[1,256,512]{2,1,0:T(8,128)S(1)}, u32[]{:S(2)}, u32[]{:S(2)}) collective-permute-start(f32[1,256,512]{2,1,0:T(8,128)S(1)} %get-tuple-element.83.refs_1_), channel_id=1, source_target_pairs={{0,4},{4,0},{8,12},{12,8},{16,20},{20,16},{24,28},{28,24},{1,5},{5... | collective-permute-start | bytes 1572872 | tf_op jit(solution)/shard_map/ppermute | solution.py:127
  49.7 14.6 %collective-permute-start.26 = (f32[1,256,512]{2,1,0:T(8,128)}, f32[1,256,512]{2,1,0:T(8,128)S(1)}, u32[]{:S(2)}, u32[]{:S(2)}) collective-permute-start(f32[1,256,512]{2,1,0:T(8,128)} %get-tuple-element.85.refs_8_), channel_id=1, source_target_pairs={{0,16},{4,20},{8,24},{12,28},{16,0},{20,4},{24,8},{28,12},{1,17},{... | collective-permute-start | bytes 1572872 | tf_op jit(solution)/shard_map/ppermute | solution.py:127
  50.8 7.0 %collective-permute-start.18 = (f32[40,512]{1,0:T(8,128)S(1)}, f32[40,512]{1,0:T(8,128)S(1)}, u32[]{:S(2)}, u32[]{:S(2)}) collective-permute-start(f32[40,512]{1,0:T(8,128)S(1)} %get-tuple-element.80), channel_id=1, source_target_pairs={{0,1},{1,0},{2,3},{3,2},{4,5},{5,4},{6,7},{7,6},{8,9},{9,8},{10,11... | collective-permute-start | bytes 245768 | tf_op jit(solution)/shard_map/ppermute | solution.py:127
  51.2 9.6 %collective-permute-start.19 = (f32[40,512]{1,0:T(8,128)S(1)}, f32[40,512]{1,0:T(8,128)S(1)}, u32[]{:S(2)}, u32[]{:S(2)}) collective-permute-start(f32[40,512]{1,0:T(8,128)S(1)} %get-tuple-element.81), channel_id=1, source_target_pairs={{0,2},{1,3},{2,0},{3,1},{4,6},{5,7},{6,4},{7,5},{8,10},{9,11},{10,... | collective-permute-start | bytes 245768 | tf_op jit(solution)/shard_map/ppermute | solution.py:127
  53.8 7.0 %collective-permute-start.20 = (f32[40,512]{1,0:T(8,128)S(1)}, f32[40,512]{1,0:T(8,128)S(1)}, u32[]{:S(2)}, u32[]{:S(2)}) collective-permute-start(f32[40,512]{1,0:T(8,128)S(1)} %get-tuple-element.82.refs_2_), channel_id=1, source_target_pairs={{0,3},{1,2},{2,1},{3,0},{4,7},{5,6},{6,5},{7,4},{8,11},{9,10},{10,... | collective-permute-start | bytes 245768 | tf_op jit(solution)/shard_map/ppermute | solution.py:127
  60.8 8.3 %copy-start.1 = (f32[2,256,512]{2,1,0:T(8,128)S(1)}, f32[2,256,512]{2,1,0:T(8,128)}, u32[]{:S(2)}) copy-start(f32[2,256,512]{2,1,0:T(8,128)} %refs_0_.7) | copy-start | bytes 3145732
  64.2 4.9 %collective-permute-start.27 = (f32[2,256,512]{2,1,0:T(8,128)S(1)}, f32[2,256,512]{2,1,0:T(8,128)S(1)}, u32[]{:S(2)}, u32[]{:S(2)}) collective-permute-start(f32[2,256,512]{2,1,0:T(8,128)S(1)} %get-tuple-element.90.refs_1_.refs_2_), channel_id=1, source_target_pairs={{0,4},{4,0},{8,12},{12,8},{16,20},{20,16},{24,28},{28,24},{1,5},{5... | collective-permute-start | bytes 3145736 | tf_op jit(solution)/shard_map/ppermute | solution.py:127
  64.2 4.9 %collective-permute-start.28 = (f32[1,256,512]{2,1,0:T(8,128)S(1)}, f32[1,256,512]{2,1,0:T(8,128)S(1)}, u32[]{:S(2)}, u32[]{:S(2)}) collective-permute-start(f32[1,256,512]{2,1,0:T(8,128)S(1)} %get-tuple-element.91.refs_3_), channel_id=1, source_target_pairs={{0,4},{4,0},{8,12},{12,8},{16,20},{20,16},{24,28},{28,24},{1,5},{5... | collective-permute-start | bytes 1572872 | tf_op jit(solution)/shard_map/ppermute | solution.py:127
  64.7 6.4 %collective-permute-start.23 = (f32[32,512]{1,0:T(8,128)S(1)}, f32[32,512]{1,0:T(8,128)S(1)}, u32[]{:S(2)}, u32[]{:S(2)}) collective-permute-start(f32[32,512]{1,0:T(8,128)S(1)} %get-tuple-element.88.refs_2_.refs_0_), channel_id=1, source_target_pairs={{0,1},{1,0},{2,3},{3,2},{4,5},{5,4},{6,7},{7,6},{8,9},{9,8},{10,11... | collective-permute-start | bytes 196616 | tf_op jit(solution)/shard_map/ppermute | solution.py:127
  65.1 7.8 %collective-permute-start.24 = (f32[32,512]{1,0:T(8,128)S(1)}, f32[32,512]{1,0:T(8,128)S(1)}, u32[]{:S(2)}, u32[]{:S(2)}) collective-permute-start(f32[32,512]{1,0:T(8,128)S(1)} %get-tuple-element.88.refs_2_.refs_0_), channel_id=1, source_target_pairs={{0,2},{1,3},{2,0},{3,1},{4,6},{5,7},{6,4},{7,5},{8,10},{9,11},{10,... | collective-permute-start | bytes 196616 | tf_op jit(solution)/shard_map/ppermute | solution.py:127
  67.7 6.2 %collective-permute-start.25 = (f32[32,512]{1,0:T(8,128)S(1)}, f32[32,512]{1,0:T(8,128)S(1)}, u32[]{:S(2)}, u32[]{:S(2)}) collective-permute-start(f32[32,512]{1,0:T(8,128)S(1)} %get-tuple-element.88.refs_2_.refs_0_), channel_id=1, source_target_pairs={{0,3},{1,2},{2,1},{3,0},{4,7},{5,6},{6,5},{7,4},{8,11},{9,10},{10,... | collective-permute-start | bytes 196616 | tf_op jit(solution)/shard_map/ppermute | solution.py:127
  76.0 5.3 %collective-permute-start.29 = (f32[32,512]{1,0:T(8,128)S(1)}, f32[32,512]{1,0:T(8,128)S(1)}, u32[]{:S(2)}, u32[]{:S(2)}) collective-permute-start(f32[32,512]{1,0:T(8,128)S(1)} %get-tuple-element.95), channel_id=1, source_target_pairs={{0,1},{1,0},{2,3},{3,2},{4,5},{5,4},{6,7},{7,6},{8,9},{9,8},{10,11... | collective-permute-start | bytes 196616 | tf_op jit(solution)/shard_map/ppermute | solution.py:127
  77.1 6.2 %collective-permute-start.30 = (f32[32,512]{1,0:T(8,128)S(1)}, f32[32,512]{1,0:T(8,128)S(1)}, u32[]{:S(2)}, u32[]{:S(2)}) collective-permute-start(f32[32,512]{1,0:T(8,128)S(1)} %get-tuple-element.96), channel_id=1, source_target_pairs={{0,2},{1,3},{2,0},{3,1},{4,6},{5,7},{6,4},{7,5},{8,10},{9,11},{10,... | collective-permute-start | bytes 196616 | tf_op jit(solution)/shard_map/ppermute | solution.py:127
  78.4 6.2 %collective-permute-start.31 = (f32[32,512]{1,0:T(8,128)S(1)}, f32[32,512]{1,0:T(8,128)S(1)}, u32[]{:S(2)}, u32[]{:S(2)}) collective-permute-start(f32[32,512]{1,0:T(8,128)S(1)} %get-tuple-element.97), channel_id=1, source_target_pairs={{0,3},{1,2},{2,1},{3,0},{4,7},{5,6},{6,5},{7,4},{8,11},{9,10},{10,... | collective-permute-start | bytes 196616 | tf_op jit(solution)/shard_map/ppermute | solution.py:127
  85.9 5.7 %collective-permute-start.32 = (f32[40,512]{1,0:T(8,128)S(1)}, f32[40,512]{1,0:T(8,128)S(1)}, u32[]{:S(2)}, u32[]{:S(2)}) collective-permute-start(f32[40,512]{1,0:T(8,128)S(1)} %get-tuple-element.99), channel_id=1, source_target_pairs={{0,1},{1,0},{2,3},{3,2},{4,5},{5,4},{6,7},{7,6},{8,9},{9,8},{10,11... | collective-permute-start | bytes 245768 | tf_op jit(solution)/shard_map/ppermute | solution.py:127
  86.6 6.4 %collective-permute-start.33 = (f32[40,512]{1,0:T(8,128)S(1)}, f32[40,512]{1,0:T(8,128)S(1)}, u32[]{:S(2)}, u32[]{:S(2)}) collective-permute-start(f32[40,512]{1,0:T(8,128)S(1)} %get-tuple-element.100), channel_id=1, source_target_pairs={{0,2},{1,3},{2,0},{3,1},{4,6},{5,7},{6,4},{7,5},{8,10},{9,11},{10,... | collective-permute-start | bytes 245768 | tf_op jit(solution)/shard_map/ppermute | solution.py:127
  88.4 6.2 %collective-permute-start.34 = (f32[40,512]{1,0:T(8,128)S(1)}, f32[40,512]{1,0:T(8,128)S(1)}, u32[]{:S(2)}, u32[]{:S(2)}) collective-permute-start(f32[40,512]{1,0:T(8,128)S(1)} %get-tuple-element.101), channel_id=1, source_target_pairs={{0,3},{1,2},{2,1},{3,0},{4,7},{5,6},{6,5},{7,4},{8,11},{9,10},{10,... | collective-permute-start | bytes 245768 | tf_op jit(solution)/shard_map/ppermute | solution.py:127
  94.7 3.6 %collective-permute-start.38 = (f32[1,256,512]{2,1,0:T(8,128)}, f32[1,256,512]{2,1,0:T(8,128)S(1)}, u32[]{:S(2)}, u32[]{:S(2)}) collective-permute-start(f32[1,256,512]{2,1,0:T(8,128)} %shard_map.199.refs_2_), channel_id=1, source_target_pairs={{0,4},{4,0},{8,12},{12,8},{16,20},{20,16},{24,28},{28,24},{1,5},{5... | collective-permute-start | bytes 1572872 | tf_op jit(solution)/shard_map/ppermute | solution.py:127
  94.8 5.2 %collective-permute-start.35 = (f32[40,512]{1,0:T(8,128)S(1)}, f32[40,512]{1,0:T(8,128)S(1)}, u32[]{:S(2)}, u32[]{:S(2)}) collective-permute-start(f32[40,512]{1,0:T(8,128)S(1)} %get-tuple-element.104), channel_id=1, source_target_pairs={{0,8},{4,12},{8,0},{12,4},{16,24},{20,28},{24,16},{28,20},{1,9},{5... | collective-permute-start | bytes 245768 | tf_op jit(solution)/shard_map/ppermute | solution.py:127
  95.4 4.6 %collective-permute-start.36 = (f32[40,512]{1,0:T(8,128)S(1)}, f32[40,512]{1,0:T(8,128)S(1)}, u32[]{:S(2)}, u32[]{:S(2)}) collective-permute-start(f32[40,512]{1,0:T(8,128)S(1)} %get-tuple-element.105), channel_id=1, source_target_pairs={{0,16},{4,20},{8,24},{12,28},{16,0},{20,4},{24,8},{28,12},{1,17},{... | collective-permute-start | bytes 245768 | tf_op jit(solution)/shard_map/ppermute | solution.py:127
  96.6 5.3 %collective-permute-start.37 = (f32[40,512]{1,0:T(8,128)S(1)}, f32[40,512]{1,0:T(8,128)S(1)}, u32[]{:S(2)}, u32[]{:S(2)}) collective-permute-start(f32[40,512]{1,0:T(8,128)S(1)} %get-tuple-element.106.refs_1_), channel_id=1, source_target_pairs={{0,24},{4,28},{8,16},{12,20},{16,8},{20,12},{24,0},{28,4},{1,25},{... | collective-permute-start | bytes 245768 | tf_op jit(solution)/shard_map/ppermute | solution.py:127
  102.7 5.2 %collective-permute-start.39 = (f32[32,512]{1,0:T(8,128)S(1)}, f32[32,512]{1,0:T(8,128)S(1)}, u32[]{:S(2)}, u32[]{:S(2)}) collective-permute-start(f32[32,512]{1,0:T(8,128)S(1)} %get-tuple-element.110), channel_id=1, source_target_pairs={{0,2},{1,3},{2,0},{3,1},{4,6},{5,7},{6,4},{7,5},{8,10},{9,11},{10,... | collective-permute-start | bytes 196616 | tf_op jit(solution)/shard_map/ppermute | solution.py:127
  108.0 1.3 %collective-permute-start.40 = (f32[32,512]{1,0:T(8,128)S(1)}, f32[32,512]{1,0:T(8,128)S(1)}, u32[]{:S(2)}, u32[]{:S(2)}) collective-permute-start(f32[32,512]{1,0:T(8,128)S(1)} %get-tuple-element.113), channel_id=1, source_target_pairs={{0,4},{4,0},{8,12},{12,8},{16,20},{20,16},{24,28},{28,24},{1,5},{5... | collective-permute-start | bytes 196616 | tf_op jit(solution)/shard_map/ppermute | solution.py:127
